TPU v7x, 512 devices: a whole 4x8x8 slice. The times are simulated.
512 devices in a mesh: tm: 32 (over x, y), rows: 16 (over z, core).
Axes of the slice: x: 4, y: 8, z: 8, core: 2. Of those that a mesh axis runs over, the one named last changes fastest.
Arguments:
- frames: bfloat16 [32, 128, 128, 128], P('tm', 'rows'), may hold values from -6 to 6
- kernel: bfloat16 [3, 3, 3, 128, 128], replicated, may hold values from -0.109375 to 0.109375
- cotangent: bfloat16 [32, 128, 128, 128], P('tm', 'rows'), may hold values from -6 to 6
Outputs:
- code: bfloat16 [32, 128, 128, 128], P('tm', 'rows')
- grad_frames: bfloat16 [32, 128, 128, 128], P('tm', 'rows')
- grad_kernel: float32 [3, 3, 3, 128, 128], replicated
All inputs are finite; a program needn't handle non-finite values.
Results may differ from a plain program's by a relative error of at most 0.013.
Values may be sent and summed in bfloat16 or wider, within the bound.
No kernel may reach another device: no remote copies, remote signals or barrier semaphores. Data moves between devices by JAX's collectives and lax.ppermute only.
A program may use at most 64 MiB of HBM per device.

v0:
```python
import math

import jax
import jax.numpy as jnp
from jax import lax
from jax.sharding import PartitionSpec as P

LEVELS = 3


band_weight = 0.75
root_half = 0.7071067811865476


def passed_along(block, axis, distance):
    devices = range(lax.axis_size(axis))
    route = [(i - distance, i) for i in devices if i - distance in devices]
    return lax.ppermute(block, axis, route)


def extended(value, sides, width):
    for axis, dim in sides:
        count, length = (lax.axis_size(axis), value.shape[dim])
        up = [(i, (i + 1) % count) for i in range(count - 1)]
        down = [(j, i) for i, j in up]
        last = lax.slice_in_dim(value, length - width, length, axis=dim)
        initial = lax.slice_in_dim(value, 0, width, axis=dim)
        before = lax.ppermute(last, axis, up)
        after = lax.ppermute(initial, axis, down)
        value = jnp.concatenate([before, value, after], axis=dim)
    return value


def from_partner(block, axis, stride):
    count = lax.axis_size(axis)
    route = []
    for low in range(count):
        high = low | 1 << stride
        if high != low and high < count:
            route += [(low, high), (high, low)]
    return lax.ppermute(block, axis, route)


def time_taps(source, direction):
    nearer = passed_along(source, "tm", direction)
    farther = passed_along(source, "tm", 2 * direction)
    stacked = jnp.concatenate([farther, nearer, source], axis=0)
    framed = extended(stacked, (("rows", 1),), 1)
    return jnp.pad(framed, ((0, 0), (0, 0), (1, 1), (0, 0)))


def spread_taps(framed, kernel, row_count, col_count):
    summed_taps = None
    for frame_tap in range(3):
        for row_tap in range(3):
            row_slab = framed[frame_tap, row_tap : row_tap + row_count]
            spread = jnp.einsum(
                "rwc,jcd->rwjd",
                row_slab,
                kernel[frame_tap, row_tap],
                preferred_element_type=jnp.float32,
            )
            partial_value = (
                spread[:, 0:col_count, 0]
                + spread[:, 1 : col_count + 1, 1]
                + spread[:, 2 : col_count + 2, 2]
            )
            summed_taps = partial_value if summed_taps is None else summed_taps + partial_value
    return summed_taps


def adjoint_taps(framed, kernel, row_count, col_count):
    summed_taps = None
    for frame_tap in range(3):
        for row_tap in range(3):
            row_slab = framed[frame_tap, 2 - row_tap : 2 - row_tap + row_count]
            spread = jnp.einsum(
                "rwd,jcd->rwjc",
                row_slab,
                kernel[frame_tap, row_tap],
                preferred_element_type=jnp.float32,
            )
            partial_value = (
                spread[:, 2 : col_count + 2, 0]
                + spread[:, 1 : col_count + 1, 1]
                + spread[:, 0:col_count, 2]
            )
            summed_taps = partial_value if summed_taps is None else summed_taps + partial_value
    return summed_taps


def weight_terms(framed, grad_linear, row_count, col_count):
    tap_blocks = []
    for frame_tap in range(3):
        for row_tap in range(3):
            row_slab = framed[frame_tap, row_tap : row_tap + row_count]
            shifted = jnp.stack(
                [row_slab[:, col_tap : col_tap + col_count] for col_tap in range(3)]
            )
            tap_blocks.append(
                jnp.einsum(
                    "jrwc,rwd->jcd", shifted, grad_linear, preferred_element_type=jnp.float32
                )
            )
    channels = grad_linear.shape[2]
    return jnp.stack(tap_blocks).reshape(3, 3, 3, channels, channels)


def sign_of(frame_index, degree):
    return (2 * (frame_index >> degree & 1) - 1).astype(jnp.float32)


def shards(frames, kernel, cotangent):
    row_count = frames.shape[1]
    col_count = frames.shape[2]
    frame_index = lax.axis_index("tm")
    framed = time_taps(frames, 1)
    linear = spread_taps(framed, kernel, row_count, col_count)
    gate_value = jax.nn.sigmoid(linear)
    active = (linear * gate_value).astype(jnp.bfloat16)
    coarse = active
    detail = jnp.zeros(linear.shape, jnp.float32)
    for degree in range(LEVELS):
        remote_band = from_partner(coarse, "tm", degree)
        current = coarse.astype(jnp.float32)
        remote = remote_band.astype(jnp.float32)
        smooth = (current + remote) * root_half
        detail = detail + sign_of(frame_index, degree) * (current - remote) * root_half
        coarse = smooth.astype(jnp.bfloat16) if degree < LEVELS - 1 else smooth
    code = (coarse + band_weight * detail).astype(jnp.bfloat16)
    incoming = cotangent[0]
    upstream = incoming.astype(jnp.float32)
    top_level = LEVELS - 1
    opposite = from_partner(incoming, "tm", top_level)
    pair_sum = upstream + opposite.astype(jnp.float32)
    carried = (
        pair_sum * root_half
        + band_weight * sign_of(frame_index, top_level) * (pair_sum * root_half)
    ).astype(jnp.bfloat16)
    for degree in range(LEVELS - 2, -1, -1):
        peer_back, peer_flow = from_partner((carried, incoming), "tm", degree)
        returned = carried.astype(jnp.float32)
        summed = (returned + peer_back.astype(jnp.float32)) * root_half + band_weight * sign_of(
            frame_index, degree
        ) * ((upstream + peer_flow.astype(jnp.float32)) * root_half)
        carried = summed.astype(jnp.bfloat16) if degree > 0 else summed
    derivative = gate_value * (1.0 + linear * (1.0 - gate_value))
    grad_linear = (carried * derivative).astype(jnp.bfloat16)
    framed_back = time_taps(grad_linear[None], -1)
    grad_frames = adjoint_taps(framed_back, kernel, row_count, col_count).astype(jnp.bfloat16)
    local_terms = weight_terms(framed, grad_linear, row_count, col_count)
    weight_sum = lax.psum(local_terms, ("tm", "rows"))
    norm_factor = 1.0 / math.sqrt(
        lax.axis_size("tm") * lax.axis_size("rows") * row_count * col_count
    )
    return (code[None], grad_frames[None], weight_sum * norm_factor)


def solution(mesh):
    in_specs = (P("tm", "rows", None, None), P(), P("tm", "rows", None, None))
    out_specs = (P("tm", "rows", None, None), P("tm", "rows", None, None), P())
    return jax.shard_map(shards, mesh=mesh, in_specs=in_specs, out_specs=out_specs, check_vma=False)
```

profile of v0, /device:TPU:1, one launch (start us, length us, event | category | flops | bytes accessed | tf_op | source)
XLA Modules:
  0.0 399.9 jit_solution(17728512806155164959)
XLA Ops:
  7.2 5.2 %collective-permute-start = (bf16[1,8,128,128]{3,2,1,0:T(8,128)(2,1)}, bf16[1,8,128,128]{3,2,1,0:T(8,128)(2,1)S(1)}, u32[]{:S(2)}, u32[]{:S(2)}) collective-permute-start(bf16[1,8,128,128]{3,2,1,0:T(8,128)(2,1)} %param.3), channel_id=1, source_target_pairs={{0,32},{16,48},{32,64},{48,80},{64,96},{80,112},{96,128},{112,144}... | collective-permute-start | bytes 786440 | tf_op jit(solution)/shard_map/ppermute | solution.py:18
  12.4 3.2 collective-permute-start.1
  15.6 4.4 %collective-permute-start.11 = (bf16[8,128,128]{2,1,0:T(8,128)(2,1)}, bf16[8,128,128]{2,1,0:T(8,128)(2,1)S(1)}, u32[]{:S(2)}, u32[]{:S(2)}) collective-permute-start(bf16[8,128,128]{2,1,0:T(8,128)(2,1)} %bitcast.320), channel_id=1, source_target_pairs={{0,16},{16,0},{32,48},{48,32},{64,80},{80,64},{96,112},{112,96},{1... | collective-permute-start | bytes 786440 | tf_op jit(solution)/shard_map/ppermute | solution.py:41
  20.0 2.4 collective-permute-start.9
  22.5 4.5 %collective-permute-start.7 = (bf16[8,128,128]{2,1,0:T(8,128)(2,1)}, bf16[8,128,128]{2,1,0:T(8,128)(2,1)S(1)}, u32[]{:S(2)}, u32[]{:S(2)}) collective-permute-start(bf16[8,128,128]{2,1,0:T(8,128)(2,1)} %bitcast.322), channel_id=1, source_target_pairs={{0,64},{64,0},{16,80},{80,16},{32,96},{96,32},{48,112},{112,48},{1... | collective-permute-start | bytes 786440 | tf_op jit(solution)/shard_map/ppermute | solution.py:41
  27.2 1.1 constant_dynamic-update-slice_fusion
  28.3 8.1 %collective-permute-start.3 = (bf16[3,1,128,128]{3,2,1,0:T(8,128)(2,1)S(1)}, bf16[3,1,128,128]{3,2,1,0:T(8,128)(2,1)S(1)}, u32[]{:S(2)}, u32[]{:S(2)}) collective-permute-start(bf16[3,1,128,128]{3,2,1,0:T(8,128)(2,1)S(1)} %get-tuple-element.17), channel_id=1, source_target_pairs={{1,0},{2,1},{3,2},{4,3},{5,4},{6,5},{7,6},{8,7},{9,8},{10,9},{11,1... | collective-permute-start | bytes 294920 | tf_op jit(solution)/shard_map/ppermute | solution.py:29
  36.4 2.3 collective-permute-start.2
  38.7 12.0 %collective-permute-done.7 = bf16[8,128,128]{2,1,0:T(8,128)(2,1)S(1)} collective-permute-done((bf16[8,128,128]{2,1,0:T(8,128)(2,1)}, bf16[8,128,128]{2,1,0:T(8,128)(2,1)S(1)}, u32[]{:S(2)}, u32[]{:S(2)}) %collective-permute-start.7) | collective-permute-done | bytes 262176 | tf_op jit(solution)/shard_map/ppermute | solution.py:41
  50.7 13.5 %collective-permute-start.8 = (bf16[8,128,128]{2,1,0:T(8,128)(2,1)S(1)}, bf16[8,128,128]{2,1,0:T(8,128)(2,1)S(1)}, u32[]{:S(2)}, u32[]{:S(2)}) collective-permute-start(bf16[8,128,128]{2,1,0:T(8,128)(2,1)S(1)} %fusion.70), channel_id=1, source_target_pairs={{0,32},{32,0},{16,48},{48,16},{64,96},{96,64},{80,112},{112,80},{1... | collective-permute-start | bytes 786440 | tf_op jit(solution)/shard_map/ppermute | solution.py:41
  64.2 0.4 select_maximum_fusion.4
  64.6 0.4 fusion.105
  65.0 0.4 fusion.107
  65.5 0.4 fusion.109
  65.9 0.4 fusion.111
  66.3 0.4 fusion.113
  66.8 0.4 fusion.115
  67.2 0.4 fusion.117
  67.7 0.4 slice_bitcast_fusion.45
  68.0 1.1 slice_bitcast_fusion.38
  69.1 1.1 slice_bitcast_fusion.32
  70.2 0.3 slice_bitcast_fusion.26
  70.6 0.4 slice_bitcast_fusion.20
  70.9 0.4 fusion.119
  71.4 0.2 fusion.73
  71.6 1.9 collective-permute-start.10
  73.5 0.4 fusion.121
  74.1 5.6 %collective-permute-done.10 = bf16[8,128,128]{2,1,0:T(8,128)(2,1)S(1)} collective-permute-done((bf16[8,128,128]{2,1,0:T(8,128)(2,1)S(1)}, bf16[8,128,128]{2,1,0:T(8,128)(2,1)S(1)}, u32[]{:S(2)}, u32[]{:S(2)}) %collective-permute-start.10) | collective-permute-done | bytes 262176 | tf_op jit(solution)/shard_map/ppermute | solution.py:41
  79.7 1.7 fusion.77
  81.5 1.4 collective-permute-start.13
  82.9 1.3 collective-permute-start.12
  84.2 0.8 multiply_convert_fusion
  85.1 4.0 collective-permute-start.4
  89.1 1.1 fusion.9
  90.2 1.1 fusion.8
  91.2 1.1 fusion.7
  92.3 1.1 fusion.6
  93.4 1.1 fusion.5
  94.5 1.1 fusion.4
  95.6 1.1 fusion.3
  96.7 1.1 fusion.2
  97.8 1.1 fusion.1
  99.1 5.8 %collective-permute-start.15 = (bf16[3,1,128,128]{3,2,1,0:T(8,128)(2,1)S(1)}, bf16[3,1,128,128]{3,2,1,0:T(8,128)(2,1)S(1)}, u32[]{:S(2)}, u32[]{:S(2)}) collective-permute-start(bf16[3,1,128,128]{3,2,1,0:T(8,128)(2,1)S(1)} %get-tuple-element.15), channel_id=1, source_target_pairs={{1,0},{2,1},{3,2},{4,3},{5,4},{6,5},{7,6},{8,7},{9,8},{10,9},{11,1... | collective-permute-start | bytes 294920 | tf_op jit(solution)/shard_map/ppermute | solution.py:29
  104.9 4.0 %collective-permute-start.14 = (bf16[3,1,128,128]{3,2,1,0:T(8,128)(2,1)S(1)}, bf16[3,1,128,128]{3,2,1,0:T(8,128)(2,1)S(1)}, u32[]{:S(2)}, u32[]{:S(2)}) collective-permute-start(bf16[3,1,128,128]{3,2,1,0:T(8,128)(2,1)S(1)} %get-tuple-element.14), channel_id=1, source_target_pairs={{0,1},{1,2},{2,3},{3,4},{4,5},{5,6},{6,7},{7,8},{8,9},{9,10},{10,1... | collective-permute-start | bytes 294920 | tf_op jit(solution)/shard_map/ppermute | solution.py:28
  109.0 0.2 fusion.57
  109.2 4.2 %collective-permute-start.5 = (bf16[8,128,128]{2,1,0:T(8,128)(2,1)S(1)}, bf16[8,128,128]{2,1,0:T(8,128)(2,1)S(1)}, u32[]{:S(2)}, u32[]{:S(2)}) collective-permute-start(bf16[8,128,128]{2,1,0:T(8,128)(2,1)S(1)} %fusion.57), channel_id=1, source_target_pairs={{0,32},{32,0},{16,48},{48,16},{64,96},{96,64},{80,112},{112,80},{1... | collective-permute-start | bytes 786440 | tf_op jit(solution)/shard_map/ppermute | solution.py:41
  113.4 0.4 select_maximum_fusion
  113.8 0.5 fusion.96
  114.2 0.5 fusion.97
  114.7 0.5 fusion.98
  115.2 0.5 fusion.99
  115.7 0.5 fusion.100
  116.1 0.5 fusion.101
  116.6 0.5 fusion.102
  117.1 0.5 fusion.103
  117.6 0.5 fusion.104
  118.0 6.9 %collective-permute-done.5 = bf16[8,128,128]{2,1,0:T(8,128)(2,1)S(1)} collective-permute-done((bf16[8,128,128]{2,1,0:T(8,128)(2,1)S(1)}, bf16[8,128,128]{2,1,0:T(8,128)(2,1)S(1)}, u32[]{:S(2)}, u32[]{:S(2)}) %collective-permute-start.5) | collective-permute-done | bytes 262176 | tf_op jit(solution)/shard_map/ppermute | solution.py:41
  124.9 0.2 fusion.65
  125.1 7.8 %collective-permute-start.6 = (bf16[8,128,128]{2,1,0:T(8,128)(2,1)S(1)}, bf16[8,128,128]{2,1,0:T(8,128)(2,1)S(1)}, u32[]{:S(2)}, u32[]{:S(2)}) collective-permute-start(bf16[8,128,128]{2,1,0:T(8,128)(2,1)S(1)} %fusion.65), channel_id=1, source_target_pairs={{0,64},{64,0},{16,80},{80,16},{32,96},{96,32},{48,112},{112,48},{1... | collective-permute-start | bytes 786440 | tf_op jit(solution)/shard_map/ppermute | solution.py:41
  133.0 2.2 fusion.133
  135.2 9.8 %collective-permute-done.6 = bf16[8,128,128]{2,1,0:T(8,128)(2,1)S(1)} collective-permute-done((bf16[8,128,128]{2,1,0:T(8,128)(2,1)S(1)}, bf16[8,128,128]{2,1,0:T(8,128)(2,1)S(1)}, u32[]{:S(2)}, u32[]{:S(2)}) %collective-permute-start.6) | collective-permute-done | bytes 262176 | tf_op jit(solution)/shard_map/ppermute | solution.py:41
  145.0 1.2 fusion.132
  146.2 244.0 %all-reduce.4.cloned.1.call-done = f32[3,3,3,128,128]{4,3,2,1,0:T(8,128)} async-done(((f32[3,3,3,128,128]{4,3,2,1,0:T(8,128)}), f32[3,3,3,128,128]{4,3,2,1,0:T(8,128)}) %all-reduce.4.cloned.1.call-update) | async-done | bytes 1769488 | tf_op jit(solution)/shard_map/psum | solution.py:152
  390.2 2.9 broadcast_multiply_fusion
  (36 shorter events, 0.8 us)
Async XLA Ops:
  7.2 43.5 %copy-start.1 = (bf16[1,8,128,128]{3,2,1,0:T(8,128)(2,1)S(1)}, bf16[1,8,128,128]{3,2,1,0:T(8,128)(2,1)}, u32[]{:S(2)}) copy-start(bf16[1,8,128,128]{3,2,1,0:T(8,128)(2,1)} %param.5) | copy-start | bytes 786436
  7.2 383.0 %all-reduce.4.cloned.1.call-start = ((), (), s32[]{:S(2)}) async-start(), calls=%async_computation | async-start | bytes 3538944 | tf_op jit(solution)/shard_map/psum | solution.py:152
  7.2 19.7 %collective-permute-start = (bf16[1,8,128,128]{3,2,1,0:T(8,128)(2,1)}, bf16[1,8,128,128]{3,2,1,0:T(8,128)(2,1)S(1)}, u32[]{:S(2)}, u32[]{:S(2)}) collective-permute-start(bf16[1,8,128,128]{3,2,1,0:T(8,128)(2,1)} %param.3), channel_id=1, source_target_pairs={{0,32},{16,48},{32,64},{48,80},{64,96},{80,112},{96,128},{112,144}... | collective-permute-start | bytes 786440 | tf_op jit(solution)/shard_map/ppermute | solution.py:18
  12.4 14.7 %collective-permute-start.1 = (bf16[1,8,128,128]{3,2,1,0:T(8,128)(2,1)}, bf16[1,8,128,128]{3,2,1,0:T(8,128)(2,1)S(1)}, u32[]{:S(2)}, u32[]{:S(2)}) collective-permute-start(bf16[1,8,128,128]{3,2,1,0:T(8,128)(2,1)} %param.3), channel_id=1, source_target_pairs={{0,16},{16,32},{32,48},{48,64},{64,80},{80,96},{96,112},{112,128},... | collective-permute-start | bytes 786440 | tf_op jit(solution)/shard_map/ppermute | solution.py:18
  15.6 58.5 %collective-permute-start.11 = (bf16[8,128,128]{2,1,0:T(8,128)(2,1)}, bf16[8,128,128]{2,1,0:T(8,128)(2,1)S(1)}, u32[]{:S(2)}, u32[]{:S(2)}) collective-permute-start(bf16[8,128,128]{2,1,0:T(8,128)(2,1)} %bitcast.320), channel_id=1, source_target_pairs={{0,16},{16,0},{32,48},{48,32},{64,80},{80,64},{96,112},{112,96},{1... | collective-permute-start | bytes 786440 | tf_op jit(solution)/shard_map/ppermute | solution.py:41
  20.0 51.3 %collective-permute-start.9 = (bf16[8,128,128]{2,1,0:T(8,128)(2,1)}, bf16[8,128,128]{2,1,0:T(8,128)(2,1)S(1)}, u32[]{:S(2)}, u32[]{:S(2)}) collective-permute-start(bf16[8,128,128]{2,1,0:T(8,128)(2,1)} %bitcast.321), channel_id=1, source_target_pairs={{0,32},{32,0},{16,48},{48,16},{64,96},{96,64},{80,112},{112,80},{1... | collective-permute-start | bytes 786440 | tf_op jit(solution)/shard_map/ppermute | solution.py:41
  22.5 28.1 %collective-permute-start.7 = (bf16[8,128,128]{2,1,0:T(8,128)(2,1)}, bf16[8,128,128]{2,1,0:T(8,128)(2,1)S(1)}, u32[]{:S(2)}, u32[]{:S(2)}) collective-permute-start(bf16[8,128,128]{2,1,0:T(8,128)(2,1)} %bitcast.322), channel_id=1, source_target_pairs={{0,64},{64,0},{16,80},{80,16},{32,96},{96,32},{48,112},{112,48},{1... | collective-permute-start | bytes 786440 | tf_op jit(solution)/shard_map/ppermute | solution.py:41
  27.2 37.4 %copy-start = (bf16[3,3,3,128,128]{4,3,2,1,0:T(8,128)(2,1)S(1)}, bf16[3,3,3,128,128]{4,3,2,1,0:T(8,128)(2,1)}, u32[]{:S(2)}) copy-start(bf16[3,3,3,128,128]{4,3,2,1,0:T(8,128)(2,1)} %param.4) | copy-start | bytes 2654212
  28.3 35.9 %collective-permute-start.3 = (bf16[3,1,128,128]{3,2,1,0:T(8,128)(2,1)S(1)}, bf16[3,1,128,128]{3,2,1,0:T(8,128)(2,1)S(1)}, u32[]{:S(2)}, u32[]{:S(2)}) collective-permute-start(bf16[3,1,128,128]{3,2,1,0:T(8,128)(2,1)S(1)} %get-tuple-element.17), channel_id=1, source_target_pairs={{1,0},{2,1},{3,2},{4,3},{5,4},{6,5},{7,6},{8,7},{9,8},{10,9},{11,1... | collective-permute-start | bytes 294920 | tf_op jit(solution)/shard_map/ppermute | solution.py:29
  36.4 27.8 %collective-permute-start.2 = (bf16[3,1,128,128]{3,2,1,0:T(8,128)(2,1)S(1)}, bf16[3,1,128,128]{3,2,1,0:T(8,128)(2,1)S(1)}, u32[]{:S(2)}, u32[]{:S(2)}) collective-permute-start(bf16[3,1,128,128]{3,2,1,0:T(8,128)(2,1)S(1)} %get-tuple-element.16), channel_id=1, source_target_pairs={{0,1},{1,2},{2,3},{3,4},{4,5},{5,6},{6,7},{7,8},{8,9},{9,10},{10,1... | collective-permute-start | bytes 294920 | tf_op jit(solution)/shard_map/ppermute | solution.py:28
  50.7 20.7 %collective-permute-start.8 = (bf16[8,128,128]{2,1,0:T(8,128)(2,1)S(1)}, bf16[8,128,128]{2,1,0:T(8,128)(2,1)S(1)}, u32[]{:S(2)}, u32[]{:S(2)}) collective-permute-start(bf16[8,128,128]{2,1,0:T(8,128)(2,1)S(1)} %fusion.70), channel_id=1, source_target_pairs={{0,32},{32,0},{16,48},{48,16},{64,96},{96,64},{80,112},{112,80},{1... | collective-permute-start | bytes 786440 | tf_op jit(solution)/shard_map/ppermute | solution.py:41
  71.6 8.1 %collective-permute-start.10 = (bf16[8,128,128]{2,1,0:T(8,128)(2,1)S(1)}, bf16[8,128,128]{2,1,0:T(8,128)(2,1)S(1)}, u32[]{:S(2)}, u32[]{:S(2)}) collective-permute-start(bf16[8,128,128]{2,1,0:T(8,128)(2,1)S(1)} %fusion.73), channel_id=1, source_target_pairs={{0,16},{16,0},{32,48},{48,32},{64,80},{80,64},{96,112},{112,96},{1... | collective-permute-start | bytes 786440 | tf_op jit(solution)/shard_map/ppermute | solution.py:41
  81.5 8.7 %copy-start.5 = (bf16[1,8,128,128]{3,2,1,0:T(8,128)(2,1)S(1)}, bf16[1,8,128,128]{3,2,1,0:T(8,128)(2,1)}, u32[]{:S(2)}) copy-start(bf16[1,8,128,128]{3,2,1,0:T(8,128)(2,1)} %get-tuple-element.54) | copy-start | bytes 786436
  81.5 8.7 %copy-start.6 = (bf16[1,8,128,128]{3,2,1,0:T(8,128)(2,1)S(1)}, bf16[1,8,128,128]{3,2,1,0:T(8,128)(2,1)}, u32[]{:S(2)}) copy-start(bf16[1,8,128,128]{3,2,1,0:T(8,128)(2,1)} %get-tuple-element.55) | copy-start | bytes 786436
  81.5 8.7 %copy-start.7 = (bf16[1,8,128,128]{3,2,1,0:T(8,128)(2,1)S(1)}, bf16[1,8,128,128]{3,2,1,0:T(8,128)(2,1)}, u32[]{:S(2)}) copy-start(bf16[1,8,128,128]{3,2,1,0:T(8,128)(2,1)} %get-tuple-element.56) | copy-start | bytes 786436
  81.5 17.4 %collective-permute-start.13 = (bf16[1,8,128,128]{3,2,1,0:T(8,128)(2,1)S(1)}, bf16[1,8,128,128]{3,2,1,0:T(8,128)(2,1)S(1)}, u32[]{:S(2)}, u32[]{:S(2)}) collective-permute-start(bf16[1,8,128,128]{3,2,1,0:T(8,128)(2,1)S(1)} %bitcast.323), channel_id=1, source_target_pairs={{16,0},{32,16},{48,32},{64,48},{80,64},{96,80},{112,96},{128,112},... | collective-permute-start | bytes 786440 | tf_op jit(solution)/shard_map/ppermute | solution.py:18
  82.9 16.1 %collective-permute-start.12 = (bf16[1,8,128,128]{3,2,1,0:T(8,128)(2,1)S(1)}, bf16[1,8,128,128]{3,2,1,0:T(8,128)(2,1)S(1)}, u32[]{:S(2)}, u32[]{:S(2)}) collective-permute-start(bf16[1,8,128,128]{3,2,1,0:T(8,128)(2,1)S(1)} %bitcast.324), channel_id=1, source_target_pairs={{32,0},{48,16},{64,32},{80,48},{96,64},{112,80},{128,96},{144,112}... | collective-permute-start | bytes 786440 | tf_op jit(solution)/shard_map/ppermute | solution.py:18
  85.1 23.9 %collective-permute-start.4 = (bf16[8,128,128]{2,1,0:T(8,128)(2,1)}, bf16[8,128,128]{2,1,0:T(8,128)(2,1)S(1)}, u32[]{:S(2)}, u32[]{:S(2)}) collective-permute-start(bf16[8,128,128]{2,1,0:T(8,128)(2,1)} %multiply_convert_fusion), channel_id=1, source_target_pairs={{0,16},{16,0},{32,48},{48,32},{64,80},{80,64},{96,112},{112,96},{1... | collective-permute-start | bytes 786440 | tf_op jit(solution)/shard_map/ppermute | solution.py:41
  91.2 1.1 copy-start.2
  91.2 1.1 copy-start.3
  91.2 1.1 copy-start.4
  99.1 14.3 %collective-permute-start.15 = (bf16[3,1,128,128]{3,2,1,0:T(8,128)(2,1)S(1)}, bf16[3,1,128,128]{3,2,1,0:T(8,128)(2,1)S(1)}, u32[]{:S(2)}, u32[]{:S(2)}) collective-permute-start(bf16[3,1,128,128]{3,2,1,0:T(8,128)(2,1)S(1)} %get-tuple-element.15), channel_id=1, source_target_pairs={{1,0},{2,1},{3,2},{4,3},{5,4},{6,5},{7,6},{8,7},{9,8},{10,9},{11,1... | collective-permute-start | bytes 294920 | tf_op jit(solution)/shard_map/ppermute | solution.py:29
  104.9 8.4 %collective-permute-start.14 = (bf16[3,1,128,128]{3,2,1,0:T(8,128)(2,1)S(1)}, bf16[3,1,128,128]{3,2,1,0:T(8,128)(2,1)S(1)}, u32[]{:S(2)}, u32[]{:S(2)}) collective-permute-start(bf16[3,1,128,128]{3,2,1,0:T(8,128)(2,1)S(1)} %get-tuple-element.14), channel_id=1, source_target_pairs={{0,1},{1,2},{2,3},{3,4},{4,5},{5,6},{6,7},{7,8},{8,9},{9,10},{10,1... | collective-permute-start | bytes 294920 | tf_op jit(solution)/shard_map/ppermute | solution.py:28
  109.2 15.8 %collective-permute-start.5 = (bf16[8,128,128]{2,1,0:T(8,128)(2,1)S(1)}, bf16[8,128,128]{2,1,0:T(8,128)(2,1)S(1)}, u32[]{:S(2)}, u32[]{:S(2)}) collective-permute-start(bf16[8,128,128]{2,1,0:T(8,128)(2,1)S(1)} %fusion.57), channel_id=1, source_target_pairs={{0,32},{32,0},{16,48},{48,16},{64,96},{96,64},{80,112},{112,80},{1... | collective-permute-start | bytes 786440 | tf_op jit(solution)/shard_map/ppermute | solution.py:41
  125.1 19.8 %collective-permute-start.6 = (bf16[8,128,128]{2,1,0:T(8,128)(2,1)S(1)}, bf16[8,128,128]{2,1,0:T(8,128)(2,1)S(1)}, u32[]{:S(2)}, u32[]{:S(2)}) collective-permute-start(bf16[8,128,128]{2,1,0:T(8,128)(2,1)S(1)} %fusion.65), channel_id=1, source_target_pairs={{0,64},{64,0},{16,80},{80,16},{32,96},{96,32},{48,112},{112,48},{1... | collective-permute-start | bytes 786440 | tf_op jit(solution)/shard_map/ppermute | solution.py:41
Sparse Core Ops, SparseCore 0:
  99.0 291.1 all-reduce.3
where the time goes:
time: 401 us; the launch traced here: 400 us
  waiting for transfers between devices  279 us (70%)
  starting transfers between devices  74 us (18%)
  matrix products  18 us (4%)
  between operations  14.5 us (4%)
  other arithmetic  10.3 us (3%)
  local copies, waits for them, and re-layouts  4.58 us (1%)
    psum x1, waiting for transfers between devices, shards(): weight_sum = lax.psum(local_terms, ('tm', 'rows'))  244 us
    ppermute x8, starting transfers between devices, from_partner(): return lax.ppermute(block, axis, route)  42.6 us
    ppermute x8, waiting for transfers between devices, from_partner(): return lax.ppermute(block, axis, route)  34.2 us
    ppermute x2, starting transfers between devices, extended(): after = lax.ppermute(initial, axis, down)  13.9 us
    ppermute x4, starting transfers between devices, passed_along(): return lax.ppermute(block, axis, route)  11.1 us
    dot_general x9, matrix products, weight_terms(): jnp.einsum('jrwc,rwd->jcd', shifted, grad_linear, preferred_element_type=...  9.79 us
  transfers between devices with their start and end apart: 17, of which 7 were waited for; matrix products, arithmetic and copies ran while one was open for 7% of the time, Pallas kernels for 0%

commit v1 on v0

v1 whole, which is shorter than its diff:
```python
import functools
import math

import jax
import jax.numpy as jnp
from jax import lax
from jax.experimental import pallas as pl
from jax.experimental.pallas import tpu as pltpu
from jax.sharding import Mesh
from jax.sharding import PartitionSpec as P

CHIPS = (4, 8, 8, 2)
LEVELS = 3
GROUP = 1 << LEVELS
ROWS = 8
STRIP = 16
TILE = ROWS * STRIP
TALL = ROWS + 2
HELD = TALL * STRIP + 2 * STRIP
CH = 128
WIDE = 9 * CH
FRAMES = GROUP + 2
EDGES = 2 * ROWS
PART = 8

band_weight = 0.75
root_half = 0.7071067811865476
f32 = jnp.float32
bf16 = jnp.bfloat16
VMEM_LIMIT = 48 * 1024 * 1024


def kernel_call(body, outs, scratch=(), flops=0):
    return pl.pallas_call(
        body,
        out_shape=outs,
        scratch_shapes=list(scratch),
        compiler_params=pltpu.CompilerParams(vmem_limit_bytes=VMEM_LIMIT),
        cost_estimate=pl.CostEstimate(flops=flops, bytes_accessed=4 << 20, transcendentals=0),
    )


def pack_body(x_ref, up_ref, down_ref, cot_ref, out_ref, left_ref, right_ref):
    left_ref[...] = jnp.zeros_like(left_ref)
    right_ref[...] = jnp.zeros_like(right_ref)
    for tall_row in range(TALL):
        if tall_row == 0:
            line = up_ref[0]
        elif tall_row == TALL - 1:
            line = down_ref[0]
        else:
            line = x_ref[tall_row - 1]
        wide = line.astype(f32)
        for strip in range(GROUP):
            low = strip * STRIP
            out_ref[strip, pl.ds(tall_row * STRIP, STRIP), :] = line[low : low + STRIP]
            if strip > 0:
                left_ref[strip, pl.ds(tall_row, 1), :] = wide[low - 1 : low]
            if strip < GROUP - 1:
                right_ref[strip, pl.ds(tall_row, 1), :] = wide[low + STRIP : low + STRIP + 1]
    for strip in range(GROUP):
        out_ref[strip, pl.ds(TALL * STRIP, STRIP), :] = left_ref[strip].astype(bf16)
        out_ref[strip, pl.ds(TALL * STRIP + STRIP, STRIP), :] = right_ref[strip].astype(bf16)
        for row in range(ROWS):
            out_ref[strip, pl.ds(HELD + row * STRIP, STRIP), :] = cot_ref[
                row, pl.ds(strip * STRIP, STRIP), :
            ]


def place_line(col_ref, base, tall_row, line, left, right):
    at = lax.broadcasted_iota(jnp.int32, (STRIP, CH), 0)
    wide = line.astype(f32)
    before = jnp.where(at == 0, left, pltpu.roll(wide, 1, 0)).astype(bf16)
    after = jnp.where(at == STRIP - 1, right, pltpu.roll(wide, STRIP - 1, 0)).astype(bf16)
    for row_tap in range(3):
        row = tall_row - row_tap
        if 0 <= row < ROWS:
            start = pl.multiple_of(base + row * STRIP, STRIP)
            for col_tap, piece in enumerate((before, line, after)):
                tap = row_tap * 3 + col_tap
                col_ref[pl.ds(start, STRIP), pl.ds(tap * CH, CH)] = piece


def forward_body(held_ref, early_ref, w_ref, code_ref, g_ref, dw_ref, col_ref, lin_ref, gt_ref):
    def spread(ref, frame, place):
        left = ref[frame, pl.ds(TALL * STRIP, STRIP), :].astype(f32)
        right = ref[frame, pl.ds(TALL * STRIP + STRIP, STRIP), :].astype(f32)
        for tall_row in range(TALL):
            line = ref[frame, pl.ds(tall_row * STRIP, STRIP), :]
            place_line(
                col_ref,
                place * TILE,
                tall_row,
                line,
                left[tall_row : tall_row + 1],
                right[tall_row : tall_row + 1],
            )

    @pl.loop(0, 2)
    def _(frame):
        spread(early_ref, frame, frame)

    @pl.loop(0, GROUP)
    def _(frame):
        spread(held_ref, frame, frame + 2)

    lin_ref[...] = (
        jnp.dot(col_ref[0 : GROUP * TILE, :], w_ref[0], preferred_element_type=f32)
        + jnp.dot(col_ref[TILE : (GROUP + 1) * TILE, :], w_ref[1], preferred_element_type=f32)
        + jnp.dot(col_ref[2 * TILE : (GROUP + 2) * TILE, :], w_ref[2], preferred_element_type=f32)
    )

    @pl.loop(0, ROWS)
    def _(row):
        low = pl.multiple_of(row * STRIP, STRIP)
        linear = [lin_ref[pl.ds(frame * TILE + low, STRIP), :] for frame in range(GROUP)]
        gate = [jax.nn.sigmoid(value) for value in linear]
        band = [(value * part).astype(bf16).astype(f32) for value, part in zip(linear, gate)]
        detail = [None] * GROUP
        for level in range(LEVELS):
            step = 1 << level
            following = [None] * GROUP
            for frame in range(0, GROUP, 2 * step):
                lower, upper = band[frame], band[frame + step]
                smooth = (lower + upper) * root_half
                if level < LEVELS - 1:
                    smooth = smooth.astype(bf16).astype(f32)
                change = (upper - lower) * root_half
                following[frame] = smooth
                for member in range(frame, frame + 2 * step, 2):
                    detail[member] = change if level == 0 else detail[member] + change
            band = following
        for member in range(0, GROUP, 2):
            code = (band[0] + band_weight * detail[member]).astype(bf16)
            code_ref[member, pl.ds(low, STRIP), :] = code
            code_ref[member + 1, pl.ds(low, STRIP), :] = code

        cot = [
            held_ref[frame, pl.ds(HELD + low, STRIP), :].astype(f32) for frame in range(GROUP)
        ]
        back = [None] * GROUP
        for level in range(LEVELS - 1, -1, -1):
            step = 1 << level
            following = [None] * GROUP
            for frame in range(GROUP):
                if frame & step:
                    continue
                pair = (cot[frame] + cot[frame + step]) * root_half
                if level == LEVELS - 1:
                    total = pair
                else:
                    total = (back[frame] + back[frame + step]) * root_half
                for member, side in ((frame, -1.0), (frame + step, 1.0)):
                    value = total + (band_weight * side) * pair
                    if level > 0:
                        value = value.astype(bf16).astype(f32)
                    following[member] = value
            back = following
        for frame in range(GROUP):
            slope = gate[frame] * (1.0 + linear[frame] * (1.0 - gate[frame]))
            g_ref[frame, pl.ds(low, STRIP), :] = (back[frame] * slope).astype(bf16)

    gt_ref[...] = jnp.zeros_like(gt_ref)
    for frame in range(GROUP):
        turned = g_ref[frame].astype(f32).T.astype(bf16)
        for tap in range(3):
            gt_ref[pl.ds(tap * CH, CH), pl.ds((frame + tap) * TILE, TILE)] = turned
    for tap in range(9):
        product = jnp.dot(
            gt_ref[...], col_ref[:, tap * CH : (tap + 1) * CH], preferred_element_type=f32
        )
        for frame_tap in range(3):
            block = product[frame_tap * CH : (frame_tap + 1) * CH]
            dw_ref[frame_tap * 9 + tap] = block.T.astype(bf16)


def backward_body(g_ref, up_ref, down_ref, late_ref, code_ref, w_ref, out_ref, col_ref, side_ref):
    nothing = jnp.zeros((1, CH), f32)

    def spread(lines, place):
        for tall_row, line in enumerate(lines):
            place_line(col_ref, place * TILE, tall_row, line, nothing, nothing)

    @pl.loop(0, GROUP)
    def _(frame):
        rows = [g_ref[frame, pl.ds(row * STRIP, STRIP), :] for row in range(ROWS)]
        spread([up_ref[frame]] + rows + [down_ref[frame]], frame)

    @pl.loop(0, 2)
    def _(frame):
        lines = [late_ref[frame, pl.ds(row * STRIP, STRIP), :] for row in range(TALL)]
        spread(lines, frame + GROUP)

    total = (
        jnp.dot(col_ref[0 : GROUP * TILE, :], w_ref[0], preferred_element_type=f32)
        + jnp.dot(col_ref[TILE : (GROUP + 1) * TILE, :], w_ref[1], preferred_element_type=f32)
        + jnp.dot(col_ref[2 * TILE : (GROUP + 2) * TILE, :], w_ref[2], preferred_element_type=f32)
    )
    for frame in range(GROUP):
        out_ref[frame, 0:TILE, :] = code_ref[frame]
        out_ref[frame, TILE : 2 * TILE, :] = total[frame * TILE : (frame + 1) * TILE].astype(bf16)
    for side, (offset, col_tap) in enumerate(((0, 2), (STRIP - 1, 0))):
        for frame in range(FRAMES):
            for row in range(ROWS):
                at = frame * TILE + row * STRIP + (0 if side == 0 else STRIP - 8)
                for row_tap in range(3):
                    mid = (row_tap * 3 + 1) * CH
                    piece = col_ref[pl.ds(frame * TILE + row * STRIP, STRIP), pl.ds(mid, CH)]
                    one = piece.astype(f32)[offset : offset + 1]
                    side_ref[pl.ds(frame * ROWS + row, 1), pl.ds(row_tap * CH, CH)] = one
        summed = None
        for frame_tap in range(3):
            rows = side_ref[pl.ds(frame_tap * ROWS, GROUP * ROWS), :].astype(bf16)
            for row_tap in range(3):
                tap = row_tap * 3 + col_tap
                part = jnp.dot(
                    rows[:, row_tap * CH : (row_tap + 1) * CH],
                    w_ref[frame_tap, pl.ds(tap * CH, CH), :],
                    preferred_element_type=f32,
                )
                summed = part if summed is None else summed + part
        if side == 0:
            first = summed
    for frame in range(GROUP):
        pair = [value[frame * ROWS : (frame + 1) * ROWS] for value in (first, summed)]
        out_ref[frame, 2 * TILE : 2 * TILE + EDGES, :] = jnp.concatenate(pair, axis=0).astype(bf16)


def unpack_body(got_ref, code_ref, grad_ref):
    at = lax.broadcasted_iota(jnp.int32, (STRIP, CH), 0)
    for strip in range(GROUP):
        columns = pl.ds(strip * STRIP, STRIP)
        if strip > 0:
            before = got_ref[strip - 1, pl.ds(2 * TILE, EDGES), :].astype(f32)
        if strip < GROUP - 1:
            after = got_ref[strip + 1, pl.ds(2 * TILE, EDGES), :].astype(f32)
        for row in range(ROWS):
            code_ref[row, columns, :] = got_ref[strip, pl.ds(row * STRIP, STRIP), :]
            value = got_ref[strip, pl.ds(TILE + row * STRIP, STRIP), :].astype(f32)
            if strip > 0:
                value = value + jnp.where(at == 0, before[ROWS + row : ROWS + row + 1], 0.0)
            if strip < GROUP - 1:
                value = value + jnp.where(at == STRIP - 1, after[row : row + 1], 0.0)
            grad_ref[row, columns, :] = value.astype(bf16)


def shifted(value, axes, by):
    count = lax.axis_size(axes)
    route = [(i, i + by) for i in range(count) if 0 <= i + by < count]
    return lax.ppermute(value, axes, route)


def swapped(value):
    return lax.ppermute(value, "core", [(0, 1), (1, 0)])


def summed_everywhere(terms, norm):
    chips = ("x", "y", "z")
    count = lax.axis_size(chips)
    core = lax.axis_index("core")
    rows = terms.shape[0] // 2
    halves = terms.reshape(2, rows, CH)
    mine = lax.dynamic_index_in_dim(halves, core, 0, keepdims=False)
    other = lax.dynamic_index_in_dim(halves, 1 - core, 0, keepdims=False)
    chip_sum = (mine.astype(f32) + swapped(other).astype(f32)).astype(bf16)
    share = PART * -(-rows // (PART * count))
    padded = jnp.pad(chip_sum, ((0, share * count - rows), (0, 0)))
    spread = lax.all_to_all(padded.reshape(count, share, CH), chips, 0, 0)
    total = (spread.astype(f32).sum(axis=0) * norm).astype(bf16)
    copies = jnp.broadcast_to(total[None], (count, share, CH))
    half = lax.all_to_all(copies, chips, 0, 0).reshape(count * share, CH)[:rows]
    paired = swapped(half)
    low = jnp.where(core == 0, half, paired)
    high = jnp.where(core == 0, paired, half)
    return jnp.concatenate([low, high], axis=0).astype(f32)


def shards(frames, kernel, cotangent):
    x = frames[0]
    weights = kernel.reshape(3, WIDE, CH)
    turned = jnp.swapaxes(kernel[::-1, ::-1, ::-1], 3, 4).reshape(3, WIDE, CH)
    lines = ("z", "core")
    up = shifted(x[ROWS - 1 : ROWS], lines, 1)
    down = shifted(x[0:1], lines, -1)
    packed = kernel_call(
        pack_body,
        jax.ShapeDtypeStruct((GROUP, HELD + TILE, CH), bf16),
        [pltpu.VMEM((GROUP, STRIP, CH), f32)] * 2,
    )(x, up, down, cotangent[0])
    held = lax.all_to_all(packed, "y", 0, 0)
    early = shifted(held[GROUP - 2 :, :HELD], "x", 1)

    flops = 2 * GROUP * TILE * 27 * CH * CH
    code, g, terms = kernel_call(
        forward_body,
        (
            jax.ShapeDtypeStruct((GROUP, TILE, CH), bf16),
            jax.ShapeDtypeStruct((GROUP, TILE, CH), bf16),
            jax.ShapeDtypeStruct((27, CH, CH), bf16),
        ),
        [
            pltpu.VMEM((FRAMES * TILE, WIDE), bf16),
            pltpu.VMEM((GROUP * TILE, CH), f32),
            pltpu.VMEM((3 * CH, FRAMES * TILE), bf16),
        ],
        flops=2 * flops,
    )(held, early, weights)

    norm = 1.0 / math.sqrt(lax.axis_size(("x", "y", "z", "core")) * GROUP * TILE)
    grad_kernel = summed_everywhere(terms.reshape(27 * CH, CH), norm)

    g_up = shifted(g[:, TILE - STRIP :], lines, 1)
    g_down = shifted(g[:, :STRIP], lines, -1)
    late = shifted(jnp.concatenate([g_up[:2], g[:2], g_down[:2]], axis=1), "x", -1)
    sent = kernel_call(
        backward_body,
        jax.ShapeDtypeStruct((GROUP, 2 * TILE + EDGES, CH), bf16),
        [
            pltpu.VMEM((FRAMES * TILE, WIDE), bf16),
            pltpu.VMEM((FRAMES * ROWS, 3 * CH), f32),
        ],
        flops=flops,
    )(g, g_up, g_down, late, code, turned)
    got = lax.all_to_all(sent, "y", 0, 0)
    whole = jax.ShapeDtypeStruct((ROWS, GROUP * STRIP, CH), bf16)
    code_out, grad_frames = kernel_call(unpack_body, (whole, whole))(got)
    return (code_out[None], grad_frames[None], grad_kernel.reshape(3, 3, 3, CH, CH))


def solution(mesh):
    split = Mesh(mesh.devices.reshape(CHIPS), ("x", "y", "z", "core"))
    block = P(("x", "y"), ("z", "core"), None, None)
    return jax.shard_map(
        shards,
        mesh=split,
        in_specs=(block, P(), block),
        out_specs=(block, block, P()),
        check_vma=False,
    )
```

time: 401 us -> 152 us (0.38)
  waiting for transfers between devices: 279 us -> 26.3 us
  blocking collectives: 0 us -> 62.9 us
  starting transfers between devices: 74 us -> 43.2 us
  matrix products: 18 us -> 0 us
  between operations: 14.5 us -> 0.82 us
  Pallas kernels: 0 us -> 10.7 us
  other arithmetic: 10.3 us -> 1.94 us
    psum x1 -> x0, waiting for transfers between devices: 244 us -> none  [shards(): weight_sum = lax.psum(local_terms, ('tm', 'rows'))]
    all_to_all x0 -> x2, blocking collectives: none -> 62.9 us  [the longest x1 37.4 us: summed_everywhere(): spread = lax.all_to_all(padded.reshape(count, share, CH), chips, 0, 0)]
    ppermute x16 -> x8, starting transfers between devices: 74 us -> 23.9 us  [the longest x6 20 us: shifted(): return lax.ppermute(value, axes, route)]
    ppermute x16 -> x8, waiting for transfers between devices: 34.6 us -> 10.6 us  [the longest x6 8.84 us: shifted(): return lax.ppermute(value, axes, route)]
    all_to_all x0 -> x2, starting transfers between devices: none -> 19.3 us  [the longest x1 10.8 us: summed_everywhere(): half = lax.all_to_all(copies, chips, 0, 0).reshape(count * share, CH)[:rows]]
    dot_general x27 -> x0, matrix products: 18 us -> none  [the longest x9 9.79 us: weight_terms(): jnp.einsum('jrwc,rwd->jcd', shifted, grad_linear, preferred_element_type=...]
    all_to_all x0 -> x2, waiting for transfers between devices: none -> 15.7 us  [the longest x1 15.7 us: shards(): got = lax.all_to_all(sent, 'y', 0, 0)]
    pallas_call x0 -> x4, Pallas kernels: none -> 10.7 us  [the longest x1 6.32 us: shards(): kernel_call(forward_body, (jax.ShapeDtypeStruct((GROUP, TILE, CH), bf16),...]
  transfers between devices with their start and end apart: 17 -> 10, of which waited for: 7 -> 7; matrix products, arithmetic and copies ran while one was open for 7% -> 1% of each run, Pallas kernels for 0% -> 3%
where the time goes in v1:
time: 152 us; the launch traced here: 151 us
  blocking collectives  62.9 us (41%)
  starting transfers between devices  43.2 us (28%)
  waiting for transfers between devices  26.3 us (17%)
  Pallas kernels  10.7 us (7%)
  local copies, waits for them, and re-layouts  5.22 us (3%)
  other arithmetic  1.94 us (1%)
    all_to_all x1, blocking collectives, summed_everywhere(): spread = lax.all_to_all(padded.reshape(count, share, CH), chips, 0, 0)  37.4 us
    all_to_all x1, blocking collectives, shards(): held = lax.all_to_all(packed, 'y', 0, 0)  25.5 us
    ppermute x6, starting transfers between devices, shifted(): return lax.ppermute(value, axes, route)  20 us
    all_to_all x1, waiting for transfers between devices, shards(): got = lax.all_to_all(sent, 'y', 0, 0)  15.7 us
    all_to_all x1, starting transfers between devices, summed_everywhere(): half = lax.all_to_all(copies, chips, 0, 0).reshape(count * share, CH)[:rows]  10.8 us
    ppermute x6, waiting for transfers between devices, shifted(): return lax.ppermute(value, axes, route)  8.84 us
    all_to_all x1, starting transfers between devices, shards(): got = lax.all_to_all(sent, 'y', 0, 0)  8.52 us
    pallas_call x1, Pallas kernels, shards(): kernel_call(forward_body, (jax.ShapeDtypeStruct((GROUP, TILE, CH), bf16),...  6.32 us
  transfers between devices with their start and end apart: 10, of which 7 were waited for; matrix products, arithmetic and copies ran while one was open for 1% of the time, Pallas kernels for 3%

profile of v1, /device:TPU:1, one launch (start us, length us, event | category | flops | bytes accessed | tf_op | source)
XLA Modules:
  0.0 151.1 jit_solution(13449389070564173375)
XLA Ops:
  0.6 0.0 copy-start
  0.6 0.9 slice_bitcast_fusion.1
  1.5 5.4 %collective-permute-start = (bf16[1,128,128]{2,1,0:T(8,128)(2,1)S(1)}, bf16[1,128,128]{2,1,0:T(8,128)(2,1)S(1)}, u32[]{:S(2)}, u32[]{:S(2)}) collective-permute-start(bf16[1,128,128]{2,1,0:T(8,128)(2,1)S(1)} %get-tuple-element.18), channel_id=1, source_target_pairs={{0,1},{1,2},{2,3},{3,4},{4,5},{5,6},{6,7},{7,8},{8,9},{9,10},{10,1... | collective-permute-start | bytes 98312 | tf_op jit(solution)/shard_map/ppermute | solution.py:250
  6.9 4.7 %collective-permute-start.1 = (bf16[1,128,128]{2,1,0:T(8,128)(2,1)S(1)}, bf16[1,128,128]{2,1,0:T(8,128)(2,1)S(1)}, u32[]{:S(2)}, u32[]{:S(2)}) collective-permute-start(bf16[1,128,128]{2,1,0:T(8,128)(2,1)S(1)} %get-tuple-element.17), channel_id=1, source_target_pairs={{1,0},{2,1},{3,2},{4,3},{5,4},{6,5},{7,6},{8,7},{9,8},{10,9},{11,1... | collective-permute-start | bytes 98312 | tf_op jit(solution)/shard_map/ppermute | solution.py:250
  11.6 0.0 collective-permute-done.up_ref
  11.6 0.8 collective-permute-done.1.down_ref
  12.4 0.0 copy-start.1
  12.4 0.9 copy-done.1
  13.4 0.0 copy-start.2
  13.4 0.9 copy-done.2
  14.3 0.1 shard_map.58
  14.4 25.5 %all_to_all.20.held_ref = bf16[8,320,128]{2,1,0:T(8,128)(2,1)S(1)} all-to-all(bf16[8,320,128]{2,1,0:T(8,128)(2,1)S(1)} %shard_map.58), channel_id=1, replica_groups=mesh['x'=4,'y'=8,'z'=8,'core'=2] {'y'}, dimensions={0} | all-to-all | bytes 1310720 | tf_op jit(solution)/shard_map/all_to_all | solution.py:290
  40.0 3.1 %collective-permute-start.2 = (bf16[2,192,128]{2,1,0:T(8,128)(2,1)S(1)}, bf16[2,192,128]{2,1,0:T(8,128)(2,1)S(1)}, u32[]{:S(2)}, u32[]{:S(2)}) collective-permute-start(bf16[2,192,128]{2,1,0:T(8,128)(2,1)S(1)} %slice.48), channel_id=1, source_target_pairs={{0,128},{128,256},{256,384},{1,129},{129,257},{257,385},{2,130},{1... | collective-permute-start | bytes 294920 | tf_op jit(solution)/shard_map/ppermute | solution.py:250
  43.1 2.0 %collective-permute-done.2.early_ref = bf16[2,192,128]{2,1,0:T(8,128)(2,1)S(1)} collective-permute-done((bf16[2,192,128]{2,1,0:T(8,128)(2,1)S(1)}, bf16[2,192,128]{2,1,0:T(8,128)(2,1)S(1)}, u32[]{:S(2)}, u32[]{:S(2)}) %collective-permute-start.2) | collective-permute-done | bytes 98336 | tf_op jit(solution)/shard_map/ppermute | solution.py:250
  45.1 0.0 copy-done
  45.1 6.3 %shard_map.59 = (bf16[8,128,128]{2,1,0:T(8,128)(2,1)S(1)}, bf16[8,128,128]{2,1,0:T(8,128)(2,1)S(1)}, bf16[27,128,128]{2,1,0:T(8,128)(2,1)S(1)}) custom-call(bf16[8,320,128]{2,1,0:T(8,128)(2,1)S(1)} %all_to_all.20.held_ref, bf16[2,192,128]{2,1,0:T(8,128)(2,1)S(1)} %collective-permute-done.2.early_ref, bf16[3,1152,128]{2,1,0:T(8,128)(2,1)S(1)} %bitcast.28), custom_call_target="tpu_custom_call" | custom-call | flops 1811939328 | bytes 4194304 | tf_op jit(solution)/shard_map/pallas_call | solution.py:294
  51.5 1.9 %collective-permute-start.6 = (bf16[1728,128]{1,0:T(8,128)(2,1)S(1)}, bf16[1728,128]{1,0:T(8,128)(2,1)S(1)}, u32[]{:S(2)}, u32[]{:S(2)}) collective-permute-start(bf16[1728,128]{1,0:T(8,128)(2,1)S(1)} %dynamic-slice_bitcast_fusion), channel_id=1, source_target_pairs={{0,1},{1,0},{2,3},{3,2},{4,5},{5,4},{6,7},{7,6},{8,9},{9,8},{10,11... | collective-permute-start | bytes 1327112 | tf_op jit(solution)/shard_map/ppermute | solution.py:254
  53.4 1.8 %collective-permute-done.6 = bf16[1728,128]{1,0:T(8,128)(2,1)S(1)} collective-permute-done((bf16[1728,128]{1,0:T(8,128)(2,1)S(1)}, bf16[1728,128]{1,0:T(8,128)(2,1)S(1)}, u32[]{:S(2)}, u32[]{:S(2)}) %collective-permute-start.6) | collective-permute-done | bytes 442400 | tf_op jit(solution)/shard_map/ppermute | solution.py:254
  55.2 0.1 fusion
  55.4 37.4 %all_to_all.21 = bf16[256,8,128]{2,1,0:T(8,128)(2,1)S(1)} all-to-all(bf16[256,8,128]{2,1,0:T(8,128)(2,1)S(1)} %pad_bitcast_fusion), channel_id=1, replica_groups=mesh['x'=4,'y'=8,'z'=8,'core'=2] {'x','y','z'}, dimensions={0} | all-to-all | bytes 1048576 | tf_op jit(solution)/shard_map/all_to_all | solution.py:268
  92.8 0.3 convert_reduce_fusion
  93.1 0.9 broadcast_in_dim.14
  93.9 10.8 %all-to-all-start.3 = ((bf16[256,8,128]{2,1,0:T(8,128)(2,1)}), bf16[256,8,128]{2,1,0:T(8,128)(2,1)S(1)}, u32[]{:S(2)}, u32[]{:S(2)}) async-start(bf16[256,8,128]{2,1,0:T(8,128)(2,1)} %broadcast_in_dim.14), calls=%async_computation.3 | async-start | bytes 1048576 | tf_op jit(solution)/shard_map/all_to_all | solution.py:271
  104.7 3.2 %collective-permute-start.4 = (bf16[8,16,128]{2,1,0:T(8,128)(2,1)S(1)}, bf16[8,16,128]{2,1,0:T(8,128)(2,1)S(1)}, u32[]{:S(2)}, u32[]{:S(2)}) collective-permute-start(bf16[8,16,128]{2,1,0:T(8,128)(2,1)S(1)} %get-tuple-element.15), channel_id=1, source_target_pairs={{1,0},{2,1},{3,2},{4,3},{5,4},{6,5},{7,6},{8,7},{9,8},{10,9},{11,1... | collective-permute-start | bytes 98312 | tf_op jit(solution)/shard_map/ppermute | solution.py:250
  108.0 2.3 %collective-permute-start.3 = (bf16[8,16,128]{2,1,0:T(8,128)(2,1)S(1)}, bf16[8,16,128]{2,1,0:T(8,128)(2,1)S(1)}, u32[]{:S(2)}, u32[]{:S(2)}) collective-permute-start(bf16[8,16,128]{2,1,0:T(8,128)(2,1)S(1)} %get-tuple-element.16), channel_id=1, source_target_pairs={{0,1},{1,2},{2,3},{3,4},{4,5},{5,6},{6,7},{7,8},{8,9},{9,10},{10,1... | collective-permute-start | bytes 98312 | tf_op jit(solution)/shard_map/ppermute | solution.py:250
  110.3 1.9 %collective-permute-done.4.down_ref = bf16[8,16,128]{2,1,0:T(8,128)(2,1)S(1)} collective-permute-done((bf16[8,16,128]{2,1,0:T(8,128)(2,1)S(1)}, bf16[8,16,128]{2,1,0:T(8,128)(2,1)S(1)}, u32[]{:S(2)}, u32[]{:S(2)}) %collective-permute-start.4) | collective-permute-done | bytes 32800 | tf_op jit(solution)/shard_map/ppermute | solution.py:250
  112.3 0.7 collective-permute-done.3.up_ref
  113.0 1.3 collective-permute-start.5
  114.3 0.1 reverse_bitcast_fusion
  114.4 1.4 copy.6
  115.8 3.3 %collective-permute-done.5.late_ref = bf16[2,160,128]{2,1,0:T(8,128)(2,1)S(1)} collective-permute-done((bf16[2,160,128]{2,1,0:T(8,128)(2,1)S(1)}, bf16[2,160,128]{2,1,0:T(8,128)(2,1)S(1)}, u32[]{:S(2)}, u32[]{:S(2)}) %collective-permute-start.5) | collective-permute-done | bytes 81952 | tf_op jit(solution)/shard_map/ppermute | solution.py:250
  119.1 3.5 %shard_map.60 = bf16[8,272,128]{2,1,0:T(8,128)(2,1)} custom-call(bf16[8,128,128]{2,1,0:T(8,128)(2,1)S(1)} %get-tuple-element.8.g_ref, bf16[8,16,128]{2,1,0:T(8,128)(2,1)S(1)} %collective-permute-done.3.up_ref, bf16[8,16,128]{2,1,0:T(8,128)(2,1)S(1)} %collective-permute-done.4.down_ref, bf16[2,160,128]{2,1,0:T(8,128)(2,1)S(1)} %collective-permute-done.5.late_ref, ...), custom_call_target="tpu_custom_call" | custom-call | flops 905969664 | bytes 4194304 | tf_op jit(solution)/shard_map/pallas_call | solution.py:315
  122.6 0.0 all-to-all-done.3
  122.6 8.5 %all-to-all-start.1 = ((bf16[8,272,128]{2,1,0:T(8,128)(2,1)}), bf16[8,272,128]{2,1,0:T(8,128)(2,1)S(1)}, u32[]{:S(2)}, u32[]{:S(2)}) async-start(bf16[8,272,128]{2,1,0:T(8,128)(2,1)} %shard_map.60), calls=%async_computation.1 | async-start | bytes 1114112 | tf_op jit(solution)/shard_map/all_to_all | solution.py:324
  131.1 1.9 %collective-permute-start.7 = (bf16[1728,128]{1,0:T(8,128)(2,1)S(1)}, bf16[1728,128]{1,0:T(8,128)(2,1)S(1)}, u32[]{:S(2)}, u32[]{:S(2)}) collective-permute-start(bf16[1728,128]{1,0:T(8,128)(2,1)S(1)} %slice_bitcast_fusion), channel_id=1, source_target_pairs={{0,1},{1,0},{2,3},{3,2},{4,5},{5,4},{6,7},{7,6},{8,9},{9,8},{10,11... | collective-permute-start | bytes 1327112 | tf_op jit(solution)/shard_map/ppermute | solution.py:254
  133.1 15.7 %all-to-all-done.1.got_ref = bf16[8,272,128]{2,1,0:T(8,128)(2,1)S(1)} async-done(((bf16[8,272,128]{2,1,0:T(8,128)(2,1)}), bf16[8,272,128]{2,1,0:T(8,128)(2,1)S(1)}, u32[]{:S(2)}, u32[]{:S(2)}) %all-to-all-start.1) | async-done | bytes 557088 | tf_op jit(solution)/shard_map/all_to_all | solution.py:324
  148.7 0.8 shard_map.61
  149.5 0.0 collective-permute-done.7
  149.6 0.1 broadcast_select_fusion.1
  149.6 0.1 pad_maximum_fusion
  149.7 1.4 convert.3
  (10 shorter events, 0.1 us)
Async XLA Ops:
  0.6 44.5 %copy-start = (bf16[3,3,3,128,128]{4,3,2,1,0:T(8,128)(2,1)S(1)}, bf16[3,3,3,128,128]{4,3,2,1,0:T(8,128)(2,1)}, u32[]{:S(2)}) copy-start(bf16[3,3,3,128,128]{4,3,2,1,0:T(8,128)(2,1)} %param.4) | copy-start | bytes 2654212
  1.5 10.1 %collective-permute-start = (bf16[1,128,128]{2,1,0:T(8,128)(2,1)S(1)}, bf16[1,128,128]{2,1,0:T(8,128)(2,1)S(1)}, u32[]{:S(2)}, u32[]{:S(2)}) collective-permute-start(bf16[1,128,128]{2,1,0:T(8,128)(2,1)S(1)} %get-tuple-element.18), channel_id=1, source_target_pairs={{0,1},{1,2},{2,3},{3,4},{4,5},{5,6},{6,7},{7,8},{8,9},{9,10},{10,1... | collective-permute-start | bytes 98312 | tf_op jit(solution)/shard_map/ppermute | solution.py:250
  6.9 5.5 %collective-permute-start.1 = (bf16[1,128,128]{2,1,0:T(8,128)(2,1)S(1)}, bf16[1,128,128]{2,1,0:T(8,128)(2,1)S(1)}, u32[]{:S(2)}, u32[]{:S(2)}) collective-permute-start(bf16[1,128,128]{2,1,0:T(8,128)(2,1)S(1)} %get-tuple-element.17), channel_id=1, source_target_pairs={{1,0},{2,1},{3,2},{4,3},{5,4},{6,5},{7,6},{8,7},{9,8},{10,9},{11,1... | collective-permute-start | bytes 98312 | tf_op jit(solution)/shard_map/ppermute | solution.py:250
  12.4 0.9 copy-start.1
  13.4 0.9 copy-start.2
  40.0 5.2 %collective-permute-start.2 = (bf16[2,192,128]{2,1,0:T(8,128)(2,1)S(1)}, bf16[2,192,128]{2,1,0:T(8,128)(2,1)S(1)}, u32[]{:S(2)}, u32[]{:S(2)}) collective-permute-start(bf16[2,192,128]{2,1,0:T(8,128)(2,1)S(1)} %slice.48), channel_id=1, source_target_pairs={{0,128},{128,256},{256,384},{1,129},{129,257},{257,385},{2,130},{1... | collective-permute-start | bytes 294920 | tf_op jit(solution)/shard_map/ppermute | solution.py:250
  51.5 3.7 %collective-permute-start.6 = (bf16[1728,128]{1,0:T(8,128)(2,1)S(1)}, bf16[1728,128]{1,0:T(8,128)(2,1)S(1)}, u32[]{:S(2)}, u32[]{:S(2)}) collective-permute-start(bf16[1728,128]{1,0:T(8,128)(2,1)S(1)} %dynamic-slice_bitcast_fusion), channel_id=1, source_target_pairs={{0,1},{1,0},{2,3},{3,2},{4,5},{5,4},{6,7},{7,6},{8,9},{9,8},{10,11... | collective-permute-start | bytes 1327112 | tf_op jit(solution)/shard_map/ppermute | solution.py:254
  93.9 28.6 %all-to-all-start.3 = ((bf16[256,8,128]{2,1,0:T(8,128)(2,1)}), bf16[256,8,128]{2,1,0:T(8,128)(2,1)S(1)}, u32[]{:S(2)}, u32[]{:S(2)}) async-start(bf16[256,8,128]{2,1,0:T(8,128)(2,1)} %broadcast_in_dim.14), calls=%async_computation.3 | async-start | bytes 1048576 | tf_op jit(solution)/shard_map/all_to_all | solution.py:271
  104.7 7.5 %collective-permute-start.4 = (bf16[8,16,128]{2,1,0:T(8,128)(2,1)S(1)}, bf16[8,16,128]{2,1,0:T(8,128)(2,1)S(1)}, u32[]{:S(2)}, u32[]{:S(2)}) collective-permute-start(bf16[8,16,128]{2,1,0:T(8,128)(2,1)S(1)} %get-tuple-element.15), channel_id=1, source_target_pairs={{1,0},{2,1},{3,2},{4,3},{5,4},{6,5},{7,6},{8,7},{9,8},{10,9},{11,1... | collective-permute-start | bytes 98312 | tf_op jit(solution)/shard_map/ppermute | solution.py:250
  108.0 5.0 %collective-permute-start.3 = (bf16[8,16,128]{2,1,0:T(8,128)(2,1)S(1)}, bf16[8,16,128]{2,1,0:T(8,128)(2,1)S(1)}, u32[]{:S(2)}, u32[]{:S(2)}) collective-permute-start(bf16[8,16,128]{2,1,0:T(8,128)(2,1)S(1)} %get-tuple-element.16), channel_id=1, source_target_pairs={{0,1},{1,2},{2,3},{3,4},{4,5},{5,6},{6,7},{7,8},{8,9},{9,10},{10,1... | collective-permute-start | bytes 98312 | tf_op jit(solution)/shard_map/ppermute | solution.py:250
  113.0 6.1 %collective-permute-start.5 = (bf16[2,160,128]{2,1,0:T(8,128)(2,1)S(1)}, bf16[2,160,128]{2,1,0:T(8,128)(2,1)S(1)}, u32[]{:S(2)}, u32[]{:S(2)}) collective-permute-start(bf16[2,160,128]{2,1,0:T(8,128)(2,1)S(1)} %pad_maximum_fusion.1), channel_id=1, source_target_pairs={{128,0},{256,128},{384,256},{129,1},{257,129},{385,257},{130,2},{2... | collective-permute-start | bytes 245768 | tf_op jit(solution)/shard_map/ppermute | solution.py:250
  122.6 26.2 %all-to-all-start.1 = ((bf16[8,272,128]{2,1,0:T(8,128)(2,1)}), bf16[8,272,128]{2,1,0:T(8,128)(2,1)S(1)}, u32[]{:S(2)}, u32[]{:S(2)}) async-start(bf16[8,272,128]{2,1,0:T(8,128)(2,1)} %shard_map.60), calls=%async_computation.1 | async-start | bytes 1114112 | tf_op jit(solution)/shard_map/all_to_all | solution.py:324
  131.1 18.4 %collective-permute-start.7 = (bf16[1728,128]{1,0:T(8,128)(2,1)S(1)}, bf16[1728,128]{1,0:T(8,128)(2,1)S(1)}, u32[]{:S(2)}, u32[]{:S(2)}) collective-permute-start(bf16[1728,128]{1,0:T(8,128)(2,1)S(1)} %slice_bitcast_fusion), channel_id=1, source_target_pairs={{0,1},{1,0},{2,3},{3,2},{4,5},{5,4},{6,7},{7,6},{8,9},{9,8},{10,11... | collective-permute-start | bytes 1327112 | tf_op jit(solution)/shard_map/ppermute | solution.py:254

commit v2 on v1

--- a/solution.py
+++ b/solution.py
@@ -16,11 +16,11 @@
 STRIP = 16
 TILE = ROWS * STRIP
 TALL = ROWS + 2
-HELD = TALL * STRIP + 2 * STRIP
 CH = 128
 WIDE = 9 * CH
 FRAMES = GROUP + 2
 EDGES = 2 * ROWS
+HELD = TILE + EDGES
 PART = 8
 
 band_weight = 0.75
@@ -40,29 +40,31 @@
     )
 
 
-def pack_body(x_ref, up_ref, down_ref, cot_ref, out_ref, left_ref, right_ref):
+def pack_body(x_hbm, cot_hbm, out_ref, cot_out_ref, x_ref, cot_ref, left_ref, right_ref, sems):
+    x_copy = pltpu.make_async_copy(x_hbm, x_ref, sems.at[0])
+    cot_copy = pltpu.make_async_copy(cot_hbm, cot_ref, sems.at[1])
+    x_copy.start()
+    cot_copy.start()
     left_ref[...] = jnp.zeros_like(left_ref)
     right_ref[...] = jnp.zeros_like(right_ref)
-    for tall_row in range(TALL):
-        if tall_row == 0:
-            line = up_ref[0]
-        elif tall_row == TALL - 1:
-            line = down_ref[0]
-        else:
-            line = x_ref[tall_row - 1]
+    x_copy.wait()
+    for row in range(ROWS):
+        line = x_ref[row]
         wide = line.astype(f32)
         for strip in range(GROUP):
             low = strip * STRIP
-            out_ref[strip, pl.ds(tall_row * STRIP, STRIP), :] = line[low : low + STRIP]
+            out_ref[strip, pl.ds(row * STRIP, STRIP), :] = line[low : low + STRIP]
             if strip > 0:
-                left_ref[strip, pl.ds(tall_row, 1), :] = wide[low - 1 : low]
+                left_ref[strip, pl.ds(row, 1), :] = wide[low - 1 : low]
             if strip < GROUP - 1:
-                right_ref[strip, pl.ds(tall_row, 1), :] = wide[low + STRIP : low + STRIP + 1]
+                right_ref[strip, pl.ds(row, 1), :] = wide[low + STRIP : low + STRIP + 1]
     for strip in range(GROUP):
-        out_ref[strip, pl.ds(TALL * STRIP, STRIP), :] = left_ref[strip].astype(bf16)
-        out_ref[strip, pl.ds(TALL * STRIP + STRIP, STRIP), :] = right_ref[strip].astype(bf16)
+        pair = jnp.concatenate([left_ref[strip], right_ref[strip]], axis=0)
+        out_ref[strip, pl.ds(TILE, EDGES), :] = pair.astype(bf16)
+    cot_copy.wait()
+    for strip in range(GROUP):
         for row in range(ROWS):
-            out_ref[strip, pl.ds(HELD + row * STRIP, STRIP), :] = cot_ref[
+            cot_out_ref[strip, pl.ds(row * STRIP, STRIP), :] = cot_ref[
                 row, pl.ds(strip * STRIP, STRIP), :
             ]
 
@@ -81,19 +83,38 @@
                 col_ref[pl.ds(start, STRIP), pl.ds(tap * CH, CH)] = piece
 
 
-def forward_body(held_ref, early_ref, w_ref, code_ref, g_ref, dw_ref, col_ref, lin_ref, gt_ref):
+def forward_body(
+    held_ref,
+    early_ref,
+    up_ref,
+    down_ref,
+    cot_ref,
+    w_ref,
+    code_ref,
+    g_ref,
+    dw_ref,
+    col_ref,
+    lin_ref,
+    gt_ref,
+):
     def spread(ref, frame, place):
-        left = ref[frame, pl.ds(TALL * STRIP, STRIP), :].astype(f32)
-        right = ref[frame, pl.ds(TALL * STRIP + STRIP, STRIP), :].astype(f32)
         for tall_row in range(TALL):
-            line = ref[frame, pl.ds(tall_row * STRIP, STRIP), :]
+            if tall_row == 0:
+                source, at, low, row = up_ref, place, 0, ROWS - 1
+            elif tall_row == TALL - 1:
+                source, at, low, row = down_ref, place, 0, 0
+            else:
+                source, at, row = ref, frame, tall_row - 1
+                low = row * STRIP
+            line = source[at, pl.ds(low, STRIP), :]
+            edge = source[at, pl.ds(source.shape[1] - EDGES, EDGES), :].astype(f32)
             place_line(
                 col_ref,
                 place * TILE,
                 tall_row,
                 line,
-                left[tall_row : tall_row + 1],
-                right[tall_row : tall_row + 1],
+                edge[row : row + 1],
+                edge[ROWS + row : ROWS + row + 1],
             )
 
     @pl.loop(0, 2)
@@ -135,9 +156,7 @@
             code_ref[member, pl.ds(low, STRIP), :] = code
             code_ref[member + 1, pl.ds(low, STRIP), :] = code
 
-        cot = [
-            held_ref[frame, pl.ds(HELD + low, STRIP), :].astype(f32) for frame in range(GROUP)
-        ]
+        cot = [cot_ref[frame, pl.ds(low, STRIP), :].astype(f32) for frame in range(GROUP)]
         back = [None] * GROUP
         for level in range(LEVELS - 1, -1, -1):
             step = 1 << level
@@ -254,7 +273,7 @@
     return lax.ppermute(value, "core", [(0, 1), (1, 0)])
 
 
-def summed_everywhere(terms, norm):
+def own_share(terms, norm):
     chips = ("x", "y", "z")
     count = lax.axis_size(chips)
     core = lax.axis_index("core")
@@ -266,9 +285,14 @@
     share = PART * -(-rows // (PART * count))
     padded = jnp.pad(chip_sum, ((0, share * count - rows), (0, 0)))
     spread = lax.all_to_all(padded.reshape(count, share, CH), chips, 0, 0)
-    total = (spread.astype(f32).sum(axis=0) * norm).astype(bf16)
-    copies = jnp.broadcast_to(total[None], (count, share, CH))
-    half = lax.all_to_all(copies, chips, 0, 0).reshape(count * share, CH)[:rows]
+    return (spread.astype(f32).sum(axis=0) * norm).astype(bf16), rows
+
+
+def all_shares(total, rows):
+    chips = ("x", "y", "z")
+    core = lax.axis_index("core")
+    copies = jnp.broadcast_to(total[None], (lax.axis_size(chips),) + total.shape)
+    half = lax.all_to_all(copies, chips, 0, 0).reshape(-1, CH)[:rows]
     paired = swapped(half)
     low = jnp.where(core == 0, half, paired)
     high = jnp.where(core == 0, paired, half)
@@ -280,15 +304,32 @@
     weights = kernel.reshape(3, WIDE, CH)
     turned = jnp.swapaxes(kernel[::-1, ::-1, ::-1], 3, 4).reshape(3, WIDE, CH)
     lines = ("z", "core")
-    up = shifted(x[ROWS - 1 : ROWS], lines, 1)
-    down = shifted(x[0:1], lines, -1)
-    packed = kernel_call(
+    packed, cot_packed = pl.pallas_call(
         pack_body,
-        jax.ShapeDtypeStruct((GROUP, HELD + TILE, CH), bf16),
-        [pltpu.VMEM((GROUP, STRIP, CH), f32)] * 2,
-    )(x, up, down, cotangent[0])
+        out_shape=(
+            jax.ShapeDtypeStruct((GROUP, HELD, CH), bf16),
+            jax.ShapeDtypeStruct((GROUP, TILE, CH), bf16),
+        ),
+        in_specs=[pl.BlockSpec(memory_space=pl.ANY)] * 2,
+        scratch_shapes=[
+            pltpu.VMEM((ROWS, GROUP * STRIP, CH), bf16),
+            pltpu.VMEM((ROWS, GROUP * STRIP, CH), bf16),
+            pltpu.VMEM((GROUP, ROWS, CH), f32),
+            pltpu.VMEM((GROUP, ROWS, CH), f32),
+            pltpu.SemaphoreType.DMA((2,)),
+        ],
+        compiler_params=pltpu.CompilerParams(vmem_limit_bytes=VMEM_LIMIT),
+    )(frames[0], cotangent[0])
     held = lax.all_to_all(packed, "y", 0, 0)
-    early = shifted(held[GROUP - 2 :, :HELD], "x", 1)
+    cot = lax.all_to_all(cot_packed, "y", 0, 0)
+    early = shifted(held[GROUP - 2 :], "x", 1)
+    last, first = [
+        jnp.concatenate([value[:, low : low + STRIP] for value in (early, held)], axis=0)
+        for low in (TILE - STRIP, 0)
+    ]
+    edges = jnp.concatenate([early[:, TILE:], held[:, TILE:]], axis=0)
+    up = shifted(jnp.concatenate([last, edges], axis=1), lines, 1)
+    down = shifted(jnp.concatenate([first, edges], axis=1), lines, -1)
 
     flops = 2 * GROUP * TILE * 27 * CH * CH
     code, g, terms = kernel_call(
@@ -304,10 +345,10 @@
             pltpu.VMEM((3 * CH, FRAMES * TILE), bf16),
         ],
         flops=2 * flops,
-    )(held, early, weights)
+    )(held, early, up, down, cot, weights)
 
     norm = 1.0 / math.sqrt(lax.axis_size(("x", "y", "z", "core")) * GROUP * TILE)
-    grad_kernel = summed_everywhere(terms.reshape(27 * CH, CH), norm)
+    total, half_rows = own_share(terms.reshape(27 * CH, CH), norm)
 
     g_up = shifted(g[:, TILE - STRIP :], lines, 1)
     g_down = shifted(g[:, :STRIP], lines, -1)
@@ -321,6 +362,8 @@
         ],
         flops=flops,
     )(g, g_up, g_down, late, code, turned)
+    total, sent = lax.optimization_barrier((total, sent))
+    grad_kernel = all_shares(total, half_rows)
     got = lax.all_to_all(sent, "y", 0, 0)
     whole = jax.ShapeDtypeStruct((ROWS, GROUP * STRIP, CH), bf16)
     code_out, grad_frames = kernel_call(unpack_body, (whole, whole))(got)

time: 152 us -> 159 us (1.046)
  starting transfers between devices: 43.2 us -> 60.1 us
  blocking collectives: 62.9 us -> 54.8 us
  waiting for transfers between devices: 26.3 us -> 24 us
    all_to_all x1 -> x2, starting transfers between devices: 10.8 us -> 29 us  [the longest x1 25.5 us: own_share(): spread = lax.all_to_all(padded.reshape(count, share, CH), chips, 0, 0)]
    all_to_all x1, blocking collectives: 25.5 us -> 17.6 us  [shards(): held = lax.all_to_all(packed, 'y', 0, 0)]
    all_to_all x1, starting transfers between devices: 8.52 us -> 5.75 us  [shards(): got = lax.all_to_all(sent, 'y', 0, 0)]
    all_to_all x1, waiting for transfers between devices: 15.7 us -> 13.6 us  [shards(): got = lax.all_to_all(sent, 'y', 0, 0)]
  transfers between devices with their start and end apart: 10 -> 11, of which waited for: 7 -> 7; matrix products, arithmetic and copies ran while one was open for 1% -> 1% of each run, Pallas kernels for 3% -> 3%
where the time goes in v2:
time: 159 us
  starting transfers between devices  60.1 us (38%)
  blocking collectives  54.8 us (34%)
  waiting for transfers between devices  24 us (15%)
  Pallas kernels  11.5 us (7%)
  local copies, waits for them, and re-layouts  4.43 us (3%)
  other arithmetic  3 us (2%)
    all_to_all x1, blocking collectives, all_shares(): half = lax.all_to_all(copies, chips, 0, 0).reshape(-1, CH)[:rows]  37.2 us
    all_to_all x1, starting transfers between devices, own_share(): spread = lax.all_to_all(padded.reshape(count, share, CH), chips, 0, 0)  25.5 us
    ppermute x6, starting transfers between devices, shifted(): return lax.ppermute(value, axes, route)  20 us
    all_to_all x1, blocking collectives, shards(): held = lax.all_to_all(packed, 'y', 0, 0)  17.6 us
    all_to_all x1, waiting for transfers between devices, shards(): got = lax.all_to_all(sent, 'y', 0, 0)  13.6 us
    ppermute x6, waiting for transfers between devices, shifted(): return lax.ppermute(value, axes, route)  8.66 us
    pallas_call x1, Pallas kernels, shards(): kernel_call(forward_body, (jax.ShapeDtypeStruct((GROUP, TILE, CH), bf16),...  6.32 us
    all_to_all x1, starting transfers between devices, shards(): got = lax.all_to_all(sent, 'y', 0, 0)  5.75 us
  transfers between devices with their start and end apart: 11, of which 7 were waited for; matrix products, arithmetic and copies ran while one was open for 1% of the time, Pallas kernels for 3%

profile of v2, /device:TPU:1, one launch (start us, length us, event | category | flops | bytes accessed | tf_op | source)
XLA Modules:
  0.0 158.6 jit_solution(2128517824746427924)
XLA Ops:
  0.6 0.0 copy-start
  0.6 0.0 copy-start.1
  0.7 1.0 copy-done.1
  1.7 0.0 copy-start.2
  1.7 0.9 copy-done.2
  2.6 0.9 shard_map.58
  3.5 17.6 %all_to_all.25.held_ref = bf16[8,144,128]{2,1,0:T(8,128)(2,1)S(1)} all-to-all(bf16[8,144,128]{2,1,0:T(8,128)(2,1)S(1)} %get-tuple-element.12), channel_id=1, replica_groups=mesh['x'=4,'y'=8,'z'=8,'core'=2] {'y'}, dimensions={0} | all-to-all | bytes 589824 | tf_op jit(solution)/shard_map/all_to_all | solution.py:323
  21.1 3.4 %all-to-all-start.1 = ((bf16[8,128,128]{2,1,0:T(8,128)(2,1)}), bf16[8,128,128]{2,1,0:T(8,128)(2,1)S(1)}, u32[]{:S(2)}, u32[]{:S(2)}) async-start(bf16[8,128,128]{2,1,0:T(8,128)(2,1)} %get-tuple-element.13), calls=%async_computation.1 | async-start | bytes 524288 | tf_op jit(solution)/shard_map/all_to_all | solution.py:324
  24.5 3.8 %collective-permute-start = (bf16[2,144,128]{2,1,0:T(8,128)(2,1)S(1)}, bf16[2,144,128]{2,1,0:T(8,128)(2,1)S(1)}, u32[]{:S(2)}, u32[]{:S(2)}) collective-permute-start(bf16[2,144,128]{2,1,0:T(8,128)(2,1)S(1)} %slice.56), channel_id=1, source_target_pairs={{0,128},{128,256},{256,384},{1,129},{129,257},{257,385},{2,130},{1... | collective-permute-start | bytes 221192 | tf_op jit(solution)/shard_map/ppermute | solution.py:269
  28.4 1.4 collective-permute-done.early_ref
  29.8 5.5 %collective-permute-start.2 = (bf16[10,32,128]{2,1,0:T(8,128)(2,1)S(1)}, bf16[10,32,128]{2,1,0:T(8,128)(2,1)S(1)}, u32[]{:S(2)}, u32[]{:S(2)}) collective-permute-start(bf16[10,32,128]{2,1,0:T(8,128)(2,1)S(1)} %get-tuple-element.31), channel_id=1, source_target_pairs={{1,0},{2,1},{3,2},{4,3},{5,4},{6,5},{7,6},{8,7},{9,8},{10,9},{11,1... | collective-permute-start | bytes 245768 | tf_op jit(solution)/shard_map/ppermute | solution.py:269
  35.2 3.9 %collective-permute-start.1 = (bf16[10,32,128]{2,1,0:T(8,128)(2,1)S(1)}, bf16[10,32,128]{2,1,0:T(8,128)(2,1)S(1)}, u32[]{:S(2)}, u32[]{:S(2)}) collective-permute-start(bf16[10,32,128]{2,1,0:T(8,128)(2,1)S(1)} %get-tuple-element.32), channel_id=1, source_target_pairs={{0,1},{1,2},{2,3},{3,4},{4,5},{5,6},{6,7},{7,8},{8,9},{9,10},{10,1... | collective-permute-start | bytes 245768 | tf_op jit(solution)/shard_map/ppermute | solution.py:269
  39.1 0.0 all-to-all-done.1.cot_ref
  39.1 0.2 collective-permute-done.2.down_ref
  39.3 1.3 collective-permute-done.1.up_ref
  40.6 0.0 copy-done
  40.6 6.3 %shard_map.59 = (bf16[8,128,128]{2,1,0:T(8,128)(2,1)S(1)}, bf16[8,128,128]{2,1,0:T(8,128)(2,1)S(1)}, bf16[27,128,128]{2,1,0:T(8,128)(2,1)S(1)}) custom-call(bf16[8,144,128]{2,1,0:T(8,128)(2,1)S(1)} %all_to_all.25.held_ref, bf16[2,144,128]{2,1,0:T(8,128)(2,1)S(1)} %collective-permute-done.early_ref, bf16[10,32,128]{2,1,0:T(8,128)(2,1)S(1)} %collective-permute-done.1.up_ref, ...), custom_call_target="tpu_custom_call" | custom-call | flops 1811939328 | bytes 4194304 | tf_op jit(solution)/shard_map/pallas_call | solution.py:335
  47.0 1.9 %collective-permute-start.3 = (bf16[1728,128]{1,0:T(8,128)(2,1)S(1)}, bf16[1728,128]{1,0:T(8,128)(2,1)S(1)}, u32[]{:S(2)}, u32[]{:S(2)}) collective-permute-start(bf16[1728,128]{1,0:T(8,128)(2,1)S(1)} %dynamic-slice_bitcast_fusion), channel_id=1, source_target_pairs={{0,1},{1,0},{2,3},{3,2},{4,5},{5,4},{6,7},{7,6},{8,9},{9,8},{10,11... | collective-permute-start | bytes 1327112 | tf_op jit(solution)/shard_map/ppermute | solution.py:273
  48.9 1.8 %collective-permute-done.3 = bf16[1728,128]{1,0:T(8,128)(2,1)S(1)} collective-permute-done((bf16[1728,128]{1,0:T(8,128)(2,1)S(1)}, bf16[1728,128]{1,0:T(8,128)(2,1)S(1)}, u32[]{:S(2)}, u32[]{:S(2)}) %collective-permute-start.3) | collective-permute-done | bytes 442400 | tf_op jit(solution)/shard_map/ppermute | solution.py:273
  50.6 0.1 fusion
  50.8 0.8 pad_bitcast_fusion
  51.6 25.5 %all-to-all-start.2 = ((bf16[256,8,128]{2,1,0:T(8,128)(2,1)}), bf16[256,8,128]{2,1,0:T(8,128)(2,1)}, u32[]{:S(2)}, u32[]{:S(2)}) async-start(bf16[256,8,128]{2,1,0:T(8,128)(2,1)} %pad_bitcast_fusion), calls=%async_computation.2 | async-start | bytes 1048576 | tf_op jit(solution)/shard_map/all_to_all | solution.py:287
  77.2 2.6 %collective-permute-start.5 = (bf16[8,16,128]{2,1,0:T(8,128)(2,1)S(1)}, bf16[8,16,128]{2,1,0:T(8,128)(2,1)S(1)}, u32[]{:S(2)}, u32[]{:S(2)}) collective-permute-start(bf16[8,16,128]{2,1,0:T(8,128)(2,1)S(1)} %get-tuple-element.26), channel_id=1, source_target_pairs={{1,0},{2,1},{3,2},{4,3},{5,4},{6,5},{7,6},{8,7},{9,8},{10,9},{11,1... | collective-permute-start | bytes 98312 | tf_op jit(solution)/shard_map/ppermute | solution.py:269
  79.7 3.0 %collective-permute-start.4 = (bf16[8,16,128]{2,1,0:T(8,128)(2,1)S(1)}, bf16[8,16,128]{2,1,0:T(8,128)(2,1)S(1)}, u32[]{:S(2)}, u32[]{:S(2)}) collective-permute-start(bf16[8,16,128]{2,1,0:T(8,128)(2,1)S(1)} %get-tuple-element.27), channel_id=1, source_target_pairs={{0,1},{1,2},{2,3},{3,4},{4,5},{5,6},{6,7},{7,8},{8,9},{9,10},{10,1... | collective-permute-start | bytes 98312 | tf_op jit(solution)/shard_map/ppermute | solution.py:269
  82.8 2.7 %collective-permute-done.5.down_ref = bf16[8,16,128]{2,1,0:T(8,128)(2,1)S(1)} collective-permute-done((bf16[8,16,128]{2,1,0:T(8,128)(2,1)S(1)}, bf16[8,16,128]{2,1,0:T(8,128)(2,1)S(1)}, u32[]{:S(2)}, u32[]{:S(2)}) %collective-permute-start.5) | collective-permute-done | bytes 32800 | tf_op jit(solution)/shard_map/ppermute | solution.py:269
  85.5 0.0 collective-permute-done.4.up_ref
  85.5 1.3 collective-permute-start.6
  86.8 0.1 reverse_bitcast_fusion
  86.8 1.4 copy.6
  88.2 3.1 %collective-permute-done.6.late_ref = bf16[2,160,128]{2,1,0:T(8,128)(2,1)S(1)} collective-permute-done((bf16[2,160,128]{2,1,0:T(8,128)(2,1)S(1)}, bf16[2,160,128]{2,1,0:T(8,128)(2,1)S(1)}, u32[]{:S(2)}, u32[]{:S(2)}) %collective-permute-start.6) | collective-permute-done | bytes 81952 | tf_op jit(solution)/shard_map/ppermute | solution.py:269
  91.4 3.5 %shard_map.60 = bf16[8,272,128]{2,1,0:T(8,128)(2,1)} custom-call(bf16[8,128,128]{2,1,0:T(8,128)(2,1)S(1)} %get-tuple-element.15.g_ref, bf16[8,16,128]{2,1,0:T(8,128)(2,1)S(1)} %collective-permute-done.4.up_ref, bf16[8,16,128]{2,1,0:T(8,128)(2,1)S(1)} %collective-permute-done.5.down_ref, bf16[2,160,128]{2,1,0:T(8,128)(2,1)S(1)} %collective-permute-done.6.late_ref, ...), custom_call_target="tpu_custom_call" | custom-call | flops 905969664 | bytes 4194304 | tf_op jit(solution)/shard_map/pallas_call | solution.py:356
  94.9 0.0 all-to-all-done.2
  94.9 1.3 convert_reduce_fusion
  96.2 0.1 broadcast_in_dim.14
  96.3 37.2 %all_to_all.26 = bf16[256,8,128]{2,1,0:T(8,128)(2,1)S(1)} all-to-all(bf16[256,8,128]{2,1,0:T(8,128)(2,1)S(1)} %broadcast_in_dim.14), channel_id=1, replica_groups=mesh['x'=4,'y'=8,'z'=8,'core'=2] {'x','y','z'}, dimensions={0} | all-to-all | bytes 1048576 | tf_op jit(solution)/shard_map/all_to_all | solution.py:295
  133.4 5.7 %all-to-all-start.3 = ((bf16[8,272,128]{2,1,0:T(8,128)(2,1)}), bf16[8,272,128]{2,1,0:T(8,128)(2,1)S(1)}, u32[]{:S(2)}, u32[]{:S(2)}) async-start(bf16[8,272,128]{2,1,0:T(8,128)(2,1)} %shard_map.60), calls=%async_computation.3 | async-start | bytes 1114112 | tf_op jit(solution)/shard_map/all_to_all | solution.py:367
  139.2 3.5 %collective-permute-start.7 = (bf16[1728,128]{1,0:T(8,128)(2,1)S(1)}, bf16[1728,128]{1,0:T(8,128)(2,1)S(1)}, u32[]{:S(2)}, u32[]{:S(2)}) collective-permute-start(bf16[1728,128]{1,0:T(8,128)(2,1)S(1)} %slice_bitcast_fusion), channel_id=1, source_target_pairs={{0,1},{1,0},{2,3},{3,2},{4,5},{5,4},{6,7},{7,6},{8,9},{9,8},{10,11... | collective-permute-start | bytes 1327112 | tf_op jit(solution)/shard_map/ppermute | solution.py:273
  142.7 13.6 %all-to-all-done.3.got_ref = bf16[8,272,128]{2,1,0:T(8,128)(2,1)S(1)} async-done(((bf16[8,272,128]{2,1,0:T(8,128)(2,1)}), bf16[8,272,128]{2,1,0:T(8,128)(2,1)S(1)}, u32[]{:S(2)}, u32[]{:S(2)}) %all-to-all-start.3) | async-done | bytes 557088 | tf_op jit(solution)/shard_map/all_to_all | solution.py:367
  156.3 0.8 shard_map.61
  157.1 0.0 collective-permute-done.7
  157.1 0.1 broadcast_select_fusion.1
  157.2 0.1 pad_maximum_fusion
  157.2 1.4 convert.3
  (12 shorter events, 0.1 us)
Async XLA Ops:
  0.6 40.0 %copy-start = (bf16[3,3,3,128,128]{4,3,2,1,0:T(8,128)(2,1)S(1)}, bf16[3,3,3,128,128]{4,3,2,1,0:T(8,128)(2,1)}, u32[]{:S(2)}) copy-start(bf16[3,3,3,128,128]{4,3,2,1,0:T(8,128)(2,1)} %param.4) | copy-start | bytes 2654212
  0.6 1.0 copy-start.1
  1.7 0.9 copy-start.2
  21.1 18.0 %all-to-all-start.1 = ((bf16[8,128,128]{2,1,0:T(8,128)(2,1)}), bf16[8,128,128]{2,1,0:T(8,128)(2,1)S(1)}, u32[]{:S(2)}, u32[]{:S(2)}) async-start(bf16[8,128,128]{2,1,0:T(8,128)(2,1)} %get-tuple-element.13), calls=%async_computation.1 | async-start | bytes 524288 | tf_op jit(solution)/shard_map/all_to_all | solution.py:324
  24.5 5.2 %collective-permute-start = (bf16[2,144,128]{2,1,0:T(8,128)(2,1)S(1)}, bf16[2,144,128]{2,1,0:T(8,128)(2,1)S(1)}, u32[]{:S(2)}, u32[]{:S(2)}) collective-permute-start(bf16[2,144,128]{2,1,0:T(8,128)(2,1)S(1)} %slice.56), channel_id=1, source_target_pairs={{0,128},{128,256},{256,384},{1,129},{129,257},{257,385},{2,130},{1... | collective-permute-start | bytes 221192 | tf_op jit(solution)/shard_map/ppermute | solution.py:269
  29.8 9.5 %collective-permute-start.2 = (bf16[10,32,128]{2,1,0:T(8,128)(2,1)S(1)}, bf16[10,32,128]{2,1,0:T(8,128)(2,1)S(1)}, u32[]{:S(2)}, u32[]{:S(2)}) collective-permute-start(bf16[10,32,128]{2,1,0:T(8,128)(2,1)S(1)} %get-tuple-element.31), channel_id=1, source_target_pairs={{1,0},{2,1},{3,2},{4,3},{5,4},{6,5},{7,6},{8,7},{9,8},{10,9},{11,1... | collective-permute-start | bytes 245768 | tf_op jit(solution)/shard_map/ppermute | solution.py:269
  35.2 5.4 %collective-permute-start.1 = (bf16[10,32,128]{2,1,0:T(8,128)(2,1)S(1)}, bf16[10,32,128]{2,1,0:T(8,128)(2,1)S(1)}, u32[]{:S(2)}, u32[]{:S(2)}) collective-permute-start(bf16[10,32,128]{2,1,0:T(8,128)(2,1)S(1)} %get-tuple-element.32), channel_id=1, source_target_pairs={{0,1},{1,2},{2,3},{3,4},{4,5},{5,6},{6,7},{7,8},{8,9},{9,10},{10,1... | collective-permute-start | bytes 245768 | tf_op jit(solution)/shard_map/ppermute | solution.py:269
  47.0 3.7 %collective-permute-start.3 = (bf16[1728,128]{1,0:T(8,128)(2,1)S(1)}, bf16[1728,128]{1,0:T(8,128)(2,1)S(1)}, u32[]{:S(2)}, u32[]{:S(2)}) collective-permute-start(bf16[1728,128]{1,0:T(8,128)(2,1)S(1)} %dynamic-slice_bitcast_fusion), channel_id=1, source_target_pairs={{0,1},{1,0},{2,3},{3,2},{4,5},{5,4},{6,7},{7,6},{8,9},{9,8},{10,11... | collective-permute-start | bytes 1327112 | tf_op jit(solution)/shard_map/ppermute | solution.py:273
  51.6 43.3 %all-to-all-start.2 = ((bf16[256,8,128]{2,1,0:T(8,128)(2,1)}), bf16[256,8,128]{2,1,0:T(8,128)(2,1)}, u32[]{:S(2)}, u32[]{:S(2)}) async-start(bf16[256,8,128]{2,1,0:T(8,128)(2,1)} %pad_bitcast_fusion), calls=%async_computation.2 | async-start | bytes 1048576 | tf_op jit(solution)/shard_map/all_to_all | solution.py:287
  77.2 8.3 %collective-permute-start.5 = (bf16[8,16,128]{2,1,0:T(8,128)(2,1)S(1)}, bf16[8,16,128]{2,1,0:T(8,128)(2,1)S(1)}, u32[]{:S(2)}, u32[]{:S(2)}) collective-permute-start(bf16[8,16,128]{2,1,0:T(8,128)(2,1)S(1)} %get-tuple-element.26), channel_id=1, source_target_pairs={{1,0},{2,1},{3,2},{4,3},{5,4},{6,5},{7,6},{8,7},{9,8},{10,9},{11,1... | collective-permute-start | bytes 98312 | tf_op jit(solution)/shard_map/ppermute | solution.py:269
  79.7 5.7 %collective-permute-start.4 = (bf16[8,16,128]{2,1,0:T(8,128)(2,1)S(1)}, bf16[8,16,128]{2,1,0:T(8,128)(2,1)S(1)}, u32[]{:S(2)}, u32[]{:S(2)}) collective-permute-start(bf16[8,16,128]{2,1,0:T(8,128)(2,1)S(1)} %get-tuple-element.27), channel_id=1, source_target_pairs={{0,1},{1,2},{2,3},{3,4},{4,5},{5,6},{6,7},{7,8},{8,9},{9,10},{10,1... | collective-permute-start | bytes 98312 | tf_op jit(solution)/shard_map/ppermute | solution.py:269
  85.5 5.9 %collective-permute-start.6 = (bf16[2,160,128]{2,1,0:T(8,128)(2,1)S(1)}, bf16[2,160,128]{2,1,0:T(8,128)(2,1)S(1)}, u32[]{:S(2)}, u32[]{:S(2)}) collective-permute-start(bf16[2,160,128]{2,1,0:T(8,128)(2,1)S(1)} %pad_maximum_fusion.2), channel_id=1, source_target_pairs={{128,0},{256,128},{384,256},{129,1},{257,129},{385,257},{130,2},{2... | collective-permute-start | bytes 245768 | tf_op jit(solution)/shard_map/ppermute | solution.py:269
  133.4 22.9 %all-to-all-start.3 = ((bf16[8,272,128]{2,1,0:T(8,128)(2,1)}), bf16[8,272,128]{2,1,0:T(8,128)(2,1)S(1)}, u32[]{:S(2)}, u32[]{:S(2)}) async-start(bf16[8,272,128]{2,1,0:T(8,128)(2,1)} %shard_map.60), calls=%async_computation.3 | async-start | bytes 1114112 | tf_op jit(solution)/shard_map/all_to_all | solution.py:367
  139.2 17.9 %collective-permute-start.7 = (bf16[1728,128]{1,0:T(8,128)(2,1)S(1)}, bf16[1728,128]{1,0:T(8,128)(2,1)S(1)}, u32[]{:S(2)}, u32[]{:S(2)}) collective-permute-start(bf16[1728,128]{1,0:T(8,128)(2,1)S(1)} %slice_bitcast_fusion), channel_id=1, source_target_pairs={{0,1},{1,0},{2,3},{3,2},{4,5},{5,4},{6,7},{7,6},{8,9},{9,8},{10,11... | collective-permute-start | bytes 1327112 | tf_op jit(solution)/shard_map/ppermute | solution.py:273

commit v3 on v2

--- a/solution.py
+++ b/solution.py
@@ -273,30 +273,65 @@
     return lax.ppermute(value, "core", [(0, 1), (1, 0)])
 
 
+def order_body(x_ref, own_ref, one_ref, two_ref, three_ref, out_ref):
+    for step, ref in enumerate((own_ref, one_ref, two_ref, three_ref)):
+        out_ref[lax.rem(x_ref[0] + step, 4)] = ref[...]
+
+
+def finish_body(core_ref, own_ref, other_ref, out_ref):
+    core = core_ref[0]
+    out_ref[core] = own_ref[...].astype(f32)
+    out_ref[1 - core] = other_ref[...].astype(f32)
+
+
+def indexed_call(body, out, index, *arrays):
+    return pl.pallas_call(
+        body,
+        out_shape=out,
+        in_specs=[pl.BlockSpec(memory_space=pltpu.SMEM)]
+        + [pl.BlockSpec(memory_space=pltpu.VMEM)] * len(arrays),
+        compiler_params=pltpu.CompilerParams(vmem_limit_bytes=VMEM_LIMIT),
+    )(index.astype(jnp.int32).reshape(1), *arrays)
+
+
 def own_share(terms, norm):
-    chips = ("x", "y", "z")
-    count = lax.axis_size(chips)
     core = lax.axis_index("core")
+    wide, planes = lax.axis_size("x"), lax.axis_size(("y", "z"))
     rows = terms.shape[0] // 2
     halves = terms.reshape(2, rows, CH)
     mine = lax.dynamic_index_in_dim(halves, core, 0, keepdims=False)
     other = lax.dynamic_index_in_dim(halves, 1 - core, 0, keepdims=False)
     chip_sum = (mine.astype(f32) + swapped(other).astype(f32)).astype(bf16)
-    share = PART * -(-rows // (PART * count))
-    padded = jnp.pad(chip_sum, ((0, share * count - rows), (0, 0)))
-    spread = lax.all_to_all(padded.reshape(count, share, CH), chips, 0, 0)
-    return (spread.astype(f32).sum(axis=0) * norm).astype(bf16), rows
+    parts = lax.all_to_all(chip_sum.reshape(wide, rows // wide, CH), "x", 0, 0)
+    part = parts.astype(f32).sum(axis=0).astype(bf16)
+    share = PART * -(-part.shape[0] // (PART * planes))
+    padded = jnp.pad(part, ((0, share * planes - part.shape[0]), (0, 0)))
+    spread = lax.all_to_all(padded.reshape(planes, share, CH), ("y", "z"), 0, 0)
+    return (spread.astype(f32).sum(axis=0) * norm).astype(bf16), part.shape[0]
 
 
 def all_shares(total, rows):
-    chips = ("x", "y", "z")
-    core = lax.axis_index("core")
-    copies = jnp.broadcast_to(total[None], (lax.axis_size(chips),) + total.shape)
-    half = lax.all_to_all(copies, chips, 0, 0).reshape(-1, CH)[:rows]
-    paired = swapped(half)
-    low = jnp.where(core == 0, half, paired)
-    high = jnp.where(core == 0, paired, half)
-    return jnp.concatenate([low, high], axis=0).astype(f32)
+    wide, planes = lax.axis_size("x"), lax.axis_size(("y", "z"))
+    copies = jnp.broadcast_to(total[None], (planes,) + total.shape)
+    part = lax.all_to_all(copies, ("y", "z"), 0, 0).reshape(-1, CH)[:rows]
+    others = [
+        lax.ppermute(part, "x", [(i, (i - step) % wide) for i in range(wide)])
+        for step in range(1, wide)
+    ]
+    half = indexed_call(
+        order_body,
+        jax.ShapeDtypeStruct((wide, rows, CH), bf16),
+        lax.axis_index("x"),
+        part,
+        *others,
+    ).reshape(wide * rows, CH)
+    return indexed_call(
+        finish_body,
+        jax.ShapeDtypeStruct((2, wide * rows, CH), f32),
+        lax.axis_index("core"),
+        half,
+        swapped(half),
+    )
 
 
 def shards(frames, kernel, cotangent):
@@ -318,7 +353,6 @@
             pltpu.VMEM((GROUP, ROWS, CH), f32),
             pltpu.SemaphoreType.DMA((2,)),
         ],
-        compiler_params=pltpu.CompilerParams(vmem_limit_bytes=VMEM_LIMIT),
     )(frames[0], cotangent[0])
     held = lax.all_to_all(packed, "y", 0, 0)
     cot = lax.all_to_all(cot_packed, "y", 0, 0)
@@ -348,7 +382,7 @@
     )(held, early, up, down, cot, weights)
 
     norm = 1.0 / math.sqrt(lax.axis_size(("x", "y", "z", "core")) * GROUP * TILE)
-    total, half_rows = own_share(terms.reshape(27 * CH, CH), norm)
+    total, part_rows = own_share(terms.reshape(27 * CH, CH), norm)
 
     g_up = shifted(g[:, TILE - STRIP :], lines, 1)
     g_down = shifted(g[:, :STRIP], lines, -1)
@@ -363,7 +397,7 @@
         flops=flops,
     )(g, g_up, g_down, late, code, turned)
     total, sent = lax.optimization_barrier((total, sent))
-    grad_kernel = all_shares(total, half_rows)
+    grad_kernel = all_shares(total, part_rows)
     got = lax.all_to_all(sent, "y", 0, 0)
     whole = jax.ShapeDtypeStruct((ROWS, GROUP * STRIP, CH), bf16)
     code_out, grad_frames = kernel_call(unpack_body, (whole, whole))(got)

time: 159 us -> 143 us (0.90)
  blocking collectives: 54.8 us -> 38 us
  starting transfers between devices: 60.1 us -> 70.9 us
  waiting for transfers between devices: 24 us -> 14.7 us
  Pallas kernels: 11.5 us -> 13.9 us
  local copies, waits for them, and re-layouts: 4.43 us -> 2.24 us
  other arithmetic: 3 us -> 1.05 us
    all_to_all x1, blocking collectives: 37.2 us -> 20.6 us  [all_shares(): part = lax.all_to_all(copies, ('y', 'z'), 0, 0).reshape(-1, CH)[:rows]]
    all_to_all x1, waiting for transfers between devices: 13.6 us -> 0.01 us  [shards(): got = lax.all_to_all(sent, 'y', 0, 0)]
    ppermute x0 -> x3, starting transfers between devices: none -> 9.61 us  [all_shares(): lax.ppermute(part, 'x', [(i, (i - step) % wide) for i in range(wide)])]
    ppermute x2, starting transfers between devices: 5.4 us -> 10.7 us  [swapped(): return lax.ppermute(value, 'core', [(0, 1), (1, 0)])]
    all_to_all x1 -> x2, starting transfers between devices: 25.5 us -> 22.2 us  [the longest x1 17.3 us: own_share(): spread = lax.all_to_all(padded.reshape(planes, share, CH), ('y', 'z'), 0, 0)]
    all_to_all x1 -> x2, waiting for transfers between devices: 0.01 us -> 3.28 us  [the longest x1 2.53 us: own_share(): spread = lax.all_to_all(padded.reshape(planes, share, CH), ('y', 'z'), 0, 0)]
    all_to_all x1, starting transfers between devices: 5.75 us -> 3.54 us  [shards(): got = lax.all_to_all(sent, 'y', 0, 0)]
    ppermute x6, waiting for transfers between devices: 8.66 us -> 6.48 us  [shifted(): return lax.ppermute(value, axes, route)]
  transfers between devices with their start and end apart: 11 -> 15, of which waited for: 7 -> 10; matrix products, arithmetic and copies ran while one was open for 1% -> 1% of each run, Pallas kernels for 3% -> 3%
where the time goes in v3:
time: 143 us; the launch traced here: 142 us
  starting transfers between devices  70.9 us (50%)
  blocking collectives  38 us (27%)
  waiting for transfers between devices  14.7 us (10%)
  Pallas kernels  13.9 us (10%)
  local copies, waits for them, and re-layouts  2.24 us (2%)
    ppermute x6, starting transfers between devices, shifted(): return lax.ppermute(value, axes, route)  21.4 us
    all_to_all x1, blocking collectives, all_shares(): part = lax.all_to_all(copies, ('y', 'z'), 0, 0).reshape(-1, CH)[:rows]  20.6 us
    all_to_all x1, blocking collectives, shards(): held = lax.all_to_all(packed, 'y', 0, 0)  17.4 us
    all_to_all x1, starting transfers between devices, own_share(): spread = lax.all_to_all(padded.reshape(planes, share, CH), ('y', 'z'), 0, 0)  17.3 us
    ppermute x2, starting transfers between devices, swapped(): return lax.ppermute(value, 'core', [(0, 1), (1, 0)])  10.7 us
    ppermute x3, starting transfers between devices, all_shares(): lax.ppermute(part, 'x', [(i, (i - step) % wide) for i in range(wide)])  9.61 us
    ppermute x6, waiting for transfers between devices, shifted(): return lax.ppermute(value, axes, route)  6.48 us
    pallas_call x1, Pallas kernels, shards(): kernel_call(forward_body, (jax.ShapeDtypeStruct((GROUP, TILE, CH), bf16),...  6.32 us
  transfers between devices with their start and end apart: 15, of which 10 were waited for; matrix products, arithmetic and copies ran while one was open for 1% of the time, Pallas kernels for 3%

profile of v3, /device:TPU:1, one launch (start us, length us, event | category | flops | bytes accessed | tf_op | source)
XLA Modules:
  0.0 141.7 jit_solution(17402810153832648595)
XLA Ops:
  0.6 0.0 copy-start
  0.6 1.9 %shard_map.58 = (bf16[8,144,128]{2,1,0:T(8,128)(2,1)}, bf16[8,128,128]{2,1,0:T(8,128)(2,1)}) custom-call(bf16[8,128,128]{2,1,0:T(8,128)(2,1)} %bitcast.30, bf16[8,128,128]{2,1,0:T(8,128)(2,1)} %bitcast.31), custom_call_target="tpu_custom_call" | custom-call | tf_op jit(solution)/shard_map/pallas_call | solution.py:342
  2.6 17.4 %all_to_all.30.held_ref = bf16[8,144,128]{2,1,0:T(8,128)(2,1)S(1)} all-to-all(bf16[8,144,128]{2,1,0:T(8,128)(2,1)} %get-tuple-element.12), channel_id=1, replica_groups=mesh['x'=4,'y'=8,'z'=8,'core'=2] {'y'}, dimensions={0} | all-to-all | bytes 589824 | tf_op jit(solution)/shard_map/all_to_all | solution.py:357
  19.9 3.4 %all-to-all-start.1 = ((bf16[8,128,128]{2,1,0:T(8,128)(2,1)}), bf16[8,128,128]{2,1,0:T(8,128)(2,1)S(1)}, u32[]{:S(2)}, u32[]{:S(2)}) async-start(bf16[8,128,128]{2,1,0:T(8,128)(2,1)} %get-tuple-element.13), calls=%async_computation.1 | async-start | bytes 524288 | tf_op jit(solution)/shard_map/all_to_all | solution.py:358
  23.4 4.3 %collective-permute-start = (bf16[2,144,128]{2,1,0:T(8,128)(2,1)S(1)}, bf16[2,144,128]{2,1,0:T(8,128)(2,1)S(1)}, u32[]{:S(2)}, u32[]{:S(2)}) collective-permute-start(bf16[2,144,128]{2,1,0:T(8,128)(2,1)S(1)} %slice.56), channel_id=1, source_target_pairs={{0,128},{128,256},{256,384},{1,129},{129,257},{257,385},{2,130},{1... | collective-permute-start | bytes 221192 | tf_op jit(solution)/shard_map/ppermute | solution.py:269
  27.7 1.4 collective-permute-done.early_ref
  29.1 5.5 %collective-permute-start.2 = (bf16[10,32,128]{2,1,0:T(8,128)(2,1)S(1)}, bf16[10,32,128]{2,1,0:T(8,128)(2,1)S(1)}, u32[]{:S(2)}, u32[]{:S(2)}) collective-permute-start(bf16[10,32,128]{2,1,0:T(8,128)(2,1)S(1)} %get-tuple-element.29), channel_id=1, source_target_pairs={{1,0},{2,1},{3,2},{4,3},{5,4},{6,5},{7,6},{8,7},{9,8},{10,9},{11,1... | collective-permute-start | bytes 245768 | tf_op jit(solution)/shard_map/ppermute | solution.py:269
  34.5 3.9 %collective-permute-start.1 = (bf16[10,32,128]{2,1,0:T(8,128)(2,1)S(1)}, bf16[10,32,128]{2,1,0:T(8,128)(2,1)S(1)}, u32[]{:S(2)}, u32[]{:S(2)}) collective-permute-start(bf16[10,32,128]{2,1,0:T(8,128)(2,1)S(1)} %get-tuple-element.30), channel_id=1, source_target_pairs={{0,1},{1,2},{2,3},{3,4},{4,5},{5,6},{6,7},{7,8},{8,9},{9,10},{10,1... | collective-permute-start | bytes 245768 | tf_op jit(solution)/shard_map/ppermute | solution.py:269
  38.4 0.0 all-to-all-done.1.cot_ref
  38.4 0.2 collective-permute-done.2.down_ref
  38.6 1.3 collective-permute-done.1.up_ref
  39.9 0.0 copy-done
  39.9 6.3 %shard_map.59 = (bf16[8,128,128]{2,1,0:T(8,128)(2,1)S(1)}, bf16[8,128,128]{2,1,0:T(8,128)(2,1)S(1)}, bf16[27,128,128]{2,1,0:T(8,128)(2,1)S(1)}) custom-call(bf16[8,144,128]{2,1,0:T(8,128)(2,1)S(1)} %all_to_all.30.held_ref, bf16[2,144,128]{2,1,0:T(8,128)(2,1)S(1)} %collective-permute-done.early_ref, bf16[10,32,128]{2,1,0:T(8,128)(2,1)S(1)} %collective-permute-done.1.up_ref, ...), custom_call_target="tpu_custom_call" | custom-call | flops 1811939328 | bytes 4194304 | tf_op jit(solution)/shard_map/pallas_call | solution.py:369
  46.3 1.9 %collective-permute-start.3 = (bf16[1728,128]{1,0:T(8,128)(2,1)S(1)}, bf16[1728,128]{1,0:T(8,128)(2,1)S(1)}, u32[]{:S(2)}, u32[]{:S(2)}) collective-permute-start(bf16[1728,128]{1,0:T(8,128)(2,1)S(1)} %dynamic-slice_bitcast_fusion), channel_id=1, source_target_pairs={{0,1},{1,0},{2,3},{3,2},{4,5},{5,4},{6,7},{7,6},{8,9},{9,8},{10,11... | collective-permute-start | bytes 1327112 | tf_op jit(solution)/shard_map/ppermute | solution.py:273
  48.2 1.8 %collective-permute-done.3 = bf16[1728,128]{1,0:T(8,128)(2,1)S(1)} collective-permute-done((bf16[1728,128]{1,0:T(8,128)(2,1)S(1)}, bf16[1728,128]{1,0:T(8,128)(2,1)S(1)}, u32[]{:S(2)}, u32[]{:S(2)}) %collective-permute-start.3) | collective-permute-done | bytes 442400 | tf_op jit(solution)/shard_map/ppermute | solution.py:273
  49.9 0.9 fusion
  50.8 4.9 %all-to-all-start.2 = ((bf16[4,432,128]{2,1,0:T(8,128)(2,1)}), bf16[4,432,128]{2,1,0:T(8,128)(2,1)S(1)}, u32[]{:S(2)}, u32[]{:S(2)}) async-start(bf16[4,432,128]{2,1,0:T(8,128)(2,1)} %bitcast.6), calls=%async_computation.2 | async-start | bytes 884736 | tf_op jit(solution)/shard_map/all_to_all | solution.py:305
  55.7 2.3 %collective-permute-start.5 = (bf16[8,16,128]{2,1,0:T(8,128)(2,1)S(1)}, bf16[8,16,128]{2,1,0:T(8,128)(2,1)S(1)}, u32[]{:S(2)}, u32[]{:S(2)}) collective-permute-start(bf16[8,16,128]{2,1,0:T(8,128)(2,1)S(1)} %get-tuple-element.24), channel_id=1, source_target_pairs={{1,0},{2,1},{3,2},{4,3},{5,4},{6,5},{7,6},{8,7},{9,8},{10,9},{11,1... | collective-permute-start | bytes 98312 | tf_op jit(solution)/shard_map/ppermute | solution.py:269
  58.1 4.2 %collective-permute-start.4 = (bf16[8,16,128]{2,1,0:T(8,128)(2,1)S(1)}, bf16[8,16,128]{2,1,0:T(8,128)(2,1)S(1)}, u32[]{:S(2)}, u32[]{:S(2)}) collective-permute-start(bf16[8,16,128]{2,1,0:T(8,128)(2,1)S(1)} %get-tuple-element.25), channel_id=1, source_target_pairs={{0,1},{1,2},{2,3},{3,4},{4,5},{5,6},{6,7},{7,8},{8,9},{9,10},{10,1... | collective-permute-start | bytes 98312 | tf_op jit(solution)/shard_map/ppermute | solution.py:269
  62.2 0.0 collective-permute-done.5.down_ref
  62.3 1.0 collective-permute-done.4.up_ref
  63.2 0.8 all-to-all-done.2
  64.0 0.1 reduce_sum.21
  64.1 0.7 pad_bitcast_fusion
  64.7 17.3 %all-to-all-start.3 = ((bf16[64,8,128]{2,1,0:T(8,128)(2,1)}), bf16[64,8,128]{2,1,0:T(8,128)(2,1)S(1)}, u32[]{:S(2)}, u32[]{:S(2)}) async-start(bf16[64,8,128]{2,1,0:T(8,128)(2,1)} %pad_bitcast_fusion), calls=%async_computation.3 | async-start | bytes 262144 | tf_op jit(solution)/shard_map/all_to_all | solution.py:309
  82.0 1.3 collective-permute-start.6
  83.3 0.1 reverse_bitcast_fusion
  83.4 1.4 copy.7
  84.8 2.7 %collective-permute-done.6.late_ref = bf16[2,160,128]{2,1,0:T(8,128)(2,1)S(1)} collective-permute-done((bf16[2,160,128]{2,1,0:T(8,128)(2,1)S(1)}, bf16[2,160,128]{2,1,0:T(8,128)(2,1)S(1)}, u32[]{:S(2)}, u32[]{:S(2)}) %collective-permute-start.6) | collective-permute-done | bytes 81952 | tf_op jit(solution)/shard_map/ppermute | solution.py:269
  87.5 3.5 %shard_map.60 = bf16[8,272,128]{2,1,0:T(8,128)(2,1)} custom-call(bf16[8,128,128]{2,1,0:T(8,128)(2,1)S(1)} %get-tuple-element.15.g_ref, bf16[8,16,128]{2,1,0:T(8,128)(2,1)S(1)} %collective-permute-done.4.up_ref, bf16[8,16,128]{2,1,0:T(8,128)(2,1)S(1)} %collective-permute-done.5.down_ref, bf16[2,160,128]{2,1,0:T(8,128)(2,1)S(1)} %collective-permute-done.6.late_ref, ...), custom_call_target="tpu_custom_call" | custom-call | flops 905969664 | bytes 4194304 | tf_op jit(solution)/shard_map/pallas_call | solution.py:390
  91.0 2.5 %all-to-all-done.3 = bf16[64,8,128]{2,1,0:T(8,128)(2,1)S(1)} async-done(((bf16[64,8,128]{2,1,0:T(8,128)(2,1)}), bf16[64,8,128]{2,1,0:T(8,128)(2,1)S(1)}, u32[]{:S(2)}, u32[]{:S(2)}) %all-to-all-start.3) | async-done | bytes 131104 | tf_op jit(solution)/shard_map/all_to_all | solution.py:309
  93.5 0.1 convert_reduce_fusion
  93.6 20.6 %all_to_all.31 = bf16[64,8,128]{2,1,0:T(8,128)(2,1)S(1)} all-to-all(bf16[64,8,128]{2,1,0:T(8,128)(2,1)S(1)} %broadcast_in_dim.14), channel_id=1, replica_groups=mesh['x'=4,'y'=8,'z'=8,'core'=2] {'y','z'}, dimensions={0} | all-to-all | bytes 262144 | tf_op jit(solution)/shard_map/all_to_all | solution.py:316
  114.2 3.5 %all-to-all-start.4 = ((bf16[8,272,128]{2,1,0:T(8,128)(2,1)}), bf16[8,272,128]{2,1,0:T(8,128)(2,1)S(1)}, u32[]{:S(2)}, u32[]{:S(2)}) async-start(bf16[8,272,128]{2,1,0:T(8,128)(2,1)} %shard_map.60), calls=%async_computation.4 | async-start | bytes 1114112 | tf_op jit(solution)/shard_map/all_to_all | solution.py:401
  117.8 2.5 %collective-permute-start.9 = (bf16[432,128]{1,0:T(8,128)(2,1)S(1)}, bf16[432,128]{1,0:T(8,128)(2,1)S(1)}, u32[]{:S(2)}, u32[]{:S(2)}) collective-permute-start(bf16[432,128]{1,0:T(8,128)(2,1)S(1)} %slice_bitcast_fusion.own_ref), channel_id=1, source_target_pairs={{0,128},{128,256},{256,384},{384,0},{1,129},{129,257},{257,385},{3... | collective-permute-start | bytes 331784 | tf_op jit(solution)/shard_map/ppermute | solution.py:318
  120.3 3.1 %collective-permute-start.8 = (bf16[432,128]{1,0:T(8,128)(2,1)S(1)}, bf16[432,128]{1,0:T(8,128)(2,1)S(1)}, u32[]{:S(2)}, u32[]{:S(2)}) collective-permute-start(bf16[432,128]{1,0:T(8,128)(2,1)S(1)} %slice_bitcast_fusion.own_ref), channel_id=1, source_target_pairs={{0,256},{128,384},{256,0},{384,128},{1,257},{129,385},{257,1},{385... | collective-permute-start | bytes 331784 | tf_op jit(solution)/shard_map/ppermute | solution.py:318
  123.5 4.0 %collective-permute-start.7 = (bf16[432,128]{1,0:T(8,128)(2,1)S(1)}, bf16[432,128]{1,0:T(8,128)(2,1)S(1)}, u32[]{:S(2)}, u32[]{:S(2)}) collective-permute-start(bf16[432,128]{1,0:T(8,128)(2,1)S(1)} %slice_bitcast_fusion.own_ref), channel_id=1, source_target_pairs={{0,384},{128,0},{256,128},{384,256},{1,385},{129,1},{257,129},{385... | collective-permute-start | bytes 331784 | tf_op jit(solution)/shard_map/ppermute | solution.py:318
  127.4 0.0 collective-permute-done.9.three_ref
  127.5 0.0 collective-permute-done.8.two_ref
  127.5 1.8 %collective-permute-done.7.one_ref = bf16[432,128]{1,0:T(8,128)(2,1)S(1)} collective-permute-done((bf16[432,128]{1,0:T(8,128)(2,1)S(1)}, bf16[432,128]{1,0:T(8,128)(2,1)S(1)}, u32[]{:S(2)}, u32[]{:S(2)}) %collective-permute-start.7) | collective-permute-done | bytes 110624 | tf_op jit(solution)/shard_map/ppermute | solution.py:318
  129.3 8.8 %collective-permute-start.10 = (bf16[1728,128]{1,0:T(8,128)(2,1)S(1)}, bf16[1728,128]{1,0:T(8,128)(2,1)S(1)}, u32[]{:S(2)}, u32[]{:S(2)}) collective-permute-start(bf16[1728,128]{1,0:T(8,128)(2,1)S(1)} %bitcast.23), channel_id=1, source_target_pairs={{0,1},{1,0},{2,3},{3,2},{4,5},{5,4},{6,7},{7,6},{8,9},{9,8},{10,11... | collective-permute-start | bytes 1327112 | tf_op jit(solution)/shard_map/ppermute | solution.py:273
  138.1 1.4 collective-permute-done.10.other_ref
  139.5 1.3 shard_map.63
  140.8 0.0 all-to-all-done.4.got_ref
  140.8 0.8 shard_map.61
  (14 shorter events, 0.2 us)
Async XLA Ops:
  0.6 39.3 %copy-start = (bf16[3,3,3,128,128]{4,3,2,1,0:T(8,128)(2,1)S(1)}, bf16[3,3,3,128,128]{4,3,2,1,0:T(8,128)(2,1)}, u32[]{:S(2)}) copy-start(bf16[3,3,3,128,128]{4,3,2,1,0:T(8,128)(2,1)} %param.4) | copy-start | bytes 2654212
  19.9 18.5 %all-to-all-start.1 = ((bf16[8,128,128]{2,1,0:T(8,128)(2,1)}), bf16[8,128,128]{2,1,0:T(8,128)(2,1)S(1)}, u32[]{:S(2)}, u32[]{:S(2)}) async-start(bf16[8,128,128]{2,1,0:T(8,128)(2,1)} %get-tuple-element.13), calls=%async_computation.1 | async-start | bytes 524288 | tf_op jit(solution)/shard_map/all_to_all | solution.py:358
  23.4 5.7 %collective-permute-start = (bf16[2,144,128]{2,1,0:T(8,128)(2,1)S(1)}, bf16[2,144,128]{2,1,0:T(8,128)(2,1)S(1)}, u32[]{:S(2)}, u32[]{:S(2)}) collective-permute-start(bf16[2,144,128]{2,1,0:T(8,128)(2,1)S(1)} %slice.56), channel_id=1, source_target_pairs={{0,128},{128,256},{256,384},{1,129},{129,257},{257,385},{2,130},{1... | collective-permute-start | bytes 221192 | tf_op jit(solution)/shard_map/ppermute | solution.py:269
  29.1 9.5 %collective-permute-start.2 = (bf16[10,32,128]{2,1,0:T(8,128)(2,1)S(1)}, bf16[10,32,128]{2,1,0:T(8,128)(2,1)S(1)}, u32[]{:S(2)}, u32[]{:S(2)}) collective-permute-start(bf16[10,32,128]{2,1,0:T(8,128)(2,1)S(1)} %get-tuple-element.29), channel_id=1, source_target_pairs={{1,0},{2,1},{3,2},{4,3},{5,4},{6,5},{7,6},{8,7},{9,8},{10,9},{11,1... | collective-permute-start | bytes 245768 | tf_op jit(solution)/shard_map/ppermute | solution.py:269
  34.5 5.4 %collective-permute-start.1 = (bf16[10,32,128]{2,1,0:T(8,128)(2,1)S(1)}, bf16[10,32,128]{2,1,0:T(8,128)(2,1)S(1)}, u32[]{:S(2)}, u32[]{:S(2)}) collective-permute-start(bf16[10,32,128]{2,1,0:T(8,128)(2,1)S(1)} %get-tuple-element.30), channel_id=1, source_target_pairs={{0,1},{1,2},{2,3},{3,4},{4,5},{5,6},{6,7},{7,8},{8,9},{9,10},{10,1... | collective-permute-start | bytes 245768 | tf_op jit(solution)/shard_map/ppermute | solution.py:269
  46.3 3.7 %collective-permute-start.3 = (bf16[1728,128]{1,0:T(8,128)(2,1)S(1)}, bf16[1728,128]{1,0:T(8,128)(2,1)S(1)}, u32[]{:S(2)}, u32[]{:S(2)}) collective-permute-start(bf16[1728,128]{1,0:T(8,128)(2,1)S(1)} %dynamic-slice_bitcast_fusion), channel_id=1, source_target_pairs={{0,1},{1,0},{2,3},{3,2},{4,5},{5,4},{6,7},{7,6},{8,9},{9,8},{10,11... | collective-permute-start | bytes 1327112 | tf_op jit(solution)/shard_map/ppermute | solution.py:273
  50.8 13.2 %all-to-all-start.2 = ((bf16[4,432,128]{2,1,0:T(8,128)(2,1)}), bf16[4,432,128]{2,1,0:T(8,128)(2,1)S(1)}, u32[]{:S(2)}, u32[]{:S(2)}) async-start(bf16[4,432,128]{2,1,0:T(8,128)(2,1)} %bitcast.6), calls=%async_computation.2 | async-start | bytes 884736 | tf_op jit(solution)/shard_map/all_to_all | solution.py:305
  55.7 6.5 %collective-permute-start.5 = (bf16[8,16,128]{2,1,0:T(8,128)(2,1)S(1)}, bf16[8,16,128]{2,1,0:T(8,128)(2,1)S(1)}, u32[]{:S(2)}, u32[]{:S(2)}) collective-permute-start(bf16[8,16,128]{2,1,0:T(8,128)(2,1)S(1)} %get-tuple-element.24), channel_id=1, source_target_pairs={{1,0},{2,1},{3,2},{4,3},{5,4},{6,5},{7,6},{8,7},{9,8},{10,9},{11,1... | collective-permute-start | bytes 98312 | tf_op jit(solution)/shard_map/ppermute | solution.py:269
  58.1 5.2 %collective-permute-start.4 = (bf16[8,16,128]{2,1,0:T(8,128)(2,1)S(1)}, bf16[8,16,128]{2,1,0:T(8,128)(2,1)S(1)}, u32[]{:S(2)}, u32[]{:S(2)}) collective-permute-start(bf16[8,16,128]{2,1,0:T(8,128)(2,1)S(1)} %get-tuple-element.25), channel_id=1, source_target_pairs={{0,1},{1,2},{2,3},{3,4},{4,5},{5,6},{6,7},{7,8},{8,9},{9,10},{10,1... | collective-permute-start | bytes 98312 | tf_op jit(solution)/shard_map/ppermute | solution.py:269
  64.7 28.8 %all-to-all-start.3 = ((bf16[64,8,128]{2,1,0:T(8,128)(2,1)}), bf16[64,8,128]{2,1,0:T(8,128)(2,1)S(1)}, u32[]{:S(2)}, u32[]{:S(2)}) async-start(bf16[64,8,128]{2,1,0:T(8,128)(2,1)} %pad_bitcast_fusion), calls=%async_computation.3 | async-start | bytes 262144 | tf_op jit(solution)/shard_map/all_to_all | solution.py:309
  82.0 5.5 %collective-permute-start.6 = (bf16[2,160,128]{2,1,0:T(8,128)(2,1)S(1)}, bf16[2,160,128]{2,1,0:T(8,128)(2,1)S(1)}, u32[]{:S(2)}, u32[]{:S(2)}) collective-permute-start(bf16[2,160,128]{2,1,0:T(8,128)(2,1)S(1)} %pad_maximum_fusion.1), channel_id=1, source_target_pairs={{128,0},{256,128},{384,256},{129,1},{257,129},{385,257},{130,2},{2... | collective-permute-start | bytes 245768 | tf_op jit(solution)/shard_map/ppermute | solution.py:269
  114.2 26.6 %all-to-all-start.4 = ((bf16[8,272,128]{2,1,0:T(8,128)(2,1)}), bf16[8,272,128]{2,1,0:T(8,128)(2,1)S(1)}, u32[]{:S(2)}, u32[]{:S(2)}) async-start(bf16[8,272,128]{2,1,0:T(8,128)(2,1)} %shard_map.60), calls=%async_computation.4 | async-start | bytes 1114112 | tf_op jit(solution)/shard_map/all_to_all | solution.py:401
  117.8 9.6 %collective-permute-start.9 = (bf16[432,128]{1,0:T(8,128)(2,1)S(1)}, bf16[432,128]{1,0:T(8,128)(2,1)S(1)}, u32[]{:S(2)}, u32[]{:S(2)}) collective-permute-start(bf16[432,128]{1,0:T(8,128)(2,1)S(1)} %slice_bitcast_fusion.own_ref), channel_id=1, source_target_pairs={{0,128},{128,256},{256,384},{384,0},{1,129},{129,257},{257,385},{3... | collective-permute-start | bytes 331784 | tf_op jit(solution)/shard_map/ppermute | solution.py:318
  120.3 7.1 %collective-permute-start.8 = (bf16[432,128]{1,0:T(8,128)(2,1)S(1)}, bf16[432,128]{1,0:T(8,128)(2,1)S(1)}, u32[]{:S(2)}, u32[]{:S(2)}) collective-permute-start(bf16[432,128]{1,0:T(8,128)(2,1)S(1)} %slice_bitcast_fusion.own_ref), channel_id=1, source_target_pairs={{0,256},{128,384},{256,0},{384,128},{1,257},{129,385},{257,1},{385... | collective-permute-start | bytes 331784 | tf_op jit(solution)/shard_map/ppermute | solution.py:318
  123.5 5.8 %collective-permute-start.7 = (bf16[432,128]{1,0:T(8,128)(2,1)S(1)}, bf16[432,128]{1,0:T(8,128)(2,1)S(1)}, u32[]{:S(2)}, u32[]{:S(2)}) collective-permute-start(bf16[432,128]{1,0:T(8,128)(2,1)S(1)} %slice_bitcast_fusion.own_ref), channel_id=1, source_target_pairs={{0,384},{128,0},{256,128},{384,256},{1,385},{129,1},{257,129},{385... | collective-permute-start | bytes 331784 | tf_op jit(solution)/shard_map/ppermute | solution.py:318
  129.3 10.2 %collective-permute-start.10 = (bf16[1728,128]{1,0:T(8,128)(2,1)S(1)}, bf16[1728,128]{1,0:T(8,128)(2,1)S(1)}, u32[]{:S(2)}, u32[]{:S(2)}) collective-permute-start(bf16[1728,128]{1,0:T(8,128)(2,1)S(1)} %bitcast.23), channel_id=1, source_target_pairs={{0,1},{1,0},{2,3},{3,2},{4,5},{5,4},{6,7},{7,6},{8,9},{9,8},{10,11... | collective-permute-start | bytes 1327112 | tf_op jit(solution)/shard_map/ppermute | solution.py:273

commit v4 on v2

--- a/solution.py
+++ b/solution.py
@@ -21,6 +21,8 @@
 FRAMES = GROUP + 2
 EDGES = 2 * ROWS
 HELD = TILE + EDGES
+SENT_ROWS = 2 * STRIP + EDGES
+RIM = 2 * STRIP
 PART = 8
 
 band_weight = 0.75
@@ -69,18 +71,42 @@
             ]
 
 
-def place_line(col_ref, base, tall_row, line, left, right):
+def place_line(col_ref, line, left, right, places):
     at = lax.broadcasted_iota(jnp.int32, (STRIP, CH), 0)
     wide = line.astype(f32)
     before = jnp.where(at == 0, left, pltpu.roll(wide, 1, 0)).astype(bf16)
     after = jnp.where(at == STRIP - 1, right, pltpu.roll(wide, STRIP - 1, 0)).astype(bf16)
-    for row_tap in range(3):
-        row = tall_row - row_tap
-        if 0 <= row < ROWS:
-            start = pl.multiple_of(base + row * STRIP, STRIP)
-            for col_tap, piece in enumerate((before, line, after)):
-                tap = row_tap * 3 + col_tap
-                col_ref[pl.ds(start, STRIP), pl.ds(tap * CH, CH)] = piece
+    for row_tap, place in places:
+        start = pl.multiple_of(place, STRIP)
+        for col_tap, piece in enumerate((before, line, after)):
+            tap = row_tap * 3 + col_tap
+            col_ref[pl.ds(start, STRIP), pl.ds(tap * CH, CH)] = piece
+
+
+def adjoint_bands(cot):
+    back = [None] * GROUP
+    for level in range(LEVELS - 1, -1, -1):
+        step = 1 << level
+        following = [None] * GROUP
+        for frame in range(GROUP):
+            if frame & step:
+                continue
+            pair = (cot[frame] + cot[frame + step]) * root_half
+            if level == LEVELS - 1:
+                total = pair
+            else:
+                total = (back[frame] + back[frame + step]) * root_half
+            for member, side in ((frame, -1.0), (frame + step, 1.0)):
+                value = total + (band_weight * side) * pair
+                if level > 0:
+                    value = value.astype(bf16).astype(f32)
+                following[member] = value
+        back = following
+    return back
+
+
+def slope_of(linear, gate):
+    return gate * (1.0 + linear * (1.0 - gate))
 
 
 def forward_body(
@@ -92,29 +118,46 @@
     w_ref,
     code_ref,
     g_ref,
+    g_up_ref,
+    g_down_ref,
     dw_ref,
     col_ref,
     lin_ref,
     gt_ref,
 ):
     def spread(ref, frame, place):
-        for tall_row in range(TALL):
-            if tall_row == 0:
-                source, at, low, row = up_ref, place, 0, ROWS - 1
-            elif tall_row == TALL - 1:
-                source, at, low, row = down_ref, place, 0, 0
+        for tall_row in range(-2, ROWS + 2):
+            if tall_row < 0:
+                source, low, edge_row = up_ref, (tall_row + 2) * STRIP, ROWS + tall_row
+                base = place * SENT_ROWS
+            elif tall_row >= ROWS:
+                source, low, edge_row = down_ref, (tall_row - ROWS) * STRIP, tall_row - ROWS
+                base = place * SENT_ROWS
             else:
-                source, at, row = ref, frame, tall_row - 1
-                low = row * STRIP
-            line = source[at, pl.ds(low, STRIP), :]
-            edge = source[at, pl.ds(source.shape[1] - EDGES, EDGES), :].astype(f32)
+                source, low, edge_row = ref, tall_row * STRIP, tall_row
+                base = None
+            if base is None:
+                line = source[frame, pl.ds(low, STRIP), :]
+                edge = source[frame, pl.ds(TILE, EDGES), :].astype(f32)
+            else:
+                line = source[pl.ds(pl.multiple_of(base + low, STRIP), STRIP), :]
+                edge_low = pl.multiple_of(base + 2 * STRIP, STRIP)
+                edge = source[pl.ds(edge_low, EDGES), :].astype(f32)
+            places = []
+            for row_tap in range(3):
+                row = tall_row + 1 - row_tap
+                if 0 <= row < ROWS:
+                    places.append((row_tap, place * TILE + row * STRIP))
+                elif row == -1:
+                    places.append((row_tap, FRAMES * TILE + place * RIM))
+                elif row == ROWS:
+                    places.append((row_tap, FRAMES * TILE + place * RIM + STRIP))
             place_line(
                 col_ref,
-                place * TILE,
-                tall_row,
                 line,
-                edge[row : row + 1],
-                edge[ROWS + row : ROWS + row + 1],
+                edge[edge_row : edge_row + 1],
+                edge[ROWS + edge_row : ROWS + edge_row + 1],
+                places,
             )
 
     @pl.loop(0, 2)
@@ -125,11 +168,14 @@
     def _(frame):
         spread(held_ref, frame, frame + 2)
 
-    lin_ref[...] = (
-        jnp.dot(col_ref[0 : GROUP * TILE, :], w_ref[0], preferred_element_type=f32)
-        + jnp.dot(col_ref[TILE : (GROUP + 1) * TILE, :], w_ref[1], preferred_element_type=f32)
-        + jnp.dot(col_ref[2 * TILE : (GROUP + 2) * TILE, :], w_ref[2], preferred_element_type=f32)
-    )
+    for low, step in ((0, TILE), (FRAMES * TILE, RIM)):
+        total = None
+        for tap in range(3):
+            rows = col_ref[low + tap * step : low + (tap + GROUP) * step, :]
+            part = jnp.dot(rows, w_ref[tap], preferred_element_type=f32)
+            total = part if total is None else total + part
+        place = 0 if step == TILE else GROUP * TILE
+        lin_ref[place : place + GROUP * step, :] = total
 
     @pl.loop(0, ROWS)
     def _(row):
@@ -155,29 +201,23 @@
             code = (band[0] + band_weight * detail[member]).astype(bf16)
             code_ref[member, pl.ds(low, STRIP), :] = code
             code_ref[member + 1, pl.ds(low, STRIP), :] = code
-
         cot = [cot_ref[frame, pl.ds(low, STRIP), :].astype(f32) for frame in range(GROUP)]
-        back = [None] * GROUP
-        for level in range(LEVELS - 1, -1, -1):
-            step = 1 << level
-            following = [None] * GROUP
-            for frame in range(GROUP):
-                if frame & step:
-                    continue
-                pair = (cot[frame] + cot[frame + step]) * root_half
-                if level == LEVELS - 1:
-                    total = pair
-                else:
-                    total = (back[frame] + back[frame + step]) * root_half
-                for member, side in ((frame, -1.0), (frame + step, 1.0)):
-                    value = total + (band_weight * side) * pair
-                    if level > 0:
-                        value = value.astype(bf16).astype(f32)
-                    following[member] = value
-            back = following
+        back = adjoint_bands(cot)
         for frame in range(GROUP):
-            slope = gate[frame] * (1.0 + linear[frame] * (1.0 - gate[frame]))
-            g_ref[frame, pl.ds(low, STRIP), :] = (back[frame] * slope).astype(bf16)
+            g_ref[frame, pl.ds(low, STRIP), :] = (
+                back[frame] * slope_of(linear[frame], gate[frame])
+            ).astype(bf16)
+
+    for offset, source, rim_ref in ((0, up_ref, g_up_ref), (STRIP, down_ref, g_down_ref)):
+        cot = [
+            source[pl.ds(FRAMES * SENT_ROWS + frame * STRIP, STRIP), :].astype(f32)
+            for frame in range(GROUP)
+        ]
+        back = adjoint_bands(cot)
+        for frame in range(GROUP):
+            linear = lin_ref[pl.ds(GROUP * TILE + frame * RIM + offset, STRIP), :]
+            slope = slope_of(linear, jax.nn.sigmoid(linear))
+            rim_ref[frame] = (back[frame] * slope).astype(bf16)
 
     gt_ref[...] = jnp.zeros_like(gt_ref)
     for frame in range(GROUP):
@@ -186,7 +226,9 @@
             gt_ref[pl.ds(tap * CH, CH), pl.ds((frame + tap) * TILE, TILE)] = turned
     for tap in range(9):
         product = jnp.dot(
-            gt_ref[...], col_ref[:, tap * CH : (tap + 1) * CH], preferred_element_type=f32
+            gt_ref[...],
+            col_ref[0 : FRAMES * TILE, tap * CH : (tap + 1) * CH],
+            preferred_element_type=f32,
         )
         for frame_tap in range(3):
             block = product[frame_tap * CH : (frame_tap + 1) * CH]
@@ -198,7 +240,12 @@
 
     def spread(lines, place):
         for tall_row, line in enumerate(lines):
-            place_line(col_ref, place * TILE, tall_row, line, nothing, nothing)
+            places = [
+                (row_tap, place * TILE + (tall_row - row_tap) * STRIP)
+                for row_tap in range(3)
+                if 0 <= tall_row - row_tap < ROWS
+            ]
+            place_line(col_ref, line, nothing, nothing, places)
 
     @pl.loop(0, GROUP)
     def _(frame):
@@ -274,29 +321,26 @@
 
 
 def own_share(terms, norm):
-    chips = ("x", "y", "z")
-    count = lax.axis_size(chips)
     core = lax.axis_index("core")
-    rows = terms.shape[0] // 2
-    halves = terms.reshape(2, rows, CH)
-    mine = lax.dynamic_index_in_dim(halves, core, 0, keepdims=False)
-    other = lax.dynamic_index_in_dim(halves, 1 - core, 0, keepdims=False)
+    deep, planes = lax.axis_size("z"), lax.axis_size(("x", "y"))
+    rows = terms.shape[0] // (2 * deep)
+    halves = terms.reshape(deep, 2, rows, CH)
+    mine = lax.dynamic_index_in_dim(halves, core, 1, keepdims=False)
+    other = lax.dynamic_index_in_dim(halves, 1 - core, 1, keepdims=False)
     chip_sum = (mine.astype(f32) + swapped(other).astype(f32)).astype(bf16)
-    share = PART * -(-rows // (PART * count))
-    padded = jnp.pad(chip_sum, ((0, share * count - rows), (0, 0)))
-    spread = lax.all_to_all(padded.reshape(count, share, CH), chips, 0, 0)
+    parts = lax.all_to_all(chip_sum, "z", 0, 0)
+    part = parts.astype(f32).sum(axis=0).astype(bf16)
+    share = PART * -(-rows // (PART * planes))
+    padded = jnp.pad(part, ((0, share * planes - rows), (0, 0)))
+    spread = lax.all_to_all(padded.reshape(planes, share, CH), ("x", "y"), 0, 0)
     return (spread.astype(f32).sum(axis=0) * norm).astype(bf16), rows
 
 
 def all_shares(total, rows):
-    chips = ("x", "y", "z")
-    core = lax.axis_index("core")
-    copies = jnp.broadcast_to(total[None], (lax.axis_size(chips),) + total.shape)
-    half = lax.all_to_all(copies, chips, 0, 0).reshape(-1, CH)[:rows]
-    paired = swapped(half)
-    low = jnp.where(core == 0, half, paired)
-    high = jnp.where(core == 0, paired, half)
-    return jnp.concatenate([low, high], axis=0).astype(f32)
+    planes = lax.axis_size(("x", "y"))
+    copies = jnp.broadcast_to(total[None], (planes,) + total.shape)
+    part = lax.all_to_all(copies, ("x", "y"), 0, 0).reshape(-1, CH)[:rows]
+    return lax.all_gather(part, ("z", "core"), tiled=True).astype(f32)
 
 
 def shards(frames, kernel, cotangent):
@@ -318,40 +362,40 @@
             pltpu.VMEM((GROUP, ROWS, CH), f32),
             pltpu.SemaphoreType.DMA((2,)),
         ],
-        compiler_params=pltpu.CompilerParams(vmem_limit_bytes=VMEM_LIMIT),
     )(frames[0], cotangent[0])
     held = lax.all_to_all(packed, "y", 0, 0)
     cot = lax.all_to_all(cot_packed, "y", 0, 0)
     early = shifted(held[GROUP - 2 :], "x", 1)
-    last, first = [
-        jnp.concatenate([value[:, low : low + STRIP] for value in (early, held)], axis=0)
-        for low in (TILE - STRIP, 0)
-    ]
-    edges = jnp.concatenate([early[:, TILE:], held[:, TILE:]], axis=0)
-    up = shifted(jnp.concatenate([last, edges], axis=1), lines, 1)
-    down = shifted(jnp.concatenate([first, edges], axis=1), lines, -1)
+    both = [jnp.concatenate([early[:, low:], held[:, low:]], axis=0) for low in (TILE - RIM, TILE)]
+    first = jnp.concatenate([early[:, :RIM], held[:, :RIM]], axis=0)
+    up_rows = both[0].reshape(FRAMES * SENT_ROWS, CH)
+    down_rows = jnp.concatenate([first, both[1]], axis=1).reshape(FRAMES * SENT_ROWS, CH)
+    up_cot = cot[:, TILE - STRIP :].reshape(GROUP * STRIP, CH)
+    down_cot = cot[:, :STRIP].reshape(GROUP * STRIP, CH)
+    up = shifted(jnp.concatenate([up_rows, up_cot], axis=0), lines, 1)
+    down = shifted(jnp.concatenate([down_rows, down_cot], axis=0), lines, -1)
 
     flops = 2 * GROUP * TILE * 27 * CH * CH
-    code, g, terms = kernel_call(
+    code, g, g_up, g_down, terms = kernel_call(
         forward_body,
         (
             jax.ShapeDtypeStruct((GROUP, TILE, CH), bf16),
             jax.ShapeDtypeStruct((GROUP, TILE, CH), bf16),
+            jax.ShapeDtypeStruct((GROUP, STRIP, CH), bf16),
+            jax.ShapeDtypeStruct((GROUP, STRIP, CH), bf16),
             jax.ShapeDtypeStruct((27, CH, CH), bf16),
         ),
         [
-            pltpu.VMEM((FRAMES * TILE, WIDE), bf16),
-            pltpu.VMEM((GROUP * TILE, CH), f32),
+            pltpu.VMEM((FRAMES * (TILE + RIM), WIDE), bf16),
+            pltpu.VMEM((GROUP * (TILE + RIM), CH), f32),
             pltpu.VMEM((3 * CH, FRAMES * TILE), bf16),
         ],
         flops=2 * flops,
     )(held, early, up, down, cot, weights)
 
     norm = 1.0 / math.sqrt(lax.axis_size(("x", "y", "z", "core")) * GROUP * TILE)
-    total, half_rows = own_share(terms.reshape(27 * CH, CH), norm)
-
-    g_up = shifted(g[:, TILE - STRIP :], lines, 1)
-    g_down = shifted(g[:, :STRIP], lines, -1)
+    total, part_rows = own_share(terms.reshape(27 * CH, CH), norm)
+
     late = shifted(jnp.concatenate([g_up[:2], g[:2], g_down[:2]], axis=1), "x", -1)
     sent = kernel_call(
         backward_body,
@@ -363,7 +407,7 @@
         flops=flops,
     )(g, g_up, g_down, late, code, turned)
     total, sent = lax.optimization_barrier((total, sent))
-    grad_kernel = all_shares(total, half_rows)
+    grad_kernel = all_shares(total, part_rows)
     got = lax.all_to_all(sent, "y", 0, 0)
     whole = jax.ShapeDtypeStruct((ROWS, GROUP * STRIP, CH), bf16)
     code_out, grad_frames = kernel_call(unpack_body, (whole, whole))(got)

time: 159 us -> 141 us (0.89)
  starting transfers between devices: 60.1 us -> 39.9 us
  waiting for transfers between devices: 24 us -> 30.5 us
  blocking collectives: 54.8 us -> 50.8 us
  Pallas kernels: 11.5 us -> 13.2 us
    all_to_all x1, blocking collectives: 37.2 us -> 14 us  [all_shares(): part = lax.all_to_all(copies, ('x', 'y'), 0, 0).reshape(-1, CH)[:rows]]
    all_gather x0 -> x1, blocking collectives: none -> 19.4 us  [all_shares(): return lax.all_gather(part, ('z', 'core'), tiled=True).astype(f32)]
    all_to_all x1 -> x2, waiting for transfers between devices: 0.01 us -> 18.8 us  [the longest x1 14.9 us: own_share(): parts = lax.all_to_all(chip_sum, 'z', 0, 0)]
    all_to_all x1, waiting for transfers between devices: 13.6 us -> 0.01 us  [shards(): got = lax.all_to_all(sent, 'y', 0, 0)]
    all_to_all x1 -> x2, starting transfers between devices: 25.5 us -> 14.9 us  [the longest x1 9.41 us: own_share(): parts = lax.all_to_all(chip_sum, 'z', 0, 0)]
    all_to_all x1, waiting for transfers between devices: 0.01 us -> 5.12 us  [shards(): cot = lax.all_to_all(cot_packed, 'y', 0, 0)]
    ppermute x6 -> x4, waiting for transfers between devices: 8.66 us -> 4.62 us  [shifted(): return lax.ppermute(value, axes, route)]
    ppermute x6 -> x4, starting transfers between devices: 20 us -> 16.2 us  [shifted(): return lax.ppermute(value, axes, route)]
  transfers between devices with their start and end apart: 11 -> 9, of which waited for: 7 -> 6; matrix products, arithmetic and copies ran while one was open for 1% -> 3% of each run, Pallas kernels for 3% -> 2%
where the time goes in v4:
time: 141 us
  blocking collectives  50.8 us (36%)
  starting transfers between devices  39.9 us (28%)
  waiting for transfers between devices  30.5 us (22%)
  Pallas kernels  13.2 us (9%)
  local copies, waits for them, and re-layouts  2.95 us (2%)
  other arithmetic  2.45 us (2%)
    all_gather x1, blocking collectives, all_shares(): return lax.all_gather(part, ('z', 'core'), tiled=True).astype(f32)  19.4 us
    all_to_all x1, blocking collectives, shards(): held = lax.all_to_all(packed, 'y', 0, 0)  17.4 us
    ppermute x4, starting transfers between devices, shifted(): return lax.ppermute(value, axes, route)  16.2 us
    all_to_all x1, waiting for transfers between devices, own_share(): parts = lax.all_to_all(chip_sum, 'z', 0, 0)  14.9 us
    all_to_all x1, blocking collectives, all_shares(): part = lax.all_to_all(copies, ('x', 'y'), 0, 0).reshape(-1, CH)[:rows]  14 us
    all_to_all x1, starting transfers between devices, own_share(): parts = lax.all_to_all(chip_sum, 'z', 0, 0)  9.41 us
    pallas_call x1, Pallas kernels, shards(): kernel_call(forward_body, (jax.ShapeDtypeStruct((GROUP, TILE, CH), bf16),...  6.95 us
    all_to_all x1, starting transfers between devices, own_share(): spread = lax.all_to_all(padded.reshape(planes, share, CH), ('x', 'y'), 0, 0)  5.48 us
  transfers between devices with their start and end apart: 9, of which 6 were waited for; matrix products, arithmetic and copies ran while one was open for 3% of the time, Pallas kernels for 2%

profile of v4, /device:TPU:1, one launch (start us, length us, event | category | flops | bytes accessed | tf_op | source)
XLA Modules:
  0.0 140.6 jit_solution(4467671544647494207)
XLA Ops:
  0.6 0.0 copy-start
  0.6 1.9 %shard_map.58 = (bf16[8,144,128]{2,1,0:T(8,128)(2,1)}, bf16[8,128,128]{2,1,0:T(8,128)(2,1)}) custom-call(bf16[8,128,128]{2,1,0:T(8,128)(2,1)} %bitcast.31, bf16[8,128,128]{2,1,0:T(8,128)(2,1)} %bitcast.32), custom_call_target="tpu_custom_call" | custom-call | tf_op jit(solution)/shard_map/pallas_call | solution.py:351
  2.6 17.4 %all_to_all.30.held_ref = bf16[8,144,128]{2,1,0:T(8,128)(2,1)S(1)} all-to-all(bf16[8,144,128]{2,1,0:T(8,128)(2,1)} %get-tuple-element.14), channel_id=1, replica_groups=mesh['x'=4,'y'=8,'z'=8,'core'=2] {'y'}, dimensions={0} | all-to-all | bytes 589824 | tf_op jit(solution)/shard_map/all_to_all | solution.py:366
  19.9 3.4 %all-to-all-start.1 = ((bf16[8,128,128]{2,1,0:T(8,128)(2,1)}), bf16[8,128,128]{2,1,0:T(8,128)(2,1)S(1)}, u32[]{:S(2)}, u32[]{:S(2)}) async-start(bf16[8,128,128]{2,1,0:T(8,128)(2,1)} %get-tuple-element.15), calls=%async_computation.1 | async-start | bytes 524288 | tf_op jit(solution)/shard_map/all_to_all | solution.py:367
  23.4 4.3 %collective-permute-start = (bf16[2,144,128]{2,1,0:T(8,128)(2,1)S(1)}, bf16[2,144,128]{2,1,0:T(8,128)(2,1)S(1)}, u32[]{:S(2)}, u32[]{:S(2)}) collective-permute-start(bf16[2,144,128]{2,1,0:T(8,128)(2,1)S(1)} %slice.56), channel_id=1, source_target_pairs={{0,128},{128,256},{256,384},{1,129},{129,257},{257,385},{2,130},{1... | collective-permute-start | bytes 221192 | tf_op jit(solution)/shard_map/ppermute | solution.py:316
  27.6 5.1 %all-to-all-done.1.cot_ref = bf16[8,128,128]{2,1,0:T(8,128)(2,1)S(1)} async-done(((bf16[8,128,128]{2,1,0:T(8,128)(2,1)}), bf16[8,128,128]{2,1,0:T(8,128)(2,1)S(1)}, u32[]{:S(2)}, u32[]{:S(2)}) %all-to-all-start.1) | async-done | bytes 262176 | tf_op jit(solution)/shard_map/all_to_all | solution.py:367
  32.8 0.0 collective-permute-done.early_ref
  32.9 8.7 %collective-permute-start.1 = (bf16[608,128]{1,0:T(8,128)(2,1)S(1)}, bf16[608,128]{1,0:T(8,128)(2,1)S(1)}, u32[]{:S(2)}, u32[]{:S(2)}) collective-permute-start(bf16[608,128]{1,0:T(8,128)(2,1)S(1)} %pad_maximum_fusion), channel_id=1, source_target_pairs={{0,1},{1,2},{2,3},{3,4},{4,5},{5,6},{6,7},{7,8},{8,9},{9,10},{10,1... | collective-permute-start | bytes 466952 | tf_op jit(solution)/shard_map/ppermute | solution.py:316
  41.7 1.9 %collective-permute-start.2 = (bf16[608,128]{1,0:T(8,128)(2,1)S(1)}, bf16[608,128]{1,0:T(8,128)(2,1)S(1)}, u32[]{:S(2)}, u32[]{:S(2)}) collective-permute-start(bf16[608,128]{1,0:T(8,128)(2,1)S(1)} %pad_maximum_fusion.1), channel_id=1, source_target_pairs={{1,0},{2,1},{3,2},{4,3},{5,4},{6,5},{7,6},{8,7},{9,8},{10,9},{11,1... | collective-permute-start | bytes 466952 | tf_op jit(solution)/shard_map/ppermute | solution.py:316
  43.6 0.2 collective-permute-done.1.up_ref
  43.7 4.5 %collective-permute-done.2.down_ref = bf16[608,128]{1,0:T(8,128)(2,1)S(1)} collective-permute-done((bf16[608,128]{1,0:T(8,128)(2,1)S(1)}, bf16[608,128]{1,0:T(8,128)(2,1)S(1)}, u32[]{:S(2)}, u32[]{:S(2)}) %collective-permute-start.2) | collective-permute-done | bytes 155680 | tf_op jit(solution)/shard_map/ppermute | solution.py:316
  48.2 0.0 copy-done
  48.2 7.0 %shard_map.59 = (bf16[8,128,128]{2,1,0:T(8,128)(2,1)S(1)}, bf16[8,128,128]{2,1,0:T(8,128)(2,1)S(1)}, bf16[8,16,128]{2,1,0:T(8,128)(2,1)S(1)}, bf16[8,16,128]{2,1,0:T(8,128)(2,1)S(1)}, bf16[27,128,128]{2,1,0:T(8,128)(2,1)S(1)}) custom-call(bf16[8,144,128]{2,1,0:T(8,128)(2,1)S(1)} %all_to_all.30.held_ref, ...), custom_call_target="tpu_custom_call" | custom-call | flops 1811939328 | bytes 4194304 | tf_op jit(solution)/shard_map/pallas_call | solution.py:379
  55.2 0.8 dynamic-slice_bitcast_fusion
  56.0 1.9 %collective-permute-start.3 = (bf16[8,216,128]{2,1,0:T(8,128)(2,1)}, bf16[8,216,128]{2,1,0:T(8,128)(2,1)S(1)}, u32[]{:S(2)}, u32[]{:S(2)}) collective-permute-start(bf16[8,216,128]{2,1,0:T(8,128)(2,1)} %dynamic-slice_bitcast_fusion), channel_id=1, source_target_pairs={{0,1},{1,0},{2,3},{3,2},{4,5},{5,4},{6,7},{7,6},{8,9},{9,8},{10,11... | collective-permute-start | bytes 1327112 | tf_op jit(solution)/shard_map/ppermute | solution.py:320
  57.9 2.0 %collective-permute-done.3 = bf16[8,216,128]{2,1,0:T(8,128)(2,1)S(1)} collective-permute-done((bf16[8,216,128]{2,1,0:T(8,128)(2,1)}, bf16[8,216,128]{2,1,0:T(8,128)(2,1)S(1)}, u32[]{:S(2)}, u32[]{:S(2)}) %collective-permute-start.3) | collective-permute-done | bytes 442400 | tf_op jit(solution)/shard_map/ppermute | solution.py:320
  59.8 0.9 fusion
  60.7 9.4 %all-to-all-start.2 = ((bf16[8,216,128]{2,1,0:T(8,128)(2,1)}), bf16[8,216,128]{2,1,0:T(8,128)(2,1)S(1)}, u32[]{:S(2)}, u32[]{:S(2)}) async-start(bf16[8,216,128]{2,1,0:T(8,128)(2,1)} %fusion), calls=%async_computation.2 | async-start | bytes 884736 | tf_op jit(solution)/shard_map/all_to_all | solution.py:331
  70.2 1.3 collective-permute-start.4
  71.5 14.9 %all-to-all-done.2 = bf16[8,216,128]{2,1,0:T(8,128)(2,1)S(1)} async-done(((bf16[8,216,128]{2,1,0:T(8,128)(2,1)}), bf16[8,216,128]{2,1,0:T(8,128)(2,1)S(1)}, u32[]{:S(2)}, u32[]{:S(2)}) %all-to-all-start.2) | async-done | bytes 442400 | tf_op jit(solution)/shard_map/all_to_all | solution.py:331
  86.3 0.1 reduce_sum.21
  86.4 0.6 pad_bitcast_fusion
  87.0 5.5 %all-to-all-start.3 = ((bf16[32,8,128]{2,1,0:T(8,128)(2,1)}), bf16[32,8,128]{2,1,0:T(8,128)(2,1)S(1)}, u32[]{:S(2)}, u32[]{:S(2)}) async-start(bf16[32,8,128]{2,1,0:T(8,128)(2,1)} %pad_bitcast_fusion), calls=%async_computation.3 | async-start | bytes 131072 | tf_op jit(solution)/shard_map/all_to_all | solution.py:335
  92.5 0.1 reverse_bitcast_fusion
  92.6 1.4 copy.7
  94.0 0.0 collective-permute-done.4.late_ref
  94.0 3.5 %shard_map.60 = bf16[8,272,128]{2,1,0:T(8,128)(2,1)} custom-call(bf16[8,128,128]{2,1,0:T(8,128)(2,1)S(1)} %get-tuple-element.17.g_ref, bf16[8,16,128]{2,1,0:T(8,128)(2,1)S(1)} %get-tuple-element.18.up_ref, bf16[8,16,128]{2,1,0:T(8,128)(2,1)S(1)} %get-tuple-element.19.down_ref, bf16[2,160,128]{2,1,0:T(8,128)(2,1)S(1)} %collective-permute-done.4.late_ref, ...), custom_call_target="tpu_custom_call" | custom-call | flops 905969664 | bytes 4194304 | tf_op jit(solution)/shard_map/pallas_call | solution.py:400
  97.5 3.9 %all-to-all-done.3 = bf16[32,8,128]{2,1,0:T(8,128)(2,1)S(1)} async-done(((bf16[32,8,128]{2,1,0:T(8,128)(2,1)}), bf16[32,8,128]{2,1,0:T(8,128)(2,1)S(1)}, u32[]{:S(2)}, u32[]{:S(2)}) %all-to-all-start.3) | async-done | bytes 65568 | tf_op jit(solution)/shard_map/all_to_all | solution.py:335
  101.5 14.0 %all_to_all.31 = bf16[32,8,128]{2,1,0:T(8,128)(2,1)S(1)} all-to-all(bf16[32,8,128]{2,1,0:T(8,128)(2,1)S(1)} %broadcast_in_dim.14), channel_id=1, replica_groups=mesh['x'=4,'y'=8,'z'=8,'core'=2] {'x','y'}, dimensions={0} | all-to-all | bytes 131072 | tf_op jit(solution)/shard_map/all_to_all | solution.py:342
  115.4 3.5 %all-to-all-start.4 = ((bf16[8,272,128]{2,1,0:T(8,128)(2,1)}), bf16[8,272,128]{2,1,0:T(8,128)(2,1)S(1)}, u32[]{:S(2)}, u32[]{:S(2)}) async-start(bf16[8,272,128]{2,1,0:T(8,128)(2,1)} %shard_map.60), calls=%async_computation.4 | async-start | bytes 1114112 | tf_op jit(solution)/shard_map/all_to_all | solution.py:411
  119.0 19.4 %all_gather.3 = bf16[3456,128]{1,0:T(8,128)(2,1)S(1)} all-gather(bf16[216,128]{1,0:T(8,128)(2,1)S(1)} %slice_bitcast_fusion), channel_id=1, replica_groups=mesh['x'=4,'y'=8,'z'=8,'core'=2] {'z','core'}, dimensions={0}, use_global_device_ids=true | all-gather | bytes 940032 | tf_op jit(solution)/shard_map/all_gather | solution.py:343
  138.4 1.4 %convert.4 = f32[3,3,3,128,128]{4,3,2,1,0:T(8,128)} convert(bf16[3,3,3,128,128]{4,3,2,1,0:T(8,128)(2,1)S(1)} %bitcast.28) | non-fusion elementwise | flops 442368 | bytes 2654208 | tf_op jit(solution)/shard_map/reshape | solution.py:414
  139.8 0.0 all-to-all-done.4.got_ref
  139.8 0.8 shard_map.61
  (20 shorter events, 0.2 us)
Async XLA Ops:
  0.6 47.6 %copy-start = (bf16[3,3,3,128,128]{4,3,2,1,0:T(8,128)(2,1)S(1)}, bf16[3,3,3,128,128]{4,3,2,1,0:T(8,128)(2,1)}, u32[]{:S(2)}) copy-start(bf16[3,3,3,128,128]{4,3,2,1,0:T(8,128)(2,1)} %param.4) | copy-start | bytes 2654212
  19.9 12.8 %all-to-all-start.1 = ((bf16[8,128,128]{2,1,0:T(8,128)(2,1)}), bf16[8,128,128]{2,1,0:T(8,128)(2,1)S(1)}, u32[]{:S(2)}, u32[]{:S(2)}) async-start(bf16[8,128,128]{2,1,0:T(8,128)(2,1)} %get-tuple-element.15), calls=%async_computation.1 | async-start | bytes 524288 | tf_op jit(solution)/shard_map/all_to_all | solution.py:367
  23.4 9.4 %collective-permute-start = (bf16[2,144,128]{2,1,0:T(8,128)(2,1)S(1)}, bf16[2,144,128]{2,1,0:T(8,128)(2,1)S(1)}, u32[]{:S(2)}, u32[]{:S(2)}) collective-permute-start(bf16[2,144,128]{2,1,0:T(8,128)(2,1)S(1)} %slice.56), channel_id=1, source_target_pairs={{0,128},{128,256},{256,384},{1,129},{129,257},{257,385},{2,130},{1... | collective-permute-start | bytes 221192 | tf_op jit(solution)/shard_map/ppermute | solution.py:316
  32.9 10.9 %collective-permute-start.1 = (bf16[608,128]{1,0:T(8,128)(2,1)S(1)}, bf16[608,128]{1,0:T(8,128)(2,1)S(1)}, u32[]{:S(2)}, u32[]{:S(2)}) collective-permute-start(bf16[608,128]{1,0:T(8,128)(2,1)S(1)} %pad_maximum_fusion), channel_id=1, source_target_pairs={{0,1},{1,2},{2,3},{3,4},{4,5},{5,6},{6,7},{7,8},{8,9},{9,10},{10,1... | collective-permute-start | bytes 466952 | tf_op jit(solution)/shard_map/ppermute | solution.py:316
  41.7 6.5 %collective-permute-start.2 = (bf16[608,128]{1,0:T(8,128)(2,1)S(1)}, bf16[608,128]{1,0:T(8,128)(2,1)S(1)}, u32[]{:S(2)}, u32[]{:S(2)}) collective-permute-start(bf16[608,128]{1,0:T(8,128)(2,1)S(1)} %pad_maximum_fusion.1), channel_id=1, source_target_pairs={{1,0},{2,1},{3,2},{4,3},{5,4},{6,5},{7,6},{8,7},{9,8},{10,9},{11,1... | collective-permute-start | bytes 466952 | tf_op jit(solution)/shard_map/ppermute | solution.py:316
  56.0 3.9 %collective-permute-start.3 = (bf16[8,216,128]{2,1,0:T(8,128)(2,1)}, bf16[8,216,128]{2,1,0:T(8,128)(2,1)S(1)}, u32[]{:S(2)}, u32[]{:S(2)}) collective-permute-start(bf16[8,216,128]{2,1,0:T(8,128)(2,1)} %dynamic-slice_bitcast_fusion), channel_id=1, source_target_pairs={{0,1},{1,0},{2,3},{3,2},{4,5},{5,4},{6,7},{7,6},{8,9},{9,8},{10,11... | collective-permute-start | bytes 1327112 | tf_op jit(solution)/shard_map/ppermute | solution.py:320
  60.7 25.6 %all-to-all-start.2 = ((bf16[8,216,128]{2,1,0:T(8,128)(2,1)}), bf16[8,216,128]{2,1,0:T(8,128)(2,1)S(1)}, u32[]{:S(2)}, u32[]{:S(2)}) async-start(bf16[8,216,128]{2,1,0:T(8,128)(2,1)} %fusion), calls=%async_computation.2 | async-start | bytes 884736 | tf_op jit(solution)/shard_map/all_to_all | solution.py:331
  70.2 23.8 %collective-permute-start.4 = (bf16[2,160,128]{2,1,0:T(8,128)(2,1)S(1)}, bf16[2,160,128]{2,1,0:T(8,128)(2,1)S(1)}, u32[]{:S(2)}, u32[]{:S(2)}) collective-permute-start(bf16[2,160,128]{2,1,0:T(8,128)(2,1)S(1)} %pad_maximum_fusion.3), channel_id=1, source_target_pairs={{128,0},{256,128},{384,256},{129,1},{257,129},{385,257},{130,2},{2... | collective-permute-start | bytes 245768 | tf_op jit(solution)/shard_map/ppermute | solution.py:316
  87.0 14.3 %all-to-all-start.3 = ((bf16[32,8,128]{2,1,0:T(8,128)(2,1)}), bf16[32,8,128]{2,1,0:T(8,128)(2,1)S(1)}, u32[]{:S(2)}, u32[]{:S(2)}) async-start(bf16[32,8,128]{2,1,0:T(8,128)(2,1)} %pad_bitcast_fusion), calls=%async_computation.3 | async-start | bytes 131072 | tf_op jit(solution)/shard_map/all_to_all | solution.py:335
  115.4 24.4 %all-to-all-start.4 = ((bf16[8,272,128]{2,1,0:T(8,128)(2,1)}), bf16[8,272,128]{2,1,0:T(8,128)(2,1)S(1)}, u32[]{:S(2)}, u32[]{:S(2)}) async-start(bf16[8,272,128]{2,1,0:T(8,128)(2,1)} %shard_map.60), calls=%async_computation.4 | async-start | bytes 1114112 | tf_op jit(solution)/shard_map/all_to_all | solution.py:411

commit v5 on v4

--- a/solution.py
+++ b/solution.py
@@ -21,7 +21,6 @@
 FRAMES = GROUP + 2
 EDGES = 2 * ROWS
 HELD = TILE + EDGES
-SENT_ROWS = 2 * STRIP + EDGES
 RIM = 2 * STRIP
 PART = 8
 
@@ -32,9 +31,10 @@
 VMEM_LIMIT = 48 * 1024 * 1024
 
 
-def kernel_call(body, outs, scratch=(), flops=0):
+def kernel_call(body, outs, scratch=(), flops=0, **specs):
     return pl.pallas_call(
         body,
+        **specs,
         out_shape=outs,
         scratch_shapes=list(scratch),
         compiler_params=pltpu.CompilerParams(vmem_limit_bytes=VMEM_LIMIT),
@@ -42,14 +42,12 @@
     )
 
 
-def pack_body(x_hbm, cot_hbm, out_ref, cot_out_ref, x_ref, cot_ref, left_ref, right_ref, sems):
-    x_copy = pltpu.make_async_copy(x_hbm, x_ref, sems.at[0])
-    cot_copy = pltpu.make_async_copy(cot_hbm, cot_ref, sems.at[1])
-    x_copy.start()
-    cot_copy.start()
+def pack_body(x_hbm, out_ref, x_ref, left_ref, right_ref, sem):
+    copy = pltpu.make_async_copy(x_hbm, x_ref, sem)
+    copy.start()
     left_ref[...] = jnp.zeros_like(left_ref)
     right_ref[...] = jnp.zeros_like(right_ref)
-    x_copy.wait()
+    copy.wait()
     for row in range(ROWS):
         line = x_ref[row]
         wide = line.astype(f32)
@@ -63,11 +61,22 @@
     for strip in range(GROUP):
         pair = jnp.concatenate([left_ref[strip], right_ref[strip]], axis=0)
         out_ref[strip, pl.ds(TILE, EDGES), :] = pair.astype(bf16)
-    cot_copy.wait()
-    for strip in range(GROUP):
-        for row in range(ROWS):
-            cot_out_ref[strip, pl.ds(row * STRIP, STRIP), :] = cot_ref[
-                row, pl.ds(strip * STRIP, STRIP), :
+
+
+def pack_cot_body(cot_hbm, up_ref, down_ref, out_ref, cot_ref, sem):
+    copy = pltpu.make_async_copy(cot_hbm, cot_ref, sem)
+    copy.start()
+    copy.wait()
+    for tall_row in range(TALL):
+        if tall_row == 0:
+            line = up_ref[0]
+        elif tall_row == TALL - 1:
+            line = down_ref[0]
+        else:
+            line = cot_ref[tall_row - 1]
+        for strip in range(GROUP):
+            out_ref[strip, pl.ds(tall_row * STRIP, STRIP), :] = line[
+                strip * STRIP : (strip + 1) * STRIP
             ]
 
 
@@ -110,6 +119,7 @@
 
 
 def forward_body(
+    core_ref,
     held_ref,
     early_ref,
     up_ref,
@@ -120,29 +130,23 @@
     g_ref,
     g_up_ref,
     g_down_ref,
-    dw_ref,
+    keep_ref,
+    send_ref,
     col_ref,
     lin_ref,
     gt_ref,
+    terms_ref,
 ):
     def spread(ref, frame, place):
         for tall_row in range(-2, ROWS + 2):
             if tall_row < 0:
-                source, low, edge_row = up_ref, (tall_row + 2) * STRIP, ROWS + tall_row
-                base = place * SENT_ROWS
+                source, at, low, edge_row = up_ref, place, (tall_row + 2) * STRIP, ROWS + tall_row
             elif tall_row >= ROWS:
-                source, low, edge_row = down_ref, (tall_row - ROWS) * STRIP, tall_row - ROWS
-                base = place * SENT_ROWS
+                source, at, low, edge_row = down_ref, place, (tall_row - ROWS) * STRIP, tall_row - ROWS
             else:
-                source, low, edge_row = ref, tall_row * STRIP, tall_row
-                base = None
-            if base is None:
-                line = source[frame, pl.ds(low, STRIP), :]
-                edge = source[frame, pl.ds(TILE, EDGES), :].astype(f32)
-            else:
-                line = source[pl.ds(pl.multiple_of(base + low, STRIP), STRIP), :]
-                edge_low = pl.multiple_of(base + 2 * STRIP, STRIP)
-                edge = source[pl.ds(edge_low, EDGES), :].astype(f32)
+                source, at, low, edge_row = ref, frame, tall_row * STRIP, tall_row
+            line = source[at, pl.ds(low, STRIP), :]
+            edge = source[at, pl.ds(source.shape[1] - EDGES, EDGES), :].astype(f32)
             places = []
             for row_tap in range(3):
                 row = tall_row + 1 - row_tap
@@ -201,17 +205,17 @@
             code = (band[0] + band_weight * detail[member]).astype(bf16)
             code_ref[member, pl.ds(low, STRIP), :] = code
             code_ref[member + 1, pl.ds(low, STRIP), :] = code
-        cot = [cot_ref[frame, pl.ds(low, STRIP), :].astype(f32) for frame in range(GROUP)]
+        tall = pl.multiple_of(low + STRIP, STRIP)
+        cot = [cot_ref[frame, pl.ds(tall, STRIP), :].astype(f32) for frame in range(GROUP)]
         back = adjoint_bands(cot)
         for frame in range(GROUP):
             g_ref[frame, pl.ds(low, STRIP), :] = (
                 back[frame] * slope_of(linear[frame], gate[frame])
             ).astype(bf16)
 
-    for offset, source, rim_ref in ((0, up_ref, g_up_ref), (STRIP, down_ref, g_down_ref)):
+    for offset, tall, rim_ref in ((0, 0, g_up_ref), (STRIP, TALL - 1, g_down_ref)):
         cot = [
-            source[pl.ds(FRAMES * SENT_ROWS + frame * STRIP, STRIP), :].astype(f32)
-            for frame in range(GROUP)
+            cot_ref[frame, pl.ds(tall * STRIP, STRIP), :].astype(f32) for frame in range(GROUP)
         ]
         back = adjoint_bands(cot)
         for frame in range(GROUP):
@@ -224,15 +228,40 @@
         turned = g_ref[frame].astype(f32).T.astype(bf16)
         for tap in range(3):
             gt_ref[pl.ds(tap * CH, CH), pl.ds((frame + tap) * TILE, TILE)] = turned
-    for tap in range(9):
+    terms_ref[...] = jnp.zeros_like(terms_ref)
+    _, wide, planes, share = terms_ref.shape[:4]
+    blocks = 27 * CH // PART
+    slots = share // PART
+    lines = 2 * (planes // GROUP)
+    for low in range(0, 9, 2):
+        high = min(low + 2, 9)
         product = jnp.dot(
             gt_ref[...],
-            col_ref[0 : FRAMES * TILE, tap * CH : (tap + 1) * CH],
+            col_ref[0 : FRAMES * TILE, low * CH : high * CH],
             preferred_element_type=f32,
         )
-        for frame_tap in range(3):
-            block = product[frame_tap * CH : (frame_tap + 1) * CH]
-            dw_ref[frame_tap * 9 + tap] = block.T.astype(bf16)
+        for tap in range(low, high):
+            for frame_tap in range(3):
+                block = product[
+                    frame_tap * CH : (frame_tap + 1) * CH, (tap - low) * CH : (tap - low + 1) * CH
+                ].T
+                for piece in range(CH // PART):
+                    at = (frame_tap * 9 + tap) * (CH // PART) + piece
+                    line, within = divmod(at, blocks // lines)
+                    owner, slot = divmod(within, slots)
+                    depth, core = divmod(line, 2)
+                    column, ring = divmod(owner, GROUP)
+                    peer = ring * (planes // GROUP) + depth
+                    terms_ref[core, column, peer, pl.ds(slot * PART, PART), :] = block[
+                        piece * PART : (piece + 1) * PART
+                    ]
+    for core in range(2):
+
+        @pl.when(core_ref[0] == core)
+        def _():
+            for column in range(wide):
+                keep_ref[column] = terms_ref[core, column].reshape(-1, CH).astype(bf16)
+                send_ref[column] = terms_ref[1 - core, column].reshape(-1, CH).astype(bf16)
 
 
 def backward_body(g_ref, up_ref, down_ref, late_ref, code_ref, w_ref, out_ref, col_ref, side_ref):
@@ -320,81 +349,82 @@
     return lax.ppermute(value, "core", [(0, 1), (1, 0)])
 
 
-def own_share(terms, norm):
-    core = lax.axis_index("core")
-    deep, planes = lax.axis_size("z"), lax.axis_size(("x", "y"))
-    rows = terms.shape[0] // (2 * deep)
-    halves = terms.reshape(deep, 2, rows, CH)
-    mine = lax.dynamic_index_in_dim(halves, core, 1, keepdims=False)
-    other = lax.dynamic_index_in_dim(halves, 1 - core, 1, keepdims=False)
-    chip_sum = (mine.astype(f32) + swapped(other).astype(f32)).astype(bf16)
-    parts = lax.all_to_all(chip_sum, "z", 0, 0)
-    part = parts.astype(f32).sum(axis=0).astype(bf16)
-    share = PART * -(-rows // (PART * planes))
-    padded = jnp.pad(part, ((0, share * planes - rows), (0, 0)))
-    spread = lax.all_to_all(padded.reshape(planes, share, CH), ("x", "y"), 0, 0)
-    return (spread.astype(f32).sum(axis=0) * norm).astype(bf16), rows
-
-
-def all_shares(total, rows):
-    planes = lax.axis_size(("x", "y"))
-    copies = jnp.broadcast_to(total[None], (planes,) + total.shape)
-    part = lax.all_to_all(copies, ("x", "y"), 0, 0).reshape(-1, CH)[:rows]
+def own_share(chip_sum, norm):
+    planes = lax.axis_size(("y", "z"))
+    parts = lax.all_to_all(chip_sum, "x", 0, 0)
+    part = parts.astype(f32).sum(axis=0).astype(bf16).reshape(planes, -1, CH)
+    spread = lax.all_to_all(part, ("y", "z"), 0, 0)
+    return (spread.astype(f32).sum(axis=0) * norm).astype(bf16)
+
+
+def all_shares(total):
+    owners, lines = lax.axis_size(("x", "y")), lax.axis_size(("z", "core"))
+    copies = jnp.broadcast_to(total[None], (owners,) + total.shape)
+    part = lax.all_to_all(copies, ("x", "y"), 0, 0).reshape(-1, CH)[: 27 * CH // lines]
     return lax.all_gather(part, ("z", "core"), tiled=True).astype(f32)
 
 
 def shards(frames, kernel, cotangent):
-    x = frames[0]
     weights = kernel.reshape(3, WIDE, CH)
     turned = jnp.swapaxes(kernel[::-1, ::-1, ::-1], 3, 4).reshape(3, WIDE, CH)
     lines = ("z", "core")
-    packed, cot_packed = pl.pallas_call(
+    whole_vmem = pltpu.VMEM((ROWS, GROUP * STRIP, CH), bf16)
+    in_hbm = pl.BlockSpec(memory_space=pl.ANY)
+    in_vmem = pl.BlockSpec(memory_space=pltpu.VMEM)
+    packed = pl.pallas_call(
         pack_body,
-        out_shape=(
-            jax.ShapeDtypeStruct((GROUP, HELD, CH), bf16),
-            jax.ShapeDtypeStruct((GROUP, TILE, CH), bf16),
-        ),
-        in_specs=[pl.BlockSpec(memory_space=pl.ANY)] * 2,
-        scratch_shapes=[
-            pltpu.VMEM((ROWS, GROUP * STRIP, CH), bf16),
-            pltpu.VMEM((ROWS, GROUP * STRIP, CH), bf16),
-            pltpu.VMEM((GROUP, ROWS, CH), f32),
-            pltpu.VMEM((GROUP, ROWS, CH), f32),
-            pltpu.SemaphoreType.DMA((2,)),
-        ],
-    )(frames[0], cotangent[0])
+        out_shape=jax.ShapeDtypeStruct((GROUP, HELD, CH), bf16),
+        in_specs=[in_hbm],
+        scratch_shapes=[whole_vmem]
+        + [pltpu.VMEM((GROUP, ROWS, CH), f32)] * 2
+        + [pltpu.SemaphoreType.DMA],
+    )(frames[0])
     held = lax.all_to_all(packed, "y", 0, 0)
+    cot_up = shifted(cotangent[0, ROWS - 1 :], lines, 1)
+    cot_down = shifted(cotangent[0, :1], lines, -1)
+    cot_packed = pl.pallas_call(
+        pack_cot_body,
+        out_shape=jax.ShapeDtypeStruct((GROUP, TALL * STRIP, CH), bf16),
+        in_specs=[in_hbm, in_vmem, in_vmem],
+        scratch_shapes=[whole_vmem, pltpu.SemaphoreType.DMA],
+    )(cotangent[0], cot_up, cot_down)
     cot = lax.all_to_all(cot_packed, "y", 0, 0)
     early = shifted(held[GROUP - 2 :], "x", 1)
-    both = [jnp.concatenate([early[:, low:], held[:, low:]], axis=0) for low in (TILE - RIM, TILE)]
+    edges = jnp.concatenate([early[:, TILE:], held[:, TILE:]], axis=0)
+    last = jnp.concatenate([early[:, TILE - RIM :], held[:, TILE - RIM :]], axis=0)
     first = jnp.concatenate([early[:, :RIM], held[:, :RIM]], axis=0)
-    up_rows = both[0].reshape(FRAMES * SENT_ROWS, CH)
-    down_rows = jnp.concatenate([first, both[1]], axis=1).reshape(FRAMES * SENT_ROWS, CH)
-    up_cot = cot[:, TILE - STRIP :].reshape(GROUP * STRIP, CH)
-    down_cot = cot[:, :STRIP].reshape(GROUP * STRIP, CH)
-    up = shifted(jnp.concatenate([up_rows, up_cot], axis=0), lines, 1)
-    down = shifted(jnp.concatenate([down_rows, down_cot], axis=0), lines, -1)
-
+    up = shifted(last, lines, 1)
+    down = shifted(jnp.concatenate([first, edges], axis=1), lines, -1)
+    turned, held = lax.optimization_barrier((turned, held))
+
+    wide, planes = lax.axis_size("x"), lax.axis_size(("y", "z"))
+    devices = lax.axis_size(("x", "y", "z", "core"))
+    share = PART * -(-27 * CH // (PART * devices))
+    mail = jax.ShapeDtypeStruct((wide, planes * share, CH), bf16)
     flops = 2 * GROUP * TILE * 27 * CH * CH
-    code, g, g_up, g_down, terms = kernel_call(
+    code, g, g_up, g_down, keep, send = kernel_call(
         forward_body,
         (
             jax.ShapeDtypeStruct((GROUP, TILE, CH), bf16),
             jax.ShapeDtypeStruct((GROUP, TILE, CH), bf16),
             jax.ShapeDtypeStruct((GROUP, STRIP, CH), bf16),
             jax.ShapeDtypeStruct((GROUP, STRIP, CH), bf16),
-            jax.ShapeDtypeStruct((27, CH, CH), bf16),
+            mail,
+            mail,
         ),
         [
             pltpu.VMEM((FRAMES * (TILE + RIM), WIDE), bf16),
             pltpu.VMEM((GROUP * (TILE + RIM), CH), f32),
             pltpu.VMEM((3 * CH, FRAMES * TILE), bf16),
+            pltpu.VMEM((2, wide, planes, share, CH), f32),
         ],
         flops=2 * flops,
-    )(held, early, up, down, cot, weights)
-
-    norm = 1.0 / math.sqrt(lax.axis_size(("x", "y", "z", "core")) * GROUP * TILE)
-    total, part_rows = own_share(terms.reshape(27 * CH, CH), norm)
+        in_specs=[pl.BlockSpec(memory_space=pltpu.SMEM)] + [in_vmem] * 6,
+    )(lax.axis_index("core").astype(jnp.int32).reshape(1), held, early, up, down, cot, weights)
+
+    norm = 1.0 / math.sqrt(devices * GROUP * TILE)
+    chip_sum = (keep.astype(f32) + swapped(send).astype(f32)).astype(bf16)
+    total = own_share(chip_sum, norm)
 
     late = shifted(jnp.concatenate([g_up[:2], g[:2], g_down[:2]], axis=1), "x", -1)
     sent = kernel_call(
@@ -407,7 +437,7 @@
         flops=flops,
     )(g, g_up, g_down, late, code, turned)
     total, sent = lax.optimization_barrier((total, sent))
-    grad_kernel = all_shares(total, part_rows)
+    grad_kernel = all_shares(total)
     got = lax.all_to_all(sent, "y", 0, 0)
     whole = jax.ShapeDtypeStruct((ROWS, GROUP * STRIP, CH), bf16)
     code_out, grad_frames = kernel_call(unpack_body, (whole, whole))(got)

time: 141 us -> 142 us (level)
  starting transfers between devices: 39.9 us -> 60.4 us
  blocking collectives: 50.8 us -> 36.1 us
  waiting for transfers between devices: 30.5 us -> 21.3 us
  local copies, waits for them, and re-layouts: 2.95 us -> 4.42 us
    all_to_all x2 -> x1, blocking collectives: 31.3 us -> 12.9 us  [all_shares(): lax.all_to_all(copies, ('x', 'y'), 0, 0).reshape(-1, CH)[:27 * CH // lines]]
    all_to_all x2 -> x3, starting transfers between devices: 14.9 us -> 29.5 us  [the longest x1 17 us: own_share(): spread = lax.all_to_all(part, ('y', 'z'), 0, 0)]
    all_to_all x2 -> x3, waiting for transfers between devices: 18.8 us -> 11.7 us  [the longest x1 9.15 us: own_share(): parts = lax.all_to_all(chip_sum, 'x', 0, 0)]
    all_to_all x1, waiting for transfers between devices: 5.12 us -> 0.01 us  [shards(): cot = lax.all_to_all(cot_packed, 'y', 0, 0)]
    all_gather x1, blocking collectives: 19.4 us -> 23.2 us  [all_shares(): return lax.all_gather(part, ('z', 'core'), tiled=True).astype(f32)]
    all_to_all x1, starting transfers between devices: 3.41 us -> 6.94 us  [shards(): cot = lax.all_to_all(cot_packed, 'y', 0, 0)]
    ppermute x4 -> x6, waiting for transfers between devices: 4.62 us -> 7.77 us  [shifted(): return lax.ppermute(value, axes, route)]
    pallas_call x1 -> x2, Pallas kernels: 1.92 us -> 4.29 us  [the longest x1 2.47 us: shards(): pl.pallas_call(pack_cot_body, out_shape=jax.ShapeDtypeStruct((GROUP, TALL...]
  transfers between devices with their start and end apart: 9 -> 12, of which waited for: 6 -> 7; matrix products, arithmetic and copies ran while one was open for 3% -> 4% of each run, Pallas kernels for 2% -> 4%
where the time goes in v5:
time: 142 us; the launch traced here: 141 us
  starting transfers between devices  60.4 us (43%)
  blocking collectives  36.1 us (25%)
  waiting for transfers between devices  21.3 us (15%)
  Pallas kernels  14.6 us (10%)
  local copies, waits for them, and re-layouts  4.42 us (3%)
  other arithmetic  3.19 us (2%)
    all_gather x1, blocking collectives, all_shares(): return lax.all_gather(part, ('z', 'core'), tiled=True).astype(f32)  23.2 us
    ppermute x6, starting transfers between devices, shifted(): return lax.ppermute(value, axes, route)  18.4 us
    all_to_all x1, starting transfers between devices, own_share(): spread = lax.all_to_all(part, ('y', 'z'), 0, 0)  17 us
    all_to_all x1, blocking collectives, all_shares(): lax.all_to_all(copies, ('x', 'y'), 0, 0).reshape(-1, CH)[:27 * CH // lines]  12.9 us
    all_to_all x1, waiting for transfers between devices, own_share(): parts = lax.all_to_all(chip_sum, 'x', 0, 0)  9.15 us
    ppermute x6, waiting for transfers between devices, shifted(): return lax.ppermute(value, axes, route)  7.77 us
    all_to_all x1, starting transfers between devices, shards(): held = lax.all_to_all(packed, 'y', 0, 0)  7.66 us
    all_to_all x1, starting transfers between devices, shards(): cot = lax.all_to_all(cot_packed, 'y', 0, 0)  6.94 us
  transfers between devices with their start and end apart: 12, of which 7 were waited for; matrix products, arithmetic and copies ran while one was open for 4% of the time, Pallas kernels for 4%

profile of v5, /device:TPU:1, one launch (start us, length us, event | category | flops | bytes accessed | tf_op | source)
XLA Modules:
  0.0 140.9 jit_solution(16188322126390239874)
XLA Ops:
  0.6 0.0 copy-start
  0.6 1.8 %shard_map.58 = bf16[8,144,128]{2,1,0:T(8,128)(2,1)} custom-call(bf16[8,128,128]{2,1,0:T(8,128)(2,1)} %bitcast.22), custom_call_target="tpu_custom_call" | custom-call | tf_op jit(solution)/shard_map/pallas_call | solution.py:374
  2.5 7.7 %all-to-all-start = ((bf16[8,144,128]{2,1,0:T(8,128)(2,1)}), bf16[8,144,128]{2,1,0:T(8,128)(2,1)S(1)}, u32[]{:S(2)}, u32[]{:S(2)}) async-start(bf16[8,144,128]{2,1,0:T(8,128)(2,1)} %shard_map.58), calls=%async_computation | async-start | bytes 589824 | tf_op jit(solution)/shard_map/all_to_all | solution.py:382
  10.1 0.8 slice_bitcast_fusion.1
  10.9 4.6 %collective-permute-start.4 = (bf16[1,128,128]{2,1,0:T(8,128)(2,1)S(1)}, bf16[1,128,128]{2,1,0:T(8,128)(2,1)S(1)}, u32[]{:S(2)}, u32[]{:S(2)}) collective-permute-start(bf16[1,128,128]{2,1,0:T(8,128)(2,1)S(1)} %get-tuple-element.27), channel_id=1, source_target_pairs={{1,0},{2,1},{3,2},{4,3},{5,4},{6,5},{7,6},{8,7},{9,8},{10,9},{11,1... | collective-permute-start | bytes 98312 | tf_op jit(solution)/shard_map/ppermute | solution.py:345
  15.5 2.2 %collective-permute-start.3 = (bf16[1,128,128]{2,1,0:T(8,128)(2,1)S(1)}, bf16[1,128,128]{2,1,0:T(8,128)(2,1)S(1)}, u32[]{:S(2)}, u32[]{:S(2)}) collective-permute-start(bf16[1,128,128]{2,1,0:T(8,128)(2,1)S(1)} %get-tuple-element.28), channel_id=1, source_target_pairs={{0,1},{1,2},{2,3},{3,4},{4,5},{5,6},{6,7},{7,8},{8,9},{9,10},{10,1... | collective-permute-start | bytes 98312 | tf_op jit(solution)/shard_map/ppermute | solution.py:345
  17.7 0.0 collective-permute-done.4.down_ref
  17.7 0.0 copy-start.1
  17.7 1.0 collective-permute-done.3.up_ref
  18.7 0.0 copy-start.2
  18.7 0.0 copy-done.1
  18.7 0.6 copy-done.2
  19.3 2.5 %shard_map.59 = bf16[8,160,128]{2,1,0:T(8,128)(2,1)} custom-call(bf16[8,128,128]{2,1,0:T(8,128)(2,1)} %bitcast.21, bf16[1,128,128]{2,1,0:T(8,128)(2,1)} %copy-done.2, bf16[1,128,128]{2,1,0:T(8,128)(2,1)} %copy-done.1), custom_call_target="tpu_custom_call" | custom-call | tf_op jit(solution)/shard_map/pallas_call | solution.py:385
  21.8 0.0 all-to-all-done.held_ref
  21.8 6.9 %all-to-all-start.1 = ((bf16[8,160,128]{2,1,0:T(8,128)(2,1)}), bf16[8,160,128]{2,1,0:T(8,128)(2,1)S(1)}, u32[]{:S(2)}, u32[]{:S(2)}) async-start(bf16[8,160,128]{2,1,0:T(8,128)(2,1)} %shard_map.59), calls=%async_computation.1 | async-start | bytes 655360 | tf_op jit(solution)/shard_map/all_to_all | solution.py:391
  28.7 3.1 %collective-permute-start = (bf16[2,144,128]{2,1,0:T(8,128)(2,1)S(1)}, bf16[2,144,128]{2,1,0:T(8,128)(2,1)S(1)}, u32[]{:S(2)}, u32[]{:S(2)}) collective-permute-start(bf16[2,144,128]{2,1,0:T(8,128)(2,1)S(1)} %slice.56), channel_id=1, source_target_pairs={{0,128},{128,256},{256,384},{1,129},{129,257},{257,385},{2,130},{1... | collective-permute-start | bytes 221192 | tf_op jit(solution)/shard_map/ppermute | solution.py:345
  31.9 1.3 collective-permute-done.early_ref
  33.3 5.4 %collective-permute-start.1 = (bf16[10,48,128]{2,1,0:T(8,128)(2,1)S(1)}, bf16[10,48,128]{2,1,0:T(8,128)(2,1)S(1)}, u32[]{:S(2)}, u32[]{:S(2)}) collective-permute-start(bf16[10,48,128]{2,1,0:T(8,128)(2,1)S(1)} %pad_maximum_fusion), channel_id=1, source_target_pairs={{0,1},{1,2},{2,3},{3,4},{4,5},{5,6},{6,7},{7,8},{8,9},{9,10},{10,1... | collective-permute-start | bytes 368648 | tf_op jit(solution)/shard_map/ppermute | solution.py:345
  38.7 1.9 %collective-permute-start.2 = (bf16[10,48,128]{2,1,0:T(8,128)(2,1)S(1)}, bf16[10,48,128]{2,1,0:T(8,128)(2,1)S(1)}, u32[]{:S(2)}, u32[]{:S(2)}) collective-permute-start(bf16[10,48,128]{2,1,0:T(8,128)(2,1)S(1)} %maximum_maximum_fusion), channel_id=1, source_target_pairs={{1,0},{2,1},{3,2},{4,3},{5,4},{6,5},{7,6},{8,7},{9,8},{10,9},{11,1... | collective-permute-start | bytes 368648 | tf_op jit(solution)/shard_map/ppermute | solution.py:345
  40.6 0.0 copy-done
  40.6 1.0 reverse_bitcast_fusion
  41.6 2.0 %copy.7 = bf16[3,3,3,128,128]{4,3,2,1,0:T(8,128)(2,1)S(1)} copy(bf16[3,3,3,128,128]{3,4,2,1,0:T(8,128)(2,1)} %reverse_bitcast_fusion) | data formatting | bytes 1769472 | tf_op jit(solution)/shard_map/transpose | solution.py:369
  43.6 0.0 all-to-all-done.1.cot_ref
  43.6 0.0 collective-permute-done.1.up_ref
  43.6 1.3 collective-permute-done.2.down_ref
  44.9 6.0 %shard_map.60 = (bf16[8,128,128]{2,1,0:T(8,128)(2,1)S(1)}, bf16[8,128,128]{2,1,0:T(8,128)(2,1)S(1)}, bf16[8,16,128]{2,1,0:T(8,128)(2,1)S(1)}, bf16[8,16,128]{2,1...) custom-call(s32[1]{0:T(128)} %bitcast.core_ref, ...), custom_call_target="tpu_custom_call" | custom-call | flops 1811939328 | bytes 4194304 | tf_op jit(solution)/shard_map/pallas_call | solution.py:405
  50.9 1.9 %collective-permute-start.5 = (bf16[4,512,128]{2,1,0:T(8,128)(2,1)S(1)}, bf16[4,512,128]{2,1,0:T(8,128)(2,1)S(1)}, u32[]{:S(2)}, u32[]{:S(2)}) collective-permute-start(bf16[4,512,128]{2,1,0:T(8,128)(2,1)S(1)} %get-tuple-element.17), channel_id=1, source_target_pairs={{0,1},{1,0},{2,3},{3,2},{4,5},{5,4},{6,7},{7,6},{8,9},{9,8},{10,11... | collective-permute-start | bytes 1572872 | tf_op jit(solution)/shard_map/ppermute | solution.py:349
  52.8 1.9 %collective-permute-done.5 = bf16[4,512,128]{2,1,0:T(8,128)(2,1)S(1)} collective-permute-done((bf16[4,512,128]{2,1,0:T(8,128)(2,1)S(1)}, bf16[4,512,128]{2,1,0:T(8,128)(2,1)S(1)}, u32[]{:S(2)}, u32[]{:S(2)}) %collective-permute-start.5) | collective-permute-done | bytes 524320 | tf_op jit(solution)/shard_map/ppermute | solution.py:349
  54.7 0.9 add_convert_fusion
  55.6 4.9 %all-to-all-start.2 = ((bf16[4,512,128]{2,1,0:T(8,128)(2,1)}), bf16[4,512,128]{2,1,0:T(8,128)(2,1)S(1)}, u32[]{:S(2)}, u32[]{:S(2)}) async-start(bf16[4,512,128]{2,1,0:T(8,128)(2,1)} %add_convert_fusion), calls=%async_computation.2 | async-start | bytes 1048576 | tf_op jit(solution)/shard_map/all_to_all | solution.py:354
  60.5 9.1 %all-to-all-done.2 = bf16[4,512,128]{2,1,0:T(8,128)(2,1)S(1)} async-done(((bf16[4,512,128]{2,1,0:T(8,128)(2,1)}), bf16[4,512,128]{2,1,0:T(8,128)(2,1)S(1)}, u32[]{:S(2)}, u32[]{:S(2)}) %all-to-all-start.2) | async-done | bytes 524320 | tf_op jit(solution)/shard_map/all_to_all | solution.py:354
  69.7 0.7 reduce_sum.21
  70.4 17.0 %all-to-all-start.3 = ((bf16[64,8,128]{2,1,0:T(8,128)(2,1)}), bf16[64,8,128]{2,1,0:T(8,128)(2,1)S(1)}, u32[]{:S(2)}, u32[]{:S(2)}) async-start(bf16[64,8,128]{2,1,0:T(8,128)(2,1)} %bitcast.8), calls=%async_computation.3 | async-start | bytes 262144 | tf_op jit(solution)/shard_map/all_to_all | solution.py:356
  87.5 1.3 collective-permute-start.6
  88.8 4.2 %collective-permute-done.6.late_ref = bf16[2,160,128]{2,1,0:T(8,128)(2,1)S(1)} collective-permute-done((bf16[2,160,128]{2,1,0:T(8,128)(2,1)S(1)}, bf16[2,160,128]{2,1,0:T(8,128)(2,1)S(1)}, u32[]{:S(2)}, u32[]{:S(2)}) %collective-permute-start.6) | collective-permute-done | bytes 81952 | tf_op jit(solution)/shard_map/ppermute | solution.py:345
  92.9 3.5 %shard_map.61 = bf16[8,272,128]{2,1,0:T(8,128)(2,1)} custom-call(bf16[8,128,128]{2,1,0:T(8,128)(2,1)S(1)} %get-tuple-element.18.g_ref, bf16[8,16,128]{2,1,0:T(8,128)(2,1)S(1)} %get-tuple-element.19.up_ref, bf16[8,16,128]{2,1,0:T(8,128)(2,1)S(1)} %get-tuple-element.20.down_ref, bf16[2,160,128]{2,1,0:T(8,128)(2,1)S(1)} %collective-permute-done.6.late_ref, ...), custom_call_target="tpu_custom_call" | custom-call | flops 905969664 | bytes 4194304 | tf_op jit(solution)/shard_map/pallas_call | solution.py:430
  96.4 2.5 %all-to-all-done.3 = bf16[64,8,128]{2,1,0:T(8,128)(2,1)S(1)} async-done(((bf16[64,8,128]{2,1,0:T(8,128)(2,1)}), bf16[64,8,128]{2,1,0:T(8,128)(2,1)S(1)}, u32[]{:S(2)}, u32[]{:S(2)}) %all-to-all-start.3) | async-done | bytes 131104 | tf_op jit(solution)/shard_map/all_to_all | solution.py:356
  98.9 0.1 convert_reduce_fusion
  99.0 12.9 %all_to_all.30 = bf16[32,8,128]{2,1,0:T(8,128)(2,1)S(1)} all-to-all(bf16[32,8,128]{2,1,0:T(8,128)(2,1)S(1)} %broadcast_in_dim.14), channel_id=1, replica_groups=mesh['x'=4,'y'=8,'z'=8,'core'=2] {'x','y'}, dimensions={0} | all-to-all | bytes 131072 | tf_op jit(solution)/shard_map/all_to_all | solution.py:363
  111.9 3.5 %all-to-all-start.4 = ((bf16[8,272,128]{2,1,0:T(8,128)(2,1)}), bf16[8,272,128]{2,1,0:T(8,128)(2,1)S(1)}, u32[]{:S(2)}, u32[]{:S(2)}) async-start(bf16[8,272,128]{2,1,0:T(8,128)(2,1)} %shard_map.61), calls=%async_computation.4 | async-start | bytes 1114112 | tf_op jit(solution)/shard_map/all_to_all | solution.py:441
  115.5 23.2 %all_gather.3 = bf16[3456,128]{1,0:T(8,128)(2,1)S(1)} all-gather(bf16[216,128]{1,0:T(8,128)(2,1)S(1)} %slice_bitcast_fusion), channel_id=1, replica_groups=mesh['x'=4,'y'=8,'z'=8,'core'=2] {'z','core'}, dimensions={0}, use_global_device_ids=true | all-gather | bytes 940032 | tf_op jit(solution)/shard_map/all_gather | solution.py:364
  138.7 1.4 convert.2
  140.1 0.0 all-to-all-done.4.got_ref
  140.1 0.8 shard_map.62
  (16 shorter events, 0.1 us)
Async XLA Ops:
  0.6 40.0 %copy-start = (bf16[3,3,3,128,128]{4,3,2,1,0:T(8,128)(2,1)S(1)}, bf16[3,3,3,128,128]{4,3,2,1,0:T(8,128)(2,1)}, u32[]{:S(2)}) copy-start(bf16[3,3,3,128,128]{4,3,2,1,0:T(8,128)(2,1)} %param.4) | copy-start | bytes 2654212
  2.5 19.3 %all-to-all-start = ((bf16[8,144,128]{2,1,0:T(8,128)(2,1)}), bf16[8,144,128]{2,1,0:T(8,128)(2,1)S(1)}, u32[]{:S(2)}, u32[]{:S(2)}) async-start(bf16[8,144,128]{2,1,0:T(8,128)(2,1)} %shard_map.58), calls=%async_computation | async-start | bytes 589824 | tf_op jit(solution)/shard_map/all_to_all | solution.py:382
  10.9 6.8 %collective-permute-start.4 = (bf16[1,128,128]{2,1,0:T(8,128)(2,1)S(1)}, bf16[1,128,128]{2,1,0:T(8,128)(2,1)S(1)}, u32[]{:S(2)}, u32[]{:S(2)}) collective-permute-start(bf16[1,128,128]{2,1,0:T(8,128)(2,1)S(1)} %get-tuple-element.27), channel_id=1, source_target_pairs={{1,0},{2,1},{3,2},{4,3},{5,4},{6,5},{7,6},{8,7},{9,8},{10,9},{11,1... | collective-permute-start | bytes 98312 | tf_op jit(solution)/shard_map/ppermute | solution.py:345
  15.5 3.2 %collective-permute-start.3 = (bf16[1,128,128]{2,1,0:T(8,128)(2,1)S(1)}, bf16[1,128,128]{2,1,0:T(8,128)(2,1)S(1)}, u32[]{:S(2)}, u32[]{:S(2)}) collective-permute-start(bf16[1,128,128]{2,1,0:T(8,128)(2,1)S(1)} %get-tuple-element.28), channel_id=1, source_target_pairs={{0,1},{1,2},{2,3},{3,4},{4,5},{5,6},{6,7},{7,8},{8,9},{9,10},{10,1... | collective-permute-start | bytes 98312 | tf_op jit(solution)/shard_map/ppermute | solution.py:345
  17.7 1.0 copy-start.1
  18.7 0.6 copy-start.2
  21.8 21.8 %all-to-all-start.1 = ((bf16[8,160,128]{2,1,0:T(8,128)(2,1)}), bf16[8,160,128]{2,1,0:T(8,128)(2,1)S(1)}, u32[]{:S(2)}, u32[]{:S(2)}) async-start(bf16[8,160,128]{2,1,0:T(8,128)(2,1)} %shard_map.59), calls=%async_computation.1 | async-start | bytes 655360 | tf_op jit(solution)/shard_map/all_to_all | solution.py:391
  28.7 4.5 %collective-permute-start = (bf16[2,144,128]{2,1,0:T(8,128)(2,1)S(1)}, bf16[2,144,128]{2,1,0:T(8,128)(2,1)S(1)}, u32[]{:S(2)}, u32[]{:S(2)}) collective-permute-start(bf16[2,144,128]{2,1,0:T(8,128)(2,1)S(1)} %slice.56), channel_id=1, source_target_pairs={{0,128},{128,256},{256,384},{1,129},{129,257},{257,385},{2,130},{1... | collective-permute-start | bytes 221192 | tf_op jit(solution)/shard_map/ppermute | solution.py:345
  33.3 10.3 %collective-permute-start.1 = (bf16[10,48,128]{2,1,0:T(8,128)(2,1)S(1)}, bf16[10,48,128]{2,1,0:T(8,128)(2,1)S(1)}, u32[]{:S(2)}, u32[]{:S(2)}) collective-permute-start(bf16[10,48,128]{2,1,0:T(8,128)(2,1)S(1)} %pad_maximum_fusion), channel_id=1, source_target_pairs={{0,1},{1,2},{2,3},{3,4},{4,5},{5,6},{6,7},{7,8},{8,9},{9,10},{10,1... | collective-permute-start | bytes 368648 | tf_op jit(solution)/shard_map/ppermute | solution.py:345
  38.7 6.2 %collective-permute-start.2 = (bf16[10,48,128]{2,1,0:T(8,128)(2,1)S(1)}, bf16[10,48,128]{2,1,0:T(8,128)(2,1)S(1)}, u32[]{:S(2)}, u32[]{:S(2)}) collective-permute-start(bf16[10,48,128]{2,1,0:T(8,128)(2,1)S(1)} %maximum_maximum_fusion), channel_id=1, source_target_pairs={{1,0},{2,1},{3,2},{4,3},{5,4},{6,5},{7,6},{8,7},{9,8},{10,9},{11,1... | collective-permute-start | bytes 368648 | tf_op jit(solution)/shard_map/ppermute | solution.py:345
  50.9 3.8 %collective-permute-start.5 = (bf16[4,512,128]{2,1,0:T(8,128)(2,1)S(1)}, bf16[4,512,128]{2,1,0:T(8,128)(2,1)S(1)}, u32[]{:S(2)}, u32[]{:S(2)}) collective-permute-start(bf16[4,512,128]{2,1,0:T(8,128)(2,1)S(1)} %get-tuple-element.17), channel_id=1, source_target_pairs={{0,1},{1,0},{2,3},{3,2},{4,5},{5,4},{6,7},{7,6},{8,9},{9,8},{10,11... | collective-permute-start | bytes 1572872 | tf_op jit(solution)/shard_map/ppermute | solution.py:349
  55.6 14.1 %all-to-all-start.2 = ((bf16[4,512,128]{2,1,0:T(8,128)(2,1)}), bf16[4,512,128]{2,1,0:T(8,128)(2,1)S(1)}, u32[]{:S(2)}, u32[]{:S(2)}) async-start(bf16[4,512,128]{2,1,0:T(8,128)(2,1)} %add_convert_fusion), calls=%async_computation.2 | async-start | bytes 1048576 | tf_op jit(solution)/shard_map/all_to_all | solution.py:354
  70.4 28.5 %all-to-all-start.3 = ((bf16[64,8,128]{2,1,0:T(8,128)(2,1)}), bf16[64,8,128]{2,1,0:T(8,128)(2,1)S(1)}, u32[]{:S(2)}, u32[]{:S(2)}) async-start(bf16[64,8,128]{2,1,0:T(8,128)(2,1)} %bitcast.8), calls=%async_computation.3 | async-start | bytes 262144 | tf_op jit(solution)/shard_map/all_to_all | solution.py:356
  87.5 5.5 %collective-permute-start.6 = (bf16[2,160,128]{2,1,0:T(8,128)(2,1)S(1)}, bf16[2,160,128]{2,1,0:T(8,128)(2,1)S(1)}, u32[]{:S(2)}, u32[]{:S(2)}) collective-permute-start(bf16[2,160,128]{2,1,0:T(8,128)(2,1)S(1)} %pad_maximum_fusion.1), channel_id=1, source_target_pairs={{128,0},{256,128},{384,256},{129,1},{257,129},{385,257},{130,2},{2... | collective-permute-start | bytes 245768 | tf_op jit(solution)/shard_map/ppermute | solution.py:345
  111.9 28.1 %all-to-all-start.4 = ((bf16[8,272,128]{2,1,0:T(8,128)(2,1)}), bf16[8,272,128]{2,1,0:T(8,128)(2,1)S(1)}, u32[]{:S(2)}, u32[]{:S(2)}) async-start(bf16[8,272,128]{2,1,0:T(8,128)(2,1)} %shard_map.61), calls=%async_computation.4 | async-start | bytes 1114112 | tf_op jit(solution)/shard_map/all_to_all | solution.py:441

commit v6 on v5

--- a/solution.py
+++ b/solution.py
@@ -21,6 +21,8 @@
 FRAMES = GROUP + 2
 EDGES = 2 * ROWS
 HELD = TILE + EDGES
+LOAD = HELD + TILE
+SENT = TILE + EDGES
 RIM = 2 * STRIP
 PART = 8
 
@@ -42,12 +44,14 @@
     )
 
 
-def pack_body(x_hbm, out_ref, x_ref, left_ref, right_ref, sem):
-    copy = pltpu.make_async_copy(x_hbm, x_ref, sem)
-    copy.start()
+def pack_body(x_hbm, cot_hbm, out_ref, x_ref, cot_ref, left_ref, right_ref, sems):
+    x_copy = pltpu.make_async_copy(x_hbm, x_ref, sems.at[0])
+    cot_copy = pltpu.make_async_copy(cot_hbm, cot_ref, sems.at[1])
+    x_copy.start()
+    cot_copy.start()
     left_ref[...] = jnp.zeros_like(left_ref)
     right_ref[...] = jnp.zeros_like(right_ref)
-    copy.wait()
+    x_copy.wait()
     for row in range(ROWS):
         line = x_ref[row]
         wide = line.astype(f32)
@@ -61,23 +65,17 @@
     for strip in range(GROUP):
         pair = jnp.concatenate([left_ref[strip], right_ref[strip]], axis=0)
         out_ref[strip, pl.ds(TILE, EDGES), :] = pair.astype(bf16)
-
-
-def pack_cot_body(cot_hbm, up_ref, down_ref, out_ref, cot_ref, sem):
-    copy = pltpu.make_async_copy(cot_hbm, cot_ref, sem)
-    copy.start()
-    copy.wait()
-    for tall_row in range(TALL):
-        if tall_row == 0:
-            line = up_ref[0]
-        elif tall_row == TALL - 1:
-            line = down_ref[0]
-        else:
-            line = cot_ref[tall_row - 1]
+    cot_copy.wait()
+    for row in range(ROWS):
+        line = cot_ref[row]
         for strip in range(GROUP):
-            out_ref[strip, pl.ds(tall_row * STRIP, STRIP), :] = line[
+            out_ref[strip, pl.ds(cot_place(row), STRIP), :] = line[
                 strip * STRIP : (strip + 1) * STRIP
             ]
+
+
+def cot_place(row):
+    return HELD + (row + 1) % ROWS * STRIP
 
 
 def place_line(col_ref, line, left, right, places):
@@ -124,7 +122,6 @@
     early_ref,
     up_ref,
     down_ref,
-    cot_ref,
     w_ref,
     code_ref,
     g_ref,
@@ -146,7 +143,8 @@
             else:
                 source, at, low, edge_row = ref, frame, tall_row * STRIP, tall_row
             line = source[at, pl.ds(low, STRIP), :]
-            edge = source[at, pl.ds(source.shape[1] - EDGES, EDGES), :].astype(f32)
+            edge_low = TILE if source is ref else RIM
+            edge = source[at, pl.ds(edge_low, EDGES), :].astype(f32)
             places = []
             for row_tap in range(3):
                 row = tall_row + 1 - row_tap
@@ -205,17 +203,17 @@
             code = (band[0] + band_weight * detail[member]).astype(bf16)
             code_ref[member, pl.ds(low, STRIP), :] = code
             code_ref[member + 1, pl.ds(low, STRIP), :] = code
-        tall = pl.multiple_of(low + STRIP, STRIP)
-        cot = [cot_ref[frame, pl.ds(tall, STRIP), :].astype(f32) for frame in range(GROUP)]
+        place = pl.multiple_of(HELD + lax.rem(row + 1, ROWS) * STRIP, STRIP)
+        cot = [held_ref[frame, pl.ds(place, STRIP), :].astype(f32) for frame in range(GROUP)]
         back = adjoint_bands(cot)
         for frame in range(GROUP):
             g_ref[frame, pl.ds(low, STRIP), :] = (
                 back[frame] * slope_of(linear[frame], gate[frame])
             ).astype(bf16)
 
-    for offset, tall, rim_ref in ((0, 0, g_up_ref), (STRIP, TALL - 1, g_down_ref)):
+    for offset, source, rim_ref in ((0, up_ref, g_up_ref), (STRIP, down_ref, g_down_ref)):
         cot = [
-            cot_ref[frame, pl.ds(tall * STRIP, STRIP), :].astype(f32) for frame in range(GROUP)
+            source[frame + 2, pl.ds(RIM + EDGES, STRIP), :].astype(f32) for frame in range(GROUP)
         ]
         back = adjoint_bands(cot)
         for frame in range(GROUP):
@@ -229,10 +227,11 @@
         for tap in range(3):
             gt_ref[pl.ds(tap * CH, CH), pl.ds((frame + tap) * TILE, TILE)] = turned
     terms_ref[...] = jnp.zeros_like(terms_ref)
-    _, wide, planes, share = terms_ref.shape[:4]
+    _, peers, ring, share = terms_ref.shape[:4]
     blocks = 27 * CH // PART
     slots = share // PART
-    lines = 2 * (planes // GROUP)
+    deep = peers // CHIPS[0]
+    lines = 2 * deep
     for low in range(0, 9, 2):
         high = min(low + 2, 9)
         product = jnp.dot(
@@ -250,21 +249,21 @@
                     line, within = divmod(at, blocks // lines)
                     owner, slot = divmod(within, slots)
                     depth, core = divmod(line, 2)
-                    column, ring = divmod(owner, GROUP)
-                    peer = ring * (planes // GROUP) + depth
-                    terms_ref[core, column, peer, pl.ds(slot * PART, PART), :] = block[
+                    column, place = divmod(owner, ring)
+                    peer = column * deep + depth
+                    terms_ref[core, peer, place, pl.ds(slot * PART, PART), :] = block[
                         piece * PART : (piece + 1) * PART
                     ]
     for core in range(2):
 
         @pl.when(core_ref[0] == core)
         def _():
-            for column in range(wide):
-                keep_ref[column] = terms_ref[core, column].reshape(-1, CH).astype(bf16)
-                send_ref[column] = terms_ref[1 - core, column].reshape(-1, CH).astype(bf16)
-
-
-def backward_body(g_ref, up_ref, down_ref, late_ref, code_ref, w_ref, out_ref, col_ref, side_ref):
+            for peer in range(peers):
+                keep_ref[peer] = terms_ref[core, peer].reshape(-1, CH).astype(bf16)
+                send_ref[peer] = terms_ref[1 - core, peer].reshape(-1, CH).astype(bf16)
+
+
+def backward_body(g_ref, up_ref, down_ref, late_ref, w_ref, out_ref, col_ref, side_ref):
     nothing = jnp.zeros((1, CH), f32)
 
     def spread(lines, place):
@@ -292,8 +291,7 @@
         + jnp.dot(col_ref[2 * TILE : (GROUP + 2) * TILE, :], w_ref[2], preferred_element_type=f32)
     )
     for frame in range(GROUP):
-        out_ref[frame, 0:TILE, :] = code_ref[frame]
-        out_ref[frame, TILE : 2 * TILE, :] = total[frame * TILE : (frame + 1) * TILE].astype(bf16)
+        out_ref[frame, 0:TILE, :] = total[frame * TILE : (frame + 1) * TILE].astype(bf16)
     for side, (offset, col_tap) in enumerate(((0, 2), (STRIP - 1, 0))):
         for frame in range(FRAMES):
             for row in range(ROWS):
@@ -318,20 +316,48 @@
             first = summed
     for frame in range(GROUP):
         pair = [value[frame * ROWS : (frame + 1) * ROWS] for value in (first, summed)]
-        out_ref[frame, 2 * TILE : 2 * TILE + EDGES, :] = jnp.concatenate(pair, axis=0).astype(bf16)
+        out_ref[frame, TILE:SENT, :] = jnp.concatenate(pair, axis=0).astype(bf16)
+
+
+def load_body(parts_ref, sent_ref, code_ref, out_ref):
+    ring, share = GROUP, parts_ref.shape[1] // GROUP
+    part = parts_ref[0].astype(f32)
+    for peer in range(1, parts_ref.shape[0]):
+        part = part + parts_ref[peer].astype(f32)
+    empty = jnp.zeros((-share % STRIP, CH), f32)
+    for place in range(ring):
+        piece = part[place * share : (place + 1) * share]
+        if empty.shape[0]:
+            piece = jnp.concatenate([piece, empty], axis=0)
+        out_ref[place, 0 : piece.shape[0], :] = piece.astype(bf16)
+        low = piece.shape[0]
+        out_ref[place, low : low + TILE, :] = code_ref[place]
+        out_ref[place, low + TILE : low + TILE + SENT, :] = sent_ref[place]
+
+
+def share_body(got_ref, out_ref, norm):
+    share = out_ref.shape[1]
+    total = got_ref[0].astype(f32)
+    for strip in range(1, GROUP):
+        total = total + got_ref[strip].astype(f32)
+    copies = (total[:share] * norm).astype(bf16)
+    for owner in range(out_ref.shape[0]):
+        out_ref[owner] = copies
 
 
 def unpack_body(got_ref, code_ref, grad_ref):
+    head = got_ref.shape[1] - TILE - SENT
+    code_low, grad_low, edge_low = head, head + TILE, head + 2 * TILE
     at = lax.broadcasted_iota(jnp.int32, (STRIP, CH), 0)
     for strip in range(GROUP):
         columns = pl.ds(strip * STRIP, STRIP)
         if strip > 0:
-            before = got_ref[strip - 1, pl.ds(2 * TILE, EDGES), :].astype(f32)
+            before = got_ref[strip - 1, pl.ds(edge_low, EDGES), :].astype(f32)
         if strip < GROUP - 1:
-            after = got_ref[strip + 1, pl.ds(2 * TILE, EDGES), :].astype(f32)
+            after = got_ref[strip + 1, pl.ds(edge_low, EDGES), :].astype(f32)
         for row in range(ROWS):
-            code_ref[row, columns, :] = got_ref[strip, pl.ds(row * STRIP, STRIP), :]
-            value = got_ref[strip, pl.ds(TILE + row * STRIP, STRIP), :].astype(f32)
+            code_ref[row, columns, :] = got_ref[strip, pl.ds(code_low + row * STRIP, STRIP), :]
+            value = got_ref[strip, pl.ds(grad_low + row * STRIP, STRIP), :].astype(f32)
             if strip > 0:
                 value = value + jnp.where(at == 0, before[ROWS + row : ROWS + row + 1], 0.0)
             if strip < GROUP - 1:
@@ -349,58 +375,36 @@
     return lax.ppermute(value, "core", [(0, 1), (1, 0)])
 
 
-def own_share(chip_sum, norm):
-    planes = lax.axis_size(("y", "z"))
-    parts = lax.all_to_all(chip_sum, "x", 0, 0)
-    part = parts.astype(f32).sum(axis=0).astype(bf16).reshape(planes, -1, CH)
-    spread = lax.all_to_all(part, ("y", "z"), 0, 0)
-    return (spread.astype(f32).sum(axis=0) * norm).astype(bf16)
-
-
-def all_shares(total):
-    owners, lines = lax.axis_size(("x", "y")), lax.axis_size(("z", "core"))
-    copies = jnp.broadcast_to(total[None], (owners,) + total.shape)
-    part = lax.all_to_all(copies, ("x", "y"), 0, 0).reshape(-1, CH)[: 27 * CH // lines]
-    return lax.all_gather(part, ("z", "core"), tiled=True).astype(f32)
-
-
 def shards(frames, kernel, cotangent):
     weights = kernel.reshape(3, WIDE, CH)
     turned = jnp.swapaxes(kernel[::-1, ::-1, ::-1], 3, 4).reshape(3, WIDE, CH)
     lines = ("z", "core")
     whole_vmem = pltpu.VMEM((ROWS, GROUP * STRIP, CH), bf16)
-    in_hbm = pl.BlockSpec(memory_space=pl.ANY)
-    in_vmem = pl.BlockSpec(memory_space=pltpu.VMEM)
     packed = pl.pallas_call(
         pack_body,
-        out_shape=jax.ShapeDtypeStruct((GROUP, HELD, CH), bf16),
-        in_specs=[in_hbm],
-        scratch_shapes=[whole_vmem]
+        out_shape=jax.ShapeDtypeStruct((GROUP, LOAD, CH), bf16),
+        in_specs=[pl.BlockSpec(memory_space=pl.ANY)] * 2,
+        scratch_shapes=[whole_vmem] * 2
         + [pltpu.VMEM((GROUP, ROWS, CH), f32)] * 2
-        + [pltpu.SemaphoreType.DMA],
-    )(frames[0])
+        + [pltpu.SemaphoreType.DMA((2,))],
+    )(frames[0], cotangent[0])
     held = lax.all_to_all(packed, "y", 0, 0)
-    cot_up = shifted(cotangent[0, ROWS - 1 :], lines, 1)
-    cot_down = shifted(cotangent[0, :1], lines, -1)
-    cot_packed = pl.pallas_call(
-        pack_cot_body,
-        out_shape=jax.ShapeDtypeStruct((GROUP, TALL * STRIP, CH), bf16),
-        in_specs=[in_hbm, in_vmem, in_vmem],
-        scratch_shapes=[whole_vmem, pltpu.SemaphoreType.DMA],
-    )(cotangent[0], cot_up, cot_down)
-    cot = lax.all_to_all(cot_packed, "y", 0, 0)
-    early = shifted(held[GROUP - 2 :], "x", 1)
-    edges = jnp.concatenate([early[:, TILE:], held[:, TILE:]], axis=0)
-    last = jnp.concatenate([early[:, TILE - RIM :], held[:, TILE - RIM :]], axis=0)
-    first = jnp.concatenate([early[:, :RIM], held[:, :RIM]], axis=0)
-    up = shifted(last, lines, 1)
-    down = shifted(jnp.concatenate([first, edges], axis=1), lines, -1)
-    turned, held = lax.optimization_barrier((turned, held))
-
-    wide, planes = lax.axis_size("x"), lax.axis_size(("y", "z"))
+    early = shifted(held[GROUP - 2 :, : HELD + 2 * STRIP], "x", 1)
+
+    def edge_rows(*places):
+        pieces = [
+            jnp.concatenate([early[:, low:high], held[:, low:high]], axis=0)
+            for low, high in places
+        ]
+        return pieces[0] if len(pieces) == 1 else jnp.concatenate(pieces, axis=1)
+
+    up = shifted(edge_rows((TILE - RIM, HELD + STRIP)), lines, 1)
+    down = shifted(edge_rows((0, RIM), (TILE, HELD), (HELD + STRIP, HELD + 2 * STRIP)), lines, -1)
+
     devices = lax.axis_size(("x", "y", "z", "core"))
+    peers, owners = lax.axis_size(("x", "z")), lax.axis_size(("x", "y"))
     share = PART * -(-27 * CH // (PART * devices))
-    mail = jax.ShapeDtypeStruct((wide, planes * share, CH), bf16)
+    mail = jax.ShapeDtypeStruct((peers, GROUP * share, CH), bf16)
     flops = 2 * GROUP * TILE * 27 * CH * CH
     code, g, g_up, g_down, keep, send = kernel_call(
         forward_body,
@@ -416,29 +420,39 @@
             pltpu.VMEM((FRAMES * (TILE + RIM), WIDE), bf16),
             pltpu.VMEM((GROUP * (TILE + RIM), CH), f32),
             pltpu.VMEM((3 * CH, FRAMES * TILE), bf16),
-            pltpu.VMEM((2, wide, planes, share, CH), f32),
+            pltpu.VMEM((2, peers, GROUP, share, CH), f32),
         ],
         flops=2 * flops,
-        in_specs=[pl.BlockSpec(memory_space=pltpu.SMEM)] + [in_vmem] * 6,
-    )(lax.axis_index("core").astype(jnp.int32).reshape(1), held, early, up, down, cot, weights)
-
-    norm = 1.0 / math.sqrt(devices * GROUP * TILE)
+        in_specs=[pl.BlockSpec(memory_space=pltpu.SMEM)]
+        + [pl.BlockSpec(memory_space=pltpu.VMEM)] * 5,
+    )(lax.axis_index("core").astype(jnp.int32).reshape(1), held, early, up, down, weights)
+
     chip_sum = (keep.astype(f32) + swapped(send).astype(f32)).astype(bf16)
-    total = own_share(chip_sum, norm)
-
+    parts = lax.all_to_all(chip_sum, ("x", "z"), 0, 0)
     late = shifted(jnp.concatenate([g_up[:2], g[:2], g_down[:2]], axis=1), "x", -1)
     sent = kernel_call(
         backward_body,
-        jax.ShapeDtypeStruct((GROUP, 2 * TILE + EDGES, CH), bf16),
+        jax.ShapeDtypeStruct((GROUP, SENT, CH), bf16),
         [
             pltpu.VMEM((FRAMES * TILE, WIDE), bf16),
             pltpu.VMEM((FRAMES * ROWS, 3 * CH), f32),
         ],
         flops=flops,
-    )(g, g_up, g_down, late, code, turned)
-    total, sent = lax.optimization_barrier((total, sent))
-    grad_kernel = all_shares(total)
-    got = lax.all_to_all(sent, "y", 0, 0)
+    )(g, g_up, g_down, late, turned)
+    head = STRIP * -(-share // STRIP)
+    load = kernel_call(
+        load_body, jax.ShapeDtypeStruct((GROUP, head + TILE + SENT, CH), bf16)
+    )(parts, sent, code)
+    got = lax.all_to_all(load, "y", 0, 0)
+    norm = 1.0 / math.sqrt(devices * GROUP * TILE)
+    copies = kernel_call(
+        functools.partial(share_body, norm=norm),
+        jax.ShapeDtypeStruct((owners, share, CH), bf16),
+    )(got[:, :head])
+    line = lax.all_to_all(copies, ("x", "y"), 0, 0).reshape(-1, CH)
+    line = line[: 27 * CH // lax.axis_size(lines)]
+    grad_kernel = lax.all_gather(line, lines, tiled=True).astype(f32)
+
     whole = jax.ShapeDtypeStruct((ROWS, GROUP * STRIP, CH), bf16)
     code_out, grad_frames = kernel_call(unpack_body, (whole, whole))(got)
     return (code_out[None], grad_frames[None], grad_kernel.reshape(3, 3, 3, CH, CH))

time: 142 us -> 143 us (level)
  blocking collectives: 36.1 us -> 64.9 us
  starting transfers between devices: 60.4 us -> 35.3 us
  waiting for transfers between devices: 21.3 us -> 25.4 us
  local copies, waits for them, and re-layouts: 4.42 us -> 1.51 us
  Pallas kernels: 14.6 us -> 12.2 us
    all_to_all x1 -> x2, blocking collectives: 12.9 us -> 41.2 us  [the longest x1 22.9 us: shards(): held = lax.all_to_all(packed, 'y', 0, 0)]
    all_to_all x5 -> x2, starting transfers between devices: 40 us -> 18.4 us  [the longest x1 13.2 us: shards(): parts = lax.all_to_all(chip_sum, ('x', 'z'), 0, 0)]
    ppermute x6 -> x4, starting transfers between devices: 18.4 us -> 14.9 us  [shifted(): return lax.ppermute(value, axes, route)]
    ppermute x6 -> x4, waiting for transfers between devices: 7.77 us -> 10.5 us  [shifted(): return lax.ppermute(value, axes, route)]
    pallas_call x3 -> x4, Pallas kernels: 7.77 us -> 5.35 us  [the longest x1 2.66 us: shards(): kernel_call(backward_body, jax.ShapeDtypeStruct((GROUP, SENT, CH), bf16),...]
    transpose x2, local copies, waits for them, and re-layouts: 2.96 us -> 1.44 us  [shards(): turned = jnp.swapaxes(kernel[::-1, ::-1, ::-1], 3, 4).reshape(3, WIDE, CH)]
    all_to_all x5 -> x2, waiting for transfers between devices: 11.7 us -> 13.1 us  [the longest x1 8.05 us: shards(): line = lax.all_to_all(copies, ('x', 'y'), 0, 0).reshape(-1, CH)]
  transfers between devices with their start and end apart: 12 -> 7, of which waited for: 7 -> 7; matrix products, arithmetic and copies ran while one was open for 4% -> 1% of each run, Pallas kernels for 4% -> 2%
where the time goes in v6:
time: 143 us
  blocking collectives  64.9 us (45%)
  starting transfers between devices  35.3 us (25%)
  waiting for transfers between devices  25.4 us (18%)
  Pallas kernels  12.2 us (9%)
  other arithmetic  2.44 us (2%)
  local copies, waits for them, and re-layouts  1.51 us (1%)
    all_gather x1, blocking collectives, shards(): grad_kernel = lax.all_gather(line, lines, tiled=True).astype(f32)  23.7 us
    all_to_all x1, blocking collectives, shards(): held = lax.all_to_all(packed, 'y', 0, 0)  22.9 us
    all_to_all x1, blocking collectives, shards(): got = lax.all_to_all(load, 'y', 0, 0)  18.2 us
    ppermute x4, starting transfers between devices, shifted(): return lax.ppermute(value, axes, route)  14.9 us
    all_to_all x1, starting transfers between devices, shards(): parts = lax.all_to_all(chip_sum, ('x', 'z'), 0, 0)  13.2 us
    ppermute x4, waiting for transfers between devices, shifted(): return lax.ppermute(value, axes, route)  10.5 us
    all_to_all x1, waiting for transfers between devices, shards(): line = lax.all_to_all(copies, ('x', 'y'), 0, 0).reshape(-1, CH)  8.05 us
    pallas_call x1, Pallas kernels, shards(): kernel_call(forward_body, (jax.ShapeDtypeStruct((GROUP, TILE, CH), bf16),...  6.04 us
  transfers between devices with their start and end apart: 7, of which 7 were waited for; matrix products, arithmetic and copies ran while one was open for 1% of the time, Pallas kernels for 2%

profile of v6, /device:TPU:1, one launch (start us, length us, event | category | flops | bytes accessed | tf_op | source)
XLA Modules:
  0.0 142.6 jit_solution(11259618939358009249)
XLA Ops:
  0.6 0.0 copy-start
  0.6 1.9 %shard_map.58 = bf16[8,272,128]{2,1,0:T(8,128)(2,1)} custom-call(bf16[8,128,128]{2,1,0:T(8,128)(2,1)} %bitcast.16, bf16[8,128,128]{2,1,0:T(8,128)(2,1)} %bitcast.17), custom_call_target="tpu_custom_call" | custom-call | tf_op jit(solution)/shard_map/pallas_call | solution.py:383
  2.6 22.9 %all_to_all.20.held_ref = bf16[8,272,128]{2,1,0:T(8,128)(2,1)S(1)} all-to-all(bf16[8,272,128]{2,1,0:T(8,128)(2,1)} %shard_map.58), channel_id=1, replica_groups=mesh['x'=4,'y'=8,'z'=8,'core'=2] {'y'}, dimensions={0} | all-to-all | bytes 1114112 | tf_op jit(solution)/shard_map/all_to_all | solution.py:391
  25.5 4.3 %collective-permute-start = (bf16[2,176,128]{2,1,0:T(8,128)(2,1)S(1)}, bf16[2,176,128]{2,1,0:T(8,128)(2,1)S(1)}, u32[]{:S(2)}, u32[]{:S(2)}) collective-permute-start(bf16[2,176,128]{2,1,0:T(8,128)(2,1)S(1)} %slice.60), channel_id=1, source_target_pairs={{0,128},{128,256},{256,384},{1,129},{129,257},{257,385},{2,130},{1... | collective-permute-start | bytes 270344 | tf_op jit(solution)/shard_map/ppermute | solution.py:371
  29.9 1.5 %collective-permute-done.early_ref = bf16[2,176,128]{2,1,0:T(8,128)(2,1)S(1)} collective-permute-done((bf16[2,176,128]{2,1,0:T(8,128)(2,1)S(1)}, bf16[2,176,128]{2,1,0:T(8,128)(2,1)S(1)}, u32[]{:S(2)}, u32[]{:S(2)}) %collective-permute-start) | collective-permute-done | bytes 90144 | tf_op jit(solution)/shard_map/ppermute | solution.py:371
  31.4 7.4 %collective-permute-start.1 = (bf16[10,64,128]{2,1,0:T(8,128)(2,1)S(1)}, bf16[10,64,128]{2,1,0:T(8,128)(2,1)S(1)}, u32[]{:S(2)}, u32[]{:S(2)}) collective-permute-start(bf16[10,64,128]{2,1,0:T(8,128)(2,1)S(1)} %pad_maximum_fusion), channel_id=1, source_target_pairs={{0,1},{1,2},{2,3},{3,4},{4,5},{5,6},{6,7},{7,8},{8,9},{9,10},{10,1... | collective-permute-start | bytes 491528 | tf_op jit(solution)/shard_map/ppermute | solution.py:371
  38.9 1.9 %collective-permute-start.2 = (bf16[10,64,128]{2,1,0:T(8,128)(2,1)S(1)}, bf16[10,64,128]{2,1,0:T(8,128)(2,1)S(1)}, u32[]{:S(2)}, u32[]{:S(2)}) collective-permute-start(bf16[10,64,128]{2,1,0:T(8,128)(2,1)S(1)} %maximum_maximum_fusion), channel_id=1, source_target_pairs={{1,0},{2,1},{3,2},{4,3},{5,4},{6,5},{7,6},{8,7},{9,8},{10,9},{11,1... | collective-permute-start | bytes 491528 | tf_op jit(solution)/shard_map/ppermute | solution.py:371
  40.8 0.3 collective-permute-done.1.up_ref
  41.1 4.4 %collective-permute-done.2.down_ref = bf16[10,64,128]{2,1,0:T(8,128)(2,1)S(1)} collective-permute-done((bf16[10,64,128]{2,1,0:T(8,128)(2,1)S(1)}, bf16[10,64,128]{2,1,0:T(8,128)(2,1)S(1)}, u32[]{:S(2)}, u32[]{:S(2)}) %collective-permute-start.2) | collective-permute-done | bytes 163872 | tf_op jit(solution)/shard_map/ppermute | solution.py:371
  45.5 0.0 copy-done
  45.5 6.0 %shard_map.59 = (bf16[8,128,128]{2,1,0:T(8,128)(2,1)S(1)}, bf16[8,128,128]{2,1,0:T(8,128)(2,1)S(1)}, bf16[8,16,128]{2,1,0:T(8,128)(2,1)S(1)}, bf16[8,16,128]{2,1...) custom-call(s32[1]{0:T(128)} %bitcast.core_ref, ...), custom_call_target="tpu_custom_call" | custom-call | flops 1811939328 | bytes 4194304 | tf_op jit(solution)/shard_map/pallas_call | solution.py:409
  51.6 1.9 %collective-permute-start.3 = (bf16[32,64,128]{2,1,0:T(8,128)(2,1)S(1)}, bf16[32,64,128]{2,1,0:T(8,128)(2,1)S(1)}, u32[]{:S(2)}, u32[]{:S(2)}) collective-permute-start(bf16[32,64,128]{2,1,0:T(8,128)(2,1)S(1)} %get-tuple-element.12), channel_id=1, source_target_pairs={{0,1},{1,0},{2,3},{3,2},{4,5},{5,4},{6,7},{7,6},{8,9},{9,8},{10,11... | collective-permute-start | bytes 1572872 | tf_op jit(solution)/shard_map/ppermute | solution.py:375
  53.5 1.9 %collective-permute-done.3 = bf16[32,64,128]{2,1,0:T(8,128)(2,1)S(1)} collective-permute-done((bf16[32,64,128]{2,1,0:T(8,128)(2,1)S(1)}, bf16[32,64,128]{2,1,0:T(8,128)(2,1)S(1)}, u32[]{:S(2)}, u32[]{:S(2)}) %collective-permute-start.3) | collective-permute-done | bytes 524320 | tf_op jit(solution)/shard_map/ppermute | solution.py:375
  55.4 1.0 add_convert_fusion
  56.4 13.2 %all-to-all-start.1 = ((bf16[32,64,128]{2,1,0:T(8,128)(2,1)}), bf16[32,64,128]{2,1,0:T(8,128)(2,1)S(1)}, u32[]{:S(2)}, u32[]{:S(2)}) async-start(bf16[32,64,128]{2,1,0:T(8,128)(2,1)} %add_convert_fusion), calls=%async_computation.1 | async-start | bytes 1048576 | tf_op jit(solution)/shard_map/all_to_all | solution.py:431
  69.6 1.3 collective-permute-start.4
  70.9 0.1 reverse_bitcast_fusion
  71.0 1.4 copy.6
  72.3 4.3 %collective-permute-done.4.late_ref = bf16[2,160,128]{2,1,0:T(8,128)(2,1)S(1)} collective-permute-done((bf16[2,160,128]{2,1,0:T(8,128)(2,1)S(1)}, bf16[2,160,128]{2,1,0:T(8,128)(2,1)S(1)}, u32[]{:S(2)}, u32[]{:S(2)}) %collective-permute-start.4) | collective-permute-done | bytes 81952 | tf_op jit(solution)/shard_map/ppermute | solution.py:371
  76.6 2.7 %shard_map.60.sent_ref = bf16[8,144,128]{2,1,0:T(8,128)(2,1)S(1)} custom-call(bf16[8,128,128]{2,1,0:T(8,128)(2,1)S(1)} %get-tuple-element.13.g_ref, bf16[8,16,128]{2,1,0:T(8,128)(2,1)S(1)} %get-tuple-element.14.up_ref, bf16[8,16,128]{2,1,0:T(8,128)(2,1)S(1)} %get-tuple-element.15.down_ref, bf16[2,160,128]{2,1,0:T(8,128)(2,1)S(1)} %collective-permute-done.4.late_ref, ...), custom_call_target="tpu_custom_call" | custom-call | flops 905969664 | bytes 4194304 | tf_op jit(solution)/shard_map/pallas_call | solution.py:433
  79.3 5.0 %all-to-all-done.1.parts_ref = bf16[32,64,128]{2,1,0:T(8,128)(2,1)S(1)} async-done(((bf16[32,64,128]{2,1,0:T(8,128)(2,1)}), bf16[32,64,128]{2,1,0:T(8,128)(2,1)S(1)}, u32[]{:S(2)}, u32[]{:S(2)}) %all-to-all-start.1) | async-done | bytes 524320 | tf_op jit(solution)/shard_map/all_to_all | solution.py:431
  84.3 0.1 shard_map.61
  84.4 18.2 %all_to_all.21.got_ref = bf16[8,288,128]{2,1,0:T(8,128)(2,1)S(1)} all-to-all(bf16[8,288,128]{2,1,0:T(8,128)(2,1)S(1)} %shard_map.61), channel_id=1, replica_groups=mesh['x'=4,'y'=8,'z'=8,'core'=2] {'y'}, dimensions={0} | all-to-all | bytes 1179648 | tf_op jit(solution)/shard_map/all_to_all | solution.py:446
  102.7 0.6 shard_map.63
  103.3 5.2 %all-to-all-start.3 = ((bf16[32,8,128]{2,1,0:T(8,128)(2,1)}), bf16[32,8,128]{2,1,0:T(8,128)(2,1)S(1)}, u32[]{:S(2)}, u32[]{:S(2)}) async-start(bf16[32,8,128]{2,1,0:T(8,128)(2,1)} %shard_map.63), calls=%async_computation.3 | async-start | bytes 131072 | tf_op jit(solution)/shard_map/all_to_all | solution.py:452
  108.6 0.8 shard_map.62
  109.4 8.0 %all-to-all-done.3 = bf16[32,8,128]{2,1,0:T(8,128)(2,1)S(1)} async-done(((bf16[32,8,128]{2,1,0:T(8,128)(2,1)}), bf16[32,8,128]{2,1,0:T(8,128)(2,1)S(1)}, u32[]{:S(2)}, u32[]{:S(2)}) %all-to-all-start.3) | async-done | bytes 65568 | tf_op jit(solution)/shard_map/all_to_all | solution.py:452
  117.4 23.7 %all_gather.3 = bf16[3456,128]{1,0:T(8,128)(2,1)S(1)} all-gather(bf16[216,128]{1,0:T(8,128)(2,1)S(1)} %slice_bitcast_fusion), channel_id=1, replica_groups=mesh['x'=4,'y'=8,'z'=8,'core'=2] {'z','core'}, dimensions={0}, use_global_device_ids=true | all-gather | bytes 940032 | tf_op jit(solution)/shard_map/all_gather | solution.py:454
  141.2 1.4 convert.1
  (15 shorter events, 0.1 us)
Async XLA Ops:
  0.6 44.9 %copy-start = (bf16[3,3,3,128,128]{4,3,2,1,0:T(8,128)(2,1)S(1)}, bf16[3,3,3,128,128]{4,3,2,1,0:T(8,128)(2,1)}, u32[]{:S(2)}) copy-start(bf16[3,3,3,128,128]{4,3,2,1,0:T(8,128)(2,1)} %param.4) | copy-start | bytes 2654212
  25.5 5.9 %collective-permute-start = (bf16[2,176,128]{2,1,0:T(8,128)(2,1)S(1)}, bf16[2,176,128]{2,1,0:T(8,128)(2,1)S(1)}, u32[]{:S(2)}, u32[]{:S(2)}) collective-permute-start(bf16[2,176,128]{2,1,0:T(8,128)(2,1)S(1)} %slice.60), channel_id=1, source_target_pairs={{0,128},{128,256},{256,384},{1,129},{129,257},{257,385},{2,130},{1... | collective-permute-start | bytes 270344 | tf_op jit(solution)/shard_map/ppermute | solution.py:371
  31.4 9.7 %collective-permute-start.1 = (bf16[10,64,128]{2,1,0:T(8,128)(2,1)S(1)}, bf16[10,64,128]{2,1,0:T(8,128)(2,1)S(1)}, u32[]{:S(2)}, u32[]{:S(2)}) collective-permute-start(bf16[10,64,128]{2,1,0:T(8,128)(2,1)S(1)} %pad_maximum_fusion), channel_id=1, source_target_pairs={{0,1},{1,2},{2,3},{3,4},{4,5},{5,6},{6,7},{7,8},{8,9},{9,10},{10,1... | collective-permute-start | bytes 491528 | tf_op jit(solution)/shard_map/ppermute | solution.py:371
  38.9 6.6 %collective-permute-start.2 = (bf16[10,64,128]{2,1,0:T(8,128)(2,1)S(1)}, bf16[10,64,128]{2,1,0:T(8,128)(2,1)S(1)}, u32[]{:S(2)}, u32[]{:S(2)}) collective-permute-start(bf16[10,64,128]{2,1,0:T(8,128)(2,1)S(1)} %maximum_maximum_fusion), channel_id=1, source_target_pairs={{1,0},{2,1},{3,2},{4,3},{5,4},{6,5},{7,6},{8,7},{9,8},{10,9},{11,1... | collective-permute-start | bytes 491528 | tf_op jit(solution)/shard_map/ppermute | solution.py:371
  51.6 3.8 %collective-permute-start.3 = (bf16[32,64,128]{2,1,0:T(8,128)(2,1)S(1)}, bf16[32,64,128]{2,1,0:T(8,128)(2,1)S(1)}, u32[]{:S(2)}, u32[]{:S(2)}) collective-permute-start(bf16[32,64,128]{2,1,0:T(8,128)(2,1)S(1)} %get-tuple-element.12), channel_id=1, source_target_pairs={{0,1},{1,0},{2,3},{3,2},{4,5},{5,4},{6,7},{7,6},{8,9},{9,8},{10,11... | collective-permute-start | bytes 1572872 | tf_op jit(solution)/shard_map/ppermute | solution.py:375
  56.4 28.0 %all-to-all-start.1 = ((bf16[32,64,128]{2,1,0:T(8,128)(2,1)}), bf16[32,64,128]{2,1,0:T(8,128)(2,1)S(1)}, u32[]{:S(2)}, u32[]{:S(2)}) async-start(bf16[32,64,128]{2,1,0:T(8,128)(2,1)} %add_convert_fusion), calls=%async_computation.1 | async-start | bytes 1048576 | tf_op jit(solution)/shard_map/all_to_all | solution.py:431
  69.6 7.0 %collective-permute-start.4 = (bf16[2,160,128]{2,1,0:T(8,128)(2,1)S(1)}, bf16[2,160,128]{2,1,0:T(8,128)(2,1)S(1)}, u32[]{:S(2)}, u32[]{:S(2)}) collective-permute-start(bf16[2,160,128]{2,1,0:T(8,128)(2,1)S(1)} %pad_maximum_fusion.1), channel_id=1, source_target_pairs={{128,0},{256,128},{384,256},{129,1},{257,129},{385,257},{130,2},{2... | collective-permute-start | bytes 245768 | tf_op jit(solution)/shard_map/ppermute | solution.py:371
  103.3 14.1 %all-to-all-start.3 = ((bf16[32,8,128]{2,1,0:T(8,128)(2,1)}), bf16[32,8,128]{2,1,0:T(8,128)(2,1)S(1)}, u32[]{:S(2)}, u32[]{:S(2)}) async-start(bf16[32,8,128]{2,1,0:T(8,128)(2,1)} %shard_map.63), calls=%async_computation.3 | async-start | bytes 131072 | tf_op jit(solution)/shard_map/all_to_all | solution.py:452

commit v7 on v6

--- a/solution.py
+++ b/solution.py
@@ -44,34 +44,35 @@
     )
 
 
-def pack_body(x_hbm, cot_hbm, out_ref, x_ref, cot_ref, left_ref, right_ref, sems):
-    x_copy = pltpu.make_async_copy(x_hbm, x_ref, sems.at[0])
-    cot_copy = pltpu.make_async_copy(cot_hbm, cot_ref, sems.at[1])
-    x_copy.start()
-    cot_copy.start()
+def pack_body(x_hbm, cot_hbm, out_ref, left_ref, right_ref, sems):
+    copies = [
+        pltpu.make_async_copy(
+            hbm.at[row], out_ref.at[:, pl.ds(place(row), STRIP), :], sems.at[side, row]
+        )
+        for side, (hbm, place) in enumerate(((x_hbm, x_place), (cot_hbm, cot_place)))
+        for row in range(ROWS)
+    ]
+    for copy in copies:
+        copy.start()
     left_ref[...] = jnp.zeros_like(left_ref)
     right_ref[...] = jnp.zeros_like(right_ref)
-    x_copy.wait()
     for row in range(ROWS):
-        line = x_ref[row]
-        wide = line.astype(f32)
+        copies[row].wait()
         for strip in range(GROUP):
-            low = strip * STRIP
-            out_ref[strip, pl.ds(row * STRIP, STRIP), :] = line[low : low + STRIP]
+            wide = out_ref[strip, pl.ds(x_place(row), STRIP), :].astype(f32)
+            if strip < GROUP - 1:
+                left_ref[strip + 1, pl.ds(row, 1), :] = wide[STRIP - 1 : STRIP]
             if strip > 0:
-                left_ref[strip, pl.ds(row, 1), :] = wide[low - 1 : low]
-            if strip < GROUP - 1:
-                right_ref[strip, pl.ds(row, 1), :] = wide[low + STRIP : low + STRIP + 1]
+                right_ref[strip - 1, pl.ds(row, 1), :] = wide[0:1]
     for strip in range(GROUP):
         pair = jnp.concatenate([left_ref[strip], right_ref[strip]], axis=0)
         out_ref[strip, pl.ds(TILE, EDGES), :] = pair.astype(bf16)
-    cot_copy.wait()
-    for row in range(ROWS):
-        line = cot_ref[row]
-        for strip in range(GROUP):
-            out_ref[strip, pl.ds(cot_place(row), STRIP), :] = line[
-                strip * STRIP : (strip + 1) * STRIP
-            ]
+    for copy in copies[ROWS:]:
+        copy.wait()
+
+
+def x_place(row):
+    return row * STRIP
 
 
 def cot_place(row):
@@ -226,12 +227,13 @@
         turned = g_ref[frame].astype(f32).T.astype(bf16)
         for tap in range(3):
             gt_ref[pl.ds(tap * CH, CH), pl.ds((frame + tap) * TILE, TILE)] = turned
-    terms_ref[...] = jnp.zeros_like(terms_ref)
     _, peers, ring, share = terms_ref.shape[:4]
     blocks = 27 * CH // PART
     slots = share // PART
     deep = peers // CHIPS[0]
     lines = 2 * deep
+    unused = terms_ref.at[:, peers - deep :]
+    unused[...] = jnp.zeros_like(unused)
     for low in range(0, 9, 2):
         high = min(low + 2, 9)
         product = jnp.dot(
@@ -320,27 +322,23 @@
 
 
 def load_body(parts_ref, sent_ref, code_ref, out_ref):
-    ring, share = GROUP, parts_ref.shape[1] // GROUP
     part = parts_ref[0].astype(f32)
     for peer in range(1, parts_ref.shape[0]):
         part = part + parts_ref[peer].astype(f32)
-    empty = jnp.zeros((-share % STRIP, CH), f32)
-    for place in range(ring):
-        piece = part[place * share : (place + 1) * share]
-        if empty.shape[0]:
-            piece = jnp.concatenate([piece, empty], axis=0)
-        out_ref[place, 0 : piece.shape[0], :] = piece.astype(bf16)
-        low = piece.shape[0]
+    part = part.astype(bf16)
+    low = part.shape[0]
+    for place in range(GROUP):
+        out_ref[place, 0:low, :] = part
         out_ref[place, low : low + TILE, :] = code_ref[place]
         out_ref[place, low + TILE : low + TILE + SENT, :] = sent_ref[place]
 
 
 def share_body(got_ref, out_ref, norm):
-    share = out_ref.shape[1]
-    total = got_ref[0].astype(f32)
+    rows = out_ref.shape[1]
+    total = got_ref[0, 0:rows, :].astype(f32)
     for strip in range(1, GROUP):
-        total = total + got_ref[strip].astype(f32)
-    copies = (total[:share] * norm).astype(bf16)
+        total = total + got_ref[strip, 0:rows, :].astype(f32)
+    copies = (total * norm).astype(bf16)
     for owner in range(out_ref.shape[0]):
         out_ref[owner] = copies
 
@@ -379,15 +377,13 @@
     weights = kernel.reshape(3, WIDE, CH)
     turned = jnp.swapaxes(kernel[::-1, ::-1, ::-1], 3, 4).reshape(3, WIDE, CH)
     lines = ("z", "core")
-    whole_vmem = pltpu.VMEM((ROWS, GROUP * STRIP, CH), bf16)
     packed = pl.pallas_call(
         pack_body,
         out_shape=jax.ShapeDtypeStruct((GROUP, LOAD, CH), bf16),
         in_specs=[pl.BlockSpec(memory_space=pl.ANY)] * 2,
-        scratch_shapes=[whole_vmem] * 2
-        + [pltpu.VMEM((GROUP, ROWS, CH), f32)] * 2
-        + [pltpu.SemaphoreType.DMA((2,))],
-    )(frames[0], cotangent[0])
+        scratch_shapes=[pltpu.VMEM((GROUP, ROWS, CH), f32)] * 2
+        + [pltpu.SemaphoreType.DMA((2, ROWS))],
+    )(frames.reshape(ROWS, GROUP, STRIP, CH), cotangent.reshape(ROWS, GROUP, STRIP, CH))
     held = lax.all_to_all(packed, "y", 0, 0)
     early = shifted(held[GROUP - 2 :, : HELD + 2 * STRIP], "x", 1)
 
@@ -402,7 +398,7 @@
     down = shifted(edge_rows((0, RIM), (TILE, HELD), (HELD + STRIP, HELD + 2 * STRIP)), lines, -1)
 
     devices = lax.axis_size(("x", "y", "z", "core"))
-    peers, owners = lax.axis_size(("x", "z")), lax.axis_size(("x", "y"))
+    peers, wide = lax.axis_size(("x", "z")), lax.axis_size("x")
     share = PART * -(-27 * CH // (PART * devices))
     mail = jax.ShapeDtypeStruct((peers, GROUP * share, CH), bf16)
     flops = 2 * GROUP * TILE * 27 * CH * CH
@@ -439,7 +435,7 @@
         ],
         flops=flops,
     )(g, g_up, g_down, late, turned)
-    head = STRIP * -(-share // STRIP)
+    head = GROUP * share
     load = kernel_call(
         load_body, jax.ShapeDtypeStruct((GROUP, head + TILE + SENT, CH), bf16)
     )(parts, sent, code)
@@ -447,9 +443,9 @@
     norm = 1.0 / math.sqrt(devices * GROUP * TILE)
     copies = kernel_call(
         functools.partial(share_body, norm=norm),
-        jax.ShapeDtypeStruct((owners, share, CH), bf16),
-    )(got[:, :head])
-    line = lax.all_to_all(copies, ("x", "y"), 0, 0).reshape(-1, CH)
+        jax.ShapeDtypeStruct((wide, head, CH), bf16),
+    )(got)
+    line = lax.all_to_all(copies, "x", 0, 0).reshape(-1, CH)
     line = line[: 27 * CH // lax.axis_size(lines)]
     grad_kernel = lax.all_gather(line, lines, tiled=True).astype(f32)
 

time: 143 us -> 141 us (0.986)
  waiting for transfers between devices: 25.4 us -> 21 us
  blocking collectives: 64.9 us -> 68.2 us
  starting transfers between devices: 35.3 us -> 33.7 us
    all_to_all x1, waiting for transfers between devices: 8.05 us -> 3.65 us  [shards(): line = lax.all_to_all(copies, 'x', 0, 0).reshape(-1, CH)]
    all_to_all x1, blocking collectives: 18.2 us -> 20 us  [shards(): got = lax.all_to_all(load, 'y', 0, 0)]
    all_to_all x1, starting transfers between devices: 5.24 us -> 3.7 us  [shards(): line = lax.all_to_all(copies, 'x', 0, 0).reshape(-1, CH)]
    all_gather x1, blocking collectives: 23.7 us -> 25.2 us  [shards(): grad_kernel = lax.all_gather(line, lines, tiled=True).astype(f32)]
where the time goes in v7:
time: 141 us; the launch traced here: 140 us
  blocking collectives  68.2 us (48%)
  starting transfers between devices  33.7 us (24%)
  waiting for transfers between devices  21 us (15%)
  Pallas kernels  12.3 us (9%)
  other arithmetic  2.44 us (2%)
  local copies, waits for them, and re-layouts  1.5 us (1%)
    all_gather x1, blocking collectives, shards(): grad_kernel = lax.all_gather(line, lines, tiled=True).astype(f32)  25.2 us
    all_to_all x1, blocking collectives, shards(): held = lax.all_to_all(packed, 'y', 0, 0)  22.9 us
    all_to_all x1, blocking collectives, shards(): got = lax.all_to_all(load, 'y', 0, 0)  20 us
    ppermute x4, starting transfers between devices, shifted(): return lax.ppermute(value, axes, route)  14.9 us
    all_to_all x1, starting transfers between devices, shards(): parts = lax.all_to_all(chip_sum, ('x', 'z'), 0, 0)  13.2 us
    ppermute x4, waiting for transfers between devices, shifted(): return lax.ppermute(value, axes, route)  10.5 us
    pallas_call x1, Pallas kernels, shards(): kernel_call(forward_body, (jax.ShapeDtypeStruct((GROUP, TILE, CH), bf16),...  6.04 us
    all_to_all x1, waiting for transfers between devices, shards(): parts = lax.all_to_all(chip_sum, ('x', 'z'), 0, 0)  5.04 us
  transfers between devices with their start and end apart: 7, of which 7 were waited for; matrix products, arithmetic and copies ran while one was open for 1% of the time, Pallas kernels for 2%

profile of v7, /device:TPU:1, one launch (start us, length us, event | category | flops | bytes accessed | tf_op | source)
XLA Modules:
  0.0 140.0 jit_solution(5976938434320859953)
XLA Ops:
  0.6 0.0 copy-start
  0.6 2.0 %shard_map.58 = bf16[8,272,128]{2,1,0:T(8,128)(2,1)} custom-call(bf16[8,8,16,128]{3,2,1,0:T(8,128)(2,1)} %bitcast.15, bf16[8,8,16,128]{3,2,1,0:T(8,128)(2,1)} %bitcast.16), custom_call_target="tpu_custom_call" | custom-call | tf_op jit(solution)/shard_map/pallas_call | solution.py:380
  2.7 22.9 %all_to_all.20.held_ref = bf16[8,272,128]{2,1,0:T(8,128)(2,1)S(1)} all-to-all(bf16[8,272,128]{2,1,0:T(8,128)(2,1)} %shard_map.58), channel_id=1, replica_groups=mesh['x'=4,'y'=8,'z'=8,'core'=2] {'y'}, dimensions={0} | all-to-all | bytes 1114112 | tf_op jit(solution)/shard_map/all_to_all | solution.py:387
  25.6 4.3 %collective-permute-start = (bf16[2,176,128]{2,1,0:T(8,128)(2,1)S(1)}, bf16[2,176,128]{2,1,0:T(8,128)(2,1)S(1)}, u32[]{:S(2)}, u32[]{:S(2)}) collective-permute-start(bf16[2,176,128]{2,1,0:T(8,128)(2,1)S(1)} %slice.52), channel_id=1, source_target_pairs={{0,128},{128,256},{256,384},{1,129},{129,257},{257,385},{2,130},{1... | collective-permute-start | bytes 270344 | tf_op jit(solution)/shard_map/ppermute | solution.py:369
  30.0 1.5 %collective-permute-done.early_ref = bf16[2,176,128]{2,1,0:T(8,128)(2,1)S(1)} collective-permute-done((bf16[2,176,128]{2,1,0:T(8,128)(2,1)S(1)}, bf16[2,176,128]{2,1,0:T(8,128)(2,1)S(1)}, u32[]{:S(2)}, u32[]{:S(2)}) %collective-permute-start) | collective-permute-done | bytes 90144 | tf_op jit(solution)/shard_map/ppermute | solution.py:369
  31.5 7.4 %collective-permute-start.1 = (bf16[10,64,128]{2,1,0:T(8,128)(2,1)S(1)}, bf16[10,64,128]{2,1,0:T(8,128)(2,1)S(1)}, u32[]{:S(2)}, u32[]{:S(2)}) collective-permute-start(bf16[10,64,128]{2,1,0:T(8,128)(2,1)S(1)} %pad_maximum_fusion), channel_id=1, source_target_pairs={{0,1},{1,2},{2,3},{3,4},{4,5},{5,6},{6,7},{7,8},{8,9},{9,10},{10,1... | collective-permute-start | bytes 491528 | tf_op jit(solution)/shard_map/ppermute | solution.py:369
  39.0 1.9 %collective-permute-start.2 = (bf16[10,64,128]{2,1,0:T(8,128)(2,1)S(1)}, bf16[10,64,128]{2,1,0:T(8,128)(2,1)S(1)}, u32[]{:S(2)}, u32[]{:S(2)}) collective-permute-start(bf16[10,64,128]{2,1,0:T(8,128)(2,1)S(1)} %maximum_maximum_fusion), channel_id=1, source_target_pairs={{1,0},{2,1},{3,2},{4,3},{5,4},{6,5},{7,6},{8,7},{9,8},{10,9},{11,1... | collective-permute-start | bytes 491528 | tf_op jit(solution)/shard_map/ppermute | solution.py:369
  40.9 0.3 collective-permute-done.1.up_ref
  41.2 4.4 %collective-permute-done.2.down_ref = bf16[10,64,128]{2,1,0:T(8,128)(2,1)S(1)} collective-permute-done((bf16[10,64,128]{2,1,0:T(8,128)(2,1)S(1)}, bf16[10,64,128]{2,1,0:T(8,128)(2,1)S(1)}, u32[]{:S(2)}, u32[]{:S(2)}) %collective-permute-start.2) | collective-permute-done | bytes 163872 | tf_op jit(solution)/shard_map/ppermute | solution.py:369
  45.6 0.0 copy-done
  45.6 6.0 %shard_map.59 = (bf16[8,128,128]{2,1,0:T(8,128)(2,1)S(1)}, bf16[8,128,128]{2,1,0:T(8,128)(2,1)S(1)}, bf16[8,16,128]{2,1,0:T(8,128)(2,1)S(1)}, bf16[8,16,128]{2,1...) custom-call(s32[1]{0:T(128)} %bitcast.core_ref, ...), custom_call_target="tpu_custom_call" | custom-call | flops 1811939328 | bytes 4194304 | tf_op jit(solution)/shard_map/pallas_call | solution.py:405
  51.7 1.9 %collective-permute-start.3 = (bf16[32,64,128]{2,1,0:T(8,128)(2,1)S(1)}, bf16[32,64,128]{2,1,0:T(8,128)(2,1)S(1)}, u32[]{:S(2)}, u32[]{:S(2)}) collective-permute-start(bf16[32,64,128]{2,1,0:T(8,128)(2,1)S(1)} %get-tuple-element.12), channel_id=1, source_target_pairs={{0,1},{1,0},{2,3},{3,2},{4,5},{5,4},{6,7},{7,6},{8,9},{9,8},{10,11... | collective-permute-start | bytes 1572872 | tf_op jit(solution)/shard_map/ppermute | solution.py:373
  53.6 1.9 %collective-permute-done.3 = bf16[32,64,128]{2,1,0:T(8,128)(2,1)S(1)} collective-permute-done((bf16[32,64,128]{2,1,0:T(8,128)(2,1)S(1)}, bf16[32,64,128]{2,1,0:T(8,128)(2,1)S(1)}, u32[]{:S(2)}, u32[]{:S(2)}) %collective-permute-start.3) | collective-permute-done | bytes 524320 | tf_op jit(solution)/shard_map/ppermute | solution.py:373
  55.5 1.0 add_convert_fusion
  56.4 13.2 %all-to-all-start.1 = ((bf16[32,64,128]{2,1,0:T(8,128)(2,1)}), bf16[32,64,128]{2,1,0:T(8,128)(2,1)S(1)}, u32[]{:S(2)}, u32[]{:S(2)}) async-start(bf16[32,64,128]{2,1,0:T(8,128)(2,1)} %add_convert_fusion), calls=%async_computation.1 | async-start | bytes 1048576 | tf_op jit(solution)/shard_map/all_to_all | solution.py:427
  69.7 1.3 collective-permute-start.4
  71.0 0.1 reverse_bitcast_fusion
  71.0 1.4 copy.6
  72.4 4.3 %collective-permute-done.4.late_ref = bf16[2,160,128]{2,1,0:T(8,128)(2,1)S(1)} collective-permute-done((bf16[2,160,128]{2,1,0:T(8,128)(2,1)S(1)}, bf16[2,160,128]{2,1,0:T(8,128)(2,1)S(1)}, u32[]{:S(2)}, u32[]{:S(2)}) %collective-permute-start.4) | collective-permute-done | bytes 81952 | tf_op jit(solution)/shard_map/ppermute | solution.py:369
  76.7 2.7 %shard_map.60.sent_ref = bf16[8,144,128]{2,1,0:T(8,128)(2,1)S(1)} custom-call(bf16[8,128,128]{2,1,0:T(8,128)(2,1)S(1)} %get-tuple-element.13.g_ref, bf16[8,16,128]{2,1,0:T(8,128)(2,1)S(1)} %get-tuple-element.14.up_ref, bf16[8,16,128]{2,1,0:T(8,128)(2,1)S(1)} %get-tuple-element.15.down_ref, bf16[2,160,128]{2,1,0:T(8,128)(2,1)S(1)} %collective-permute-done.4.late_ref, ...), custom_call_target="tpu_custom_call" | custom-call | flops 905969664 | bytes 4194304 | tf_op jit(solution)/shard_map/pallas_call | solution.py:429
  79.4 5.0 %all-to-all-done.1.parts_ref = bf16[32,64,128]{2,1,0:T(8,128)(2,1)S(1)} async-done(((bf16[32,64,128]{2,1,0:T(8,128)(2,1)}), bf16[32,64,128]{2,1,0:T(8,128)(2,1)S(1)}, u32[]{:S(2)}, u32[]{:S(2)}) %all-to-all-start.1) | async-done | bytes 524320 | tf_op jit(solution)/shard_map/all_to_all | solution.py:427
  84.4 0.1 shard_map.61
  84.5 20.0 %all_to_all.21.got_ref = bf16[8,336,128]{2,1,0:T(8,128)(2,1)S(1)} all-to-all(bf16[8,336,128]{2,1,0:T(8,128)(2,1)S(1)} %shard_map.61), channel_id=1, replica_groups=mesh['x'=4,'y'=8,'z'=8,'core'=2] {'y'}, dimensions={0} | all-to-all | bytes 1376256 | tf_op jit(solution)/shard_map/all_to_all | solution.py:442
  104.5 0.7 shard_map.63
  105.2 3.7 %all-to-all-start.3 = ((bf16[4,64,128]{2,1,0:T(8,128)(2,1)}), bf16[4,64,128]{2,1,0:T(8,128)(2,1)S(1)}, u32[]{:S(2)}, u32[]{:S(2)}) async-start(bf16[4,64,128]{2,1,0:T(8,128)(2,1)} %shard_map.63), calls=%async_computation.3 | async-start | bytes 131072 | tf_op jit(solution)/shard_map/all_to_all | solution.py:448
  108.9 0.8 shard_map.62
  109.7 3.7 %all-to-all-done.3 = bf16[4,64,128]{2,1,0:T(8,128)(2,1)S(1)} async-done(((bf16[4,64,128]{2,1,0:T(8,128)(2,1)}), bf16[4,64,128]{2,1,0:T(8,128)(2,1)S(1)}, u32[]{:S(2)}, u32[]{:S(2)}) %all-to-all-start.3) | async-done | bytes 65568 | tf_op jit(solution)/shard_map/all_to_all | solution.py:448
  113.4 25.2 %all_gather.3 = bf16[3456,128]{1,0:T(8,128)(2,1)S(1)} all-gather(bf16[216,128]{1,0:T(8,128)(2,1)S(1)} %slice.61), channel_id=1, replica_groups=mesh['x'=4,'y'=8,'z'=8,'core'=2] {'z','core'}, dimensions={0}, use_global_device_ids=true | all-gather | bytes 940032 | tf_op jit(solution)/shard_map/all_gather | solution.py:450
  138.6 1.4 %convert.1 = f32[3,3,3,128,128]{4,3,2,1,0:T(8,128)} convert(bf16[3,3,3,128,128]{4,3,2,1,0:T(8,128)(2,1)S(1)} %bitcast.14) | non-fusion elementwise | flops 442368 | bytes 2654208 | tf_op jit(solution)/shard_map/reshape | solution.py:454
  (14 shorter events, 0.1 us)
Async XLA Ops:
  0.6 45.0 %copy-start = (bf16[3,3,3,128,128]{4,3,2,1,0:T(8,128)(2,1)S(1)}, bf16[3,3,3,128,128]{4,3,2,1,0:T(8,128)(2,1)}, u32[]{:S(2)}) copy-start(bf16[3,3,3,128,128]{4,3,2,1,0:T(8,128)(2,1)} %param.4) | copy-start | bytes 2654212
  25.6 5.9 %collective-permute-start = (bf16[2,176,128]{2,1,0:T(8,128)(2,1)S(1)}, bf16[2,176,128]{2,1,0:T(8,128)(2,1)S(1)}, u32[]{:S(2)}, u32[]{:S(2)}) collective-permute-start(bf16[2,176,128]{2,1,0:T(8,128)(2,1)S(1)} %slice.52), channel_id=1, source_target_pairs={{0,128},{128,256},{256,384},{1,129},{129,257},{257,385},{2,130},{1... | collective-permute-start | bytes 270344 | tf_op jit(solution)/shard_map/ppermute | solution.py:369
  31.5 9.7 %collective-permute-start.1 = (bf16[10,64,128]{2,1,0:T(8,128)(2,1)S(1)}, bf16[10,64,128]{2,1,0:T(8,128)(2,1)S(1)}, u32[]{:S(2)}, u32[]{:S(2)}) collective-permute-start(bf16[10,64,128]{2,1,0:T(8,128)(2,1)S(1)} %pad_maximum_fusion), channel_id=1, source_target_pairs={{0,1},{1,2},{2,3},{3,4},{4,5},{5,6},{6,7},{7,8},{8,9},{9,10},{10,1... | collective-permute-start | bytes 491528 | tf_op jit(solution)/shard_map/ppermute | solution.py:369
  39.0 6.6 %collective-permute-start.2 = (bf16[10,64,128]{2,1,0:T(8,128)(2,1)S(1)}, bf16[10,64,128]{2,1,0:T(8,128)(2,1)S(1)}, u32[]{:S(2)}, u32[]{:S(2)}) collective-permute-start(bf16[10,64,128]{2,1,0:T(8,128)(2,1)S(1)} %maximum_maximum_fusion), channel_id=1, source_target_pairs={{1,0},{2,1},{3,2},{4,3},{5,4},{6,5},{7,6},{8,7},{9,8},{10,9},{11,1... | collective-permute-start | bytes 491528 | tf_op jit(solution)/shard_map/ppermute | solution.py:369
  51.7 3.8 %collective-permute-start.3 = (bf16[32,64,128]{2,1,0:T(8,128)(2,1)S(1)}, bf16[32,64,128]{2,1,0:T(8,128)(2,1)S(1)}, u32[]{:S(2)}, u32[]{:S(2)}) collective-permute-start(bf16[32,64,128]{2,1,0:T(8,128)(2,1)S(1)} %get-tuple-element.12), channel_id=1, source_target_pairs={{0,1},{1,0},{2,3},{3,2},{4,5},{5,4},{6,7},{7,6},{8,9},{9,8},{10,11... | collective-permute-start | bytes 1572872 | tf_op jit(solution)/shard_map/ppermute | solution.py:373
  56.4 28.0 %all-to-all-start.1 = ((bf16[32,64,128]{2,1,0:T(8,128)(2,1)}), bf16[32,64,128]{2,1,0:T(8,128)(2,1)S(1)}, u32[]{:S(2)}, u32[]{:S(2)}) async-start(bf16[32,64,128]{2,1,0:T(8,128)(2,1)} %add_convert_fusion), calls=%async_computation.1 | async-start | bytes 1048576 | tf_op jit(solution)/shard_map/all_to_all | solution.py:427
  69.7 7.0 %collective-permute-start.4 = (bf16[2,160,128]{2,1,0:T(8,128)(2,1)S(1)}, bf16[2,160,128]{2,1,0:T(8,128)(2,1)S(1)}, u32[]{:S(2)}, u32[]{:S(2)}) collective-permute-start(bf16[2,160,128]{2,1,0:T(8,128)(2,1)S(1)} %pad_maximum_fusion.1), channel_id=1, source_target_pairs={{128,0},{256,128},{384,256},{129,1},{257,129},{385,257},{130,2},{2... | collective-permute-start | bytes 245768 | tf_op jit(solution)/shard_map/ppermute | solution.py:369
  105.2 8.2 %all-to-all-start.3 = ((bf16[4,64,128]{2,1,0:T(8,128)(2,1)}), bf16[4,64,128]{2,1,0:T(8,128)(2,1)S(1)}, u32[]{:S(2)}, u32[]{:S(2)}) async-start(bf16[4,64,128]{2,1,0:T(8,128)(2,1)} %shard_map.63), calls=%async_computation.3 | async-start | bytes 131072 | tf_op jit(solution)/shard_map/all_to_all | solution.py:448

commit v8 on v7

--- a/solution.py
+++ b/solution.py
@@ -22,7 +22,7 @@
 EDGES = 2 * ROWS
 HELD = TILE + EDGES
 LOAD = HELD + TILE
-SENT = TILE + EDGES
+SENT = 2 * TILE + EDGES
 RIM = 2 * STRIP
 PART = 8
 
@@ -265,7 +265,7 @@
                 send_ref[peer] = terms_ref[1 - core, peer].reshape(-1, CH).astype(bf16)
 
 
-def backward_body(g_ref, up_ref, down_ref, late_ref, w_ref, out_ref, col_ref, side_ref):
+def backward_body(g_ref, up_ref, down_ref, late_ref, code_ref, w_ref, out_ref, col_ref, side_ref):
     nothing = jnp.zeros((1, CH), f32)
 
     def spread(lines, place):
@@ -293,7 +293,8 @@
         + jnp.dot(col_ref[2 * TILE : (GROUP + 2) * TILE, :], w_ref[2], preferred_element_type=f32)
     )
     for frame in range(GROUP):
-        out_ref[frame, 0:TILE, :] = total[frame * TILE : (frame + 1) * TILE].astype(bf16)
+        out_ref[frame, 0:TILE, :] = code_ref[frame]
+        out_ref[frame, TILE : 2 * TILE, :] = total[frame * TILE : (frame + 1) * TILE].astype(bf16)
     for side, (offset, col_tap) in enumerate(((0, 2), (STRIP - 1, 0))):
         for frame in range(FRAMES):
             for row in range(ROWS):
@@ -318,44 +319,38 @@
             first = summed
     for frame in range(GROUP):
         pair = [value[frame * ROWS : (frame + 1) * ROWS] for value in (first, summed)]
-        out_ref[frame, TILE:SENT, :] = jnp.concatenate(pair, axis=0).astype(bf16)
-
-
-def load_body(parts_ref, sent_ref, code_ref, out_ref):
+        out_ref[frame, 2 * TILE : SENT, :] = jnp.concatenate(pair, axis=0).astype(bf16)
+
+
+def part_body(parts_ref, out_ref):
     part = parts_ref[0].astype(f32)
     for peer in range(1, parts_ref.shape[0]):
         part = part + parts_ref[peer].astype(f32)
     part = part.astype(bf16)
-    low = part.shape[0]
-    for place in range(GROUP):
-        out_ref[place, 0:low, :] = part
-        out_ref[place, low : low + TILE, :] = code_ref[place]
-        out_ref[place, low + TILE : low + TILE + SENT, :] = sent_ref[place]
+    for place in range(out_ref.shape[0]):
+        out_ref[place] = part
 
 
 def share_body(got_ref, out_ref, norm):
-    rows = out_ref.shape[1]
-    total = got_ref[0, 0:rows, :].astype(f32)
-    for strip in range(1, GROUP):
-        total = total + got_ref[strip, 0:rows, :].astype(f32)
+    total = got_ref[0].astype(f32)
+    for place in range(1, got_ref.shape[0]):
+        total = total + got_ref[place].astype(f32)
     copies = (total * norm).astype(bf16)
     for owner in range(out_ref.shape[0]):
         out_ref[owner] = copies
 
 
 def unpack_body(got_ref, code_ref, grad_ref):
-    head = got_ref.shape[1] - TILE - SENT
-    code_low, grad_low, edge_low = head, head + TILE, head + 2 * TILE
     at = lax.broadcasted_iota(jnp.int32, (STRIP, CH), 0)
     for strip in range(GROUP):
         columns = pl.ds(strip * STRIP, STRIP)
         if strip > 0:
-            before = got_ref[strip - 1, pl.ds(edge_low, EDGES), :].astype(f32)
+            before = got_ref[strip - 1, pl.ds(2 * TILE, EDGES), :].astype(f32)
         if strip < GROUP - 1:
-            after = got_ref[strip + 1, pl.ds(edge_low, EDGES), :].astype(f32)
+            after = got_ref[strip + 1, pl.ds(2 * TILE, EDGES), :].astype(f32)
         for row in range(ROWS):
-            code_ref[row, columns, :] = got_ref[strip, pl.ds(code_low + row * STRIP, STRIP), :]
-            value = got_ref[strip, pl.ds(grad_low + row * STRIP, STRIP), :].astype(f32)
+            code_ref[row, columns, :] = got_ref[strip, pl.ds(row * STRIP, STRIP), :]
+            value = got_ref[strip, pl.ds(TILE + row * STRIP, STRIP), :].astype(f32)
             if strip > 0:
                 value = value + jnp.where(at == 0, before[ROWS + row : ROWS + row + 1], 0.0)
             if strip < GROUP - 1:
@@ -434,21 +429,19 @@
             pltpu.VMEM((FRAMES * ROWS, 3 * CH), f32),
         ],
         flops=flops,
-    )(g, g_up, g_down, late, turned)
-    head = GROUP * share
-    load = kernel_call(
-        load_body, jax.ShapeDtypeStruct((GROUP, head + TILE + SENT, CH), bf16)
-    )(parts, sent, code)
-    got = lax.all_to_all(load, "y", 0, 0)
+    )(g, g_up, g_down, late, code, turned)
+    parts, sent = lax.optimization_barrier((parts, sent))
+    part = kernel_call(part_body, jax.ShapeDtypeStruct((GROUP, GROUP * share, CH), bf16))(parts)
     norm = 1.0 / math.sqrt(devices * GROUP * TILE)
     copies = kernel_call(
         functools.partial(share_body, norm=norm),
-        jax.ShapeDtypeStruct((wide, head, CH), bf16),
-    )(got)
+        jax.ShapeDtypeStruct((wide, GROUP * share, CH), bf16),
+    )(lax.all_to_all(part, "y", 0, 0))
     line = lax.all_to_all(copies, "x", 0, 0).reshape(-1, CH)
     line = line[: 27 * CH // lax.axis_size(lines)]
     grad_kernel = lax.all_gather(line, lines, tiled=True).astype(f32)
 
+    got = lax.all_to_all(sent, "y", 0, 0)
     whole = jax.ShapeDtypeStruct((ROWS, GROUP * STRIP, CH), bf16)
     code_out, grad_frames = kernel_call(unpack_body, (whole, whole))(got)
     return (code_out[None], grad_frames[None], grad_kernel.reshape(3, 3, 3, CH, CH))

time: 141 us -> 132 us (0.936)
  waiting for transfers between devices: 21 us -> 16.6 us
  blocking collectives: 68.2 us -> 64.5 us
    all_to_all x1, waiting for transfers between devices: 3.65 us -> 0.01 us  [shards(): got = lax.all_to_all(sent, 'y', 0, 0)]
    all_to_all x1 -> x2, blocking collectives: 20 us -> 18 us  [the longest x1 10.3 us: shards(): lax.all_to_all(part, 'y', 0, 0)]
    all_gather x1, blocking collectives: 25.2 us -> 23.6 us  [shards(): grad_kernel = lax.all_gather(line, lines, tiled=True).astype(f32)]
  transfers between devices with their start and end apart: 7 -> 7, of which waited for: 7 -> 6; matrix products, arithmetic and copies ran while one was open for 1% -> 2% of each run, Pallas kernels for 2% -> 3%
where the time goes in v8:
time: 132 us
  blocking collectives  64.5 us (49%)
  starting transfers between devices  33.6 us (25%)
  waiting for transfers between devices  16.6 us (13%)
  Pallas kernels  12.5 us (9%)
  other arithmetic  2.43 us (2%)
  local copies, waits for them, and re-layouts  1.51 us (1%)
    all_gather x1, blocking collectives, shards(): grad_kernel = lax.all_gather(line, lines, tiled=True).astype(f32)  23.6 us
    all_to_all x1, blocking collectives, shards(): held = lax.all_to_all(packed, 'y', 0, 0)  22.9 us
    ppermute x4, starting transfers between devices, shifted(): return lax.ppermute(value, axes, route)  14.9 us
    all_to_all x1, starting transfers between devices, shards(): parts = lax.all_to_all(chip_sum, ('x', 'z'), 0, 0)  13.2 us
    ppermute x4, waiting for transfers between devices, shifted(): return lax.ppermute(value, axes, route)  10.5 us
    all_to_all x1, blocking collectives, shards(): lax.all_to_all(part, 'y', 0, 0)  10.3 us
    all_to_all x1, blocking collectives, shards(): line = lax.all_to_all(copies, 'x', 0, 0).reshape(-1, CH)  7.66 us
    pallas_call x1, Pallas kernels, shards(): kernel_call(forward_body, (jax.ShapeDtypeStruct((GROUP, TILE, CH), bf16),...  6.04 us
  transfers between devices with their start and end apart: 7, of which 6 were waited for; matrix products, arithmetic and copies ran while one was open for 2% of the time, Pallas kernels for 3%

profile of v8, /device:TPU:1, one launch (start us, length us, event | category | flops | bytes accessed | tf_op | source)
XLA Modules:
  0.0 131.9 jit_solution(3358932348311561205)
XLA Ops:
  0.6 0.0 copy-start
  0.6 2.0 %shard_map.58 = bf16[8,272,128]{2,1,0:T(8,128)(2,1)} custom-call(bf16[8,8,16,128]{3,2,1,0:T(8,128)(2,1)} %bitcast.15, bf16[8,8,16,128]{3,2,1,0:T(8,128)(2,1)} %bitcast.16), custom_call_target="tpu_custom_call" | custom-call | tf_op jit(solution)/shard_map/pallas_call | solution.py:375
  2.7 22.9 %all_to_all.25.held_ref = bf16[8,272,128]{2,1,0:T(8,128)(2,1)S(1)} all-to-all(bf16[8,272,128]{2,1,0:T(8,128)(2,1)} %shard_map.58), channel_id=1, replica_groups=mesh['x'=4,'y'=8,'z'=8,'core'=2] {'y'}, dimensions={0} | all-to-all | bytes 1114112 | tf_op jit(solution)/shard_map/all_to_all | solution.py:382
  25.6 4.3 %collective-permute-start = (bf16[2,176,128]{2,1,0:T(8,128)(2,1)S(1)}, bf16[2,176,128]{2,1,0:T(8,128)(2,1)S(1)}, u32[]{:S(2)}, u32[]{:S(2)}) collective-permute-start(bf16[2,176,128]{2,1,0:T(8,128)(2,1)S(1)} %slice.52), channel_id=1, source_target_pairs={{0,128},{128,256},{256,384},{1,129},{129,257},{257,385},{2,130},{1... | collective-permute-start | bytes 270344 | tf_op jit(solution)/shard_map/ppermute | solution.py:364
  30.0 1.5 %collective-permute-done.early_ref = bf16[2,176,128]{2,1,0:T(8,128)(2,1)S(1)} collective-permute-done((bf16[2,176,128]{2,1,0:T(8,128)(2,1)S(1)}, bf16[2,176,128]{2,1,0:T(8,128)(2,1)S(1)}, u32[]{:S(2)}, u32[]{:S(2)}) %collective-permute-start) | collective-permute-done | bytes 90144 | tf_op jit(solution)/shard_map/ppermute | solution.py:364
  31.5 7.4 %collective-permute-start.1 = (bf16[10,64,128]{2,1,0:T(8,128)(2,1)S(1)}, bf16[10,64,128]{2,1,0:T(8,128)(2,1)S(1)}, u32[]{:S(2)}, u32[]{:S(2)}) collective-permute-start(bf16[10,64,128]{2,1,0:T(8,128)(2,1)S(1)} %pad_maximum_fusion), channel_id=1, source_target_pairs={{0,1},{1,2},{2,3},{3,4},{4,5},{5,6},{6,7},{7,8},{8,9},{9,10},{10,1... | collective-permute-start | bytes 491528 | tf_op jit(solution)/shard_map/ppermute | solution.py:364
  39.0 1.9 %collective-permute-start.2 = (bf16[10,64,128]{2,1,0:T(8,128)(2,1)S(1)}, bf16[10,64,128]{2,1,0:T(8,128)(2,1)S(1)}, u32[]{:S(2)}, u32[]{:S(2)}) collective-permute-start(bf16[10,64,128]{2,1,0:T(8,128)(2,1)S(1)} %maximum_maximum_fusion), channel_id=1, source_target_pairs={{1,0},{2,1},{3,2},{4,3},{5,4},{6,5},{7,6},{8,7},{9,8},{10,9},{11,1... | collective-permute-start | bytes 491528 | tf_op jit(solution)/shard_map/ppermute | solution.py:364
  40.9 0.3 collective-permute-done.1.up_ref
  41.2 4.4 %collective-permute-done.2.down_ref = bf16[10,64,128]{2,1,0:T(8,128)(2,1)S(1)} collective-permute-done((bf16[10,64,128]{2,1,0:T(8,128)(2,1)S(1)}, bf16[10,64,128]{2,1,0:T(8,128)(2,1)S(1)}, u32[]{:S(2)}, u32[]{:S(2)}) %collective-permute-start.2) | collective-permute-done | bytes 163872 | tf_op jit(solution)/shard_map/ppermute | solution.py:364
  45.6 0.0 copy-done
  45.6 6.0 %shard_map.59 = (bf16[8,128,128]{2,1,0:T(8,128)(2,1)S(1)}, bf16[8,128,128]{2,1,0:T(8,128)(2,1)S(1)}, bf16[8,16,128]{2,1,0:T(8,128)(2,1)S(1)}, bf16[8,16,128]{2,1...) custom-call(s32[1]{0:T(128)} %bitcast.core_ref, ...), custom_call_target="tpu_custom_call" | custom-call | flops 1811939328 | bytes 4194304 | tf_op jit(solution)/shard_map/pallas_call | solution.py:400
  51.7 1.9 %collective-permute-start.3 = (bf16[32,64,128]{2,1,0:T(8,128)(2,1)S(1)}, bf16[32,64,128]{2,1,0:T(8,128)(2,1)S(1)}, u32[]{:S(2)}, u32[]{:S(2)}) collective-permute-start(bf16[32,64,128]{2,1,0:T(8,128)(2,1)S(1)} %get-tuple-element.14), channel_id=1, source_target_pairs={{0,1},{1,0},{2,3},{3,2},{4,5},{5,4},{6,7},{7,6},{8,9},{9,8},{10,11... | collective-permute-start | bytes 1572872 | tf_op jit(solution)/shard_map/ppermute | solution.py:368
  53.6 1.9 %collective-permute-done.3 = bf16[32,64,128]{2,1,0:T(8,128)(2,1)S(1)} collective-permute-done((bf16[32,64,128]{2,1,0:T(8,128)(2,1)S(1)}, bf16[32,64,128]{2,1,0:T(8,128)(2,1)S(1)}, u32[]{:S(2)}, u32[]{:S(2)}) %collective-permute-start.3) | collective-permute-done | bytes 524320 | tf_op jit(solution)/shard_map/ppermute | solution.py:368
  55.5 1.0 add_convert_fusion
  56.4 13.2 %all-to-all-start.1 = ((bf16[32,64,128]{2,1,0:T(8,128)(2,1)}), bf16[32,64,128]{2,1,0:T(8,128)(2,1)S(1)}, u32[]{:S(2)}, u32[]{:S(2)}) async-start(bf16[32,64,128]{2,1,0:T(8,128)(2,1)} %add_convert_fusion), calls=%async_computation.1 | async-start | bytes 1048576 | tf_op jit(solution)/shard_map/all_to_all | solution.py:422
  69.7 1.3 collective-permute-start.4
  71.0 0.1 reverse_bitcast_fusion
  71.0 1.4 %copy.6 = bf16[3,3,3,128,128]{4,3,2,1,0:T(8,128)(2,1)S(1)} copy(bf16[3,3,3,128,128]{3,4,2,1,0:T(8,128)(2,1)S(1)} %reverse_bitcast_fusion) | data formatting | bytes 1769472 | tf_op jit(solution)/shard_map/transpose | solution.py:373
  72.4 4.3 %collective-permute-done.4.late_ref = bf16[2,160,128]{2,1,0:T(8,128)(2,1)S(1)} collective-permute-done((bf16[2,160,128]{2,1,0:T(8,128)(2,1)S(1)}, bf16[2,160,128]{2,1,0:T(8,128)(2,1)S(1)}, u32[]{:S(2)}, u32[]{:S(2)}) %collective-permute-start.4) | collective-permute-done | bytes 81952 | tf_op jit(solution)/shard_map/ppermute | solution.py:364
  76.7 3.5 %shard_map.60 = bf16[8,272,128]{2,1,0:T(8,128)(2,1)} custom-call(bf16[8,128,128]{2,1,0:T(8,128)(2,1)S(1)} %get-tuple-element.15.g_ref, bf16[8,16,128]{2,1,0:T(8,128)(2,1)S(1)} %get-tuple-element.16.up_ref, bf16[8,16,128]{2,1,0:T(8,128)(2,1)S(1)} %get-tuple-element.17.down_ref, bf16[2,160,128]{2,1,0:T(8,128)(2,1)S(1)} %collective-permute-done.4.late_ref, ...), custom_call_target="tpu_custom_call" | custom-call | flops 905969664 | bytes 4194304 | tf_op jit(solution)/shard_map/pallas_call | solution.py:424
  80.2 4.2 %all-to-all-done.1.parts_ref = bf16[32,64,128]{2,1,0:T(8,128)(2,1)S(1)} async-done(((bf16[32,64,128]{2,1,0:T(8,128)(2,1)}), bf16[32,64,128]{2,1,0:T(8,128)(2,1)S(1)}, u32[]{:S(2)}, u32[]{:S(2)}) %all-to-all-start.1) | async-done | bytes 524320 | tf_op jit(solution)/shard_map/all_to_all | solution.py:422
  84.4 0.1 shard_map.62
  84.5 10.3 %all_to_all.26.got_ref = bf16[8,64,128]{2,1,0:T(8,128)(2,1)S(1)} all-to-all(bf16[8,64,128]{2,1,0:T(8,128)(2,1)S(1)} %shard_map.62), channel_id=1, replica_groups=mesh['x'=4,'y'=8,'z'=8,'core'=2] {'y'}, dimensions={0} | all-to-all | bytes 262144 | tf_op jit(solution)/shard_map/all_to_all | solution.py:439
  94.8 7.7 %all_to_all.27 = bf16[4,64,128]{2,1,0:T(8,128)(2,1)S(1)} all-to-all(bf16[4,64,128]{2,1,0:T(8,128)(2,1)S(1)} %shard_map.63), channel_id=1, replica_groups=mesh['x'=4,'y'=8,'z'=8,'core'=2] {'x'}, dimensions={0} | all-to-all | bytes 131072 | tf_op jit(solution)/shard_map/all_to_all | solution.py:440
  102.5 3.5 %all-to-all-start.2 = ((bf16[8,272,128]{2,1,0:T(8,128)(2,1)}), bf16[8,272,128]{2,1,0:T(8,128)(2,1)S(1)}, u32[]{:S(2)}, u32[]{:S(2)}) async-start(bf16[8,272,128]{2,1,0:T(8,128)(2,1)} %shard_map.60), calls=%async_computation.2 | async-start | bytes 1114112 | tf_op jit(solution)/shard_map/all_to_all | solution.py:444
  106.0 23.6 %all_gather.3 = bf16[3456,128]{1,0:T(8,128)(2,1)S(1)} all-gather(bf16[216,128]{1,0:T(8,128)(2,1)S(1)} %slice.61), channel_id=1, replica_groups=mesh['x'=4,'y'=8,'z'=8,'core'=2] {'z','core'}, dimensions={0}, use_global_device_ids=true | all-gather | bytes 940032 | tf_op jit(solution)/shard_map/all_gather | solution.py:442
  129.7 1.4 %convert.1 = f32[3,3,3,128,128]{4,3,2,1,0:T(8,128)} convert(bf16[3,3,3,128,128]{4,3,2,1,0:T(8,128)(2,1)S(1)} %bitcast.14) | non-fusion elementwise | flops 442368 | bytes 2654208 | tf_op jit(solution)/shard_map/reshape | solution.py:447
  131.1 0.0 all-to-all-done.2.got_ref
  131.1 0.8 shard_map.61
  (15 shorter events, 0.1 us)
Async XLA Ops:
  0.6 45.0 %copy-start = (bf16[3,3,3,128,128]{4,3,2,1,0:T(8,128)(2,1)S(1)}, bf16[3,3,3,128,128]{4,3,2,1,0:T(8,128)(2,1)}, u32[]{:S(2)}) copy-start(bf16[3,3,3,128,128]{4,3,2,1,0:T(8,128)(2,1)} %param.4) | copy-start | bytes 2654212
  25.6 5.9 %collective-permute-start = (bf16[2,176,128]{2,1,0:T(8,128)(2,1)S(1)}, bf16[2,176,128]{2,1,0:T(8,128)(2,1)S(1)}, u32[]{:S(2)}, u32[]{:S(2)}) collective-permute-start(bf16[2,176,128]{2,1,0:T(8,128)(2,1)S(1)} %slice.52), channel_id=1, source_target_pairs={{0,128},{128,256},{256,384},{1,129},{129,257},{257,385},{2,130},{1... | collective-permute-start | bytes 270344 | tf_op jit(solution)/shard_map/ppermute | solution.py:364
  31.5 9.7 %collective-permute-start.1 = (bf16[10,64,128]{2,1,0:T(8,128)(2,1)S(1)}, bf16[10,64,128]{2,1,0:T(8,128)(2,1)S(1)}, u32[]{:S(2)}, u32[]{:S(2)}) collective-permute-start(bf16[10,64,128]{2,1,0:T(8,128)(2,1)S(1)} %pad_maximum_fusion), channel_id=1, source_target_pairs={{0,1},{1,2},{2,3},{3,4},{4,5},{5,6},{6,7},{7,8},{8,9},{9,10},{10,1... | collective-permute-start | bytes 491528 | tf_op jit(solution)/shard_map/ppermute | solution.py:364
  39.0 6.6 %collective-permute-start.2 = (bf16[10,64,128]{2,1,0:T(8,128)(2,1)S(1)}, bf16[10,64,128]{2,1,0:T(8,128)(2,1)S(1)}, u32[]{:S(2)}, u32[]{:S(2)}) collective-permute-start(bf16[10,64,128]{2,1,0:T(8,128)(2,1)S(1)} %maximum_maximum_fusion), channel_id=1, source_target_pairs={{1,0},{2,1},{3,2},{4,3},{5,4},{6,5},{7,6},{8,7},{9,8},{10,9},{11,1... | collective-permute-start | bytes 491528 | tf_op jit(solution)/shard_map/ppermute | solution.py:364
  51.7 3.8 %collective-permute-start.3 = (bf16[32,64,128]{2,1,0:T(8,128)(2,1)S(1)}, bf16[32,64,128]{2,1,0:T(8,128)(2,1)S(1)}, u32[]{:S(2)}, u32[]{:S(2)}) collective-permute-start(bf16[32,64,128]{2,1,0:T(8,128)(2,1)S(1)} %get-tuple-element.14), channel_id=1, source_target_pairs={{0,1},{1,0},{2,3},{3,2},{4,5},{5,4},{6,7},{7,6},{8,9},{9,8},{10,11... | collective-permute-start | bytes 1572872 | tf_op jit(solution)/shard_map/ppermute | solution.py:368
  56.4 28.0 %all-to-all-start.1 = ((bf16[32,64,128]{2,1,0:T(8,128)(2,1)}), bf16[32,64,128]{2,1,0:T(8,128)(2,1)S(1)}, u32[]{:S(2)}, u32[]{:S(2)}) async-start(bf16[32,64,128]{2,1,0:T(8,128)(2,1)} %add_convert_fusion), calls=%async_computation.1 | async-start | bytes 1048576 | tf_op jit(solution)/shard_map/all_to_all | solution.py:422
  69.7 7.0 %collective-permute-start.4 = (bf16[2,160,128]{2,1,0:T(8,128)(2,1)S(1)}, bf16[2,160,128]{2,1,0:T(8,128)(2,1)S(1)}, u32[]{:S(2)}, u32[]{:S(2)}) collective-permute-start(bf16[2,160,128]{2,1,0:T(8,128)(2,1)S(1)} %pad_maximum_fusion.1), channel_id=1, source_target_pairs={{128,0},{256,128},{384,256},{129,1},{257,129},{385,257},{130,2},{2... | collective-permute-start | bytes 245768 | tf_op jit(solution)/shard_map/ppermute | solution.py:364
  102.5 28.6 %all-to-all-start.2 = ((bf16[8,272,128]{2,1,0:T(8,128)(2,1)}), bf16[8,272,128]{2,1,0:T(8,128)(2,1)S(1)}, u32[]{:S(2)}, u32[]{:S(2)}) async-start(bf16[8,272,128]{2,1,0:T(8,128)(2,1)} %shard_map.60), calls=%async_computation.2 | async-start | bytes 1114112 | tf_op jit(solution)/shard_map/all_to_all | solution.py:444

commit v9 on v8

--- a/solution.py
+++ b/solution.py
@@ -25,6 +25,7 @@
 SENT = 2 * TILE + EDGES
 RIM = 2 * STRIP
 PART = 8
+CHUNK = 8
 
 band_weight = 0.75
 root_half = 0.7071067811865476
@@ -121,8 +122,8 @@
     core_ref,
     held_ref,
     early_ref,
-    up_ref,
-    down_ref,
+    near_ref,
+    far_ref,
     w_ref,
     code_ref,
     g_ref,
@@ -134,7 +135,16 @@
     lin_ref,
     gt_ref,
     terms_ref,
+    up_ref,
+    down_ref,
 ):
+    for core, (above, below) in enumerate(((far_ref, near_ref), (near_ref, far_ref))):
+
+        @pl.when(core_ref[0] == core)
+        def _():
+            up_ref[...] = above[...]
+            down_ref[...] = below[...]
+
     def spread(ref, frame, place):
         for tall_row in range(-2, ROWS + 2):
             if tall_row < 0:
@@ -227,13 +237,11 @@
         turned = g_ref[frame].astype(f32).T.astype(bf16)
         for tap in range(3):
             gt_ref[pl.ds(tap * CH, CH), pl.ds((frame + tap) * TILE, TILE)] = turned
-    _, peers, ring, share = terms_ref.shape[:4]
-    blocks = 27 * CH // PART
-    slots = share // PART
-    deep = peers // CHIPS[0]
-    lines = 2 * deep
-    unused = terms_ref.at[:, peers - deep :]
-    unused[...] = jnp.zeros_like(unused)
+    _, peers, _, _ = terms_ref.shape
+    wide = CHIPS[0]
+    deep = peers // wide
+    part = 27 * CH // (2 * peers)
+    terms_ref[...] = jnp.zeros_like(terms_ref)
     for low in range(0, 9, 2):
         high = min(low + 2, 9)
         product = jnp.dot(
@@ -246,23 +254,24 @@
                 block = product[
                     frame_tap * CH : (frame_tap + 1) * CH, (tap - low) * CH : (tap - low + 1) * CH
                 ].T
-                for piece in range(CH // PART):
-                    at = (frame_tap * 9 + tap) * (CH // PART) + piece
-                    line, within = divmod(at, blocks // lines)
-                    owner, slot = divmod(within, slots)
+                first = (frame_tap * 9 + tap) * CH
+                at = first
+                while at < first + CH:
+                    place, row = divmod(at, part)
+                    count = min(part - row, first + CH - at)
+                    line, column = divmod(place, wide)
                     depth, core = divmod(line, 2)
-                    column, place = divmod(owner, ring)
-                    peer = column * deep + depth
-                    terms_ref[core, peer, place, pl.ds(slot * PART, PART), :] = block[
-                        piece * PART : (piece + 1) * PART
+                    terms_ref[core, column * deep + depth, pl.ds(row, count), :] = block[
+                        at - first : at - first + count
                     ]
+                    at += count
     for core in range(2):
 
         @pl.when(core_ref[0] == core)
         def _():
             for peer in range(peers):
-                keep_ref[peer] = terms_ref[core, peer].reshape(-1, CH).astype(bf16)
-                send_ref[peer] = terms_ref[1 - core, peer].reshape(-1, CH).astype(bf16)
+                keep_ref[peer] = terms_ref[core, peer].astype(bf16)
+                send_ref[peer] = terms_ref[1 - core, peer].astype(bf16)
 
 
 def backward_body(g_ref, up_ref, down_ref, late_ref, code_ref, w_ref, out_ref, col_ref, side_ref):
@@ -322,6 +331,10 @@
         out_ref[frame, 2 * TILE : SENT, :] = jnp.concatenate(pair, axis=0).astype(bf16)
 
 
+def add_body(one_ref, other_ref, out_ref):
+    out_ref[...] = (one_ref[...].astype(f32) + other_ref[...].astype(f32)).astype(bf16)
+
+
 def part_body(parts_ref, out_ref):
     part = parts_ref[0].astype(f32)
     for peer in range(1, parts_ref.shape[0]):
@@ -340,7 +353,7 @@
         out_ref[owner] = copies
 
 
-def unpack_body(got_ref, code_ref, grad_ref):
+def unpack(got_ref, code_ref, grad_ref):
     at = lax.broadcasted_iota(jnp.int32, (STRIP, CH), 0)
     for strip in range(GROUP):
         columns = pl.ds(strip * STRIP, STRIP)
@@ -358,10 +371,38 @@
             grad_ref[row, columns, :] = value.astype(bf16)
 
 
+def finish_body(
+    got_ref, terms_ref, code_hbm, grad_hbm, kernel_hbm, code_ref, grad_ref, kernel_ref, sems
+):
+    copies = []
+    chunks = kernel_ref.shape[0]
+    part = kernel_ref.shape[1] // CHUNK
+    for chunk in range(chunks):
+        for place in range(CHUNK):
+            rows = terms_ref[chunk * CHUNK + place].astype(f32)
+            kernel_ref[chunk, pl.ds(place * part, part), :] = rows[:part]
+        copies.append(
+            pltpu.make_async_copy(kernel_ref.at[chunk], kernel_hbm.at[chunk], sems.at[chunk])
+        )
+        copies[-1].start()
+    unpack(got_ref, code_ref, grad_ref)
+    for at, (ref, hbm) in enumerate(((code_ref, code_hbm), (grad_ref, grad_hbm))):
+        copies.append(pltpu.make_async_copy(ref, hbm, sems.at[chunks + at]))
+        copies[-1].start()
+    for copy in copies:
+        copy.wait()
+
+
 def shifted(value, axes, by):
     count = lax.axis_size(axes)
     route = [(i, i + by) for i in range(count) if 0 <= i + by < count]
     return lax.ppermute(value, axes, route)
+
+
+def between_chips(value):
+    count = lax.axis_size(("z", "core"))
+    pairs = [(i, i + 1) for i in range(1, count - 1, 2)]
+    return lax.ppermute(value, ("z", "core"), pairs + [(j, i) for i, j in pairs])
 
 
 def swapped(value):
@@ -389,13 +430,16 @@
         ]
         return pieces[0] if len(pieces) == 1 else jnp.concatenate(pieces, axis=1)
 
-    up = shifted(edge_rows((TILE - RIM, HELD + STRIP)), lines, 1)
-    down = shifted(edge_rows((0, RIM), (TILE, HELD), (HELD + STRIP, HELD + 2 * STRIP)), lines, -1)
+    core = lax.axis_index("core")
+    last = edge_rows((TILE - RIM, HELD + STRIP))
+    first = edge_rows((0, RIM), (TILE, HELD), (HELD + STRIP, HELD + 2 * STRIP))
+    near = swapped(jnp.where(core == 0, last, first))
+    far = between_chips(jnp.where(core == 0, first, last))
 
     devices = lax.axis_size(("x", "y", "z", "core"))
     peers, wide = lax.axis_size(("x", "z")), lax.axis_size("x")
-    share = PART * -(-27 * CH // (PART * devices))
-    mail = jax.ShapeDtypeStruct((peers, GROUP * share, CH), bf16)
+    share = PART * -(-27 * CH // (2 * PART * peers))
+    mail = jax.ShapeDtypeStruct((peers, share, CH), bf16)
     flops = 2 * GROUP * TILE * 27 * CH * CH
     code, g, g_up, g_down, keep, send = kernel_call(
         forward_body,
@@ -411,14 +455,15 @@
             pltpu.VMEM((FRAMES * (TILE + RIM), WIDE), bf16),
             pltpu.VMEM((GROUP * (TILE + RIM), CH), f32),
             pltpu.VMEM((3 * CH, FRAMES * TILE), bf16),
-            pltpu.VMEM((2, peers, GROUP, share, CH), f32),
-        ],
+            pltpu.VMEM((2, peers, share, CH), f32),
+        ]
+        + [pltpu.VMEM((FRAMES, RIM + EDGES + STRIP, CH), bf16)] * 2,
         flops=2 * flops,
         in_specs=[pl.BlockSpec(memory_space=pltpu.SMEM)]
         + [pl.BlockSpec(memory_space=pltpu.VMEM)] * 5,
-    )(lax.axis_index("core").astype(jnp.int32).reshape(1), held, early, up, down, weights)
-
-    chip_sum = (keep.astype(f32) + swapped(send).astype(f32)).astype(bf16)
+    )(core.astype(jnp.int32).reshape(1), held, early, near, far, weights)
+
+    chip_sum = kernel_call(add_body, mail)(keep, swapped(send))
     parts = lax.all_to_all(chip_sum, ("x", "z"), 0, 0)
     late = shifted(jnp.concatenate([g_up[:2], g[:2], g_down[:2]], axis=1), "x", -1)
     sent = kernel_call(
@@ -431,19 +476,35 @@
         flops=flops,
     )(g, g_up, g_down, late, code, turned)
     parts, sent = lax.optimization_barrier((parts, sent))
-    part = kernel_call(part_body, jax.ShapeDtypeStruct((GROUP, GROUP * share, CH), bf16))(parts)
+    part = kernel_call(part_body, jax.ShapeDtypeStruct((GROUP, share, CH), bf16))(parts)
     norm = 1.0 / math.sqrt(devices * GROUP * TILE)
     copies = kernel_call(
         functools.partial(share_body, norm=norm),
-        jax.ShapeDtypeStruct((wide, GROUP * share, CH), bf16),
+        jax.ShapeDtypeStruct((wide, share, CH), bf16),
     )(lax.all_to_all(part, "y", 0, 0))
-    line = lax.all_to_all(copies, "x", 0, 0).reshape(-1, CH)
-    line = line[: 27 * CH // lax.axis_size(lines)]
-    grad_kernel = lax.all_gather(line, lines, tiled=True).astype(f32)
+    line = lax.all_to_all(copies, "x", 0, 0).reshape(wide * share, CH)
+    terms = lax.all_gather(line, lines, tiled=True).reshape(-1, share, CH)
 
     got = lax.all_to_all(sent, "y", 0, 0)
-    whole = jax.ShapeDtypeStruct((ROWS, GROUP * STRIP, CH), bf16)
-    code_out, grad_frames = kernel_call(unpack_body, (whole, whole))(got)
+    whole = (ROWS, GROUP * STRIP, CH)
+    part = 27 * CH // terms.shape[0]
+    code_out, grad_frames, grad_kernel = pl.pallas_call(
+        finish_body,
+        out_shape=(
+            jax.ShapeDtypeStruct(whole, bf16),
+            jax.ShapeDtypeStruct(whole, bf16),
+            jax.ShapeDtypeStruct((terms.shape[0] // CHUNK, CHUNK * part, CH), f32),
+        ),
+        in_specs=[pl.BlockSpec(memory_space=pltpu.VMEM)] * 2,
+        out_specs=[pl.BlockSpec(memory_space=pl.ANY)] * 3,
+        scratch_shapes=[
+            pltpu.VMEM(whole, bf16),
+            pltpu.VMEM(whole, bf16),
+            pltpu.VMEM((terms.shape[0] // CHUNK, CHUNK * part, CH), f32),
+            pltpu.SemaphoreType.DMA((2 + terms.shape[0] // CHUNK,)),
+        ],
+        compiler_params=pltpu.CompilerParams(vmem_limit_bytes=VMEM_LIMIT),
+    )(got, terms)
     return (code_out[None], grad_frames[None], grad_kernel.reshape(3, 3, 3, CH, CH))
 
 

time: 132 us -> 128 us (0.970)
  blocking collectives: 64.5 us -> 41.7 us
  waiting for transfers between devices: 16.6 us -> 27 us
  starting transfers between devices: 33.6 us -> 41.9 us
  other arithmetic: 2.43 us -> 0.09 us
  Pallas kernels: 12.5 us -> 14.1 us
    all_to_all x2 -> x1, blocking collectives: 30.6 us -> 7.52 us  [shards(): line = lax.all_to_all(copies, 'x', 0, 0).reshape(wide * share, CH)]
    all_to_all x0 -> x1, waiting for transfers between devices: none -> 15.6 us  [shards(): held = lax.all_to_all(packed, 'y', 0, 0)]
    all_to_all x0 -> x1, starting transfers between devices: none -> 7.66 us  [shards(): held = lax.all_to_all(packed, 'y', 0, 0)]
    ppermute x4 -> x2, starting transfers between devices: 14.9 us -> 7.49 us  [shifted(): return lax.ppermute(value, axes, route)]
    ppermute x4 -> x2, waiting for transfers between devices: 10.5 us -> 5.2 us  [shifted(): return lax.ppermute(value, axes, route)]
    ppermute x0 -> x1, starting transfers between devices: none -> 5.23 us  [between_chips(): lax.ppermute(value, ('z', 'core'), pairs + [(j, i) for i, j in pairs])]
    ppermute x1 -> x2, starting transfers between devices: 1.92 us -> 3.94 us  [swapped(): return lax.ppermute(value, 'core', [(0, 1), (1, 0)])]
    pallas_call x2 -> x3, Pallas kernels: 0.91 us -> 2.44 us  [the longest x1 1.48 us: shards(): pl.pallas_call(finish_body, out_shape=(jax.ShapeDtypeStruct(whole, bf16),...]
  transfers between devices with their start and end apart: 7 -> 8, of which waited for: 6 -> 7; matrix products, arithmetic and copies ran while one was open for 2% -> 1% of each run, Pallas kernels for 3% -> 3%
where the time goes in v9:
time: 128 us; the launch traced here: 127 us
  starting transfers between devices  41.9 us (33%)
  blocking collectives  41.7 us (33%)
  waiting for transfers between devices  27 us (21%)
  Pallas kernels  14.1 us (11%)
  local copies, waits for them, and re-layouts  1.5 us (1%)
    all_gather x1, blocking collectives, shards(): terms = lax.all_gather(line, lines, tiled=True).reshape(-1, share, CH)  24 us
    all_to_all x1, waiting for transfers between devices, shards(): held = lax.all_to_all(packed, 'y', 0, 0)  15.6 us
    all_to_all x1, starting transfers between devices, shards(): parts = lax.all_to_all(chip_sum, ('x', 'z'), 0, 0)  14 us
    all_to_all x1, blocking collectives, shards(): lax.all_to_all(part, 'y', 0, 0)  10.2 us
    all_to_all x1, starting transfers between devices, shards(): held = lax.all_to_all(packed, 'y', 0, 0)  7.66 us
    all_to_all x1, blocking collectives, shards(): line = lax.all_to_all(copies, 'x', 0, 0).reshape(wide * share, CH)  7.52 us
    ppermute x2, starting transfers between devices, shifted(): return lax.ppermute(value, axes, route)  7.49 us
    pallas_call x1, Pallas kernels, shards(): kernel_call(forward_body, (jax.ShapeDtypeStruct((GROUP, TILE, CH), bf16),...  6.14 us
  transfers between devices with their start and end apart: 8, of which 7 were waited for; matrix products, arithmetic and copies ran while one was open for 1% of the time, Pallas kernels for 3%

profile of v9, /device:TPU:1, one launch (start us, length us, event | category | flops | bytes accessed | tf_op | source)
XLA Modules:
  0.0 127.1 jit_solution(11402552609676673999)
XLA Ops:
  0.6 0.0 copy-start
  0.6 2.0 %shard_map.58 = bf16[8,272,128]{2,1,0:T(8,128)(2,1)} custom-call(bf16[8,8,16,128]{3,2,1,0:T(8,128)(2,1)} %bitcast.15, bf16[8,8,16,128]{3,2,1,0:T(8,128)(2,1)} %bitcast.16), custom_call_target="tpu_custom_call" | custom-call | tf_op jit(solution)/shard_map/pallas_call | solution.py:416
  2.7 7.7 %all-to-all-start = ((bf16[8,272,128]{2,1,0:T(8,128)(2,1)}), bf16[8,272,128]{2,1,0:T(8,128)(2,1)S(1)}, u32[]{:S(2)}, u32[]{:S(2)}) async-start(bf16[8,272,128]{2,1,0:T(8,128)(2,1)} %shard_map.58), calls=%async_computation | async-start | bytes 1114112 | tf_op jit(solution)/shard_map/all_to_all | solution.py:423
  10.3 15.6 %all-to-all-done.held_ref = bf16[8,272,128]{2,1,0:T(8,128)(2,1)S(1)} async-done(((bf16[8,272,128]{2,1,0:T(8,128)(2,1)}), bf16[8,272,128]{2,1,0:T(8,128)(2,1)S(1)}, u32[]{:S(2)}, u32[]{:S(2)}) %all-to-all-start) | async-done | bytes 557088 | tf_op jit(solution)/shard_map/all_to_all | solution.py:423
  25.9 6.2 %collective-permute-start = (bf16[2,176,128]{2,1,0:T(8,128)(2,1)S(1)}, bf16[2,176,128]{2,1,0:T(8,128)(2,1)S(1)}, u32[]{:S(2)}, u32[]{:S(2)}) collective-permute-start(bf16[2,176,128]{2,1,0:T(8,128)(2,1)S(1)} %slice.48), channel_id=1, source_target_pairs={{0,128},{128,256},{256,384},{1,129},{129,257},{257,385},{2,130},{1... | collective-permute-start | bytes 270344 | tf_op jit(solution)/shard_map/ppermute | solution.py:399
  32.2 1.5 %collective-permute-done.early_ref = bf16[2,176,128]{2,1,0:T(8,128)(2,1)S(1)} collective-permute-done((bf16[2,176,128]{2,1,0:T(8,128)(2,1)S(1)}, bf16[2,176,128]{2,1,0:T(8,128)(2,1)S(1)}, u32[]{:S(2)}, u32[]{:S(2)}) %collective-permute-start) | collective-permute-done | bytes 90144 | tf_op jit(solution)/shard_map/ppermute | solution.py:399
  33.7 0.1 broadcast_select_fusion
  33.8 5.2 %collective-permute-start.2 = (bf16[10,64,128]{2,1,0:T(8,128)(2,1)S(1)}, bf16[10,64,128]{2,1,0:T(8,128)(2,1)S(1)}, u32[]{:S(2)}, u32[]{:S(2)}) collective-permute-start(bf16[10,64,128]{2,1,0:T(8,128)(2,1)S(1)} %get-tuple-element.27), channel_id=1, source_target_pairs={{1,2},{3,4},{5,6},{7,8},{9,10},{11,12},{13,14},{2,1},{4,3},{6,5},{... | collective-permute-start | bytes 491528 | tf_op jit(solution)/shard_map/ppermute | solution.py:405
  39.0 1.9 %collective-permute-start.1 = (bf16[10,64,128]{2,1,0:T(8,128)(2,1)S(1)}, bf16[10,64,128]{2,1,0:T(8,128)(2,1)S(1)}, u32[]{:S(2)}, u32[]{:S(2)}) collective-permute-start(bf16[10,64,128]{2,1,0:T(8,128)(2,1)S(1)} %get-tuple-element.28), channel_id=1, source_target_pairs={{0,1},{1,0},{2,3},{3,2},{4,5},{5,4},{6,7},{7,6},{8,9},{9,8},{10,11... | collective-permute-start | bytes 491528 | tf_op jit(solution)/shard_map/ppermute | solution.py:409
  40.9 1.1 collective-permute-done.2.far_ref
  42.0 0.3 collective-permute-done.1.near_ref
  42.3 0.0 copy-done
  42.3 6.1 %shard_map.59 = (bf16[8,128,128]{2,1,0:T(8,128)(2,1)S(1)}, bf16[8,128,128]{2,1,0:T(8,128)(2,1)S(1)}, bf16[8,16,128]{2,1,0:T(8,128)(2,1)S(1)}, bf16[8,16,128]{2,1...) custom-call(s32[1]{0:T(128)} %bitcast.core_ref, ...), custom_call_target="tpu_custom_call" | custom-call | flops 1811939328 | bytes 4194304 | tf_op jit(solution)/shard_map/pallas_call | solution.py:444
  48.4 2.0 %collective-permute-start.3 = (bf16[32,56,128]{2,1,0:T(8,128)(2,1)S(1)}, bf16[32,56,128]{2,1,0:T(8,128)(2,1)S(1)}, u32[]{:S(2)}, u32[]{:S(2)}) collective-permute-start(bf16[32,56,128]{2,1,0:T(8,128)(2,1)S(1)} %get-tuple-element.15), channel_id=1, source_target_pairs={{0,1},{1,0},{2,3},{3,2},{4,5},{5,4},{6,7},{7,6},{8,9},{9,8},{10,11... | collective-permute-start | bytes 1376264 | tf_op jit(solution)/shard_map/ppermute | solution.py:409
  50.5 1.7 %collective-permute-done.3.other_ref = bf16[32,56,128]{2,1,0:T(8,128)(2,1)S(1)} collective-permute-done((bf16[32,56,128]{2,1,0:T(8,128)(2,1)S(1)}, bf16[32,56,128]{2,1,0:T(8,128)(2,1)S(1)}, u32[]{:S(2)}, u32[]{:S(2)}) %collective-permute-start.3) | collective-permute-done | bytes 458784 | tf_op jit(solution)/shard_map/ppermute | solution.py:409
  52.1 0.9 shard_map.60
  53.0 14.0 %all-to-all-start.1 = ((bf16[32,56,128]{2,1,0:T(8,128)(2,1)}), bf16[32,56,128]{2,1,0:T(8,128)(2,1)S(1)}, u32[]{:S(2)}, u32[]{:S(2)}) async-start(bf16[32,56,128]{2,1,0:T(8,128)(2,1)} %shard_map.60), calls=%async_computation.1 | async-start | bytes 917504 | tf_op jit(solution)/shard_map/all_to_all | solution.py:467
  67.1 1.3 %collective-permute-start.4 = (bf16[2,160,128]{2,1,0:T(8,128)(2,1)S(1)}, bf16[2,160,128]{2,1,0:T(8,128)(2,1)S(1)}, u32[]{:S(2)}, u32[]{:S(2)}) collective-permute-start(bf16[2,160,128]{2,1,0:T(8,128)(2,1)S(1)} %pad_maximum_fusion.1), channel_id=1, source_target_pairs={{128,0},{256,128},{384,256},{129,1},{257,129},{385,257},{130,2},{2... | collective-permute-start | bytes 245768 | tf_op jit(solution)/shard_map/ppermute | solution.py:399
  68.4 0.1 reverse_bitcast_fusion
  68.5 1.4 %copy.6 = bf16[3,3,3,128,128]{4,3,2,1,0:T(8,128)(2,1)S(1)} copy(bf16[3,3,3,128,128]{3,4,2,1,0:T(8,128)(2,1)S(1)} %reverse_bitcast_fusion) | data formatting | bytes 1769472 | tf_op jit(solution)/shard_map/transpose | solution.py:414
  69.9 3.7 %collective-permute-done.4.late_ref = bf16[2,160,128]{2,1,0:T(8,128)(2,1)S(1)} collective-permute-done((bf16[2,160,128]{2,1,0:T(8,128)(2,1)S(1)}, bf16[2,160,128]{2,1,0:T(8,128)(2,1)S(1)}, u32[]{:S(2)}, u32[]{:S(2)}) %collective-permute-start.4) | collective-permute-done | bytes 81952 | tf_op jit(solution)/shard_map/ppermute | solution.py:399
  73.6 3.5 %shard_map.61 = bf16[8,272,128]{2,1,0:T(8,128)(2,1)} custom-call(bf16[8,128,128]{2,1,0:T(8,128)(2,1)S(1)} %get-tuple-element.16.g_ref, bf16[8,16,128]{2,1,0:T(8,128)(2,1)S(1)} %get-tuple-element.17.up_ref, bf16[8,16,128]{2,1,0:T(8,128)(2,1)S(1)} %get-tuple-element.18.down_ref, bf16[2,160,128]{2,1,0:T(8,128)(2,1)S(1)} %collective-permute-done.4.late_ref, ...), custom_call_target="tpu_custom_call" | custom-call | flops 905969664 | bytes 4194304 | tf_op jit(solution)/shard_map/pallas_call | solution.py:469
  77.1 3.2 %all-to-all-done.1.parts_ref = bf16[32,56,128]{2,1,0:T(8,128)(2,1)S(1)} async-done(((bf16[32,56,128]{2,1,0:T(8,128)(2,1)}), bf16[32,56,128]{2,1,0:T(8,128)(2,1)S(1)}, u32[]{:S(2)}, u32[]{:S(2)}) %all-to-all-start.1) | async-done | bytes 458784 | tf_op jit(solution)/shard_map/all_to_all | solution.py:467
  80.2 0.1 shard_map.62
  80.3 10.2 %all_to_all.25.got_ref = bf16[8,56,128]{2,1,0:T(8,128)(2,1)S(1)} all-to-all(bf16[8,56,128]{2,1,0:T(8,128)(2,1)S(1)} %shard_map.62), channel_id=1, replica_groups=mesh['x'=4,'y'=8,'z'=8,'core'=2] {'y'}, dimensions={0} | all-to-all | bytes 229376 | tf_op jit(solution)/shard_map/all_to_all | solution.py:484
  90.6 7.5 %all_to_all.26 = bf16[4,56,128]{2,1,0:T(8,128)(2,1)S(1)} all-to-all(bf16[4,56,128]{2,1,0:T(8,128)(2,1)S(1)} %shard_map.63), channel_id=1, replica_groups=mesh['x'=4,'y'=8,'z'=8,'core'=2] {'x'}, dimensions={0} | all-to-all | bytes 114688 | tf_op jit(solution)/shard_map/all_to_all | solution.py:485
  98.1 3.5 %all-to-all-start.2 = ((bf16[8,272,128]{2,1,0:T(8,128)(2,1)}), bf16[8,272,128]{2,1,0:T(8,128)(2,1)S(1)}, u32[]{:S(2)}, u32[]{:S(2)}) async-start(bf16[8,272,128]{2,1,0:T(8,128)(2,1)} %shard_map.61), calls=%async_computation.2 | async-start | bytes 1114112 | tf_op jit(solution)/shard_map/all_to_all | solution.py:488
  101.6 24.0 %all_gather.3 = bf16[3584,128]{1,0:T(8,128)(2,1)S(1)} all-gather(bf16[224,128]{1,0:T(8,128)(2,1)S(1)} %bitcast.17), channel_id=1, replica_groups=mesh['x'=4,'y'=8,'z'=8,'core'=2] {'z','core'}, dimensions={0}, use_global_device_ids=true | all-gather | bytes 974848 | tf_op jit(solution)/shard_map/all_gather | solution.py:486
  125.6 0.0 all-to-all-done.2.got_ref
  125.6 1.5 %shard_map.64 = (bf16[8,128,128]{2,1,0:T(8,128)(2,1)}, bf16[8,128,128]{2,1,0:T(8,128)(2,1)}, f32[8,432,128]{2,1,0:T(8,128)}) custom-call(bf16[8,272,128]{2,1,0:T(8,128)(2,1)S(1)} %all-to-all-done.2.got_ref, bf16[64,56,128]{2,1,0:T(8,128)(2,1)S(1)} %bitcast.12), custom_call_target="tpu_custom_call" | custom-call | tf_op jit(solution)/shard_map/pallas_call | solution.py:491
  (12 shorter events, 0.1 us)
Async XLA Ops:
  0.6 41.7 %copy-start = (bf16[3,3,3,128,128]{4,3,2,1,0:T(8,128)(2,1)S(1)}, bf16[3,3,3,128,128]{4,3,2,1,0:T(8,128)(2,1)}, u32[]{:S(2)}) copy-start(bf16[3,3,3,128,128]{4,3,2,1,0:T(8,128)(2,1)} %param.4) | copy-start | bytes 2654212
  2.7 23.2 %all-to-all-start = ((bf16[8,272,128]{2,1,0:T(8,128)(2,1)}), bf16[8,272,128]{2,1,0:T(8,128)(2,1)S(1)}, u32[]{:S(2)}, u32[]{:S(2)}) async-start(bf16[8,272,128]{2,1,0:T(8,128)(2,1)} %shard_map.58), calls=%async_computation | async-start | bytes 1114112 | tf_op jit(solution)/shard_map/all_to_all | solution.py:423
  25.9 7.7 %collective-permute-start = (bf16[2,176,128]{2,1,0:T(8,128)(2,1)S(1)}, bf16[2,176,128]{2,1,0:T(8,128)(2,1)S(1)}, u32[]{:S(2)}, u32[]{:S(2)}) collective-permute-start(bf16[2,176,128]{2,1,0:T(8,128)(2,1)S(1)} %slice.48), channel_id=1, source_target_pairs={{0,128},{128,256},{256,384},{1,129},{129,257},{257,385},{2,130},{1... | collective-permute-start | bytes 270344 | tf_op jit(solution)/shard_map/ppermute | solution.py:399
  33.8 8.2 %collective-permute-start.2 = (bf16[10,64,128]{2,1,0:T(8,128)(2,1)S(1)}, bf16[10,64,128]{2,1,0:T(8,128)(2,1)S(1)}, u32[]{:S(2)}, u32[]{:S(2)}) collective-permute-start(bf16[10,64,128]{2,1,0:T(8,128)(2,1)S(1)} %get-tuple-element.27), channel_id=1, source_target_pairs={{1,2},{3,4},{5,6},{7,8},{9,10},{11,12},{13,14},{2,1},{4,3},{6,5},{... | collective-permute-start | bytes 491528 | tf_op jit(solution)/shard_map/ppermute | solution.py:405
  39.0 3.3 %collective-permute-start.1 = (bf16[10,64,128]{2,1,0:T(8,128)(2,1)S(1)}, bf16[10,64,128]{2,1,0:T(8,128)(2,1)S(1)}, u32[]{:S(2)}, u32[]{:S(2)}) collective-permute-start(bf16[10,64,128]{2,1,0:T(8,128)(2,1)S(1)} %get-tuple-element.28), channel_id=1, source_target_pairs={{0,1},{1,0},{2,3},{3,2},{4,5},{5,4},{6,7},{7,6},{8,9},{9,8},{10,11... | collective-permute-start | bytes 491528 | tf_op jit(solution)/shard_map/ppermute | solution.py:409
  48.4 3.7 %collective-permute-start.3 = (bf16[32,56,128]{2,1,0:T(8,128)(2,1)S(1)}, bf16[32,56,128]{2,1,0:T(8,128)(2,1)S(1)}, u32[]{:S(2)}, u32[]{:S(2)}) collective-permute-start(bf16[32,56,128]{2,1,0:T(8,128)(2,1)S(1)} %get-tuple-element.15), channel_id=1, source_target_pairs={{0,1},{1,0},{2,3},{3,2},{4,5},{5,4},{6,7},{7,6},{8,9},{9,8},{10,11... | collective-permute-start | bytes 1376264 | tf_op jit(solution)/shard_map/ppermute | solution.py:409
  53.0 27.2 %all-to-all-start.1 = ((bf16[32,56,128]{2,1,0:T(8,128)(2,1)}), bf16[32,56,128]{2,1,0:T(8,128)(2,1)S(1)}, u32[]{:S(2)}, u32[]{:S(2)}) async-start(bf16[32,56,128]{2,1,0:T(8,128)(2,1)} %shard_map.60), calls=%async_computation.1 | async-start | bytes 917504 | tf_op jit(solution)/shard_map/all_to_all | solution.py:467
  67.1 6.5 %collective-permute-start.4 = (bf16[2,160,128]{2,1,0:T(8,128)(2,1)S(1)}, bf16[2,160,128]{2,1,0:T(8,128)(2,1)S(1)}, u32[]{:S(2)}, u32[]{:S(2)}) collective-permute-start(bf16[2,160,128]{2,1,0:T(8,128)(2,1)S(1)} %pad_maximum_fusion.1), channel_id=1, source_target_pairs={{128,0},{256,128},{384,256},{129,1},{257,129},{385,257},{130,2},{2... | collective-permute-start | bytes 245768 | tf_op jit(solution)/shard_map/ppermute | solution.py:399
  98.1 27.5 %all-to-all-start.2 = ((bf16[8,272,128]{2,1,0:T(8,128)(2,1)}), bf16[8,272,128]{2,1,0:T(8,128)(2,1)S(1)}, u32[]{:S(2)}, u32[]{:S(2)}) async-start(bf16[8,272,128]{2,1,0:T(8,128)(2,1)} %shard_map.61), calls=%async_computation.2 | async-start | bytes 1114112 | tf_op jit(solution)/shard_map/all_to_all | solution.py:488

commit v10 on v9

--- a/solution.py
+++ b/solution.py
@@ -45,10 +45,12 @@
     )
 
 
-def pack_body(x_hbm, cot_hbm, out_ref, left_ref, right_ref, sems):
+def pack_body(x_hbm, cot_hbm, out_hbm, x_ref, edge_ref, left_ref, right_ref, sems, own_sems):
+    own = pltpu.make_async_copy(x_hbm, x_ref, own_sems.at[0])
+    own.start()
     copies = [
         pltpu.make_async_copy(
-            hbm.at[row], out_ref.at[:, pl.ds(place(row), STRIP), :], sems.at[side, row]
+            hbm.at[row], out_hbm.at[:, pl.ds(place(row), STRIP), :], sems.at[side, row]
         )
         for side, (hbm, place) in enumerate(((x_hbm, x_place), (cot_hbm, cot_place)))
         for row in range(ROWS)
@@ -57,18 +59,20 @@
         copy.start()
     left_ref[...] = jnp.zeros_like(left_ref)
     right_ref[...] = jnp.zeros_like(right_ref)
+    own.wait()
     for row in range(ROWS):
-        copies[row].wait()
         for strip in range(GROUP):
-            wide = out_ref[strip, pl.ds(x_place(row), STRIP), :].astype(f32)
+            wide = x_ref[row, strip].astype(f32)
             if strip < GROUP - 1:
                 left_ref[strip + 1, pl.ds(row, 1), :] = wide[STRIP - 1 : STRIP]
             if strip > 0:
                 right_ref[strip - 1, pl.ds(row, 1), :] = wide[0:1]
     for strip in range(GROUP):
         pair = jnp.concatenate([left_ref[strip], right_ref[strip]], axis=0)
-        out_ref[strip, pl.ds(TILE, EDGES), :] = pair.astype(bf16)
-    for copy in copies[ROWS:]:
+        edge_ref[strip] = pair.astype(bf16)
+    edges = pltpu.make_async_copy(edge_ref, out_hbm.at[:, pl.ds(TILE, EDGES), :], own_sems.at[1])
+    edges.start()
+    for copy in copies + [edges]:
         copy.wait()
 
 
@@ -92,25 +96,38 @@
             col_ref[pl.ds(start, STRIP), pl.ds(tap * CH, CH)] = piece
 
 
+def gate_of(linear):
+    return 0.5 * jnp.tanh(0.5 * linear) + 0.5
+
+
+def bands(active):
+    sums, code = active, [0.0] * (GROUP // 2)
+    scale = 1.0
+    for level in range(LEVELS):
+        scale = scale * root_half
+        changes = [(sums[at + 1] - sums[at]) * (band_weight * scale) for at in range(0, len(sums), 2)]
+        sums = [sums[at] + sums[at + 1] for at in range(0, len(sums), 2)]
+        if level == LEVELS - 1:
+            changes = [changes[0] + sums[0] * scale]
+        code = [value + changes[at >> level] for at, value in enumerate(code)]
+    return code
+
+
 def adjoint_bands(cot):
-    back = [None] * GROUP
+    levels = [cot]
+    for level in range(LEVELS):
+        last = levels[-1]
+        levels.append([last[at] + last[at + 1] for at in range(0, len(last), 2)])
+    scale = root_half**LEVELS
+    back = [levels[LEVELS][0] * scale]
     for level in range(LEVELS - 1, -1, -1):
-        step = 1 << level
-        following = [None] * GROUP
-        for frame in range(GROUP):
-            if frame & step:
-                continue
-            pair = (cot[frame] + cot[frame + step]) * root_half
-            if level == LEVELS - 1:
-                total = pair
-            else:
-                total = (back[frame] + back[frame + step]) * root_half
-            for member, side in ((frame, -1.0), (frame + step, 1.0)):
-                value = total + (band_weight * side) * pair
-                if level > 0:
-                    value = value.astype(bf16).astype(f32)
-                following[member] = value
-        back = following
+        weight = band_weight * root_half ** (level + 1)
+        steps = [value * weight for value in levels[level + 1]]
+        back = [
+            value
+            for at, step in enumerate(steps)
+            for value in (back[at] - step, back[at] + step)
+        ]
     return back
 
 
@@ -194,26 +211,12 @@
     def _(row):
         low = pl.multiple_of(row * STRIP, STRIP)
         linear = [lin_ref[pl.ds(frame * TILE + low, STRIP), :] for frame in range(GROUP)]
-        gate = [jax.nn.sigmoid(value) for value in linear]
-        band = [(value * part).astype(bf16).astype(f32) for value, part in zip(linear, gate)]
-        detail = [None] * GROUP
-        for level in range(LEVELS):
-            step = 1 << level
-            following = [None] * GROUP
-            for frame in range(0, GROUP, 2 * step):
-                lower, upper = band[frame], band[frame + step]
-                smooth = (lower + upper) * root_half
-                if level < LEVELS - 1:
-                    smooth = smooth.astype(bf16).astype(f32)
-                change = (upper - lower) * root_half
-                following[frame] = smooth
-                for member in range(frame, frame + 2 * step, 2):
-                    detail[member] = change if level == 0 else detail[member] + change
-            band = following
-        for member in range(0, GROUP, 2):
-            code = (band[0] + band_weight * detail[member]).astype(bf16)
-            code_ref[member, pl.ds(low, STRIP), :] = code
-            code_ref[member + 1, pl.ds(low, STRIP), :] = code
+        gate = [gate_of(value) for value in linear]
+        codes = bands([value * part for value, part in zip(linear, gate)])
+        for pair, value in enumerate(codes):
+            code = value.astype(bf16)
+            code_ref[2 * pair, pl.ds(low, STRIP), :] = code
+            code_ref[2 * pair + 1, pl.ds(low, STRIP), :] = code
         place = pl.multiple_of(HELD + lax.rem(row + 1, ROWS) * STRIP, STRIP)
         cot = [held_ref[frame, pl.ds(place, STRIP), :].astype(f32) for frame in range(GROUP)]
         back = adjoint_bands(cot)
@@ -229,7 +232,7 @@
         back = adjoint_bands(cot)
         for frame in range(GROUP):
             linear = lin_ref[pl.ds(GROUP * TILE + frame * RIM + offset, STRIP), :]
-            slope = slope_of(linear, jax.nn.sigmoid(linear))
+            slope = slope_of(linear, gate_of(linear))
             rim_ref[frame] = (back[frame] * slope).astype(bf16)
 
     gt_ref[...] = jnp.zeros_like(gt_ref)
@@ -331,8 +334,18 @@
         out_ref[frame, 2 * TILE : SENT, :] = jnp.concatenate(pair, axis=0).astype(bf16)
 
 
-def add_body(one_ref, other_ref, out_ref):
-    out_ref[...] = (one_ref[...].astype(f32) + other_ref[...].astype(f32)).astype(bf16)
+def add_body(one_ref, other_ref, out_hbm, sum_ref, sems):
+    copies = []
+    count = out_hbm.shape[0] // sems.shape[0]
+    for chunk in range(sems.shape[0]):
+        pieces = pl.ds(chunk * count, count)
+        sum_ref[pieces] = (one_ref[pieces].astype(f32) + other_ref[pieces].astype(f32)).astype(bf16)
+        copies.append(
+            pltpu.make_async_copy(sum_ref.at[pieces], out_hbm.at[pieces], sems.at[chunk])
+        )
+        copies[-1].start()
+    for copy in copies:
+        copy.wait()
 
 
 def part_body(parts_ref, out_ref):
@@ -410,15 +423,23 @@
 
 
 def shards(frames, kernel, cotangent):
-    weights = kernel.reshape(3, WIDE, CH)
+    taps = kernel.reshape(3, WIDE, CH)
+    weights = taps
     turned = jnp.swapaxes(kernel[::-1, ::-1, ::-1], 3, 4).reshape(3, WIDE, CH)
     lines = ("z", "core")
     packed = pl.pallas_call(
         pack_body,
         out_shape=jax.ShapeDtypeStruct((GROUP, LOAD, CH), bf16),
         in_specs=[pl.BlockSpec(memory_space=pl.ANY)] * 2,
-        scratch_shapes=[pltpu.VMEM((GROUP, ROWS, CH), f32)] * 2
-        + [pltpu.SemaphoreType.DMA((2, ROWS))],
+        out_specs=pl.BlockSpec(memory_space=pl.ANY),
+        scratch_shapes=[
+            pltpu.VMEM((ROWS, GROUP, STRIP, CH), bf16),
+            pltpu.VMEM((GROUP, EDGES, CH), bf16),
+            pltpu.VMEM((GROUP, ROWS, CH), f32),
+            pltpu.VMEM((GROUP, ROWS, CH), f32),
+            pltpu.SemaphoreType.DMA((2, ROWS)),
+            pltpu.SemaphoreType.DMA((2,)),
+        ],
     )(frames.reshape(ROWS, GROUP, STRIP, CH), cotangent.reshape(ROWS, GROUP, STRIP, CH))
     held = lax.all_to_all(packed, "y", 0, 0)
     early = shifted(held[GROUP - 2 :, : HELD + 2 * STRIP], "x", 1)
@@ -463,7 +484,13 @@
         + [pl.BlockSpec(memory_space=pltpu.VMEM)] * 5,
     )(core.astype(jnp.int32).reshape(1), held, early, near, far, weights)
 
-    chip_sum = kernel_call(add_body, mail)(keep, swapped(send))
+    chip_sum = kernel_call(
+        add_body,
+        mail,
+        [pltpu.VMEM(mail.shape, bf16), pltpu.SemaphoreType.DMA((4,))],
+        in_specs=[pl.BlockSpec(memory_space=pltpu.VMEM)] * 2,
+        out_specs=pl.BlockSpec(memory_space=pl.ANY),
+    )(keep, swapped(send))
     parts = lax.all_to_all(chip_sum, ("x", "z"), 0, 0)
     late = shifted(jnp.concatenate([g_up[:2], g[:2], g_down[:2]], axis=1), "x", -1)
     sent = kernel_call(

time: 128 us -> 142 us (1.11)
  Pallas kernels: 14.1 us -> 28.9 us
    pallas_call x1, Pallas kernels: 2.02 us -> 17.1 us  [shards(): pl.pallas_call(pack_body, out_shape=jax.ShapeDtypeStruct((GROUP, LOAD, CH...]
  transfers between devices with their start and end apart: 8 -> 8, of which waited for: 7 -> 7; matrix products, arithmetic and copies ran while one was open for 1% -> 1% of each run, Pallas kernels for 3% -> 2%
where the time goes in v10:
time: 142 us
  starting transfers between devices  41.9 us (30%)
  blocking collectives  41.7 us (29%)
  Pallas kernels  28.9 us (20%)
  waiting for transfers between devices  27 us (19%)
  local copies, waits for them, and re-layouts  1.5 us (1%)
    all_gather x1, blocking collectives, shards(): terms = lax.all_gather(line, lines, tiled=True).reshape(-1, share, CH)  24 us
    pallas_call x1, Pallas kernels, shards(): pl.pallas_call(pack_body, out_shape=jax.ShapeDtypeStruct((GROUP, LOAD, CH...  17.1 us
    all_to_all x1, waiting for transfers between devices, shards(): held = lax.all_to_all(packed, 'y', 0, 0)  15.6 us
    all_to_all x1, starting transfers between devices, shards(): parts = lax.all_to_all(chip_sum, ('x', 'z'), 0, 0)  14.1 us
    all_to_all x1, blocking collectives, shards(): lax.all_to_all(part, 'y', 0, 0)  10.2 us
    all_to_all x1, starting transfers between devices, shards(): held = lax.all_to_all(packed, 'y', 0, 0)  7.66 us
    all_to_all x1, blocking collectives, shards(): line = lax.all_to_all(copies, 'x', 0, 0).reshape(wide * share, CH)  7.52 us
    ppermute x2, starting transfers between devices, shifted(): return lax.ppermute(value, axes, route)  7.49 us
  transfers between devices with their start and end apart: 8, of which 7 were waited for; matrix products, arithmetic and copies ran while one was open for 1% of the time, Pallas kernels for 2%

profile of v10, /device:TPU:1, one launch (start us, length us, event | category | flops | bytes accessed | tf_op | source)
XLA Modules:
  0.0 141.9 jit_solution(4206972833655561685)
XLA Ops:
  0.6 0.0 copy-start
  0.6 17.1 %shard_map.58 = bf16[8,272,128]{2,1,0:T(8,128)(2,1)} custom-call(bf16[8,8,16,128]{3,2,1,0:T(8,128)(2,1)} %bitcast.15, bf16[8,8,16,128]{3,2,1,0:T(8,128)(2,1)} %bitcast.16), custom_call_target="tpu_custom_call" | custom-call | tf_op jit(solution)/shard_map/pallas_call | solution.py:430
  17.8 7.7 %all-to-all-start = ((bf16[8,272,128]{2,1,0:T(8,128)(2,1)}), bf16[8,272,128]{2,1,0:T(8,128)(2,1)S(1)}, u32[]{:S(2)}, u32[]{:S(2)}) async-start(bf16[8,272,128]{2,1,0:T(8,128)(2,1)} %shard_map.58), calls=%async_computation | async-start | bytes 1114112 | tf_op jit(solution)/shard_map/all_to_all | solution.py:444
  25.5 15.6 %all-to-all-done.held_ref = bf16[8,272,128]{2,1,0:T(8,128)(2,1)S(1)} async-done(((bf16[8,272,128]{2,1,0:T(8,128)(2,1)}), bf16[8,272,128]{2,1,0:T(8,128)(2,1)S(1)}, u32[]{:S(2)}, u32[]{:S(2)}) %all-to-all-start) | async-done | bytes 557088 | tf_op jit(solution)/shard_map/all_to_all | solution.py:444
  41.0 6.2 %collective-permute-start = (bf16[2,176,128]{2,1,0:T(8,128)(2,1)S(1)}, bf16[2,176,128]{2,1,0:T(8,128)(2,1)S(1)}, u32[]{:S(2)}, u32[]{:S(2)}) collective-permute-start(bf16[2,176,128]{2,1,0:T(8,128)(2,1)S(1)} %slice.48), channel_id=1, source_target_pairs={{0,128},{128,256},{256,384},{1,129},{129,257},{257,385},{2,130},{1... | collective-permute-start | bytes 270344 | tf_op jit(solution)/shard_map/ppermute | solution.py:412
  47.3 1.5 %collective-permute-done.early_ref = bf16[2,176,128]{2,1,0:T(8,128)(2,1)S(1)} collective-permute-done((bf16[2,176,128]{2,1,0:T(8,128)(2,1)S(1)}, bf16[2,176,128]{2,1,0:T(8,128)(2,1)S(1)}, u32[]{:S(2)}, u32[]{:S(2)}) %collective-permute-start) | collective-permute-done | bytes 90144 | tf_op jit(solution)/shard_map/ppermute | solution.py:412
  48.8 0.1 broadcast_select_fusion
  48.9 5.2 %collective-permute-start.2 = (bf16[10,64,128]{2,1,0:T(8,128)(2,1)S(1)}, bf16[10,64,128]{2,1,0:T(8,128)(2,1)S(1)}, u32[]{:S(2)}, u32[]{:S(2)}) collective-permute-start(bf16[10,64,128]{2,1,0:T(8,128)(2,1)S(1)} %get-tuple-element.27), channel_id=1, source_target_pairs={{1,2},{3,4},{5,6},{7,8},{9,10},{11,12},{13,14},{2,1},{4,3},{6,5},{... | collective-permute-start | bytes 491528 | tf_op jit(solution)/shard_map/ppermute | solution.py:418
  54.1 1.9 %collective-permute-start.1 = (bf16[10,64,128]{2,1,0:T(8,128)(2,1)S(1)}, bf16[10,64,128]{2,1,0:T(8,128)(2,1)S(1)}, u32[]{:S(2)}, u32[]{:S(2)}) collective-permute-start(bf16[10,64,128]{2,1,0:T(8,128)(2,1)S(1)} %get-tuple-element.28), channel_id=1, source_target_pairs={{0,1},{1,0},{2,3},{3,2},{4,5},{5,4},{6,7},{7,6},{8,9},{9,8},{10,11... | collective-permute-start | bytes 491528 | tf_op jit(solution)/shard_map/ppermute | solution.py:422
  56.1 1.1 collective-permute-done.2.far_ref
  57.1 0.3 collective-permute-done.1.near_ref
  57.4 0.0 copy-done
  57.4 5.8 %shard_map.59 = (bf16[8,128,128]{2,1,0:T(8,128)(2,1)S(1)}, bf16[8,128,128]{2,1,0:T(8,128)(2,1)S(1)}, bf16[8,16,128]{2,1,0:T(8,128)(2,1)S(1)}, bf16[8,16,128]{2,1...) custom-call(s32[1]{0:T(128)} %bitcast.core_ref, ...), custom_call_target="tpu_custom_call" | custom-call | flops 1811939328 | bytes 4194304 | tf_op jit(solution)/shard_map/pallas_call | solution.py:465
  63.3 2.0 %collective-permute-start.3 = (bf16[32,56,128]{2,1,0:T(8,128)(2,1)S(1)}, bf16[32,56,128]{2,1,0:T(8,128)(2,1)S(1)}, u32[]{:S(2)}, u32[]{:S(2)}) collective-permute-start(bf16[32,56,128]{2,1,0:T(8,128)(2,1)S(1)} %get-tuple-element.15), channel_id=1, source_target_pairs={{0,1},{1,0},{2,3},{3,2},{4,5},{5,4},{6,7},{7,6},{8,9},{9,8},{10,11... | collective-permute-start | bytes 1376264 | tf_op jit(solution)/shard_map/ppermute | solution.py:422
  65.3 1.7 %collective-permute-done.3.other_ref = bf16[32,56,128]{2,1,0:T(8,128)(2,1)S(1)} collective-permute-done((bf16[32,56,128]{2,1,0:T(8,128)(2,1)S(1)}, bf16[32,56,128]{2,1,0:T(8,128)(2,1)S(1)}, u32[]{:S(2)}, u32[]{:S(2)}) %collective-permute-start.3) | collective-permute-done | bytes 458784 | tf_op jit(solution)/shard_map/ppermute | solution.py:422
  67.0 0.8 shard_map.60
  67.8 14.1 %all-to-all-start.1 = ((bf16[32,56,128]{2,1,0:T(8,128)(2,1)}), bf16[32,56,128]{2,1,0:T(8,128)(2,1)S(1)}, u32[]{:S(2)}, u32[]{:S(2)}) async-start(bf16[32,56,128]{2,1,0:T(8,128)(2,1)} %shard_map.60), calls=%async_computation.1 | async-start | bytes 917504 | tf_op jit(solution)/shard_map/all_to_all | solution.py:494
  81.9 1.3 collective-permute-start.4
  83.2 0.1 reverse_bitcast_fusion
  83.3 1.4 copy.6
  84.7 3.7 %collective-permute-done.4.late_ref = bf16[2,160,128]{2,1,0:T(8,128)(2,1)S(1)} collective-permute-done((bf16[2,160,128]{2,1,0:T(8,128)(2,1)S(1)}, bf16[2,160,128]{2,1,0:T(8,128)(2,1)S(1)}, u32[]{:S(2)}, u32[]{:S(2)}) %collective-permute-start.4) | collective-permute-done | bytes 81952 | tf_op jit(solution)/shard_map/ppermute | solution.py:412
  88.4 3.5 %shard_map.61 = bf16[8,272,128]{2,1,0:T(8,128)(2,1)} custom-call(bf16[8,128,128]{2,1,0:T(8,128)(2,1)S(1)} %get-tuple-element.16.g_ref, bf16[8,16,128]{2,1,0:T(8,128)(2,1)S(1)} %get-tuple-element.17.up_ref, bf16[8,16,128]{2,1,0:T(8,128)(2,1)S(1)} %get-tuple-element.18.down_ref, bf16[2,160,128]{2,1,0:T(8,128)(2,1)S(1)} %collective-permute-done.4.late_ref, ...), custom_call_target="tpu_custom_call" | custom-call | flops 905969664 | bytes 4194304 | tf_op jit(solution)/shard_map/pallas_call | solution.py:496
  91.9 3.2 %all-to-all-done.1.parts_ref = bf16[32,56,128]{2,1,0:T(8,128)(2,1)S(1)} async-done(((bf16[32,56,128]{2,1,0:T(8,128)(2,1)}), bf16[32,56,128]{2,1,0:T(8,128)(2,1)S(1)}, u32[]{:S(2)}, u32[]{:S(2)}) %all-to-all-start.1) | async-done | bytes 458784 | tf_op jit(solution)/shard_map/all_to_all | solution.py:494
  95.0 0.1 shard_map.62
  95.1 10.2 %all_to_all.25.got_ref = bf16[8,56,128]{2,1,0:T(8,128)(2,1)S(1)} all-to-all(bf16[8,56,128]{2,1,0:T(8,128)(2,1)S(1)} %shard_map.62), channel_id=1, replica_groups=mesh['x'=4,'y'=8,'z'=8,'core'=2] {'y'}, dimensions={0} | all-to-all | bytes 229376 | tf_op jit(solution)/shard_map/all_to_all | solution.py:511
  105.4 7.5 %all_to_all.26 = bf16[4,56,128]{2,1,0:T(8,128)(2,1)S(1)} all-to-all(bf16[4,56,128]{2,1,0:T(8,128)(2,1)S(1)} %shard_map.63), channel_id=1, replica_groups=mesh['x'=4,'y'=8,'z'=8,'core'=2] {'x'}, dimensions={0} | all-to-all | bytes 114688 | tf_op jit(solution)/shard_map/all_to_all | solution.py:512
  112.9 3.5 %all-to-all-start.2 = ((bf16[8,272,128]{2,1,0:T(8,128)(2,1)}), bf16[8,272,128]{2,1,0:T(8,128)(2,1)S(1)}, u32[]{:S(2)}, u32[]{:S(2)}) async-start(bf16[8,272,128]{2,1,0:T(8,128)(2,1)} %shard_map.61), calls=%async_computation.2 | async-start | bytes 1114112 | tf_op jit(solution)/shard_map/all_to_all | solution.py:515
  116.4 24.0 %all_gather.3 = bf16[3584,128]{1,0:T(8,128)(2,1)S(1)} all-gather(bf16[224,128]{1,0:T(8,128)(2,1)S(1)} %bitcast.17), channel_id=1, replica_groups=mesh['x'=4,'y'=8,'z'=8,'core'=2] {'z','core'}, dimensions={0}, use_global_device_ids=true | all-gather | bytes 974848 | tf_op jit(solution)/shard_map/all_gather | solution.py:513
  140.4 0.0 all-to-all-done.2.got_ref
  140.4 1.5 %shard_map.64 = (bf16[8,128,128]{2,1,0:T(8,128)(2,1)}, bf16[8,128,128]{2,1,0:T(8,128)(2,1)}, f32[8,432,128]{2,1,0:T(8,128)}) custom-call(bf16[8,272,128]{2,1,0:T(8,128)(2,1)S(1)} %all-to-all-done.2.got_ref, bf16[64,56,128]{2,1,0:T(8,128)(2,1)S(1)} %bitcast.12), custom_call_target="tpu_custom_call" | custom-call | tf_op jit(solution)/shard_map/pallas_call | solution.py:518
  (12 shorter events, 0.1 us)
Async XLA Ops:
  0.6 56.8 %copy-start = (bf16[3,3,3,128,128]{4,3,2,1,0:T(8,128)(2,1)S(1)}, bf16[3,3,3,128,128]{4,3,2,1,0:T(8,128)(2,1)}, u32[]{:S(2)}) copy-start(bf16[3,3,3,128,128]{4,3,2,1,0:T(8,128)(2,1)} %param.4) | copy-start | bytes 2654212
  17.8 23.2 %all-to-all-start = ((bf16[8,272,128]{2,1,0:T(8,128)(2,1)}), bf16[8,272,128]{2,1,0:T(8,128)(2,1)S(1)}, u32[]{:S(2)}, u32[]{:S(2)}) async-start(bf16[8,272,128]{2,1,0:T(8,128)(2,1)} %shard_map.58), calls=%async_computation | async-start | bytes 1114112 | tf_op jit(solution)/shard_map/all_to_all | solution.py:444
  41.0 7.7 %collective-permute-start = (bf16[2,176,128]{2,1,0:T(8,128)(2,1)S(1)}, bf16[2,176,128]{2,1,0:T(8,128)(2,1)S(1)}, u32[]{:S(2)}, u32[]{:S(2)}) collective-permute-start(bf16[2,176,128]{2,1,0:T(8,128)(2,1)S(1)} %slice.48), channel_id=1, source_target_pairs={{0,128},{128,256},{256,384},{1,129},{129,257},{257,385},{2,130},{1... | collective-permute-start | bytes 270344 | tf_op jit(solution)/shard_map/ppermute | solution.py:412
  48.9 8.2 %collective-permute-start.2 = (bf16[10,64,128]{2,1,0:T(8,128)(2,1)S(1)}, bf16[10,64,128]{2,1,0:T(8,128)(2,1)S(1)}, u32[]{:S(2)}, u32[]{:S(2)}) collective-permute-start(bf16[10,64,128]{2,1,0:T(8,128)(2,1)S(1)} %get-tuple-element.27), channel_id=1, source_target_pairs={{1,2},{3,4},{5,6},{7,8},{9,10},{11,12},{13,14},{2,1},{4,3},{6,5},{... | collective-permute-start | bytes 491528 | tf_op jit(solution)/shard_map/ppermute | solution.py:418
  54.1 3.3 %collective-permute-start.1 = (bf16[10,64,128]{2,1,0:T(8,128)(2,1)S(1)}, bf16[10,64,128]{2,1,0:T(8,128)(2,1)S(1)}, u32[]{:S(2)}, u32[]{:S(2)}) collective-permute-start(bf16[10,64,128]{2,1,0:T(8,128)(2,1)S(1)} %get-tuple-element.28), channel_id=1, source_target_pairs={{0,1},{1,0},{2,3},{3,2},{4,5},{5,4},{6,7},{7,6},{8,9},{9,8},{10,11... | collective-permute-start | bytes 491528 | tf_op jit(solution)/shard_map/ppermute | solution.py:422
  63.3 3.7 %collective-permute-start.3 = (bf16[32,56,128]{2,1,0:T(8,128)(2,1)S(1)}, bf16[32,56,128]{2,1,0:T(8,128)(2,1)S(1)}, u32[]{:S(2)}, u32[]{:S(2)}) collective-permute-start(bf16[32,56,128]{2,1,0:T(8,128)(2,1)S(1)} %get-tuple-element.15), channel_id=1, source_target_pairs={{0,1},{1,0},{2,3},{3,2},{4,5},{5,4},{6,7},{7,6},{8,9},{9,8},{10,11... | collective-permute-start | bytes 1376264 | tf_op jit(solution)/shard_map/ppermute | solution.py:422
  67.8 27.2 %all-to-all-start.1 = ((bf16[32,56,128]{2,1,0:T(8,128)(2,1)}), bf16[32,56,128]{2,1,0:T(8,128)(2,1)S(1)}, u32[]{:S(2)}, u32[]{:S(2)}) async-start(bf16[32,56,128]{2,1,0:T(8,128)(2,1)} %shard_map.60), calls=%async_computation.1 | async-start | bytes 917504 | tf_op jit(solution)/shard_map/all_to_all | solution.py:494
  81.9 6.5 %collective-permute-start.4 = (bf16[2,160,128]{2,1,0:T(8,128)(2,1)S(1)}, bf16[2,160,128]{2,1,0:T(8,128)(2,1)S(1)}, u32[]{:S(2)}, u32[]{:S(2)}) collective-permute-start(bf16[2,160,128]{2,1,0:T(8,128)(2,1)S(1)} %pad_maximum_fusion.1), channel_id=1, source_target_pairs={{128,0},{256,128},{384,256},{129,1},{257,129},{385,257},{130,2},{2... | collective-permute-start | bytes 245768 | tf_op jit(solution)/shard_map/ppermute | solution.py:412
  112.9 27.5 %all-to-all-start.2 = ((bf16[8,272,128]{2,1,0:T(8,128)(2,1)}), bf16[8,272,128]{2,1,0:T(8,128)(2,1)S(1)}, u32[]{:S(2)}, u32[]{:S(2)}) async-start(bf16[8,272,128]{2,1,0:T(8,128)(2,1)} %shard_map.61), calls=%async_computation.2 | async-start | bytes 1114112 | tf_op jit(solution)/shard_map/all_to_all | solution.py:515

commit v11 on v10

--- a/solution.py
+++ b/solution.py
@@ -31,7 +31,7 @@
 root_half = 0.7071067811865476
 f32 = jnp.float32
 bf16 = jnp.bfloat16
-VMEM_LIMIT = 48 * 1024 * 1024
+VMEM_LIMIT = 24 * 1024 * 1024
 
 
 def kernel_call(body, outs, scratch=(), flops=0, **specs):
@@ -45,12 +45,10 @@
     )
 
 
-def pack_body(x_hbm, cot_hbm, out_hbm, x_ref, edge_ref, left_ref, right_ref, sems, own_sems):
-    own = pltpu.make_async_copy(x_hbm, x_ref, own_sems.at[0])
-    own.start()
+def pack_body(x_hbm, cot_hbm, out_ref, left_ref, right_ref, sems):
     copies = [
         pltpu.make_async_copy(
-            hbm.at[row], out_hbm.at[:, pl.ds(place(row), STRIP), :], sems.at[side, row]
+            hbm.at[row], out_ref.at[:, pl.ds(place(row), STRIP), :], sems.at[side, row]
         )
         for side, (hbm, place) in enumerate(((x_hbm, x_place), (cot_hbm, cot_place)))
         for row in range(ROWS)
@@ -59,20 +57,18 @@
         copy.start()
     left_ref[...] = jnp.zeros_like(left_ref)
     right_ref[...] = jnp.zeros_like(right_ref)
-    own.wait()
     for row in range(ROWS):
+        copies[row].wait()
         for strip in range(GROUP):
-            wide = x_ref[row, strip].astype(f32)
+            wide = out_ref[strip, pl.ds(x_place(row), STRIP), :].astype(f32)
             if strip < GROUP - 1:
                 left_ref[strip + 1, pl.ds(row, 1), :] = wide[STRIP - 1 : STRIP]
             if strip > 0:
                 right_ref[strip - 1, pl.ds(row, 1), :] = wide[0:1]
     for strip in range(GROUP):
         pair = jnp.concatenate([left_ref[strip], right_ref[strip]], axis=0)
-        edge_ref[strip] = pair.astype(bf16)
-    edges = pltpu.make_async_copy(edge_ref, out_hbm.at[:, pl.ds(TILE, EDGES), :], own_sems.at[1])
-    edges.start()
-    for copy in copies + [edges]:
+        out_ref[strip, pl.ds(TILE, EDGES), :] = pair.astype(bf16)
+    for copy in copies[ROWS:]:
         copy.wait()
 
 
@@ -135,6 +131,73 @@
     return gate * (1.0 + linear * (1.0 - gate))
 
 
+def spread(ref, frame, place, col_ref, tall_rows, wanted, up_ref=None, down_ref=None):
+    for tall_row in tall_rows:
+        if tall_row < 0:
+            source, at, low, edge_row = up_ref, place, (tall_row + 2) * STRIP, ROWS + tall_row
+        elif tall_row >= ROWS:
+            source, at, low, edge_row = down_ref, place, (tall_row - ROWS) * STRIP, tall_row - ROWS
+        else:
+            source, at, low, edge_row = ref, frame, tall_row * STRIP, tall_row
+        line = source[at, pl.ds(low, STRIP), :]
+        edge_low = TILE if source is ref else RIM
+        edge = source[at, pl.ds(edge_low, EDGES), :].astype(f32)
+        places = []
+        for row_tap in range(3):
+            row = tall_row + 1 - row_tap
+            if row not in wanted:
+                continue
+            if 0 <= row < ROWS:
+                places.append((row_tap, place * TILE + row * STRIP))
+            elif row == -1:
+                places.append((row_tap, FRAMES * TILE + place * RIM))
+            else:
+                places.append((row_tap, FRAMES * TILE + place * RIM + STRIP))
+        place_line(
+            col_ref,
+            line,
+            edge[edge_row : edge_row + 1],
+            edge[ROWS + edge_row : ROWS + edge_row + 1],
+            places,
+        )
+
+
+def products(col_ref, w_ref, lin_ref, ranges, first=0):
+    total = None
+    for tap in range(3):
+        rows = [
+            col_ref[pl.ds(low + (frame + tap - first) * step, count), :]
+            for frame, low, count, step in ranges
+        ]
+        part = jnp.dot(jnp.concatenate(rows, axis=0), w_ref[tap], preferred_element_type=f32)
+        total = part if total is None else total + part
+    at = 0
+    for frame, low, count, step in ranges:
+        out = low if step == TILE else low - (FRAMES - GROUP) * TILE
+        lin_ref[out + frame * step : out + frame * step + count, :] = total[at : at + count]
+        at += count
+
+
+INNER = [(frame, STRIP, (ROWS - 2) * STRIP, TILE) for frame in range(GROUP)]
+OUTER = [
+    piece
+    for frame in range(GROUP)
+    for piece in (
+        (frame, 0, STRIP, TILE),
+        (frame, TILE - STRIP, STRIP, TILE),
+        (frame, FRAMES * TILE, RIM, RIM),
+    )
+]
+
+
+def ahead_body(held_ref, w_ref, col_ref, lin_ref):
+    @pl.loop(0, GROUP)
+    def _(frame):
+        spread(held_ref, frame, frame, col_ref, range(ROWS), range(ROWS))
+
+    products(col_ref, w_ref, lin_ref, INNER[2:], first=2)
+
+
 def forward_body(
     core_ref,
     held_ref,
@@ -142,6 +205,8 @@
     near_ref,
     far_ref,
     w_ref,
+    col_in_ref,
+    lin_in_ref,
     code_ref,
     g_ref,
     g_up_ref,
@@ -162,50 +227,21 @@
             up_ref[...] = above[...]
             down_ref[...] = below[...]
 
-    def spread(ref, frame, place):
-        for tall_row in range(-2, ROWS + 2):
-            if tall_row < 0:
-                source, at, low, edge_row = up_ref, place, (tall_row + 2) * STRIP, ROWS + tall_row
-            elif tall_row >= ROWS:
-                source, at, low, edge_row = down_ref, place, (tall_row - ROWS) * STRIP, tall_row - ROWS
-            else:
-                source, at, low, edge_row = ref, frame, tall_row * STRIP, tall_row
-            line = source[at, pl.ds(low, STRIP), :]
-            edge_low = TILE if source is ref else RIM
-            edge = source[at, pl.ds(edge_low, EDGES), :].astype(f32)
-            places = []
-            for row_tap in range(3):
-                row = tall_row + 1 - row_tap
-                if 0 <= row < ROWS:
-                    places.append((row_tap, place * TILE + row * STRIP))
-                elif row == -1:
-                    places.append((row_tap, FRAMES * TILE + place * RIM))
-                elif row == ROWS:
-                    places.append((row_tap, FRAMES * TILE + place * RIM + STRIP))
-            place_line(
-                col_ref,
-                line,
-                edge[edge_row : edge_row + 1],
-                edge[ROWS + edge_row : ROWS + edge_row + 1],
-                places,
-            )
+    col_ref[2 * TILE : FRAMES * TILE, :] = col_in_ref[...]
+    lin_ref[2 * TILE : GROUP * TILE, :] = lin_in_ref[2 * TILE :, :]
+    tall = range(-1, ROWS + 1)
 
     @pl.loop(0, 2)
     def _(frame):
-        spread(early_ref, frame, frame)
+        spread(early_ref, frame, frame, col_ref, range(-2, ROWS + 2), tall, up_ref, down_ref)
 
     @pl.loop(0, GROUP)
     def _(frame):
-        spread(held_ref, frame, frame + 2)
-
-    for low, step in ((0, TILE), (FRAMES * TILE, RIM)):
-        total = None
-        for tap in range(3):
-            rows = col_ref[low + tap * step : low + (tap + GROUP) * step, :]
-            part = jnp.dot(rows, w_ref[tap], preferred_element_type=f32)
-            total = part if total is None else total + part
-        place = 0 if step == TILE else GROUP * TILE
-        lin_ref[place : place + GROUP * step, :] = total
+        beyond = (-2, -1, ROWS, ROWS + 1)
+        spread(held_ref, frame, frame + 2, col_ref, beyond, tall, up_ref, down_ref)
+        spread(held_ref, frame, frame + 2, col_ref, (0, ROWS - 1), (-1, ROWS))
+
+    products(col_ref, w_ref, lin_ref, INNER[:2] + OUTER)
 
     @pl.loop(0, ROWS)
     def _(row):
@@ -431,15 +467,8 @@
         pack_body,
         out_shape=jax.ShapeDtypeStruct((GROUP, LOAD, CH), bf16),
         in_specs=[pl.BlockSpec(memory_space=pl.ANY)] * 2,
-        out_specs=pl.BlockSpec(memory_space=pl.ANY),
-        scratch_shapes=[
-            pltpu.VMEM((ROWS, GROUP, STRIP, CH), bf16),
-            pltpu.VMEM((GROUP, EDGES, CH), bf16),
-            pltpu.VMEM((GROUP, ROWS, CH), f32),
-            pltpu.VMEM((GROUP, ROWS, CH), f32),
-            pltpu.SemaphoreType.DMA((2, ROWS)),
-            pltpu.SemaphoreType.DMA((2,)),
-        ],
+        scratch_shapes=[pltpu.VMEM((GROUP, ROWS, CH), f32)] * 2
+        + [pltpu.SemaphoreType.DMA((2, ROWS))],
     )(frames.reshape(ROWS, GROUP, STRIP, CH), cotangent.reshape(ROWS, GROUP, STRIP, CH))
     held = lax.all_to_all(packed, "y", 0, 0)
     early = shifted(held[GROUP - 2 :, : HELD + 2 * STRIP], "x", 1)
@@ -462,6 +491,14 @@
     share = PART * -(-27 * CH // (2 * PART * peers))
     mail = jax.ShapeDtypeStruct((peers, share, CH), bf16)
     flops = 2 * GROUP * TILE * 27 * CH * CH
+    ahead = kernel_call(
+        ahead_body,
+        (
+            jax.ShapeDtypeStruct((GROUP * TILE, WIDE), bf16),
+            jax.ShapeDtypeStruct((GROUP * TILE, CH), f32),
+        ),
+        flops=flops // 2,
+    )(held, weights)
     code, g, g_up, g_down, keep, send = kernel_call(
         forward_body,
         (
@@ -481,8 +518,8 @@
         + [pltpu.VMEM((FRAMES, RIM + EDGES + STRIP, CH), bf16)] * 2,
         flops=2 * flops,
         in_specs=[pl.BlockSpec(memory_space=pltpu.SMEM)]
-        + [pl.BlockSpec(memory_space=pltpu.VMEM)] * 5,
-    )(core.astype(jnp.int32).reshape(1), held, early, near, far, weights)
+        + [pl.BlockSpec(memory_space=pltpu.VMEM)] * 7,
+    )(core.astype(jnp.int32).reshape(1), held, early, near, far, weights, *ahead)
 
     chip_sum = kernel_call(
         add_body,

time: 142 us -> 128 us (0.901)
  Pallas kernels: 28.9 us -> 14.1 us
    pallas_call x1, Pallas kernels: 17.1 us -> 2.02 us  [shards(): pl.pallas_call(pack_body, out_shape=jax.ShapeDtypeStruct((GROUP, LOAD, CH...]
    pallas_call x0 -> x1, Pallas kernels: none -> 1.58 us  [shards(): kernel_call(ahead_body, (jax.ShapeDtypeStruct((GROUP * TILE, WIDE), bf16)...]
  transfers between devices with their start and end apart: 8 -> 8, of which waited for: 7 -> 6; matrix products, arithmetic and copies ran while one was open for 1% -> 1% of each run, Pallas kernels for 2% -> 4%
where the time goes in v11:
time: 128 us; the launch traced here: 127 us
  starting transfers between devices  42.1 us (33%)
  blocking collectives  41.7 us (33%)
  waiting for transfers between devices  27.1 us (21%)
  Pallas kernels  14.1 us (11%)
  local copies, waits for them, and re-layouts  1.52 us (1%)
    all_gather x1, blocking collectives, shards(): terms = lax.all_gather(line, lines, tiled=True).reshape(-1, share, CH)  24 us
    all_to_all x1, waiting for transfers between devices, shards(): held = lax.all_to_all(packed, 'y', 0, 0)  15.6 us
    all_to_all x1, starting transfers between devices, shards(): parts = lax.all_to_all(chip_sum, ('x', 'z'), 0, 0)  14.4 us
    all_to_all x1, blocking collectives, shards(): lax.all_to_all(part, 'y', 0, 0)  10.2 us
    all_to_all x1, starting transfers between devices, shards(): held = lax.all_to_all(packed, 'y', 0, 0)  7.66 us
    all_to_all x1, blocking collectives, shards(): line = lax.all_to_all(copies, 'x', 0, 0).reshape(wide * share, CH)  7.52 us
    ppermute x2, starting transfers between devices, shifted(): return lax.ppermute(value, axes, route)  7.49 us
    ppermute x2, starting transfers between devices, swapped(): return lax.ppermute(value, 'core', [(0, 1), (1, 0)])  5.18 us
  transfers between devices with their start and end apart: 8, of which 6 were waited for; matrix products, arithmetic and copies ran while one was open for 1% of the time, Pallas kernels for 4%

profile of v11, /device:TPU:1, one launch (start us, length us, event | category | flops | bytes accessed | tf_op | source)
XLA Modules:
  0.0 127.5 jit_solution(13361923406495320700)
XLA Ops:
  0.6 0.0 copy-start
  0.6 2.0 %shard_map.58 = bf16[8,272,128]{2,1,0:T(8,128)(2,1)} custom-call(bf16[8,8,16,128]{3,2,1,0:T(8,128)(2,1)} %bitcast.16, bf16[8,8,16,128]{3,2,1,0:T(8,128)(2,1)} %bitcast.17), custom_call_target="tpu_custom_call" | custom-call | tf_op jit(solution)/shard_map/pallas_call | solution.py:466
  2.7 7.7 %all-to-all-start = ((bf16[8,272,128]{2,1,0:T(8,128)(2,1)}), bf16[8,272,128]{2,1,0:T(8,128)(2,1)S(1)}, u32[]{:S(2)}, u32[]{:S(2)}) async-start(bf16[8,272,128]{2,1,0:T(8,128)(2,1)} %shard_map.58), calls=%async_computation | async-start | bytes 1114112 | tf_op jit(solution)/shard_map/all_to_all | solution.py:473
  10.3 15.6 %all-to-all-done.held_ref = bf16[8,272,128]{2,1,0:T(8,128)(2,1)S(1)} async-done(((bf16[8,272,128]{2,1,0:T(8,128)(2,1)}), bf16[8,272,128]{2,1,0:T(8,128)(2,1)S(1)}, u32[]{:S(2)}, u32[]{:S(2)}) %all-to-all-start) | async-done | bytes 557088 | tf_op jit(solution)/shard_map/all_to_all | solution.py:473
  25.9 6.2 %collective-permute-start = (bf16[2,176,128]{2,1,0:T(8,128)(2,1)S(1)}, bf16[2,176,128]{2,1,0:T(8,128)(2,1)S(1)}, u32[]{:S(2)}, u32[]{:S(2)}) collective-permute-start(bf16[2,176,128]{2,1,0:T(8,128)(2,1)S(1)} %slice.48), channel_id=1, source_target_pairs={{0,128},{128,256},{256,384},{1,129},{129,257},{257,385},{2,130},{1... | collective-permute-start | bytes 270344 | tf_op jit(solution)/shard_map/ppermute | solution.py:448
  32.2 1.5 %collective-permute-done.early_ref = bf16[2,176,128]{2,1,0:T(8,128)(2,1)S(1)} collective-permute-done((bf16[2,176,128]{2,1,0:T(8,128)(2,1)S(1)}, bf16[2,176,128]{2,1,0:T(8,128)(2,1)S(1)}, u32[]{:S(2)}, u32[]{:S(2)}) %collective-permute-start) | collective-permute-done | bytes 90144 | tf_op jit(solution)/shard_map/ppermute | solution.py:448
  33.7 0.1 broadcast_select_fusion
  33.8 3.3 %collective-permute-start.1 = (bf16[10,64,128]{2,1,0:T(8,128)(2,1)S(1)}, bf16[10,64,128]{2,1,0:T(8,128)(2,1)S(1)}, u32[]{:S(2)}, u32[]{:S(2)}) collective-permute-start(bf16[10,64,128]{2,1,0:T(8,128)(2,1)S(1)} %get-tuple-element.32), channel_id=1, source_target_pairs={{0,1},{1,0},{2,3},{3,2},{4,5},{5,4},{6,7},{7,6},{8,9},{9,8},{10,11... | collective-permute-start | bytes 491528 | tf_op jit(solution)/shard_map/ppermute | solution.py:458
  37.0 3.9 %collective-permute-start.2 = (bf16[10,64,128]{2,1,0:T(8,128)(2,1)S(1)}, bf16[10,64,128]{2,1,0:T(8,128)(2,1)S(1)}, u32[]{:S(2)}, u32[]{:S(2)}) collective-permute-start(bf16[10,64,128]{2,1,0:T(8,128)(2,1)S(1)} %get-tuple-element.31), channel_id=1, source_target_pairs={{1,2},{3,4},{5,6},{7,8},{9,10},{11,12},{13,14},{2,1},{4,3},{6,5},{... | collective-permute-start | bytes 491528 | tf_op jit(solution)/shard_map/ppermute | solution.py:454
  40.9 0.0 copy-done
  40.9 1.6 %shard_map.59 = (bf16[1024,1152]{1,0:T(8,128)(2,1)S(1)}, f32[1024,128]{1,0:T(8,128)S(1)}) custom-call(bf16[8,272,128]{2,1,0:T(8,128)(2,1)S(1)} %all-to-all-done.held_ref, bf16[3,1152,128]{2,1,0:T(8,128)(2,1)S(1)} %bitcast.13), custom_call_target="tpu_custom_call" | custom-call | flops 452984832 | bytes 4194304 | tf_op jit(solution)/shard_map/pallas_call | solution.py:494
  42.5 0.0 collective-permute-done.1.near_ref
  42.5 1.4 %collective-permute-done.2.far_ref = bf16[10,64,128]{2,1,0:T(8,128)(2,1)S(1)} collective-permute-done((bf16[10,64,128]{2,1,0:T(8,128)(2,1)S(1)}, bf16[10,64,128]{2,1,0:T(8,128)(2,1)S(1)}, u32[]{:S(2)}, u32[]{:S(2)}) %collective-permute-start.2) | collective-permute-done | bytes 163872 | tf_op jit(solution)/shard_map/ppermute | solution.py:454
  43.9 4.6 %shard_map.60 = (bf16[8,128,128]{2,1,0:T(8,128)(2,1)S(1)}, bf16[8,128,128]{2,1,0:T(8,128)(2,1)S(1)}, bf16[8,16,128]{2,1,0:T(8,128)(2,1)S(1)}, bf16[8,16,128]{2,1...) custom-call(s32[1]{0:T(128)} %bitcast.core_ref, ...), custom_call_target="tpu_custom_call" | custom-call | flops 1811939328 | bytes 4194304 | tf_op jit(solution)/shard_map/pallas_call | solution.py:502
  48.5 1.9 %collective-permute-start.3 = (bf16[32,56,128]{2,1,0:T(8,128)(2,1)S(1)}, bf16[32,56,128]{2,1,0:T(8,128)(2,1)S(1)}, u32[]{:S(2)}, u32[]{:S(2)}) collective-permute-start(bf16[32,56,128]{2,1,0:T(8,128)(2,1)S(1)} %get-tuple-element.19), channel_id=1, source_target_pairs={{0,1},{1,0},{2,3},{3,2},{4,5},{5,4},{6,7},{7,6},{8,9},{9,8},{10,11... | collective-permute-start | bytes 1376264 | tf_op jit(solution)/shard_map/ppermute | solution.py:458
  50.5 1.8 %collective-permute-done.3.other_ref = bf16[32,56,128]{2,1,0:T(8,128)(2,1)S(1)} collective-permute-done((bf16[32,56,128]{2,1,0:T(8,128)(2,1)S(1)}, bf16[32,56,128]{2,1,0:T(8,128)(2,1)S(1)}, u32[]{:S(2)}, u32[]{:S(2)}) %collective-permute-start.3) | collective-permute-done | bytes 458784 | tf_op jit(solution)/shard_map/ppermute | solution.py:458
  52.3 0.8 shard_map.61
  53.1 14.4 %all-to-all-start.1 = ((bf16[32,56,128]{2,1,0:T(8,128)(2,1)}), bf16[32,56,128]{2,1,0:T(8,128)(2,1)S(1)}, u32[]{:S(2)}, u32[]{:S(2)}) async-start(bf16[32,56,128]{2,1,0:T(8,128)(2,1)} %shard_map.61), calls=%async_computation.1 | async-start | bytes 917504 | tf_op jit(solution)/shard_map/all_to_all | solution.py:531
  67.5 1.3 %collective-permute-start.4 = (bf16[2,160,128]{2,1,0:T(8,128)(2,1)S(1)}, bf16[2,160,128]{2,1,0:T(8,128)(2,1)S(1)}, u32[]{:S(2)}, u32[]{:S(2)}) collective-permute-start(bf16[2,160,128]{2,1,0:T(8,128)(2,1)S(1)} %pad_maximum_fusion.1), channel_id=1, source_target_pairs={{128,0},{256,128},{384,256},{129,1},{257,129},{385,257},{130,2},{2... | collective-permute-start | bytes 245768 | tf_op jit(solution)/shard_map/ppermute | solution.py:448
  68.8 0.1 reverse_bitcast_fusion
  68.9 1.4 %copy.6 = bf16[3,3,3,128,128]{4,3,2,1,0:T(8,128)(2,1)S(1)} copy(bf16[3,3,3,128,128]{3,4,2,1,0:T(8,128)(2,1)S(1)} %reverse_bitcast_fusion) | data formatting | bytes 1769472 | tf_op jit(solution)/shard_map/transpose | solution.py:464
  70.3 3.7 %collective-permute-done.4.late_ref = bf16[2,160,128]{2,1,0:T(8,128)(2,1)S(1)} collective-permute-done((bf16[2,160,128]{2,1,0:T(8,128)(2,1)S(1)}, bf16[2,160,128]{2,1,0:T(8,128)(2,1)S(1)}, u32[]{:S(2)}, u32[]{:S(2)}) %collective-permute-start.4) | collective-permute-done | bytes 81952 | tf_op jit(solution)/shard_map/ppermute | solution.py:448
  74.0 3.5 %shard_map.62 = bf16[8,272,128]{2,1,0:T(8,128)(2,1)} custom-call(bf16[8,128,128]{2,1,0:T(8,128)(2,1)S(1)} %get-tuple-element.20.g_ref, bf16[8,16,128]{2,1,0:T(8,128)(2,1)S(1)} %get-tuple-element.21.up_ref, bf16[8,16,128]{2,1,0:T(8,128)(2,1)S(1)} %get-tuple-element.22.down_ref, bf16[2,160,128]{2,1,0:T(8,128)(2,1)S(1)} %collective-permute-done.4.late_ref, ...), custom_call_target="tpu_custom_call" | custom-call | flops 905969664 | bytes 4194304 | tf_op jit(solution)/shard_map/pallas_call | solution.py:533
  77.4 3.2 %all-to-all-done.1.parts_ref = bf16[32,56,128]{2,1,0:T(8,128)(2,1)S(1)} async-done(((bf16[32,56,128]{2,1,0:T(8,128)(2,1)}), bf16[32,56,128]{2,1,0:T(8,128)(2,1)S(1)}, u32[]{:S(2)}, u32[]{:S(2)}) %all-to-all-start.1) | async-done | bytes 458784 | tf_op jit(solution)/shard_map/all_to_all | solution.py:531
  80.6 0.1 shard_map.63
  80.7 10.2 %all_to_all.25.got_ref = bf16[8,56,128]{2,1,0:T(8,128)(2,1)S(1)} all-to-all(bf16[8,56,128]{2,1,0:T(8,128)(2,1)S(1)} %shard_map.63), channel_id=1, replica_groups=mesh['x'=4,'y'=8,'z'=8,'core'=2] {'y'}, dimensions={0} | all-to-all | bytes 229376 | tf_op jit(solution)/shard_map/all_to_all | solution.py:548
  90.9 7.5 %all_to_all.26 = bf16[4,56,128]{2,1,0:T(8,128)(2,1)S(1)} all-to-all(bf16[4,56,128]{2,1,0:T(8,128)(2,1)S(1)} %shard_map.64), channel_id=1, replica_groups=mesh['x'=4,'y'=8,'z'=8,'core'=2] {'x'}, dimensions={0} | all-to-all | bytes 114688 | tf_op jit(solution)/shard_map/all_to_all | solution.py:549
  98.5 3.5 %all-to-all-start.2 = ((bf16[8,272,128]{2,1,0:T(8,128)(2,1)}), bf16[8,272,128]{2,1,0:T(8,128)(2,1)S(1)}, u32[]{:S(2)}, u32[]{:S(2)}) async-start(bf16[8,272,128]{2,1,0:T(8,128)(2,1)} %shard_map.62), calls=%async_computation.2 | async-start | bytes 1114112 | tf_op jit(solution)/shard_map/all_to_all | solution.py:552
  102.0 24.0 %all_gather.3 = bf16[3584,128]{1,0:T(8,128)(2,1)S(1)} all-gather(bf16[224,128]{1,0:T(8,128)(2,1)S(1)} %bitcast.18), channel_id=1, replica_groups=mesh['x'=4,'y'=8,'z'=8,'core'=2] {'z','core'}, dimensions={0}, use_global_device_ids=true | all-gather | bytes 974848 | tf_op jit(solution)/shard_map/all_gather | solution.py:550
  126.0 0.0 all-to-all-done.2.got_ref
  126.0 1.5 %shard_map.65 = (bf16[8,128,128]{2,1,0:T(8,128)(2,1)}, bf16[8,128,128]{2,1,0:T(8,128)(2,1)}, f32[8,432,128]{2,1,0:T(8,128)}) custom-call(bf16[8,272,128]{2,1,0:T(8,128)(2,1)S(1)} %all-to-all-done.2.got_ref, bf16[64,56,128]{2,1,0:T(8,128)(2,1)S(1)} %bitcast.12), custom_call_target="tpu_custom_call" | custom-call | tf_op jit(solution)/shard_map/pallas_call | solution.py:555
  (12 shorter events, 0.1 us)
Async XLA Ops:
  0.6 40.3 %copy-start = (bf16[3,3,3,128,128]{4,3,2,1,0:T(8,128)(2,1)S(1)}, bf16[3,3,3,128,128]{4,3,2,1,0:T(8,128)(2,1)}, u32[]{:S(2)}) copy-start(bf16[3,3,3,128,128]{4,3,2,1,0:T(8,128)(2,1)} %param.4) | copy-start | bytes 2654212
  2.7 23.2 %all-to-all-start = ((bf16[8,272,128]{2,1,0:T(8,128)(2,1)}), bf16[8,272,128]{2,1,0:T(8,128)(2,1)S(1)}, u32[]{:S(2)}, u32[]{:S(2)}) async-start(bf16[8,272,128]{2,1,0:T(8,128)(2,1)} %shard_map.58), calls=%async_computation | async-start | bytes 1114112 | tf_op jit(solution)/shard_map/all_to_all | solution.py:473
  25.9 7.7 %collective-permute-start = (bf16[2,176,128]{2,1,0:T(8,128)(2,1)S(1)}, bf16[2,176,128]{2,1,0:T(8,128)(2,1)S(1)}, u32[]{:S(2)}, u32[]{:S(2)}) collective-permute-start(bf16[2,176,128]{2,1,0:T(8,128)(2,1)S(1)} %slice.48), channel_id=1, source_target_pairs={{0,128},{128,256},{256,384},{1,129},{129,257},{257,385},{2,130},{1... | collective-permute-start | bytes 270344 | tf_op jit(solution)/shard_map/ppermute | solution.py:448
  33.8 8.8 %collective-permute-start.1 = (bf16[10,64,128]{2,1,0:T(8,128)(2,1)S(1)}, bf16[10,64,128]{2,1,0:T(8,128)(2,1)S(1)}, u32[]{:S(2)}, u32[]{:S(2)}) collective-permute-start(bf16[10,64,128]{2,1,0:T(8,128)(2,1)S(1)} %get-tuple-element.32), channel_id=1, source_target_pairs={{0,1},{1,0},{2,3},{3,2},{4,5},{5,4},{6,7},{7,6},{8,9},{9,8},{10,11... | collective-permute-start | bytes 491528 | tf_op jit(solution)/shard_map/ppermute | solution.py:458
  37.0 6.9 %collective-permute-start.2 = (bf16[10,64,128]{2,1,0:T(8,128)(2,1)S(1)}, bf16[10,64,128]{2,1,0:T(8,128)(2,1)S(1)}, u32[]{:S(2)}, u32[]{:S(2)}) collective-permute-start(bf16[10,64,128]{2,1,0:T(8,128)(2,1)S(1)} %get-tuple-element.31), channel_id=1, source_target_pairs={{1,2},{3,4},{5,6},{7,8},{9,10},{11,12},{13,14},{2,1},{4,3},{6,5},{... | collective-permute-start | bytes 491528 | tf_op jit(solution)/shard_map/ppermute | solution.py:454
  48.5 3.7 %collective-permute-start.3 = (bf16[32,56,128]{2,1,0:T(8,128)(2,1)S(1)}, bf16[32,56,128]{2,1,0:T(8,128)(2,1)S(1)}, u32[]{:S(2)}, u32[]{:S(2)}) collective-permute-start(bf16[32,56,128]{2,1,0:T(8,128)(2,1)S(1)} %get-tuple-element.19), channel_id=1, source_target_pairs={{0,1},{1,0},{2,3},{3,2},{4,5},{5,4},{6,7},{7,6},{8,9},{9,8},{10,11... | collective-permute-start | bytes 1376264 | tf_op jit(solution)/shard_map/ppermute | solution.py:458
  53.1 27.5 %all-to-all-start.1 = ((bf16[32,56,128]{2,1,0:T(8,128)(2,1)}), bf16[32,56,128]{2,1,0:T(8,128)(2,1)S(1)}, u32[]{:S(2)}, u32[]{:S(2)}) async-start(bf16[32,56,128]{2,1,0:T(8,128)(2,1)} %shard_map.61), calls=%async_computation.1 | async-start | bytes 917504 | tf_op jit(solution)/shard_map/all_to_all | solution.py:531
  67.5 6.5 %collective-permute-start.4 = (bf16[2,160,128]{2,1,0:T(8,128)(2,1)S(1)}, bf16[2,160,128]{2,1,0:T(8,128)(2,1)S(1)}, u32[]{:S(2)}, u32[]{:S(2)}) collective-permute-start(bf16[2,160,128]{2,1,0:T(8,128)(2,1)S(1)} %pad_maximum_fusion.1), channel_id=1, source_target_pairs={{128,0},{256,128},{384,256},{129,1},{257,129},{385,257},{130,2},{2... | collective-permute-start | bytes 245768 | tf_op jit(solution)/shard_map/ppermute | solution.py:448
  98.5 27.5 %all-to-all-start.2 = ((bf16[8,272,128]{2,1,0:T(8,128)(2,1)}), bf16[8,272,128]{2,1,0:T(8,128)(2,1)S(1)}, u32[]{:S(2)}, u32[]{:S(2)}) async-start(bf16[8,272,128]{2,1,0:T(8,128)(2,1)} %shard_map.62), calls=%async_computation.2 | async-start | bytes 1114112 | tf_op jit(solution)/shard_map/all_to_all | solution.py:552

commit v12 on v11

--- a/solution.py
+++ b/solution.py
@@ -473,23 +473,6 @@
     held = lax.all_to_all(packed, "y", 0, 0)
     early = shifted(held[GROUP - 2 :, : HELD + 2 * STRIP], "x", 1)
 
-    def edge_rows(*places):
-        pieces = [
-            jnp.concatenate([early[:, low:high], held[:, low:high]], axis=0)
-            for low, high in places
-        ]
-        return pieces[0] if len(pieces) == 1 else jnp.concatenate(pieces, axis=1)
-
-    core = lax.axis_index("core")
-    last = edge_rows((TILE - RIM, HELD + STRIP))
-    first = edge_rows((0, RIM), (TILE, HELD), (HELD + STRIP, HELD + 2 * STRIP))
-    near = swapped(jnp.where(core == 0, last, first))
-    far = between_chips(jnp.where(core == 0, first, last))
-
-    devices = lax.axis_size(("x", "y", "z", "core"))
-    peers, wide = lax.axis_size(("x", "z")), lax.axis_size("x")
-    share = PART * -(-27 * CH // (2 * PART * peers))
-    mail = jax.ShapeDtypeStruct((peers, share, CH), bf16)
     flops = 2 * GROUP * TILE * 27 * CH * CH
     ahead = kernel_call(
         ahead_body,
@@ -499,6 +482,25 @@
         ),
         flops=flops // 2,
     )(held, weights)
+    early, ahead = lax.optimization_barrier((early, tuple(ahead)))
+
+    def edge_rows(*places):
+        pieces = [
+            jnp.concatenate([early[:, low:high], held[:, low:high]], axis=0)
+            for low, high in places
+        ]
+        return pieces[0] if len(pieces) == 1 else jnp.concatenate(pieces, axis=1)
+
+    core = lax.axis_index("core")
+    last = edge_rows((TILE - RIM, HELD + STRIP))
+    first = edge_rows((0, RIM), (TILE, HELD), (HELD + STRIP, HELD + 2 * STRIP))
+    near = swapped(jnp.where(core == 0, last, first))
+    far = between_chips(jnp.where(core == 0, first, last))
+
+    devices = lax.axis_size(("x", "y", "z", "core"))
+    peers, wide = lax.axis_size(("x", "z")), lax.axis_size("x")
+    share = PART * -(-27 * CH // (2 * PART * peers))
+    mail = jax.ShapeDtypeStruct((peers, share, CH), bf16)
     code, g, g_up, g_down, keep, send = kernel_call(
         forward_body,
         (

time: 128 us -> 128 us (level)
    ppermute x1, waiting for transfers between devices: 1.38 us -> 2.98 us  [between_chips(): lax.ppermute(value, ('z', 'core'), pairs + [(j, i) for i, j in pairs])]
    ppermute x2, waiting for transfers between devices: 5.18 us -> 3.71 us  [shifted(): return lax.ppermute(value, axes, route)]
  transfers between devices with their start and end apart: 8 -> 8, of which waited for: 6 -> 5; matrix products, arithmetic and copies ran while one was open for 1% -> 1% of each run, Pallas kernels for 4% -> 4%
where the time goes in v12:
time: 128 us; the launch traced here: 127 us
  starting transfers between devices  42 us (33%)
  blocking collectives  41.7 us (33%)
  waiting for transfers between devices  27.2 us (21%)
  Pallas kernels  14.1 us (11%)
  local copies, waits for them, and re-layouts  1.5 us (1%)
    all_gather x1, blocking collectives, shards(): terms = lax.all_gather(line, lines, tiled=True).reshape(-1, share, CH)  24 us
    all_to_all x1, waiting for transfers between devices, shards(): held = lax.all_to_all(packed, 'y', 0, 0)  15.6 us
    all_to_all x1, starting transfers between devices, shards(): parts = lax.all_to_all(chip_sum, ('x', 'z'), 0, 0)  14.4 us
    all_to_all x1, blocking collectives, shards(): lax.all_to_all(part, 'y', 0, 0)  10.2 us
    all_to_all x1, starting transfers between devices, shards(): held = lax.all_to_all(packed, 'y', 0, 0)  7.66 us
    all_to_all x1, blocking collectives, shards(): line = lax.all_to_all(copies, 'x', 0, 0).reshape(wide * share, CH)  7.52 us
    ppermute x2, starting transfers between devices, shifted(): return lax.ppermute(value, axes, route)  7.49 us
    ppermute x2, starting transfers between devices, swapped(): return lax.ppermute(value, 'core', [(0, 1), (1, 0)])  5.05 us
  transfers between devices with their start and end apart: 8, of which 5 were waited for; matrix products, arithmetic and copies ran while one was open for 1% of the time, Pallas kernels for 4%

profile of v12, /device:TPU:1, one launch (start us, length us, event | category | flops | bytes accessed | tf_op | source)
XLA Modules:
  0.0 127.5 jit_solution(16229909380953647580)
XLA Ops:
  0.6 0.0 copy-start
  0.6 2.0 %shard_map.58 = bf16[8,272,128]{2,1,0:T(8,128)(2,1)} custom-call(bf16[8,8,16,128]{3,2,1,0:T(8,128)(2,1)} %bitcast.16, bf16[8,8,16,128]{3,2,1,0:T(8,128)(2,1)} %bitcast.17), custom_call_target="tpu_custom_call" | custom-call | tf_op jit(solution)/shard_map/pallas_call | solution.py:466
  2.7 7.7 %all-to-all-start = ((bf16[8,272,128]{2,1,0:T(8,128)(2,1)}), bf16[8,272,128]{2,1,0:T(8,128)(2,1)S(1)}, u32[]{:S(2)}, u32[]{:S(2)}) async-start(bf16[8,272,128]{2,1,0:T(8,128)(2,1)} %shard_map.58), calls=%async_computation | async-start | bytes 1114112 | tf_op jit(solution)/shard_map/all_to_all | solution.py:473
  10.3 15.6 %all-to-all-done.held_ref = bf16[8,272,128]{2,1,0:T(8,128)(2,1)S(1)} async-done(((bf16[8,272,128]{2,1,0:T(8,128)(2,1)}), bf16[8,272,128]{2,1,0:T(8,128)(2,1)S(1)}, u32[]{:S(2)}, u32[]{:S(2)}) %all-to-all-start) | async-done | bytes 557088 | tf_op jit(solution)/shard_map/all_to_all | solution.py:473
  25.9 6.2 %collective-permute-start = (bf16[2,176,128]{2,1,0:T(8,128)(2,1)S(1)}, bf16[2,176,128]{2,1,0:T(8,128)(2,1)S(1)}, u32[]{:S(2)}, u32[]{:S(2)}) collective-permute-start(bf16[2,176,128]{2,1,0:T(8,128)(2,1)S(1)} %slice.48), channel_id=1, source_target_pairs={{0,128},{128,256},{256,384},{1,129},{129,257},{257,385},{2,130},{1... | collective-permute-start | bytes 270344 | tf_op jit(solution)/shard_map/ppermute | solution.py:448
  32.2 0.0 copy-done
  32.2 1.6 %shard_map.59 = (bf16[1024,1152]{1,0:T(8,128)(2,1)S(1)}, f32[1024,128]{1,0:T(8,128)S(1)}) custom-call(bf16[8,272,128]{2,1,0:T(8,128)(2,1)S(1)} %all-to-all-done.held_ref, bf16[3,1152,128]{2,1,0:T(8,128)(2,1)S(1)} %bitcast.13), custom_call_target="tpu_custom_call" | custom-call | flops 452984832 | bytes 4194304 | tf_op jit(solution)/shard_map/pallas_call | solution.py:477
  33.8 0.0 collective-permute-done.early_ref
  33.8 0.1 broadcast_select_fusion
  33.9 3.1 %collective-permute-start.1 = (bf16[10,64,128]{2,1,0:T(8,128)(2,1)S(1)}, bf16[10,64,128]{2,1,0:T(8,128)(2,1)S(1)}, u32[]{:S(2)}, u32[]{:S(2)}) collective-permute-start(bf16[10,64,128]{2,1,0:T(8,128)(2,1)S(1)} %get-tuple-element.38), channel_id=1, source_target_pairs={{0,1},{1,0},{2,3},{3,2},{4,5},{5,4},{6,7},{7,6},{8,9},{9,8},{10,11... | collective-permute-start | bytes 491528 | tf_op jit(solution)/shard_map/ppermute | solution.py:458
  37.0 3.9 %collective-permute-start.2 = (bf16[10,64,128]{2,1,0:T(8,128)(2,1)S(1)}, bf16[10,64,128]{2,1,0:T(8,128)(2,1)S(1)}, u32[]{:S(2)}, u32[]{:S(2)}) collective-permute-start(bf16[10,64,128]{2,1,0:T(8,128)(2,1)S(1)} %get-tuple-element.37), channel_id=1, source_target_pairs={{1,2},{3,4},{5,6},{7,8},{9,10},{11,12},{13,14},{2,1},{4,3},{6,5},{... | collective-permute-start | bytes 491528 | tf_op jit(solution)/shard_map/ppermute | solution.py:454
  40.9 0.0 collective-permute-done.1.near_ref
  40.9 3.0 %collective-permute-done.2.far_ref = bf16[10,64,128]{2,1,0:T(8,128)(2,1)S(1)} collective-permute-done((bf16[10,64,128]{2,1,0:T(8,128)(2,1)S(1)}, bf16[10,64,128]{2,1,0:T(8,128)(2,1)S(1)}, u32[]{:S(2)}, u32[]{:S(2)}) %collective-permute-start.2) | collective-permute-done | bytes 163872 | tf_op jit(solution)/shard_map/ppermute | solution.py:454
  43.9 4.6 %shard_map.60 = (bf16[8,128,128]{2,1,0:T(8,128)(2,1)S(1)}, bf16[8,128,128]{2,1,0:T(8,128)(2,1)S(1)}, bf16[8,16,128]{2,1,0:T(8,128)(2,1)S(1)}, bf16[8,16,128]{2,1...) custom-call(s32[1]{0:T(128)} %bitcast.core_ref, ...), custom_call_target="tpu_custom_call" | custom-call | flops 1811939328 | bytes 4194304 | tf_op jit(solution)/shard_map/pallas_call | solution.py:504
  48.5 1.9 %collective-permute-start.3 = (bf16[32,56,128]{2,1,0:T(8,128)(2,1)S(1)}, bf16[32,56,128]{2,1,0:T(8,128)(2,1)S(1)}, u32[]{:S(2)}, u32[]{:S(2)}) collective-permute-start(bf16[32,56,128]{2,1,0:T(8,128)(2,1)S(1)} %get-tuple-element.25), channel_id=1, source_target_pairs={{0,1},{1,0},{2,3},{3,2},{4,5},{5,4},{6,7},{7,6},{8,9},{9,8},{10,11... | collective-permute-start | bytes 1376264 | tf_op jit(solution)/shard_map/ppermute | solution.py:458
  50.5 1.8 %collective-permute-done.3.other_ref = bf16[32,56,128]{2,1,0:T(8,128)(2,1)S(1)} collective-permute-done((bf16[32,56,128]{2,1,0:T(8,128)(2,1)S(1)}, bf16[32,56,128]{2,1,0:T(8,128)(2,1)S(1)}, u32[]{:S(2)}, u32[]{:S(2)}) %collective-permute-start.3) | collective-permute-done | bytes 458784 | tf_op jit(solution)/shard_map/ppermute | solution.py:458
  52.3 0.8 shard_map.61
  53.1 14.4 %all-to-all-start.1 = ((bf16[32,56,128]{2,1,0:T(8,128)(2,1)}), bf16[32,56,128]{2,1,0:T(8,128)(2,1)S(1)}, u32[]{:S(2)}, u32[]{:S(2)}) async-start(bf16[32,56,128]{2,1,0:T(8,128)(2,1)} %shard_map.61), calls=%async_computation.1 | async-start | bytes 917504 | tf_op jit(solution)/shard_map/all_to_all | solution.py:533
  67.5 1.3 %collective-permute-start.4 = (bf16[2,160,128]{2,1,0:T(8,128)(2,1)S(1)}, bf16[2,160,128]{2,1,0:T(8,128)(2,1)S(1)}, u32[]{:S(2)}, u32[]{:S(2)}) collective-permute-start(bf16[2,160,128]{2,1,0:T(8,128)(2,1)S(1)} %pad_maximum_fusion.1), channel_id=1, source_target_pairs={{128,0},{256,128},{384,256},{129,1},{257,129},{385,257},{130,2},{2... | collective-permute-start | bytes 245768 | tf_op jit(solution)/shard_map/ppermute | solution.py:448
  68.8 0.1 reverse_bitcast_fusion
  68.9 1.4 %copy.6 = bf16[3,3,3,128,128]{4,3,2,1,0:T(8,128)(2,1)S(1)} copy(bf16[3,3,3,128,128]{3,4,2,1,0:T(8,128)(2,1)S(1)} %reverse_bitcast_fusion) | data formatting | bytes 1769472 | tf_op jit(solution)/shard_map/transpose | solution.py:464
  70.3 3.7 %collective-permute-done.4.late_ref = bf16[2,160,128]{2,1,0:T(8,128)(2,1)S(1)} collective-permute-done((bf16[2,160,128]{2,1,0:T(8,128)(2,1)S(1)}, bf16[2,160,128]{2,1,0:T(8,128)(2,1)S(1)}, u32[]{:S(2)}, u32[]{:S(2)}) %collective-permute-start.4) | collective-permute-done | bytes 81952 | tf_op jit(solution)/shard_map/ppermute | solution.py:448
  74.0 3.5 %shard_map.62 = bf16[8,272,128]{2,1,0:T(8,128)(2,1)} custom-call(bf16[8,128,128]{2,1,0:T(8,128)(2,1)S(1)} %get-tuple-element.26.g_ref, bf16[8,16,128]{2,1,0:T(8,128)(2,1)S(1)} %get-tuple-element.27.up_ref, bf16[8,16,128]{2,1,0:T(8,128)(2,1)S(1)} %get-tuple-element.28.down_ref, bf16[2,160,128]{2,1,0:T(8,128)(2,1)S(1)} %collective-permute-done.4.late_ref, ...), custom_call_target="tpu_custom_call" | custom-call | flops 905969664 | bytes 4194304 | tf_op jit(solution)/shard_map/pallas_call | solution.py:535
  77.4 3.2 %all-to-all-done.1.parts_ref = bf16[32,56,128]{2,1,0:T(8,128)(2,1)S(1)} async-done(((bf16[32,56,128]{2,1,0:T(8,128)(2,1)}), bf16[32,56,128]{2,1,0:T(8,128)(2,1)S(1)}, u32[]{:S(2)}, u32[]{:S(2)}) %all-to-all-start.1) | async-done | bytes 458784 | tf_op jit(solution)/shard_map/all_to_all | solution.py:533
  80.6 0.1 shard_map.63
  80.7 10.2 %all_to_all.25.got_ref = bf16[8,56,128]{2,1,0:T(8,128)(2,1)S(1)} all-to-all(bf16[8,56,128]{2,1,0:T(8,128)(2,1)S(1)} %shard_map.63), channel_id=1, replica_groups=mesh['x'=4,'y'=8,'z'=8,'core'=2] {'y'}, dimensions={0} | all-to-all | bytes 229376 | tf_op jit(solution)/shard_map/all_to_all | solution.py:550
  90.9 7.5 %all_to_all.26 = bf16[4,56,128]{2,1,0:T(8,128)(2,1)S(1)} all-to-all(bf16[4,56,128]{2,1,0:T(8,128)(2,1)S(1)} %shard_map.64), channel_id=1, replica_groups=mesh['x'=4,'y'=8,'z'=8,'core'=2] {'x'}, dimensions={0} | all-to-all | bytes 114688 | tf_op jit(solution)/shard_map/all_to_all | solution.py:551
  98.5 3.5 %all-to-all-start.2 = ((bf16[8,272,128]{2,1,0:T(8,128)(2,1)}), bf16[8,272,128]{2,1,0:T(8,128)(2,1)S(1)}, u32[]{:S(2)}, u32[]{:S(2)}) async-start(bf16[8,272,128]{2,1,0:T(8,128)(2,1)} %shard_map.62), calls=%async_computation.2 | async-start | bytes 1114112 | tf_op jit(solution)/shard_map/all_to_all | solution.py:554
  102.0 24.0 %all_gather.3 = bf16[3584,128]{1,0:T(8,128)(2,1)S(1)} all-gather(bf16[224,128]{1,0:T(8,128)(2,1)S(1)} %bitcast.18), channel_id=1, replica_groups=mesh['x'=4,'y'=8,'z'=8,'core'=2] {'z','core'}, dimensions={0}, use_global_device_ids=true | all-gather | bytes 974848 | tf_op jit(solution)/shard_map/all_gather | solution.py:552
  126.0 0.0 all-to-all-done.2.got_ref
  126.0 1.5 %shard_map.65 = (bf16[8,128,128]{2,1,0:T(8,128)(2,1)}, bf16[8,128,128]{2,1,0:T(8,128)(2,1)}, f32[8,432,128]{2,1,0:T(8,128)}) custom-call(bf16[8,272,128]{2,1,0:T(8,128)(2,1)S(1)} %all-to-all-done.2.got_ref, bf16[64,56,128]{2,1,0:T(8,128)(2,1)S(1)} %bitcast.12), custom_call_target="tpu_custom_call" | custom-call | tf_op jit(solution)/shard_map/pallas_call | solution.py:557
  (12 shorter events, 0.1 us)
Async XLA Ops:
  0.6 31.5 %copy-start = (bf16[3,3,3,128,128]{4,3,2,1,0:T(8,128)(2,1)S(1)}, bf16[3,3,3,128,128]{4,3,2,1,0:T(8,128)(2,1)}, u32[]{:S(2)}) copy-start(bf16[3,3,3,128,128]{4,3,2,1,0:T(8,128)(2,1)} %param.4) | copy-start | bytes 2654212
  2.7 23.2 %all-to-all-start = ((bf16[8,272,128]{2,1,0:T(8,128)(2,1)}), bf16[8,272,128]{2,1,0:T(8,128)(2,1)S(1)}, u32[]{:S(2)}, u32[]{:S(2)}) async-start(bf16[8,272,128]{2,1,0:T(8,128)(2,1)} %shard_map.58), calls=%async_computation | async-start | bytes 1114112 | tf_op jit(solution)/shard_map/all_to_all | solution.py:473
  25.9 7.8 %collective-permute-start = (bf16[2,176,128]{2,1,0:T(8,128)(2,1)S(1)}, bf16[2,176,128]{2,1,0:T(8,128)(2,1)S(1)}, u32[]{:S(2)}, u32[]{:S(2)}) collective-permute-start(bf16[2,176,128]{2,1,0:T(8,128)(2,1)S(1)} %slice.48), channel_id=1, source_target_pairs={{0,128},{128,256},{256,384},{1,129},{129,257},{257,385},{2,130},{1... | collective-permute-start | bytes 270344 | tf_op jit(solution)/shard_map/ppermute | solution.py:448
  33.9 7.0 %collective-permute-start.1 = (bf16[10,64,128]{2,1,0:T(8,128)(2,1)S(1)}, bf16[10,64,128]{2,1,0:T(8,128)(2,1)S(1)}, u32[]{:S(2)}, u32[]{:S(2)}) collective-permute-start(bf16[10,64,128]{2,1,0:T(8,128)(2,1)S(1)} %get-tuple-element.38), channel_id=1, source_target_pairs={{0,1},{1,0},{2,3},{3,2},{4,5},{5,4},{6,7},{7,6},{8,9},{9,8},{10,11... | collective-permute-start | bytes 491528 | tf_op jit(solution)/shard_map/ppermute | solution.py:458
  37.0 6.9 %collective-permute-start.2 = (bf16[10,64,128]{2,1,0:T(8,128)(2,1)S(1)}, bf16[10,64,128]{2,1,0:T(8,128)(2,1)S(1)}, u32[]{:S(2)}, u32[]{:S(2)}) collective-permute-start(bf16[10,64,128]{2,1,0:T(8,128)(2,1)S(1)} %get-tuple-element.37), channel_id=1, source_target_pairs={{1,2},{3,4},{5,6},{7,8},{9,10},{11,12},{13,14},{2,1},{4,3},{6,5},{... | collective-permute-start | bytes 491528 | tf_op jit(solution)/shard_map/ppermute | solution.py:454
  48.5 3.7 %collective-permute-start.3 = (bf16[32,56,128]{2,1,0:T(8,128)(2,1)S(1)}, bf16[32,56,128]{2,1,0:T(8,128)(2,1)S(1)}, u32[]{:S(2)}, u32[]{:S(2)}) collective-permute-start(bf16[32,56,128]{2,1,0:T(8,128)(2,1)S(1)} %get-tuple-element.25), channel_id=1, source_target_pairs={{0,1},{1,0},{2,3},{3,2},{4,5},{5,4},{6,7},{7,6},{8,9},{9,8},{10,11... | collective-permute-start | bytes 1376264 | tf_op jit(solution)/shard_map/ppermute | solution.py:458
  53.1 27.5 %all-to-all-start.1 = ((bf16[32,56,128]{2,1,0:T(8,128)(2,1)}), bf16[32,56,128]{2,1,0:T(8,128)(2,1)S(1)}, u32[]{:S(2)}, u32[]{:S(2)}) async-start(bf16[32,56,128]{2,1,0:T(8,128)(2,1)} %shard_map.61), calls=%async_computation.1 | async-start | bytes 917504 | tf_op jit(solution)/shard_map/all_to_all | solution.py:533
  67.5 6.5 %collective-permute-start.4 = (bf16[2,160,128]{2,1,0:T(8,128)(2,1)S(1)}, bf16[2,160,128]{2,1,0:T(8,128)(2,1)S(1)}, u32[]{:S(2)}, u32[]{:S(2)}) collective-permute-start(bf16[2,160,128]{2,1,0:T(8,128)(2,1)S(1)} %pad_maximum_fusion.1), channel_id=1, source_target_pairs={{128,0},{256,128},{384,256},{129,1},{257,129},{385,257},{130,2},{2... | collective-permute-start | bytes 245768 | tf_op jit(solution)/shard_map/ppermute | solution.py:448
  98.5 27.5 %all-to-all-start.2 = ((bf16[8,272,128]{2,1,0:T(8,128)(2,1)}), bf16[8,272,128]{2,1,0:T(8,128)(2,1)S(1)}, u32[]{:S(2)}, u32[]{:S(2)}) async-start(bf16[8,272,128]{2,1,0:T(8,128)(2,1)} %shard_map.62), calls=%async_computation.2 | async-start | bytes 1114112 | tf_op jit(solution)/shard_map/all_to_all | solution.py:554
